TPU v7x, 512 devices: a whole 4x8x8 slice. The times are simulated.
512 devices in a mesh: dict: 64 (over y_lo, z, core), dp: 8 (over x, y_hi).
Axes of the slice: x: 4, y: 8 (y_hi: 2, y_lo: 4; y = y_hi * 4 + y_lo), z: 8, core: 2. Of those that a mesh axis runs over, the one named last changes fastest.
Arguments:
- activations: bfloat16 [2048, 4608], P('dp', 'dict'), may hold values from -6 to 6
- enc_weight: bfloat16 [4608, 8192], P(None, 'dict'), may hold values from -0.09375 to 0.09375
- enc_bias: bfloat16 [8192], P('dict'), may hold values from -3 to 3
- dec_weight: bfloat16 [8192, 4608], P('dict'), may hold values from -0.125 to 0.125
- dec_bias: bfloat16 [4608], replicated, may hold values from -4 to 4
- thresholds: int32 [8192], P('dict'), may hold values from 4 to 16
- active_blocks: int32 [16, 32], P('dp'), may hold values from 0 to 63, all different within a row
Outputs:
- grad_enc_weight: bfloat16 [4608, 8192], P(None, 'dict')
- grad_dec_weight: bfloat16 [8192, 4608], P('dict')
- grad_enc_bias: bfloat16 [8192], P('dict')
- grad_dec_bias: bfloat16 [4608], replicated
Inputs may be any that keep to these rules, and one draw needn't show every extreme that they name: `active_blocks`: each row lists 32 different blocks, and every block is listed by some row.
All inputs are finite; a program needn't handle non-finite values.
Results may differ from a plain program's by a relative error of at most 0.02.
Values may be sent and summed in bfloat16 or wider, within the bound.
No kernel may reach another device: no remote copies, remote signals or barrier semaphores. Data moves between devices by JAX's collectives and lax.ppermute only.
A program may use at most 64 MiB of HBM per device.

v0:
```python
import math

import jax
import jax.numpy as jnp
from jax import lax
from jax.sharding import PartitionSpec as P

TILE = 128


sharpness = 4.0


def local(activations, enc_weight, enc_bias, dec_weight, dec_bias, thresholds, active_blocks):
    tok_rows = activations.shape[0]
    col_count = activations.shape[1]
    total_rows = tok_rows * lax.axis_size("dp")
    scale_root = math.sqrt(total_rows)
    gathered = lax.all_gather(activations, "dict", axis=1, tiled=True)
    dict_index = lax.axis_index("dict")
    tile_live = jnp.any(active_blocks == dict_index, axis=1).astype(jnp.float32)
    row_live = jnp.repeat(tile_live, TILE)[:, None]
    theta = thresholds.astype(jnp.float32) / 16.0
    bias_enc = enc_bias.astype(jnp.float32)
    forward_pre_act = (
        jnp.dot(gathered, enc_weight, preferred_element_type=jnp.float32) + bias_enc[None, :]
    )
    forward_gate_prob = jax.nn.sigmoid(sharpness * (forward_pre_act - theta[None, :]))
    forward_features = (row_live * forward_pre_act * forward_gate_prob).astype(jnp.bfloat16)
    bias_slice = lax.dynamic_slice_in_dim(dec_bias, dict_index * col_count, col_count).astype(
        jnp.float32
    )
    partial_value = jnp.dot(forward_features, dec_weight, preferred_element_type=jnp.float32)
    recon_share = (
        lax.psum_scatter(partial_value, "dict", scatter_dimension=1, tiled=True)
        + bias_slice[None, :]
    )
    recon_whole = lax.all_gather(
        recon_share.astype(jnp.bfloat16), "dict", axis=1, tiled=True
    ).astype(recon_share.dtype)
    residual = ((recon_whole - gathered.astype(jnp.float32)) / scale_root).astype(jnp.bfloat16)
    dfeat = lax.dot_general(
        residual, dec_weight, (((1,), (1,)), ((), ())), preferred_element_type=jnp.float32
    )
    dpre = (
        dfeat
        * row_live
        * (
            forward_gate_prob
            + sharpness * forward_pre_act * forward_gate_prob * (1.0 - forward_gate_prob)
        )
    )
    dpre_b = dpre.astype(jnp.bfloat16)
    enc_part = lax.dot_general(
        gathered, dpre_b, (((0,), (0,)), ((), ())), preferred_element_type=jnp.float32
    )
    dec_part = lax.dot_general(
        forward_features, residual, (((0,), (0,)), ((), ())), preferred_element_type=jnp.float32
    )
    enc_part, dec_part, ebias_part = (enc_part, dec_part, jnp.sum(dpre, axis=0))
    dbias_part = jnp.sum(residual.astype(jnp.float32), axis=0)
    enc_sum, dec_sum, ebias_sum, dbias_sum = (
        lax.psum(enc_part.astype(jnp.bfloat16), "dp").astype(jnp.float32),
        lax.psum(dec_part.astype(jnp.bfloat16), "dp").astype(jnp.float32),
        lax.psum(ebias_part.astype(jnp.bfloat16), "dp").astype(jnp.float32),
        lax.psum(dbias_part.astype(jnp.bfloat16), "dp").astype(jnp.float32),
    )
    return (
        enc_sum.astype(jnp.bfloat16),
        dec_sum.astype(jnp.bfloat16),
        ebias_sum.astype(jnp.bfloat16),
        dbias_sum.astype(jnp.bfloat16),
    )


def solution(mesh):
    placed = (
        P("dp", "dict"),
        P(None, "dict"),
        P("dict"),
        P("dict", None),
        P(),
        P("dict"),
        P("dp", None),
    )
    return jax.shard_map(
        local,
        mesh=mesh,
        in_specs=placed,
        out_specs=(P(None, "dict"), P("dict", None), P("dict"), P()),
        check_vma=False,
    )
```

profile of v0, /device:TPU:6, one launch (start us, length us, event | category | flops | bytes accessed | tf_op | source)
XLA Modules:
  0.0 777.5 jit_solution(1961752663873189159)
XLA Ops:
  7.2 0.0 copy-start
  7.2 0.0 all-gather.3.cloned.1.call-start
  7.2 0.7 all-gather.3.cloned.1.call-update
  7.9 0.0 reduce-scatter.2.cloned.1.call-start
  8.0 0.8 compare_reduce_fusion
  8.8 0.7 convert_element_type.53
  9.4 0.7 convert_multiply_fusion
  10.1 0.1 broadcast_bitcast_fusion
  10.2 122.5 %all-gather.3.cloned.1.call-done = bf16[256,4608]{0,1:T(8,128)(2,1)} async-done(((bf16[256,72]{0,1:T(8,128)(2,1)}), bf16[256,4608]{0,1:T(8,128)(2,1)}) %all-gather.3.cloned.1.call-update) | async-done | bytes 2359312 | tf_op jit(solution)/shard_map/all_gather | solution.py:19
  132.6 2.8 convolution_add_fusion
  135.5 0.0 copy-start.4
  135.5 0.6 copy-done.4
  136.1 0.0 copy-done
  136.1 3.0 fusion.3
  139.1 0.0 copy-start.1
  139.1 0.0 reduce-scatter.2.cloned.1.call-update
  139.1 0.0 all-gather.5.cloned.1.call-start
  139.2 0.9 dynamic-slice_convert_fusion
  140.1 286.5 %reduce-scatter.2.cloned.1.call-done = f32[256,72]{0,1:T(8,128)} async-done(((f32[256,4608]{0,1:T(8,128)}), f32[256,72]{0,1:T(8,128)}) %reduce-scatter.2.cloned.1.call-update) | async-done | bytes 73744 | tf_op jit(solution)/shard_map/reduce_scatter | solution.py:35
  426.6 1.6 add_convert_fusion
  428.2 0.0 all-gather.5.cloned.1.call-update
  428.2 0.0 all-reduce.4.cloned.1.call-start
  428.3 112.1 %all-gather.5.cloned.1.call-done = bf16[256,4608]{0,1:T(8,128)(2,1)} async-done(((bf16[256,72]{0,1:T(8,128)(2,1)}), bf16[256,4608]{0,1:T(8,128)(2,1)}) %all-gather.5.cloned.1.call-update) | async-done | bytes 2359312 | tf_op jit(solution)/shard_map/all_gather | solution.py:38
  540.3 0.0 copy-done.1
  540.3 0.0 copy-start.2
  540.3 0.0 copy-start.5
  540.3 2.7 fusion.5
  543.1 0.0 copy-done.2
  543.1 0.0 copy-done.5
  543.1 2.1 convolution_convert_fusion
  545.2 1.9 fusion
  547.1 0.0 all-reduce.4.cloned.1.call-update
  547.1 2.5 fusion.4
  549.7 53.9 %all-reduce = (bf16[128]{0:T(256)(128)(2,1)}, bf16[4608]{0:T(1024)(128)(2,1)}) all-reduce(bf16[128]{0:T(256)(128)(2,1)S(1)} %get-tuple-element.12, bf16[4608]{0:T(1024)(128)(2,1)S(1)} %fusion.4), channel_id=1, replica_groups=mesh['dict'=64,'dp'=8] {'dp'}, use_global_device_ids=true, to_apply=%region_5.0 | all-reduce | flops 4736 | bytes 18944 | tf_op jit(solution)/shard_map/psum | solution.py:65
  603.6 163.9 %all-reduce.4.cloned.1.call-done = (bf16[4608,128]{0,1:T(8,128)(2,1)}, bf16[128,4608]{1,0:T(8,128)(2,1)}) async-done(((bf16[4608,128]{0,1:T(8,128)(2,1)}, bf16[128,4608]{1,0:T(8,128)(2,1)}), (bf16[4608,128]{0,1:T(8,128)(2,1)}, bf16[128,4608]{1,0:T(8,128)(2,1)})) %all-reduce.4.cloned.1.call-update) | async-done | bytes 2359312 | tf_op jit(solution)/shard_map/psum | solution.py:63
  767.5 0.0 copy-start.3
  767.5 2.5 copy.11
  769.9 0.0 copy-done.3
  769.9 1.0 copy.14
  (1 shorter events, 0.0 us)
Async XLA Ops:
  7.2 129.0 %copy-start = (bf16[128,4608]{1,0:T(8,128)(2,1)S(1)}, bf16[128,4608]{1,0:T(8,128)(2,1)}, u32[]{:S(2)}) copy-start(bf16[128,4608]{1,0:T(8,128)(2,1)} %param.10) | copy-start | bytes 3538948
  7.2 125.5 %all-gather.3.cloned.1.call-start = ((), (), s32[]{:S(2)}) async-start(), calls=%async_computation.1 | async-start | bytes 2396160 | tf_op jit(solution)/shard_map/all_gather | solution.py:19
  7.9 418.7 %reduce-scatter.2.cloned.1.call-start = ((), (), s32[]{:S(2)}) async-start(), calls=%async_computation.2 | async-start | bytes 4792320 | tf_op jit(solution)/shard_map/reduce_scatter | solution.py:35
  135.5 0.7 copy-start.4
  139.1 401.2 %copy-start.1 = (bf16[256,4608]{0,1:T(8,128)(2,1)S(1)}, bf16[256,4608]{0,1:T(8,128)(2,1)}, u32[]{:S(2)}) copy-start(bf16[256,4608]{0,1:T(8,128)(2,1)} %all-gather.3.cloned.1.call-done) | copy-start | bytes 7077892
  139.1 401.2 %all-gather.5.cloned.1.call-start = ((), (), s32[]{:S(2)}) async-start(), calls=%async_computation.3 | async-start | bytes 2396160 | tf_op jit(solution)/shard_map/all_gather | solution.py:38
  428.2 339.3 %all-reduce.4.cloned.1.call-start = ((), (), s32[]{:S(2)}) async-start(), calls=%async_computation.4 | async-start | bytes 4718592 | tf_op jit(solution)/shard_map/psum | solution.py:63
  540.3 2.7 copy-start.2
  540.3 2.7 copy-start.5
  767.5 2.5 copy-start.3
Sparse Core Ops, SparseCore 0:
  10.2 122.4 all-gather.2
  139.3 287.2 reduce-scatter.1
  429.3 110.9 all-gather.4
  547.3 220.1 all-reduce.3
where the time goes:
time: 778 us; the launch traced here: 777 us
  waiting for transfers between devices  686 us (88%)
  blocking collectives  53.9 us (7%)
  between operations  13.8 us (2%)
  matrix products  12.6 us (2%)
    reduce_scatter x1, waiting for transfers between devices, local(): lax.psum_scatter(partial_value, 'dict', scatter_dimension=1, tiled=True)  286 us
    psum x1, waiting for transfers between devices, local(): lax.psum(enc_part.astype(jnp.bfloat16), 'dp').astype(jnp.float32)  164 us
    all_gather x1, waiting for transfers between devices, local(): gathered = lax.all_gather(activations, 'dict', axis=1, tiled=True)  122 us
    all_gather x1, waiting for transfers between devices, local(): lax.all_gather(recon_share.astype(jnp.bfloat16), 'dict', axis=1, tiled=True)  112 us
    psum x1, blocking collectives, local(): lax.psum(ebias_part.astype(jnp.bfloat16), 'dp').astype(jnp.float32)  53.9 us
  transfers between devices with their start and end apart: 4, of which 4 were waited for; matrix products, arithmetic and copies ran while one was open for 1% of the time, Pallas kernels for 0%

commit v1 on v0

v1 whole, which is shorter than its diff:
```python
import math

import jax
import jax.numpy as jnp
import numpy as np
from jax import lax
from jax.sharding import PartitionSpec as P

TILE = 128
SHARPNESS = 4.0
F32 = jnp.float32
BF16 = jnp.bfloat16

GRID = (2, 2, 4, 2, 2)
FAR, NEAR, CORE = (0, 2), (1, 3), (4,)


def groups(axes):
    index = np.arange(math.prod(GRID)).reshape(GRID)
    rest = [axis for axis in range(len(GRID)) if axis not in axes]
    size = math.prod(GRID[axis] for axis in axes)
    return index.transpose(rest + list(axes)).reshape(-1, size).tolist()


def exchange(parts, axes):
    return lax.all_to_all(parts, "dict", 0, 0, axis_index_groups=groups(axes))


def spread(block, axes):
    size = math.prod(GRID[axis] for axis in axes)
    return exchange(jnp.broadcast_to(block[None], (size,) + block.shape), axes)


def gather_dict(block):
    whole = spread(spread(spread(block, FAR), NEAR), CORE)
    whole = whole.reshape((2, 2, 2, 2, 4) + block.shape)
    return whole.transpose(3, 1, 4, 2, 0, 5, 6).reshape(-1, block.shape[1])


def scatter_dict(total):
    cols, rows = total.shape[0] // math.prod(GRID), total.shape[1]
    parts = total.reshape(GRID + (cols, rows)).transpose(4, 1, 3, 0, 2, 5, 6)
    for axes in (CORE, NEAR, FAR):
        size = math.prod(GRID[axis] for axis in axes)
        parts = exchange(parts.astype(BF16).reshape(size, -1, rows), axes)
        parts = jnp.sum(parts.astype(F32), axis=0)
    return parts


def sum_dp(partial, count):
    parts = lax.all_to_all(partial.reshape(count, -1, partial.shape[1]), "dp", 0, 0)
    mine = jnp.sum(parts.astype(F32), axis=0).astype(BF16)
    whole = lax.all_to_all(jnp.broadcast_to(mine[None], (count,) + mine.shape), "dp", 0, 0)
    return whole.reshape(partial.shape)


def local(activations, enc_weight, enc_bias, dec_weight, dec_bias, thresholds, active_blocks):
    n_dp = lax.axis_size("dp")
    scale_root = math.sqrt(activations.shape[0] * n_dp)
    own = activations.T
    cols = own.shape[0]
    act = gather_dict(own)
    dict_index = lax.axis_index("dict")
    tile_live = jnp.any(active_blocks == dict_index, axis=1).astype(F32)
    row_live = jnp.repeat(tile_live, TILE)[:, None]
    theta = thresholds.astype(F32) / 16.0
    pre = lax.dot_general(act, enc_weight, (((0,), (0,)), ((), ())), preferred_element_type=F32)
    pre = pre + enc_bias.astype(F32)[None, :]
    gate = jax.nn.sigmoid(SHARPNESS * (pre - theta[None, :]))
    features = (row_live * pre * gate).astype(BF16)

    partial = lax.dot_general(
        dec_weight, features, (((0,), (1,)), ((), ())), preferred_element_type=F32
    ).astype(BF16)
    bias = lax.dynamic_slice_in_dim(dec_bias, dict_index * cols, cols).astype(F32)
    recon = scatter_dict(partial) + bias[:, None]
    residual = gather_dict(((recon - own.astype(F32)) / scale_root).astype(BF16))

    dec_part = lax.dot_general(
        features, residual, (((0,), (1,)), ((), ())), preferred_element_type=F32
    ).astype(BF16)
    dfeat = lax.dot_general(
        residual, dec_weight, (((0,), (1,)), ((), ())), preferred_element_type=F32
    )
    dpre = dfeat * row_live * (gate + SHARPNESS * pre * gate * (1.0 - gate))
    enc_part = lax.dot_general(
        act, dpre.astype(BF16), (((1,), (0,)), ((), ())), preferred_element_type=F32
    ).astype(BF16)
    bias_part = jnp.concatenate(
        [jnp.sum(dpre, axis=0), jnp.sum(residual.astype(F32), axis=1)]
    ).astype(BF16)
    bias_part = bias_part.reshape(-1, TILE)
    bias_parts = lax.all_to_all(
        jnp.broadcast_to(bias_part[None], (n_dp,) + bias_part.shape), "dp", 0, 0
    )
    bias_sum = jnp.sum(bias_parts.astype(F32), axis=0).astype(BF16)
    return (
        sum_dp(enc_part, n_dp),
        sum_dp(dec_part, n_dp),
        bias_sum[0],
        bias_sum[1:].reshape(-1),
    )


def solution(mesh):
    placed = (
        P("dp", "dict"),
        P(None, "dict"),
        P("dict"),
        P("dict", None),
        P(),
        P("dict"),
        P("dp", None),
    )
    return jax.shard_map(
        local,
        mesh=mesh,
        in_specs=placed,
        out_specs=(P(None, "dict"), P("dict", None), P("dict"), P()),
        check_vma=False,
    )
```

time: 778 us -> 305 us (0.39)
  the two profiles are of different devices: /device:TPU:6 before, /device:TPU:8 now
where the time goes in v1:
time: 305 us; the launch traced here: 303 us
  waiting for transfers between devices  133 us (44%)
  blocking collectives  96.1 us (32%)
  starting transfers between devices  34.3 us (11%)
  local copies, waits for them, and re-layouts  18.8 us (6%)
  matrix products  12.1 us (4%)
  other arithmetic  8.11 us (3%)
    all_to_all x7, blocking collectives, exchange(): return lax.all_to_all(parts, 'dict', 0, 0, axis_index_groups=groups(axes))  96.1 us
    all_to_all x2, waiting for transfers between devices, sum_dp(): lax.all_to_all(partial.reshape(count, -1, partial.shape[1]), 'dp', 0, 0)  59.2 us
    all_to_all x2, waiting for transfers between devices, sum_dp(): lax.all_to_all(jnp.broadcast_to(mine[None], (count,) + mine.shape), 'dp',...  42.7 us
    all_to_all x2, waiting for transfers between devices, exchange(): return lax.all_to_all(parts, 'dict', 0, 0, axis_index_groups=groups(axes))  23.7 us
    all_to_all x2, starting transfers between devices, exchange(): return lax.all_to_all(parts, 'dict', 0, 0, axis_index_groups=groups(axes))  9.67 us
    all_to_all x1, starting transfers between devices, local(): lax.all_to_all(jnp.broadcast_to(bias_part[None], (n_dp,) + bias_part.shap...  9.35 us
    all_to_all x2, starting transfers between devices, sum_dp(): lax.all_to_all(partial.reshape(count, -1, partial.shape[1]), 'dp', 0, 0)  8.19 us
    all_to_all x1, waiting for transfers between devices, local(): lax.all_to_all(jnp.broadcast_to(bias_part[None], (n_dp,) + bias_part.shap...  7.58 us
  transfers between devices with their start and end apart: 7, of which 7 were waited for; matrix products, arithmetic and copies ran while one was open for 4% of the time, Pallas kernels for 0%

profile of v1, /device:TPU:8, one launch (start us, length us, event | category | flops | bytes accessed | tf_op | source)
XLA Modules:
  0.0 303.4 jit_solution(13866188513097158201)
XLA Ops:
  0.6 0.9 broadcast_in_dim.21
  1.5 24.7 %all_to_all.70 = bf16[8,72,256]{2,1,0:T(8,128)(2,1)S(1)} all-to-all(bf16[8,72,256]{2,1,0:T(8,128)(2,1)S(1)} %broadcast_in_dim.21), channel_id=1, replica_groups={{0,32,64,96,256,288,320,352},{8,40,72,104,264,296,328,360},{16,48,80,11..., dimensions={0} | all-to-all | bytes 589824 | tf_op jit(solution)/shard_map/all_to_all | solution.py:26
  26.2 1.1 broadcast_in_dim.22
  27.3 6.2 %all-to-all-start.1 = ((bf16[4,8,72,256]{3,2,1,0:T(8,128)(2,1)}), bf16[4,8,72,256]{3,2,1,0:T(8,128)(2,1)S(1)}, u32[]{:S(2)}, u32[]{:S(2)}) async-start(bf16[4,8,72,256]{3,2,1,0:T(8,128)(2,1)} %broadcast_in_dim.22), calls=%async_computation.1 | async-start | bytes 2359296 | tf_op jit(solution)/shard_map/all_to_all | solution.py:26
  33.7 12.9 %all-to-all-done.1 = bf16[4,8,72,256]{3,2,1,0:T(8,128)(2,1)S(1)} async-done(((bf16[4,8,72,256]{3,2,1,0:T(8,128)(2,1)}), bf16[4,8,72,256]{3,2,1,0:T(8,128)(2,1)S(1)}, u32[]{:S(2)}, u32[]{:S(2)}) %all-to-all-start.1) | async-done | bytes 1179680 | tf_op jit(solution)/shard_map/all_to_all | solution.py:26
  46.7 5.6 %all_to_all.71 = bf16[2,4,8,72,256]{4,3,2,1,0:T(8,128)(2,1)S(1)} all-to-all(bf16[2,4,8,72,256]{4,3,2,1,0:T(8,128)(2,1)S(1)} %broadcast_in_dim.23), channel_id=1, replica_groups={{0,8},{16,24},{32,40},{48,56},{64,72},{80,88},{96,104},{112,120},{128,1..., dimensions={0} | all-to-all | bytes 4718592 | tf_op jit(solution)/shard_map/all_to_all | solution.py:26
  52.6 1.3 copy-done.5
  53.9 0.8 convolution_add_fusion
  54.8 0.6 copy-done.4
  55.4 2.2 fusion
  57.6 2.8 copy.37
  60.5 0.2 copy.38
  60.7 5.6 %all_to_all.72 = bf16[2,2304,256]{2,1,0:T(8,128)(2,1)S(1)} all-to-all(bf16[2,2304,256]{2,1,0:T(8,128)(2,1)S(1)} %bitcast.48), channel_id=1, replica_groups={{0,8},{16,24},{32,40},{48,56},{64,72},{80,88},{96,104},{112,120},{128,1..., dimensions={0} | all-to-all | bytes 4718592 | tf_op jit(solution)/shard_map/all_to_all | solution.py:26
  66.3 1.8 reduce_sum.89
  68.1 19.1 %all_to_all.73 = bf16[4,576,256]{2,1,0:T(8,128)(2,1)S(1)} all-to-all(bf16[4,576,256]{2,1,0:T(8,128)(2,1)} %bitcast.52), channel_id=1, replica_groups={{0,16,128,144},{8,24,136,152},{32,48,160,176},{40,56,168,184},{64,80,19..., dimensions={0} | all-to-all | bytes 2359296 | tf_op jit(solution)/shard_map/all_to_all | solution.py:26
  87.2 0.9 reduce_sum.90
  88.2 3.5 %all-to-all-start.5 = ((bf16[8,72,256]{2,1,0:T(8,128)(2,1)}), bf16[8,72,256]{2,1,0:T(8,128)(2,1)S(1)}, u32[]{:S(2)}, u32[]{:S(2)}) async-start(bf16[8,72,256]{2,1,0:T(8,128)(2,1)} %bitcast.10), calls=%async_computation.5 | async-start | bytes 589824 | tf_op jit(solution)/shard_map/all_to_all | solution.py:26
  91.6 0.8 dynamic-slice_convert_fusion
  92.4 10.9 %all-to-all-done.5 = bf16[8,72,256]{2,1,0:T(8,128)(2,1)S(1)} async-done(((bf16[8,72,256]{2,1,0:T(8,128)(2,1)}), bf16[8,72,256]{2,1,0:T(8,128)(2,1)S(1)}, u32[]{:S(2)}, u32[]{:S(2)}) %all-to-all-start.5) | async-done | bytes 294944 | tf_op jit(solution)/shard_map/all_to_all | solution.py:26
  103.4 16.7 %all_to_all.74 = bf16[8,72,256]{2,1,0:T(8,128)(2,1)S(1)} all-to-all(bf16[8,72,256]{2,1,0:T(8,128)(2,1)S(1)} %broadcast_in_dim.24), channel_id=1, replica_groups={{0,32,64,96,256,288,320,352},{8,40,72,104,264,296,328,360},{16,48,80,11..., dimensions={0} | all-to-all | bytes 589824 | tf_op jit(solution)/shard_map/all_to_all | solution.py:26
  120.3 18.7 %all_to_all.75 = bf16[4,8,72,256]{3,2,1,0:T(8,128)(2,1)S(1)} all-to-all(bf16[4,8,72,256]{3,2,1,0:T(8,128)(2,1)S(1)} %broadcast_in_dim.25), channel_id=1, replica_groups={{0,16,128,144},{8,24,136,152},{32,48,160,176},{40,56,168,184},{64,80,19..., dimensions={0} | all-to-all | bytes 2359296 | tf_op jit(solution)/shard_map/all_to_all | solution.py:26
  139.1 5.6 %all_to_all.76 = bf16[2,4,8,72,256]{4,3,2,1,0:T(8,128)(2,1)S(1)} all-to-all(bf16[2,4,8,72,256]{4,3,2,1,0:T(8,128)(2,1)S(1)} %broadcast_in_dim.26), channel_id=1, replica_groups={{0,8},{16,24},{32,40},{48,56},{64,72},{80,88},{96,104},{112,120},{128,1..., dimensions={0} | all-to-all | bytes 4718592 | tf_op jit(solution)/shard_map/all_to_all | solution.py:26
  144.7 1.2 reduce.6
  145.9 1.6 copy.39
  147.7 3.3 %fusion.4 = (bf16[128]{0:T(256)(128)(2,1)S(1)}, bf16[256,128]{1,0:T(8,128)(2,1)}) fusion(f32[256,128]{1,0:T(8,128)} %copy-done.4, f32[128]{0:T(128)} %copy-done.9, f32[256]{0:T(256)} %copy-done.7, bf16[4608,256]{1,0:T(8,128)(2,1)} %bitcast.44, bf16[128,4608]{1,0:T(8,128)(2,1)S(1)} %copy-done), kind=kOutput, calls=%fused_computation.20 | convolution fusion | flops 302448512 | bytes 3737344 | tf_op jit(solution)/shard_map/dot_general | solution.py:82
  151.0 0.6 broadcast_in_dim.29
  151.7 9.4 %all-to-all-start.13 = ((bf16[8,37,128]{2,1,0:T(8,128)(2,1)}), bf16[8,37,128]{2,1,0:T(8,128)(2,1)}, u32[]{:S(2)}, u32[]{:S(2)}) async-start(bf16[8,37,128]{2,1,0:T(8,128)(2,1)} %broadcast_in_dim.29), calls=%async_computation.13 | async-start | bytes 163840 | tf_op jit(solution)/shard_map/all_to_all | solution.py:93
  161.1 2.9 convolution_convert_fusion.1
  164.0 7.6 %all-to-all-done.13 = bf16[8,37,128]{2,1,0:T(8,128)(2,1)} async-done(((bf16[8,37,128]{2,1,0:T(8,128)(2,1)}), bf16[8,37,128]{2,1,0:T(8,128)(2,1)}, u32[]{:S(2)}, u32[]{:S(2)}) %all-to-all-start.13) | async-done | bytes 75808 | tf_op jit(solution)/shard_map/all_to_all | solution.py:93
  171.5 4.4 %all-to-all-start.11 = ((bf16[8,16,4608]{2,1,0:T(8,128)(2,1)}), bf16[8,16,4608]{2,1,0:T(8,128)(2,1)}, u32[]{:S(2)}, u32[]{:S(2)}) async-start(bf16[8,16,4608]{2,1,0:T(8,128)(2,1)} %bitcast.51), calls=%async_computation.11 | async-start | bytes 2359296 | tf_op jit(solution)/shard_map/all_to_all | solution.py:51
  175.9 2.8 fusion.1
  178.7 2.4 copy.40
  181.1 27.7 %all-to-all-done.11 = bf16[8,16,4608]{2,1,0:T(8,128)(2,1)} async-done(((bf16[8,16,4608]{2,1,0:T(8,128)(2,1)}), bf16[8,16,4608]{2,1,0:T(8,128)(2,1)}, u32[]{:S(2)}, u32[]{:S(2)}) %all-to-all-start.11) | async-done | bytes 1179680 | tf_op jit(solution)/shard_map/all_to_all | solution.py:51
  208.8 3.8 %all-to-all-start.9 = ((bf16[8,576,128]{2,1,0:T(8,128)(2,1)}), bf16[8,576,128]{2,1,0:T(8,128)(2,1)S(1)}, u32[]{:S(2)}, u32[]{:S(2)}) async-start(bf16[8,576,128]{2,1,0:T(8,128)(2,1)} %bitcast.15), calls=%async_computation.9 | async-start | bytes 2359296 | tf_op jit(solution)/shard_map/all_to_all | solution.py:51
  212.6 1.4 reduce_sum.93
  214.0 31.5 %all-to-all-done.9 = bf16[8,576,128]{2,1,0:T(8,128)(2,1)S(1)} async-done(((bf16[8,576,128]{2,1,0:T(8,128)(2,1)}), bf16[8,576,128]{2,1,0:T(8,128)(2,1)S(1)}, u32[]{:S(2)}, u32[]{:S(2)}) %all-to-all-start.9) | async-done | bytes 1179680 | tf_op jit(solution)/shard_map/all_to_all | solution.py:51
  245.5 1.1 broadcast_in_dim.28
  246.6 3.6 %all-to-all-start.12 = ((bf16[8,16,4608]{2,1,0:T(8,128)(2,1)}), bf16[8,16,4608]{2,1,0:T(8,128)(2,1)S(1)}, u32[]{:S(2)}, u32[]{:S(2)}) async-start(bf16[8,16,4608]{2,1,0:T(8,128)(2,1)} %broadcast_in_dim.28), calls=%async_computation.12 | async-start | bytes 2359296 | tf_op jit(solution)/shard_map/all_to_all | solution.py:53
  250.2 0.8 reduce_sum.92
  251.0 26.0 %all-to-all-done.12 = bf16[8,16,4608]{2,1,0:T(8,128)(2,1)S(1)} async-done(((bf16[8,16,4608]{2,1,0:T(8,128)(2,1)}), bf16[8,16,4608]{2,1,0:T(8,128)(2,1)S(1)}, u32[]{:S(2)}, u32[]{:S(2)}) %all-to-all-start.12) | async-done | bytes 1179680 | tf_op jit(solution)/shard_map/all_to_all | solution.py:53
  277.0 2.1 broadcast_in_dim.27
  279.1 3.6 %all-to-all-start.10 = ((bf16[8,576,128]{2,1,0:T(8,128)(2,1)}), bf16[8,576,128]{2,1,0:T(8,128)(2,1)S(1)}, u32[]{:S(2)}, u32[]{:S(2)}) async-start(bf16[8,576,128]{2,1,0:T(8,128)(2,1)} %broadcast_in_dim.27), calls=%async_computation.10 | async-start | bytes 2359296 | tf_op jit(solution)/shard_map/all_to_all | solution.py:53
  282.6 0.9 reduce_sum.97
  283.5 0.5 slice_bitcast_fusion.1
  284.1 0.6 slice_bitcast_fusion
  284.7 16.8 %all-to-all-done.10 = bf16[8,576,128]{2,1,0:T(8,128)(2,1)S(1)} async-done(((bf16[8,576,128]{2,1,0:T(8,128)(2,1)}), bf16[8,576,128]{2,1,0:T(8,128)(2,1)S(1)}, u32[]{:S(2)}, u32[]{:S(2)}) %all-to-all-start.10) | async-done | bytes 1179680 | tf_op jit(solution)/shard_map/all_to_all | solution.py:53
  301.4 1.0 copy.48
  302.4 1.0 copy.49
  (39 shorter events, 1.1 us)
Async XLA Ops:
  0.6 54.8 %copy-start = (bf16[128,4608]{1,0:T(8,128)(2,1)S(1)}, bf16[128,4608]{1,0:T(8,128)(2,1)}, u32[]{:S(2)}) copy-start(bf16[128,4608]{1,0:T(8,128)(2,1)} %param.10) | copy-start | bytes 3538948
  27.3 6.2 %copy-start.10 = (s32[2,32]{1,0:T(2,128)S(1)}, s32[2,32]{1,0:T(2,128)}, u32[]{:S(2)}) copy-start(s32[2,32]{1,0:T(2,128)} %param.13) | copy-start | bytes 772
  27.3 6.3 %copy-start.11 = (bf16[128]{0:T(256)(128)(2,1)S(1)}, bf16[128]{0:T(256)(128)(2,1)}, u32[]{:S(2)}) copy-start(bf16[128]{0:T(256)(128)(2,1)} %param.9) | copy-start | bytes 772
  27.3 6.3 %copy-start.12 = (s32[128]{0:T(128)S(1)}, s32[128]{0:T(128)}, u32[]{:S(2)}) copy-start(s32[128]{0:T(128)} %param.12) | copy-start | bytes 1540
  27.3 19.3 %all-to-all-start.1 = ((bf16[4,8,72,256]{3,2,1,0:T(8,128)(2,1)}), bf16[4,8,72,256]{3,2,1,0:T(8,128)(2,1)S(1)}, u32[]{:S(2)}, u32[]{:S(2)}) async-start(bf16[4,8,72,256]{3,2,1,0:T(8,128)(2,1)} %broadcast_in_dim.22), calls=%async_computation.1 | async-start | bytes 2359296 | tf_op jit(solution)/shard_map/all_to_all | solution.py:26
  33.6 21.1 %copy-start.9 = (f32[128]{0:T(128)}, f32[128]{0:T(128)S(1)}, u32[]{:S(2)}) copy-start(f32[128]{0:T(128)S(1)} %convert_multiply_fusion) | copy-start | bytes 1540
  33.7 21.0 %copy-start.7 = (f32[256]{0:T(256)}, f32[256]{0:T(256)S(1)}, u32[]{:S(2)}) copy-start(f32[256]{0:T(256)S(1)} %broadcast_bitcast_fusion) | copy-start | bytes 3076
  52.4 1.5 copy-start.5
  52.6 2.1 copy-start.1
  54.7 0.7 copy-start.4
  87.2 16.1 %copy-start.6 = (bf16[256,72]{0,1:T(8,128)(2,1)S(1)}, bf16[256,72]{0,1:T(8,128)(2,1)}, u32[]{:S(2)}) copy-start(bf16[256,72]{0,1:T(8,128)(2,1)} %param.7) | copy-start | bytes 110596
  88.2 15.1 %all-to-all-start.5 = ((bf16[8,72,256]{2,1,0:T(8,128)(2,1)}), bf16[8,72,256]{2,1,0:T(8,128)(2,1)S(1)}, u32[]{:S(2)}, u32[]{:S(2)}) async-start(bf16[8,72,256]{2,1,0:T(8,128)(2,1)} %bitcast.10), calls=%async_computation.5 | async-start | bytes 589824 | tf_op jit(solution)/shard_map/all_to_all | solution.py:26
  147.7 13.4 %copy-start.3 = (bf16[2,2,4,2,2,72,256]{6,5,4,3,2,1,0:T(8,128)(2,1)S(1)}, bf16[2,2,4,2,2,72,256]{6,5,4,3,2,1,0:T(8,128)(2,1)}, u32[]{:S(2)}) copy-start(bf16[2,2,4,2,2,72,256]{6,5,4,3,2,1,0:T(8,128)(2,1)} %copy.39) | copy-start | bytes 7077892
  147.7 13.4 %copy-start.8 = (f32[256]{0:T(256)S(1)}, f32[256]{0:T(256)}, u32[]{:S(2)}) copy-start(f32[256]{0:T(256)} %copy-done.7) | copy-start | bytes 3076
  151.7 19.8 %all-to-all-start.13 = ((bf16[8,37,128]{2,1,0:T(8,128)(2,1)}), bf16[8,37,128]{2,1,0:T(8,128)(2,1)}, u32[]{:S(2)}, u32[]{:S(2)}) async-start(bf16[8,37,128]{2,1,0:T(8,128)(2,1)} %broadcast_in_dim.29), calls=%async_computation.13 | async-start | bytes 163840 | tf_op jit(solution)/shard_map/all_to_all | solution.py:93
  171.5 4.4 %copy-start.2 = (bf16[2,2,4,2,2,72,256]{6,5,4,3,2,1,0:T(8,128)(2,1)S(1)}, bf16[2,2,4,2,2,72,256]{6,5,4,3,2,1,0:T(8,128)(2,1)}, u32[]{:S(2)}) copy-start(bf16[2,2,4,2,2,72,256]{6,5,4,3,2,1,0:T(8,128)(2,1)} %copy-done.1) | copy-start | bytes 7077892
  171.5 37.2 %all-to-all-start.11 = ((bf16[8,16,4608]{2,1,0:T(8,128)(2,1)}), bf16[8,16,4608]{2,1,0:T(8,128)(2,1)}, u32[]{:S(2)}, u32[]{:S(2)}) async-start(bf16[8,16,4608]{2,1,0:T(8,128)(2,1)} %bitcast.51), calls=%async_computation.11 | async-start | bytes 2359296 | tf_op jit(solution)/shard_map/all_to_all | solution.py:51
  208.8 36.7 %all-to-all-start.9 = ((bf16[8,576,128]{2,1,0:T(8,128)(2,1)}), bf16[8,576,128]{2,1,0:T(8,128)(2,1)S(1)}, u32[]{:S(2)}, u32[]{:S(2)}) async-start(bf16[8,576,128]{2,1,0:T(8,128)(2,1)} %bitcast.15), calls=%async_computation.9 | async-start | bytes 2359296 | tf_op jit(solution)/shard_map/all_to_all | solution.py:51
  246.6 30.4 %all-to-all-start.12 = ((bf16[8,16,4608]{2,1,0:T(8,128)(2,1)}), bf16[8,16,4608]{2,1,0:T(8,128)(2,1)S(1)}, u32[]{:S(2)}, u32[]{:S(2)}) async-start(bf16[8,16,4608]{2,1,0:T(8,128)(2,1)} %broadcast_in_dim.28), calls=%async_computation.12 | async-start | bytes 2359296 | tf_op jit(solution)/shard_map/all_to_all | solution.py:53
  279.1 22.4 %all-to-all-start.10 = ((bf16[8,576,128]{2,1,0:T(8,128)(2,1)}), bf16[8,576,128]{2,1,0:T(8,128)(2,1)S(1)}, u32[]{:S(2)}, u32[]{:S(2)}) async-start(bf16[8,576,128]{2,1,0:T(8,128)(2,1)} %broadcast_in_dim.27), calls=%async_computation.10 | async-start | bytes 2359296 | tf_op jit(solution)/shard_map/all_to_all | solution.py:53

commit v2 on v1

v2 whole, which is shorter than its diff:
```python
import math

import jax
import jax.numpy as jnp
import numpy as np
from jax import lax
from jax.experimental import pallas as pl
from jax.experimental.pallas import tpu as pltpu
from jax.sharding import PartitionSpec as P

TILE = 128
SHARPNESS = 4.0
F32 = jnp.float32
BF16 = jnp.bfloat16

GRID = (2, 2, 4, 2, 2)
FAR, NEAR, CORE = (0, 2), (1, 3), (4,)
CHIPS = 32
NX = 4
BIAS_ROWS = 48
VMEM = 48 * 1024 * 1024


def size_of(axes):
    return math.prod(GRID[axis] for axis in axes)


def groups(axes):
    index = np.arange(math.prod(GRID)).reshape(GRID)
    rest = [axis for axis in range(len(GRID)) if axis not in axes]
    return index.transpose(rest + list(axes)).reshape(-1, size_of(axes)).tolist()


X_GROUPS = np.arange(8).reshape(NX, 2).T.tolist()
CORE_SWAP = [(i, i ^ 1) for i in range(64)]
Y_SWAP = [(i, i ^ 1) for i in range(8)]


def exchange(parts, axes):
    return lax.all_to_all(parts, "dict", 0, 0, axis_index_groups=groups(axes))


def spread(block, axes):
    return exchange(jnp.broadcast_to(block[None], (size_of(axes),) + block.shape), axes)


def gather_chips(block):
    return spread(spread(block, FAR), NEAR)


def chip_blocks():
    for near in range(4):
        for far in range(8):
            y, z = (far // 4) * 2 + near // 2, (far % 4) * 2 + near % 2
            yield near, far, y * 8 + z


def in_order(parts_ref, whole_ref):
    cols = parts_ref.shape[2]
    for near, far, chip in chip_blocks():
        whole_ref[chip * cols : (chip + 1) * cols, :] = parts_ref[near, far]


def dot(a, b, dims):
    return lax.dot_general(a, b, (dims, ((), ())), preferred_element_type=F32)


def forward_kernel(
    act_ref, we_own, we_other, wd_own, wd_other, row_ref, parts_ref, feat_ref, slope_ref, act
):
    in_order(act_ref, act)
    for n, we in enumerate((we_own, we_other)):
        lanes = slice(n * TILE, (n + 1) * TILE)
        bias, theta, live = row_ref[0:1, lanes], row_ref[1:2, lanes], row_ref[2:3, lanes]
        pre = dot(act[...], we[...], ((0,), (0,))) + bias
        gate = jax.nn.sigmoid(SHARPNESS * (pre - theta))
        feat_ref[:, lanes] = (live * pre * gate).astype(BF16)
        slope_ref[:, lanes] = live * (gate + SHARPNESS * pre * gate * (1.0 - gate))
    cols = parts_ref.shape[2]
    step = 8 * cols
    place = {chip: (near, far) for near, far, chip in chip_blocks()}
    for first in range(0, act.shape[0], step):
        span = slice(first, first + step)
        total = dot(feat_ref[:, :TILE], wd_own[:, span], ((1,), (0,)))
        total = total + dot(feat_ref[:, TILE:], wd_other[:, span], ((1,), (0,)))
        turned = total.astype(BF16).T
        for i in range(8):
            near, far = place[first // cols + i]
            parts_ref[near, far] = turned[i * cols : (i + 1) * cols, :]


def backward_kernel(
    res_ref, act_ref, wd_own, wd_other, feat_ref, slope_ref, own_ref, other_ref, act, res, bias
):
    in_order(act_ref, act)
    in_order(res_ref, res)
    d = act.shape[0]
    quarter, lat = d // NX, TILE // NX
    res_t = res[...].T
    feat_t = jnp.concatenate([feat_ref[...].T, jnp.ones((16, TILE), BF16)], axis=0)
    bias[...] = jnp.zeros_like(bias)
    for i in range(d // TILE):
        tile = dot(feat_t, res[i * TILE : (i + 1) * TILE, :], ((1,), (1,)))
        bias[i + 1 : i + 2, :] = tile[2 * TILE : 2 * TILE + 1, :]
        tile = tile.astype(BF16)
        for x in range(NX):
            rows = slice(quarter + i * lat, quarter + (i + 1) * lat)
            own_ref[x, rows, :] = tile[x * lat : (x + 1) * lat, :]
            other_ref[x, rows, :] = tile[TILE + x * lat : TILE + (x + 1) * lat, :]
    for n, (wd, out) in enumerate(((wd_own, own_ref), (wd_other, other_ref))):
        dfeat = dot(res_t, wd[...], ((1,), (1,)))
        dpre = dfeat * slope_ref[:, n * TILE : (n + 1) * TILE]
        bias[0:1, :] = jnp.sum(dpre, axis=0, keepdims=True)
        dpre = dpre.astype(BF16)
        rows = bias[...].astype(BF16)
        for x in range(NX):
            enc = dot(act[x * quarter : (x + 1) * quarter, :], dpre, ((1,), (0,)))
            out[x, :quarter, :] = enc.astype(BF16)
            out[x, 2 * quarter :, :] = rows


def unpack_kernel(first_ref, second_ref, third_ref, enc_ref, dec_ref):
    quarter, lat = enc_ref.shape[0] // NX, TILE // NX
    size = first_ref.shape[1]
    rest = quarter - size
    for x in range(NX):
        enc_ref[x * quarter : x * quarter + size, :] = first_ref[x]
        enc_ref[x * quarter + size : (x + 1) * quarter, :] = second_ref[x, :rest, :]
        for i in range(enc_ref.shape[0] // TILE):
            at = rest + i * lat
            ref = second_ref if at < size else third_ref
            at = at % size
            dec_ref[x * lat : (x + 1) * lat, i * TILE : (i + 1) * TILE] = ref[x, at : at + lat, :]


def call(kernel, outs, args, scratch=(), flops=0):
    whole = pl.BlockSpec(memory_space=pltpu.VMEM)
    moved = sum(a.size * a.dtype.itemsize for a in args)
    moved += sum(math.prod(s.shape) * s.dtype.itemsize for s in outs)
    return pl.pallas_call(
        kernel,
        out_shape=outs,
        in_specs=[whole] * len(args),
        out_specs=[whole] * len(outs),
        scratch_shapes=list(scratch),
        compiler_params=pltpu.CompilerParams(vmem_limit_bytes=VMEM),
        cost_estimate=pl.CostEstimate(flops=flops, bytes_accessed=moved, transcendentals=0),
    )(*args)


def shape(dims, dtype=BF16):
    return jax.ShapeDtypeStruct(dims, dtype)


def local(activations, enc_weight, enc_bias, dec_weight, dec_bias, thresholds, active_blocks):
    n_dp = lax.axis_size("dp")
    d = enc_weight.shape[0]
    scale_root = math.sqrt(activations.shape[0] * n_dp)
    dict_index = lax.axis_index("dict")
    core = dict_index % 2

    turned = activations.T
    halves = jnp.stack([turned[:, :TILE], turned[:, TILE:]])
    own = exchange(halves, CORE).reshape(-1, TILE)
    cols = own.shape[0]
    act = gather_chips(own)

    enc_other = lax.ppermute(enc_weight, "dict", CORE_SWAP)
    dec_other = lax.ppermute(dec_weight, "dict", CORE_SWAP)
    rows = jnp.stack([enc_bias.astype(F32), thresholds.astype(F32) / 16.0])
    rows = jnp.concatenate([rows, lax.ppermute(rows, "dict", CORE_SWAP)], axis=1)
    listed = lax.dynamic_slice_in_dim(active_blocks, core, 1)
    live = jnp.stack([jnp.any(listed == dict_index), jnp.any(listed == (dict_index ^ 1))])
    live = jnp.repeat(live.astype(F32), TILE)[None, :]
    rows = jnp.concatenate([rows, live, jnp.zeros((5, 2 * TILE), F32)], axis=0)

    work = 2 * d * 2 * TILE * TILE
    parts, feat, slope = call(
        forward_kernel,
        [shape(act.shape), shape((TILE, 2 * TILE)), shape((TILE, 2 * TILE), F32)],
        (act, enc_weight, enc_other, dec_weight, dec_other, rows),
        [pltpu.VMEM((d, TILE), BF16)],
        2 * work,
    )

    near_sum = jnp.sum(exchange(parts, NEAR).astype(F32), axis=0).astype(BF16)
    recon = jnp.sum(exchange(near_sum, FAR).astype(F32), axis=0)
    bias = lax.dynamic_slice_in_dim(dec_bias, dict_index // 2 * cols, cols).astype(F32)
    residual = (recon + bias[:, None] - own.astype(F32)) / scale_root
    res = gather_chips(residual.astype(BF16))

    packed = shape((NX, 2 * d // NX + BIAS_ROWS, TILE))
    mine, other = call(
        backward_kernel,
        [packed, packed],
        (res, act, dec_weight, dec_other, feat, slope),
        [
            pltpu.VMEM((d, TILE), BF16),
            pltpu.VMEM((d, TILE), BF16),
            pltpu.VMEM((BIAS_ROWS, TILE), F32),
        ],
        3 * work,
    )
    other = lax.ppermute(other, "dict", CORE_SWAP)
    mine = (mine.astype(F32) + other.astype(F32)).astype(BF16)

    parts = lax.all_to_all(mine, "dp", 0, 0, axis_index_groups=X_GROUPS)
    quarter = jnp.sum(parts.astype(F32), axis=0).astype(BF16)
    size = 2 * d // NX // 3
    bounds = [0, size, 2 * size, 3 * size + BIAS_ROWS]
    pieces = [lax.optimization_barrier(quarter[a:b]) for a, b in zip(bounds, bounds[1:])]
    swapped = [lax.ppermute(piece, "dp", Y_SWAP) for piece in pieces]
    pieces = [
        (a.astype(F32) + b.astype(F32)).astype(BF16) for a, b in zip(pieces, swapped)
    ]
    whole = [
        lax.all_gather(piece[:size], "dp", axis=0, axis_index_groups=X_GROUPS)
        for piece in pieces
    ]
    enc, dec = call(unpack_kernel, [shape((d, TILE)), shape((TILE, d))], whole)
    tail = pieces[2][size:]
    return enc, dec, tail[0], tail[1 : 1 + d // TILE].reshape(-1)


def solution(mesh):
    placed = (
        P("dp", "dict"),
        P(None, "dict"),
        P("dict"),
        P("dict", None),
        P(),
        P("dict"),
        P("dp", None),
    )
    return jax.shard_map(
        local,
        mesh=mesh,
        in_specs=placed,
        out_specs=(P(None, "dict"), P("dict", None), P("dict"), P()),
        check_vma=False,
    )
```

time: 305 us -> 241 us (0.79)
  the two profiles are of different devices: /device:TPU:8 before, /device:TPU:6 now
where the time goes in v2:
time: 241 us; the launch traced here: 239 us
  blocking collectives  160 us (66%)
  starting transfers between devices  32.1 us (13%)
  waiting for transfers between devices  20.6 us (9%)
  Pallas kernels  10.4 us (4%)
  other arithmetic  9.39 us (4%)
  local copies, waits for them, and re-layouts  6.01 us (2%)
    all_to_all x5, blocking collectives, exchange(): return lax.all_to_all(parts, 'dict', 0, 0, axis_index_groups=groups(axes))  84.8 us
    all_gather x3, blocking collectives, local(): lax.all_gather(piece[:size], 'dp', axis=0, axis_index_groups=X_GROUPS)  42.4 us
    all_to_all x1, blocking collectives, local(): parts = lax.all_to_all(mine, 'dp', 0, 0, axis_index_groups=X_GROUPS)  32.5 us
    ppermute x3, starting transfers between devices, local(): swapped = [lax.ppermute(piece, 'dp', Y_SWAP) for piece in pieces]  16.9 us
    all_to_all x2, waiting for transfers between devices, exchange(): return lax.all_to_all(parts, 'dict', 0, 0, axis_index_groups=groups(axes))  15.5 us
    pallas_call x3, Pallas kernels, call(): pl.pallas_call(kernel, out_shape=outs, in_specs=[whole] * len(args), out_...  10.4 us
    all_to_all x2, starting transfers between devices, exchange(): return lax.all_to_all(parts, 'dict', 0, 0, axis_index_groups=groups(axes))  7.08 us
  transfers between devices with their start and end apart: 9, of which 4 were waited for; matrix products, arithmetic and copies ran while one was open for 2% of the time, Pallas kernels for 0%

profile of v2, /device:TPU:6, one launch (start us, length us, event | category | flops | bytes accessed | tf_op | source)
XLA Modules:
  0.0 239.0 jit_solution(3435779452098013540)
XLA Ops:
  0.6 0.7 slice_bitcast_fusion.1
  1.4 4.5 %all_to_all.40 = bf16[2,72,128]{2,1,0:T(8,128)(2,1)} all-to-all(bf16[2,72,128]{2,1,0:T(8,128)(2,1)S(1)} %pad_maximum_fusion), channel_id=1, replica_groups={{0,8},{16,24},{32,40},{48,56},{64,72},{80,88},{96,104},{112,120},{128,1..., dimensions={0} | all-to-all | bytes 73728 | tf_op jit(solution)/shard_map/all_to_all | solution.py:40
  5.8 0.8 broadcast_in_dim.15
  6.7 27.1 %all_to_all.41 = bf16[8,144,128]{2,1,0:T(8,128)(2,1)S(1)} all-to-all(bf16[8,144,128]{2,1,0:T(8,128)(2,1)S(1)} %broadcast_in_dim.15), channel_id=1, replica_groups={{0,32,64,96,256,288,320,352},{8,40,72,104,264,296,328,360},{16,48,80,11..., dimensions={0} | all-to-all | bytes 589824 | tf_op jit(solution)/shard_map/all_to_all | solution.py:40
  33.8 1.2 broadcast_in_dim.16
  35.0 3.7 %all-to-all-start.2 = ((bf16[4,8,144,128]{3,2,1,0:T(8,128)(2,1)}), bf16[4,8,144,128]{3,2,1,0:T(8,128)(2,1)S(1)}, u32[]{:S(2)}, u32[]{:S(2)}) async-start(bf16[4,8,144,128]{3,2,1,0:T(8,128)(2,1)} %broadcast_in_dim.16), calls=%async_computation.2 | async-start | bytes 2359296 | tf_op jit(solution)/shard_map/all_to_all | solution.py:40
  38.6 1.9 collective-permute-start
  40.6 2.4 %collective-permute-start.1 = (bf16[128,4608]{1,0:T(8,128)(2,1)S(1)}, bf16[128,4608]{1,0:T(8,128)(2,1)S(1)}, u32[]{:S(2)}, u32[]{:S(2)}) collective-permute-start(bf16[128,4608]{1,0:T(8,128)(2,1)S(1)} %copy-done), channel_id=1, source_target_pairs={{0,8},{8,0},{16,24},{24,16},{32,40},{40,32},{48,56},{56,48},{64,72... | collective-permute-start | bytes 3538952 | tf_op jit(solution)/shard_map/ppermute | solution.py:169
  43.0 1.9 collective-permute-start.2
  45.0 1.3 compare_reduce_fusion.1
  46.3 1.4 add_convert_fusion.4
  47.7 0.1 pad.4.clone
  47.8 0.1 broadcast_in_dim.17
  47.8 0.5 copy-done.7
  48.3 0.7 maximum_maximum_fusion.row_ref
  49.1 3.5 %all-to-all-done.2.act_ref = bf16[4,8,144,128]{3,2,1,0:T(8,128)(2,1)S(1)} async-done(((bf16[4,8,144,128]{3,2,1,0:T(8,128)(2,1)}), bf16[4,8,144,128]{3,2,1,0:T(8,128)(2,1)S(1)}, u32[]{:S(2)}, u32[]{:S(2)}) %all-to-all-start.2) | async-done | bytes 1179680 | tf_op jit(solution)/shard_map/all_to_all | solution.py:40
  52.6 3.7 %shard_map.102 = (bf16[4,8,144,128]{3,2,1,0:T(8,128)(2,1)S(1)}, bf16[128,256]{1,0:T(8,128)(2,1)S(1)}, f32[128,256]{1,0:T(8,128)S(1)}) custom-call(bf16[4,8,144,128]{3,2,1,0:T(8,128)(2,1)S(1)} %all-to-all-done.2.act_ref, bf16[4608,128]{1,0:T(8,128)(2,1)} %we_own.1, bf16[4608,128]{1,0:T(8,128)(2,1)} %collective-permute-done.we_other, ...), custom_call_target="tpu_custom_call" | custom-call | flops 603979776 | bytes 7282688 | tf_op jit(solution)/shard_map/pallas_call | solution.py:140
  56.4 0.6 copy-done.3
  57.0 0.6 copy-done.5
  57.6 18.2 %all_to_all.42 = bf16[4,8,144,128]{3,2,1,0:T(8,128)(2,1)S(1)} all-to-all(bf16[4,8,144,128]{3,2,1,0:T(8,128)(2,1)S(1)} %get-tuple-element.11), channel_id=1, replica_groups={{0,16,128,144},{8,24,136,152},{32,48,160,176},{40,56,168,184},{64,80,19..., dimensions={0} | all-to-all | bytes 2359296 | tf_op jit(solution)/shard_map/all_to_all | solution.py:40
  75.8 0.9 reduce_sum.33
  76.8 3.4 %all-to-all-start.4 = ((bf16[8,144,128]{2,1,0:T(8,128)(2,1)}), bf16[8,144,128]{2,1,0:T(8,128)(2,1)S(1)}, u32[]{:S(2)}, u32[]{:S(2)}) async-start(bf16[8,144,128]{2,1,0:T(8,128)(2,1)} %reduce_sum.33), calls=%async_computation.4 | async-start | bytes 589824 | tf_op jit(solution)/shard_map/all_to_all | solution.py:40
  80.2 0.8 dynamic-slice_convert_fusion
  81.0 11.9 %all-to-all-done.4 = bf16[8,144,128]{2,1,0:T(8,128)(2,1)S(1)} async-done(((bf16[8,144,128]{2,1,0:T(8,128)(2,1)}), bf16[8,144,128]{2,1,0:T(8,128)(2,1)S(1)}, u32[]{:S(2)}, u32[]{:S(2)}) %all-to-all-start.4) | async-done | bytes 294944 | tf_op jit(solution)/shard_map/all_to_all | solution.py:40
  92.9 0.9 multiply_convert_fusion
  93.9 16.7 %all_to_all.43 = bf16[8,144,128]{2,1,0:T(8,128)(2,1)S(1)} all-to-all(bf16[8,144,128]{2,1,0:T(8,128)(2,1)S(1)} %broadcast_in_dim.37), channel_id=1, replica_groups={{0,32,64,96,256,288,320,352},{8,40,72,104,264,296,328,360},{16,48,80,11..., dimensions={0} | all-to-all | bytes 589824 | tf_op jit(solution)/shard_map/all_to_all | solution.py:40
  110.6 0.2 broadcast_in_dim.38
  110.7 0.0 copy-start.2
  110.8 18.2 %all_to_all.44.res_ref = bf16[4,8,144,128]{3,2,1,0:T(8,128)(2,1)S(1)} all-to-all(bf16[4,8,144,128]{3,2,1,0:T(8,128)(2,1)S(1)} %broadcast_in_dim.38), channel_id=1, replica_groups={{0,16,128,144},{8,24,136,152},{32,48,160,176},{40,56,168,184},{64,80,19..., dimensions={0} | all-to-all | bytes 2359296 | tf_op jit(solution)/shard_map/all_to_all | solution.py:40
  129.0 5.0 %shard_map.103 = (bf16[4,2352,128]{2,1,0:T(8,128)(2,1)}, bf16[4,2352,128]{2,1,0:T(8,128)(2,1)}) custom-call(bf16[4,8,144,128]{3,2,1,0:T(8,128)(2,1)S(1)} %all_to_all.44.res_ref, bf16[4,8,144,128]{3,2,1,0:T(8,128)(2,1)S(1)} %all-to-all-done.2.act_ref, bf16[128,4608]{1,0:T(8,128)(2,1)S(1)} %copy-done, bf16[128,4608]{1,0:T(8,128)(2,1)S(1)} %copy-done.2, ...), custom_call_target="tpu_custom_call" | custom-call | flops 905969664 | bytes 9732096 | tf_op jit(solution)/shard_map/pallas_call | solution.py:140
  134.0 1.9 collective-permute-start.3
  135.9 4.8 %collective-permute-done.3 = bf16[4,2352,128]{2,1,0:T(8,128)(2,1)S(1)} collective-permute-done((bf16[4,2352,128]{2,1,0:T(8,128)(2,1)}, bf16[4,2352,128]{2,1,0:T(8,128)(2,1)S(1)}, u32[]{:S(2)}, u32[]{:S(2)}) %collective-permute-start.3) | collective-permute-done | bytes 2408480 | tf_op jit(solution)/shard_map/ppermute | solution.py:204
  140.7 2.4 %add_convert_fusion = bf16[4,2352,128]{2,1,0:T(8,128)(2,1)S(1)} fusion(bf16[4,2352,128]{2,1,0:T(8,128)(2,1)S(1)} %collective-permute-done.3, bf16[4,2352,128]{2,1,0:T(8,128)(2,1)} %get-tuple-element.14), kind=kLoop, calls=%fused_computation | loop fusion | flops 4816896 | bytes 7225344 | tf_op jit(solution)/shard_map/convert_element_type | solution.py:205
  143.1 32.5 %all_to_all.45 = bf16[4,2352,128]{2,1,0:T(8,128)(2,1)S(1)} all-to-all(bf16[4,2352,128]{2,1,0:T(8,128)(2,1)S(1)} %add_convert_fusion), channel_id=1, replica_groups={{0,2,4,6},{1,3,5,7},{8,10,12,14},{9,11,13,15},{16,18,20,22},{17,19,21,2..., dimensions={0} | all-to-all | bytes 4816896 | tf_op jit(solution)/shard_map/all_to_all | solution.py:207
  175.6 0.7 reduce_sum.35
  176.4 7.1 %collective-permute-start.5 = (bf16[768,128]{1,0:T(8,128)(2,1)S(1)}, bf16[768,128]{1,0:T(8,128)(2,1)S(1)}, u32[]{:S(2)}, u32[]{:S(2)}) collective-permute-start(bf16[768,128]{1,0:T(8,128)(2,1)S(1)} %get-tuple-element.20), channel_id=1, source_target_pairs={{0,1},{1,0},{2,3},{3,2},{4,5},{5,4},{6,7},{7,6},{8,9},{9,8},{10,11... | collective-permute-start | bytes 589832 | tf_op jit(solution)/shard_map/ppermute | solution.py:212
  183.5 2.6 %collective-permute-start.4 = (bf16[768,128]{1,0:T(8,128)(2,1)S(1)}, bf16[768,128]{1,0:T(8,128)(2,1)S(1)}, u32[]{:S(2)}, u32[]{:S(2)}) collective-permute-start(bf16[768,128]{1,0:T(8,128)(2,1)S(1)} %get-tuple-element.21), channel_id=1, source_target_pairs={{0,1},{1,0},{2,3},{3,2},{4,5},{5,4},{6,7},{7,6},{8,9},{9,8},{10,11... | collective-permute-start | bytes 589832 | tf_op jit(solution)/shard_map/ppermute | solution.py:212
  186.2 7.1 %collective-permute-start.6 = (bf16[816,128]{1,0:T(8,128)(2,1)S(1)}, bf16[816,128]{1,0:T(8,128)(2,1)S(1)}, u32[]{:S(2)}, u32[]{:S(2)}) collective-permute-start(bf16[816,128]{1,0:T(8,128)(2,1)S(1)} %slice.39), channel_id=1, source_target_pairs={{0,1},{1,0},{2,3},{3,2},{4,5},{5,4},{6,7},{7,6},{8,9},{9,8},{10,11... | collective-permute-start | bytes 626696 | tf_op jit(solution)/shard_map/ppermute | solution.py:212
  193.3 0.3 collective-permute-done.5
  193.6 0.1 add_convert_fusion.2
  193.7 14.4 %all-gather.1 = bf16[3072,128]{1,0:T(8,128)(2,1)S(1)} all-gather(bf16[768,128]{1,0:T(8,128)(2,1)S(1)} %add_convert_fusion.2), channel_id=3, replica_groups={{0,2,4,6},{1,3,5,7},{8,10,12,14},{9,11,13,15},{16,18,20,22},{17,19,21,2..., dimensions={0}, use_global_device_ids=true | all-gather | bytes 983040 | tf_op jit(solution)/shard_map/all_gather | solution.py:217
  208.2 0.1 add_convert_fusion.3
  208.2 14.6 %all-gather = bf16[3072,128]{1,0:T(8,128)(2,1)S(1)} all-gather(bf16[768,128]{1,0:T(8,128)(2,1)S(1)} %add_convert_fusion.3), channel_id=2, replica_groups={{0,2,4,6},{1,3,5,7},{8,10,12,14},{9,11,13,15},{16,18,20,22},{17,19,21,2..., dimensions={0}, use_global_device_ids=true | all-gather | bytes 983040 | tf_op jit(solution)/shard_map/all_gather | solution.py:217
  222.8 0.1 add_convert_fusion.1
  222.9 0.5 slice_bitcast_fusion.3
  223.4 0.6 slice_bitcast_fusion.2
  224.0 13.3 %all-gather.2 = bf16[3072,128]{1,0:T(8,128)(2,1)S(1)} all-gather(bf16[768,128]{1,0:T(8,128)(2,1)S(1)} %slice.40), channel_id=4, replica_groups={{0,2,4,6},{1,3,5,7},{8,10,12,14},{9,11,13,15},{16,18,20,22},{17,19,21,2..., dimensions={0}, use_global_device_ids=true | all-gather | bytes 983040 | tf_op jit(solution)/shard_map/all_gather | solution.py:217
  237.3 1.7 shard_map.104
  (31 shorter events, 0.2 us)
Async XLA Ops:
  35.0 5.6 %copy-start = (bf16[128,4608]{1,0:T(8,128)(2,1)S(1)}, bf16[128,4608]{1,0:T(8,128)(2,1)}, u32[]{:S(2)}) copy-start(bf16[128,4608]{1,0:T(8,128)(2,1)} %wd_own.3) | copy-start | bytes 3538948
  35.0 8.0 %copy-start.8 = (bf16[128]{0:T(256)(128)(2,1)S(1)}, bf16[128]{0:T(256)(128)(2,1)}, u32[]{:S(2)}) copy-start(bf16[128]{0:T(256)(128)(2,1)} %param.9) | copy-start | bytes 772
  35.0 8.0 %copy-start.9 = (s32[128]{0:T(128)S(1)}, s32[128]{0:T(128)}, u32[]{:S(2)}) copy-start(s32[128]{0:T(128)} %param.12) | copy-start | bytes 1540
  35.0 17.7 %all-to-all-start.2 = ((bf16[4,8,144,128]{3,2,1,0:T(8,128)(2,1)}), bf16[4,8,144,128]{3,2,1,0:T(8,128)(2,1)S(1)}, u32[]{:S(2)}, u32[]{:S(2)}) async-start(bf16[4,8,144,128]{3,2,1,0:T(8,128)(2,1)} %broadcast_in_dim.16), calls=%async_computation.2 | async-start | bytes 2359296 | tf_op jit(solution)/shard_map/all_to_all | solution.py:40
  38.6 10.5 %collective-permute-start = (bf16[4608,128]{1,0:T(8,128)(2,1)}, bf16[4608,128]{1,0:T(8,128)(2,1)}, u32[]{:S(2)}, u32[]{:S(2)}) collective-permute-start(bf16[4608,128]{1,0:T(8,128)(2,1)} %we_own.1), channel_id=1, source_target_pairs={{0,8},{8,0},{16,24},{24,16},{32,40},{40,32},{48,56},{56,48},{64,72... | collective-permute-start | bytes 3538952 | tf_op jit(solution)/shard_map/ppermute | solution.py:168
  40.6 8.5 %collective-permute-start.1 = (bf16[128,4608]{1,0:T(8,128)(2,1)S(1)}, bf16[128,4608]{1,0:T(8,128)(2,1)S(1)}, u32[]{:S(2)}, u32[]{:S(2)}) collective-permute-start(bf16[128,4608]{1,0:T(8,128)(2,1)S(1)} %copy-done), channel_id=1, source_target_pairs={{0,8},{8,0},{16,24},{24,16},{32,40},{40,32},{48,56},{56,48},{64,72... | collective-permute-start | bytes 3538952 | tf_op jit(solution)/shard_map/ppermute | solution.py:169
  43.0 4.7 %collective-permute-start.2 = (f32[2,128]{1,0:T(2,128)S(1)}, f32[2,128]{1,0:T(2,128)S(1)}, u32[]{:S(2)}, u32[]{:S(2)}) collective-permute-start(f32[2,128]{1,0:T(2,128)S(1)} %pad_maximum_fusion.1), channel_id=1, source_target_pairs={{0,8},{8,0},{16,24},{24,16},{32,40},{40,32},{48,56},{56,48},{64,72... | collective-permute-start | bytes 3080 | tf_op jit(solution)/shard_map/ppermute | solution.py:171
  47.8 0.6 copy-start.7
  49.1 3.6 %copy-start.1 = (bf16[128,4608]{1,0:T(8,128)(2,1)}, bf16[128,4608]{1,0:T(8,128)(2,1)S(1)}, u32[]{:S(2)}) copy-start(bf16[128,4608]{1,0:T(8,128)(2,1)S(1)} %collective-permute-done.1.wd_other) | copy-start | bytes 3538948
  56.4 0.7 copy-start.3
  57.0 0.6 copy-start.5
  76.8 16.1 %all-to-all-start.4 = ((bf16[8,144,128]{2,1,0:T(8,128)(2,1)}), bf16[8,144,128]{2,1,0:T(8,128)(2,1)S(1)}, u32[]{:S(2)}, u32[]{:S(2)}) async-start(bf16[8,144,128]{2,1,0:T(8,128)(2,1)} %reduce_sum.33), calls=%async_computation.4 | async-start | bytes 589824 | tf_op jit(solution)/shard_map/all_to_all | solution.py:40
  110.7 18.3 %copy-start.2 = (bf16[128,4608]{1,0:T(8,128)(2,1)S(1)}, bf16[128,4608]{1,0:T(8,128)(2,1)}, u32[]{:S(2)}) copy-start(bf16[128,4608]{1,0:T(8,128)(2,1)} %copy-done.1) | copy-start | bytes 3538948
  110.7 18.3 %copy-start.4 = (f32[128,256]{1,0:T(8,128)S(1)}, f32[128,256]{1,0:T(8,128)}, u32[]{:S(2)}) copy-start(f32[128,256]{1,0:T(8,128)} %copy-done.3) | copy-start | bytes 393220
  110.8 18.3 %copy-start.6 = (bf16[128,256]{1,0:T(8,128)(2,1)S(1)}, bf16[128,256]{1,0:T(8,128)(2,1)}, u32[]{:S(2)}) copy-start(bf16[128,256]{1,0:T(8,128)(2,1)} %copy-done.5) | copy-start | bytes 196612
  134.0 6.7 %collective-permute-start.3 = (bf16[4,2352,128]{2,1,0:T(8,128)(2,1)}, bf16[4,2352,128]{2,1,0:T(8,128)(2,1)S(1)}, u32[]{:S(2)}, u32[]{:S(2)}) collective-permute-start(bf16[4,2352,128]{2,1,0:T(8,128)(2,1)} %get-tuple-element.15), channel_id=1, source_target_pairs={{0,8},{8,0},{16,24},{24,16},{32,40},{40,32},{48,56},{56,48},{64,72... | collective-permute-start | bytes 7225352 | tf_op jit(solution)/shard_map/ppermute | solution.py:204
  176.4 17.3 %collective-permute-start.5 = (bf16[768,128]{1,0:T(8,128)(2,1)S(1)}, bf16[768,128]{1,0:T(8,128)(2,1)S(1)}, u32[]{:S(2)}, u32[]{:S(2)}) collective-permute-start(bf16[768,128]{1,0:T(8,128)(2,1)S(1)} %get-tuple-element.20), channel_id=1, source_target_pairs={{0,1},{1,0},{2,3},{3,2},{4,5},{5,4},{6,7},{7,6},{8,9},{9,8},{10,11... | collective-permute-start | bytes 589832 | tf_op jit(solution)/shard_map/ppermute | solution.py:212
  183.5 24.6 %collective-permute-start.4 = (bf16[768,128]{1,0:T(8,128)(2,1)S(1)}, bf16[768,128]{1,0:T(8,128)(2,1)S(1)}, u32[]{:S(2)}, u32[]{:S(2)}) collective-permute-start(bf16[768,128]{1,0:T(8,128)(2,1)S(1)} %get-tuple-element.21), channel_id=1, source_target_pairs={{0,1},{1,0},{2,3},{3,2},{4,5},{5,4},{6,7},{7,6},{8,9},{9,8},{10,11... | collective-permute-start | bytes 589832 | tf_op jit(solution)/shard_map/ppermute | solution.py:212
  186.2 36.7 %collective-permute-start.6 = (bf16[816,128]{1,0:T(8,128)(2,1)S(1)}, bf16[816,128]{1,0:T(8,128)(2,1)S(1)}, u32[]{:S(2)}, u32[]{:S(2)}) collective-permute-start(bf16[816,128]{1,0:T(8,128)(2,1)S(1)} %slice.39), channel_id=1, source_target_pairs={{0,1},{1,0},{2,3},{3,2},{4,5},{5,4},{6,7},{7,6},{8,9},{9,8},{10,11... | collective-permute-start | bytes 626696 | tf_op jit(solution)/shard_map/ppermute | solution.py:212

commit v3 on v2

--- a/solution.py
+++ b/solution.py
@@ -17,7 +17,7 @@
 FAR, NEAR, CORE = (0, 2), (1, 3), (4,)
 CHIPS = 32
 NX = 4
-BIAS_ROWS = 48
+DEC_BIAS_ROWS, ENC_BIAS_ROWS = 48, 16
 VMEM = 48 * 1024 * 1024
 
 
@@ -40,12 +40,12 @@
     return lax.all_to_all(parts, "dict", 0, 0, axis_index_groups=groups(axes))
 
 
-def spread(block, axes):
-    return exchange(jnp.broadcast_to(block[None], (size_of(axes),) + block.shape), axes)
-
-
-def gather_chips(block):
-    return spread(spread(block, FAR), NEAR)
+def gather_near(blocks):
+    half = blocks.shape[0] // 2
+    return [
+        lax.all_gather(part, "dict", axis=0, axis_index_groups=groups(NEAR))
+        for part in (blocks[:half], blocks[half:])
+    ]
 
 
 def chip_blocks():
@@ -55,10 +55,11 @@
             yield near, far, y * 8 + z
 
 
-def in_order(parts_ref, whole_ref):
-    cols = parts_ref.shape[2]
+def in_order(first_ref, second_ref, whole_ref):
+    half, cols = first_ref.shape[1:3]
     for near, far, chip in chip_blocks():
-        whole_ref[chip * cols : (chip + 1) * cols, :] = parts_ref[near, far]
+        ref = first_ref if far < half else second_ref
+        whole_ref[chip * cols : (chip + 1) * cols, :] = ref[near, far % half]
 
 
 def dot(a, b, dims):
@@ -66,9 +67,9 @@
 
 
 def forward_kernel(
-    act_ref, we_own, we_other, wd_own, wd_other, row_ref, parts_ref, feat_ref, slope_ref, act
+    act_0, act_1, we_own, we_other, wd_own, wd_other, row_ref, parts_ref, feat_ref, slope_ref, act
 ):
-    in_order(act_ref, act)
+    in_order(act_0, act_1, act)
     for n, we in enumerate((we_own, we_other)):
         lanes = slice(n * TILE, (n + 1) * TILE)
         bias, theta, live = row_ref[0:1, lanes], row_ref[1:2, lanes], row_ref[2:3, lanes]
@@ -89,34 +90,43 @@
             parts_ref[near, far] = turned[i * cols : (i + 1) * cols, :]
 
 
-def backward_kernel(
-    res_ref, act_ref, wd_own, wd_other, feat_ref, slope_ref, own_ref, other_ref, act, res, bias
-):
-    in_order(act_ref, act)
-    in_order(res_ref, res)
-    d = act.shape[0]
+def decoder_kernel(res_0, res_1, feat_ref, own_ref, other_ref, res, bias):
+    in_order(res_0, res_1, res)
+    d = res.shape[0]
     quarter, lat = d // NX, TILE // NX
-    res_t = res[...].T
     feat_t = jnp.concatenate([feat_ref[...].T, jnp.ones((16, TILE), BF16)], axis=0)
     bias[...] = jnp.zeros_like(bias)
     for i in range(d // TILE):
         tile = dot(feat_t, res[i * TILE : (i + 1) * TILE, :], ((1,), (1,)))
-        bias[i + 1 : i + 2, :] = tile[2 * TILE : 2 * TILE + 1, :]
+        bias[i : i + 1, :] = tile[2 * TILE : 2 * TILE + 1, :]
         tile = tile.astype(BF16)
+        rows = slice(i * lat, (i + 1) * lat)
         for x in range(NX):
-            rows = slice(quarter + i * lat, quarter + (i + 1) * lat)
             own_ref[x, rows, :] = tile[x * lat : (x + 1) * lat, :]
             other_ref[x, rows, :] = tile[TILE + x * lat : TILE + (x + 1) * lat, :]
+    rows = bias[...].astype(BF16)
+    for x in range(NX):
+        own_ref[x, quarter:, :] = rows
+        other_ref[x, quarter:, :] = rows
+
+
+def encoder_kernel(
+    res_0, res_1, act_0, act_1, wd_own, wd_other, slope_ref, own_ref, other_ref, act, res
+):
+    in_order(act_0, act_1, act)
+    in_order(res_0, res_1, res)
+    quarter = act.shape[0] // NX
+    res_t = res[...].T
     for n, (wd, out) in enumerate(((wd_own, own_ref), (wd_other, other_ref))):
         dfeat = dot(res_t, wd[...], ((1,), (1,)))
         dpre = dfeat * slope_ref[:, n * TILE : (n + 1) * TILE]
-        bias[0:1, :] = jnp.sum(dpre, axis=0, keepdims=True)
+        row = jnp.sum(dpre, axis=0, keepdims=True)
+        rows = jnp.broadcast_to(row, (ENC_BIAS_ROWS, TILE)).astype(BF16)
         dpre = dpre.astype(BF16)
-        rows = bias[...].astype(BF16)
         for x in range(NX):
             enc = dot(act[x * quarter : (x + 1) * quarter, :], dpre, ((1,), (0,)))
             out[x, :quarter, :] = enc.astype(BF16)
-            out[x, 2 * quarter :, :] = rows
+            out[x, quarter:, :] = rows
 
 
 def unpack_kernel(first_ref, second_ref, third_ref, enc_ref, dec_ref):
@@ -124,12 +134,10 @@
     size = first_ref.shape[1]
     rest = quarter - size
     for x in range(NX):
-        enc_ref[x * quarter : x * quarter + size, :] = first_ref[x]
-        enc_ref[x * quarter + size : (x + 1) * quarter, :] = second_ref[x, :rest, :]
+        enc_ref[x * quarter : x * quarter + size - rest, :] = second_ref[x, rest:, :]
+        enc_ref[x * quarter + size - rest : (x + 1) * quarter, :] = third_ref[x]
         for i in range(enc_ref.shape[0] // TILE):
-            at = rest + i * lat
-            ref = second_ref if at < size else third_ref
-            at = at % size
+            ref, at = (first_ref, i * lat) if i * lat < size else (second_ref, i * lat - size)
             dec_ref[x * lat : (x + 1) * lat, i * TILE : (i + 1) * TILE] = ref[x, at : at + lat, :]
 
 
@@ -152,6 +160,18 @@
     return jax.ShapeDtypeStruct(dims, dtype)
 
 
+def sum_cores(own_part, other_part):
+    other_part = lax.ppermute(other_part, "dict", CORE_SWAP)
+    return (own_part.astype(F32) + other_part.astype(F32)).astype(BF16)
+
+
+def sum_dp(total):
+    parts = lax.all_to_all(total, "dp", 0, 0, axis_index_groups=X_GROUPS)
+    piece = lax.optimization_barrier(jnp.sum(parts.astype(F32), axis=0).astype(BF16))
+    swapped = lax.ppermute(piece, "dp", Y_SWAP)
+    return (piece.astype(F32) + swapped.astype(F32)).astype(BF16)
+
+
 def local(activations, enc_weight, enc_bias, dec_weight, dec_bias, thresholds, active_blocks):
     n_dp = lax.axis_size("dp")
     d = enc_weight.shape[0]
@@ -161,9 +181,13 @@
 
     turned = activations.T
     halves = jnp.stack([turned[:, :TILE], turned[:, TILE:]])
-    own = exchange(halves, CORE).reshape(-1, TILE)
+    far = size_of(FAR)
+    halves = jnp.broadcast_to(halves[None], (far,) + halves.shape).reshape((-1,) + halves.shape[1:])
+    act = exchange(halves, FAR + CORE).reshape(far, -1, TILE)
+    chip = dict_index // 2
+    own = lax.dynamic_index_in_dim(act, chip // 16 * 4 + chip % 8 // 2, keepdims=False)
     cols = own.shape[0]
-    act = gather_chips(own)
+    act = gather_near(act)
 
     enc_other = lax.ppermute(enc_weight, "dict", CORE_SWAP)
     dec_other = lax.ppermute(dec_weight, "dict", CORE_SWAP)
@@ -177,8 +201,12 @@
     work = 2 * d * 2 * TILE * TILE
     parts, feat, slope = call(
         forward_kernel,
-        [shape(act.shape), shape((TILE, 2 * TILE)), shape((TILE, 2 * TILE), F32)],
-        (act, enc_weight, enc_other, dec_weight, dec_other, rows),
+        [
+            shape((size_of(NEAR), far, cols, TILE)),
+            shape((TILE, 2 * TILE)),
+            shape((TILE, 2 * TILE), F32),
+        ],
+        (*act, enc_weight, enc_other, dec_weight, dec_other, rows),
         [pltpu.VMEM((d, TILE), BF16)],
         2 * work,
     )
@@ -187,39 +215,44 @@
     recon = jnp.sum(exchange(near_sum, FAR).astype(F32), axis=0)
     bias = lax.dynamic_slice_in_dim(dec_bias, dict_index // 2 * cols, cols).astype(F32)
     residual = (recon + bias[:, None] - own.astype(F32)) / scale_root
-    res = gather_chips(residual.astype(BF16))
-
-    packed = shape((NX, 2 * d // NX + BIAS_ROWS, TILE))
-    mine, other = call(
-        backward_kernel,
+    residual = residual.astype(BF16)
+    residual = jnp.broadcast_to(residual[None], (far,) + residual.shape)
+    res = gather_near(exchange(residual, FAR))
+
+    quarter = d // NX
+    packed = shape((NX, quarter + DEC_BIAS_ROWS, TILE))
+    room = pltpu.VMEM((d, TILE), BF16)
+    dec_parts = call(
+        decoder_kernel,
         [packed, packed],
-        (res, act, dec_weight, dec_other, feat, slope),
-        [
-            pltpu.VMEM((d, TILE), BF16),
-            pltpu.VMEM((d, TILE), BF16),
-            pltpu.VMEM((BIAS_ROWS, TILE), F32),
-        ],
-        3 * work,
-    )
-    other = lax.ppermute(other, "dict", CORE_SWAP)
-    mine = (mine.astype(F32) + other.astype(F32)).astype(BF16)
-
-    parts = lax.all_to_all(mine, "dp", 0, 0, axis_index_groups=X_GROUPS)
-    quarter = jnp.sum(parts.astype(F32), axis=0).astype(BF16)
-    size = 2 * d // NX // 3
-    bounds = [0, size, 2 * size, 3 * size + BIAS_ROWS]
-    pieces = [lax.optimization_barrier(quarter[a:b]) for a, b in zip(bounds, bounds[1:])]
-    swapped = [lax.ppermute(piece, "dp", Y_SWAP) for piece in pieces]
-    pieces = [
-        (a.astype(F32) + b.astype(F32)).astype(BF16) for a, b in zip(pieces, swapped)
-    ]
+        (*res, feat),
+        [room, pltpu.VMEM((DEC_BIAS_ROWS, TILE), F32)],
+        work,
+    )
+    dec_total = sum_cores(*dec_parts)
+    dec_total, res = lax.optimization_barrier((dec_total, res))
+    packed = shape((NX, quarter + ENC_BIAS_ROWS, TILE))
+    enc_parts = call(
+        encoder_kernel,
+        [packed, packed],
+        (*res, *act, dec_weight, dec_other, slope),
+        [room, room],
+        2 * work,
+    )
+
+    dec_piece, enc_piece = sum_dp(dec_total), sum_dp(sum_cores(*enc_parts))
+    size = 2 * quarter // 3
+    pieces = (
+        dec_piece[:size],
+        jnp.concatenate([dec_piece[size:quarter], enc_piece[: 2 * size - quarter]]),
+        enc_piece[2 * size - quarter : quarter],
+    )
     whole = [
-        lax.all_gather(piece[:size], "dp", axis=0, axis_index_groups=X_GROUPS)
-        for piece in pieces
+        lax.all_gather(piece, "dp", axis=0, axis_index_groups=X_GROUPS) for piece in pieces
     ]
     enc, dec = call(unpack_kernel, [shape((d, TILE)), shape((TILE, d))], whole)
-    tail = pieces[2][size:]
-    return enc, dec, tail[0], tail[1 : 1 + d // TILE].reshape(-1)
+    dec_bias_sum = dec_piece[quarter : quarter + d // TILE].reshape(-1)
+    return enc, dec, enc_piece[quarter], dec_bias_sum
 
 
 def solution(mesh):

time: 241 us -> 259 us (1.075)
  blocking collectives: 160 us -> 129 us
  waiting for transfers between devices: 20.6 us -> 43.7 us
  starting transfers between devices: 32.1 us -> 52.3 us
  other arithmetic: 9.39 us -> 12.8 us
    all_gather x3 -> x7, blocking collectives: 42.4 us -> 97.6 us  [the longest x4 56.7 us: gather_near(): lax.all_gather(part, 'dict', axis=0, axis_index_groups=groups(NEAR))]
    all_to_all x5 -> x2, blocking collectives: 84.8 us -> 31.1 us  [exchange(): return lax.all_to_all(parts, 'dict', 0, 0, axis_index_groups=groups(axes))]
    all_to_all x1 -> x0, blocking collectives: 32.5 us -> none  [local(): parts = lax.all_to_all(mine, 'dp', 0, 0, axis_index_groups=X_GROUPS)]
    all_to_all x0 -> x2, waiting for transfers between devices: none -> 13.2 us  [sum_dp(): parts = lax.all_to_all(total, 'dp', 0, 0, axis_index_groups=X_GROUPS)]
    all_to_all x2, starting transfers between devices: 7.08 us -> 18.5 us  [exchange(): return lax.all_to_all(parts, 'dict', 0, 0, axis_index_groups=groups(axes))]
    ppermute x4, waiting for transfers between devices: 5.13 us -> 16.3 us  [the longest x2 13.4 us: sum_dp(): swapped = lax.ppermute(piece, 'dp', Y_SWAP)]
    all_to_all x0 -> x2, starting transfers between devices: none -> 10.4 us  [sum_dp(): parts = lax.all_to_all(total, 'dp', 0, 0, axis_index_groups=X_GROUPS)]
    pallas_call x3 -> x4, Pallas kernels: 10.4 us -> 10.5 us  [call(): pl.pallas_call(kernel, out_shape=outs, in_specs=[whole] * len(args), out_...]
  transfers between devices with their start and end apart: 9 -> 11, of which waited for: 4 -> 5; matrix products, arithmetic and copies ran while one was open for 2% -> 4% of each run, Pallas kernels for 0% -> 0%
where the time goes in v3:
time: 259 us; the launch traced here: 256 us
  blocking collectives  129 us (50%)
  starting transfers between devices  52.3 us (20%)
  waiting for transfers between devices  43.7 us (17%)
  other arithmetic  12.8 us (5%)
  Pallas kernels  10.5 us (4%)
  local copies, waits for them, and re-layouts  7.43 us (3%)
    all_gather x4, blocking collectives, gather_near(): lax.all_gather(part, 'dict', axis=0, axis_index_groups=groups(NEAR))  56.7 us
    all_gather x3, blocking collectives, local(): lax.all_gather(piece, 'dp', axis=0, axis_index_groups=X_GROUPS)  40.8 us
    all_to_all x2, blocking collectives, exchange(): return lax.all_to_all(parts, 'dict', 0, 0, axis_index_groups=groups(axes))  31.1 us
    all_to_all x2, starting transfers between devices, exchange(): return lax.all_to_all(parts, 'dict', 0, 0, axis_index_groups=groups(axes))  18.5 us
    all_to_all x2, waiting for transfers between devices, exchange(): return lax.all_to_all(parts, 'dict', 0, 0, axis_index_groups=groups(axes))  14.1 us
    ppermute x2, waiting for transfers between devices, sum_dp(): swapped = lax.ppermute(piece, 'dp', Y_SWAP)  13.4 us
    all_to_all x2, waiting for transfers between devices, sum_dp(): parts = lax.all_to_all(total, 'dp', 0, 0, axis_index_groups=X_GROUPS)  13.2 us
    ppermute x2, starting transfers between devices, sum_dp(): swapped = lax.ppermute(piece, 'dp', Y_SWAP)  12.6 us
  transfers between devices with their start and end apart: 11, of which 5 were waited for; matrix products, arithmetic and copies ran while one was open for 4% of the time, Pallas kernels for 0%

profile of v3, /device:TPU:6, one launch (start us, length us, event | category | flops | bytes accessed | tf_op | source)
XLA Modules:
  0.0 256.1 jit_solution(11637343885009722151)
XLA Ops:
  0.6 0.7 slice_bitcast_fusion.1
  1.4 0.8 broadcast_in_dim.10
  2.1 12.4 %all-to-all-start = ((bf16[16,72,128]{2,1,0:T(8,128)(2,1)}), bf16[16,72,128]{2,1,0:T(8,128)(2,1)S(1)}, u32[]{:S(2)}, u32[]{:S(2)}) async-start(bf16[16,72,128]{2,1,0:T(8,128)(2,1)} %bitcast.3), calls=%async_computation | async-start | bytes 589824 | tf_op jit(solution)/shard_map/all_to_all | solution.py:40
  14.6 2.4 collective-permute-start
  17.1 2.0 collective-permute-start.1
  19.1 0.7 bitcast_convert_fusion
  19.7 0.7 multiply_bitcast_fusion
  20.4 2.3 collective-permute-start.2
  22.7 1.3 compare_reduce_fusion.1
  24.1 1.4 add_convert_fusion.4
  25.7 2.6 %all-to-all-done = bf16[16,72,128]{2,1,0:T(8,128)(2,1)S(1)} async-done(((bf16[16,72,128]{2,1,0:T(8,128)(2,1)}), bf16[16,72,128]{2,1,0:T(8,128)(2,1)S(1)}, u32[]{:S(2)}, u32[]{:S(2)}) %all-to-all-start) | async-done | bytes 294944 | tf_op jit(solution)/shard_map/all_to_all | solution.py:40
  28.3 0.7 copy-done.8
  29.0 14.5 %all_gather.43.act_0 = bf16[4,4,144,128]{3,2,1,0:T(8,128)(2,1)S(1)} all-gather(bf16[1,4,144,128]{3,2,1,0:T(8,128)(2,1)S(1)} %bitcast.47), channel_id=1, replica_groups={{0,16,128,144},{8,24,136,152},{32,48,160,176},{40,56,168,184},{64,80,19..., dimensions={0}, use_global_device_ids=true | all-gather | bytes 737280 | tf_op jit(solution)/shard_map/all_gather | solution.py:46
  43.6 14.7 %all_gather.45.act_1 = bf16[4,4,144,128]{3,2,1,0:T(8,128)(2,1)S(1)} all-gather(bf16[1,4,144,128]{3,2,1,0:T(8,128)(2,1)S(1)} %bitcast.46), channel_id=1, replica_groups={{0,16,128,144},{8,24,136,152},{32,48,160,176},{40,56,168,184},{64,80,19..., dimensions={0}, use_global_device_ids=true | all-gather | bytes 737280 | tf_op jit(solution)/shard_map/all_gather | solution.py:46
  58.2 1.0 copy-done.1
  59.2 1.3 copy-done.3
  60.5 3.4 %shard_map.102 = (bf16[4,8,144,128]{3,2,1,0:T(8,128)(2,1)S(1)}, bf16[128,256]{1,0:T(8,128)(2,1)S(1)}, f32[128,256]{1,0:T(8,128)S(1)}) custom-call(bf16[4,4,144,128]{3,2,1,0:T(8,128)(2,1)S(1)} %all_gather.43.act_0, bf16[4,4,144,128]{3,2,1,0:T(8,128)(2,1)S(1)} %all_gather.45.act_1, bf16[4608,128]{1,0:T(8,128)(2,1)S(1)} %copy-done.3, ...), custom_call_target="tpu_custom_call" | custom-call | flops 603979776 | bytes 7282688 | tf_op jit(solution)/shard_map/pallas_call | solution.py:148
  63.9 0.7 copy-done.4
  64.5 0.6 copy-done.6
  65.2 15.9 %all_to_all.30 = bf16[4,8,144,128]{3,2,1,0:T(8,128)(2,1)S(1)} all-to-all(bf16[4,8,144,128]{3,2,1,0:T(8,128)(2,1)S(1)} %get-tuple-element.16), channel_id=1, replica_groups={{0,16,128,144},{8,24,136,152},{32,48,160,176},{40,56,168,184},{64,80,19..., dimensions={0} | all-to-all | bytes 2359296 | tf_op jit(solution)/shard_map/all_to_all | solution.py:40
  81.0 0.9 reduce_sum.47
  82.0 6.1 %all-to-all-start.2 = ((bf16[8,144,128]{2,1,0:T(8,128)(2,1)}), bf16[8,144,128]{2,1,0:T(8,128)(2,1)S(1)}, u32[]{:S(2)}, u32[]{:S(2)}) async-start(bf16[8,144,128]{2,1,0:T(8,128)(2,1)} %reduce_sum.47), calls=%async_computation.2 | async-start | bytes 589824 | tf_op jit(solution)/shard_map/all_to_all | solution.py:40
  88.1 0.8 dynamic-slice_convert_fusion
  88.8 11.5 %all-to-all-done.2 = bf16[8,144,128]{2,1,0:T(8,128)(2,1)S(1)} async-done(((bf16[8,144,128]{2,1,0:T(8,128)(2,1)}), bf16[8,144,128]{2,1,0:T(8,128)(2,1)S(1)}, u32[]{:S(2)}, u32[]{:S(2)}) %all-to-all-start.2) | async-done | bytes 294944 | tf_op jit(solution)/shard_map/all_to_all | solution.py:40
  100.3 0.9 fusion.3
  101.3 15.2 %all_to_all.31 = bf16[8,144,128]{2,1,0:T(8,128)(2,1)S(1)} all-to-all(bf16[8,144,128]{2,1,0:T(8,128)(2,1)S(1)} %broadcast_in_dim.25), channel_id=1, replica_groups={{0,32,64,96,256,288,320,352},{8,40,72,104,264,296,328,360},{16,48,80,11..., dimensions={0} | all-to-all | bytes 589824 | tf_op jit(solution)/shard_map/all_to_all | solution.py:40
  116.5 14.7 %all-gather.1 = bf16[16,144,128]{2,1,0:T(8,128)(2,1)S(1)} all-gather(bf16[4,144,128]{2,1,0:T(8,128)(2,1)S(1)} %get-tuple-element.30), channel_id=3, replica_groups={{0,16,128,144},{8,24,136,152},{32,48,160,176},{40,56,168,184},{64,80,19..., dimensions={0}, use_global_device_ids=true | all-gather | bytes 737280 | tf_op jit(solution)/shard_map/all_gather | solution.py:46
  131.1 12.9 %all-gather = bf16[16,144,128]{2,1,0:T(8,128)(2,1)S(1)} all-gather(bf16[4,144,128]{2,1,0:T(8,128)(2,1)S(1)} %get-tuple-element.31), channel_id=2, replica_groups={{0,16,128,144},{8,24,136,152},{32,48,160,176},{40,56,168,184},{64,80,19..., dimensions={0}, use_global_device_ids=true | all-gather | bytes 737280 | tf_op jit(solution)/shard_map/all_gather | solution.py:46
  144.0 1.5 shard_map.103
  145.5 1.9 collective-permute-start.3
  147.4 2.9 %collective-permute-done.3 = bf16[4,1200,128]{2,1,0:T(8,128)(2,1)S(1)} collective-permute-done((bf16[4,1200,128]{2,1,0:T(8,128)(2,1)S(1)}, bf16[4,1200,128]{2,1,0:T(8,128)(2,1)S(1)}, u32[]{:S(2)}, u32[]{:S(2)}) %collective-permute-start.3) | collective-permute-done | bytes 1228832 | tf_op jit(solution)/shard_map/ppermute | solution.py:164
  150.3 1.4 add_convert_fusion
  151.7 4.0 %shard_map.104 = (bf16[4,1168,128]{2,1,0:T(8,128)(2,1)S(1)}, bf16[4,1168,128]{2,1,0:T(8,128)(2,1)}) custom-call(bf16[4,4,144,128]{3,2,1,0:T(8,128)(2,1)S(1)} %bitcast.41, bf16[4,4,144,128]{3,2,1,0:T(8,128)(2,1)S(1)} %bitcast.39, bf16[4,4,144,128]{3,2,1,0:T(8,128)(2,1)S(1)} %all_gather.43.act_0, bf16[4,4,144,128]{3,2,1,0:T(8,128)(2,1)S(1)} %all_gather.45.act_1, ...), custom_call_target="tpu_custom_call" | custom-call | flops 603979776 | bytes 7241728 | tf_op jit(solution)/shard_map/pallas_call | solution.py:148
  155.7 2.0 collective-permute-start.5
  157.8 4.8 %all-to-all-start.4 = ((bf16[4,1200,128]{2,1,0:T(8,128)(2,1)}), bf16[4,1200,128]{2,1,0:T(8,128)(2,1)}, u32[]{:S(2)}, u32[]{:S(2)}) async-start(bf16[4,1200,128]{2,1,0:T(8,128)(2,1)} %add_convert_fusion), calls=%async_computation.4 | async-start | bytes 2457600 | tf_op jit(solution)/shard_map/all_to_all | solution.py:169
  162.5 2.6 %add_convert_fusion.1 = bf16[4,1168,128]{2,1,0:T(8,128)(2,1)} fusion(bf16[4,1168,128]{2,1,0:T(8,128)(2,1)} %collective-permute-done.5, bf16[4,1168,128]{2,1,0:T(8,128)(2,1)S(1)} %get-tuple-element.24), kind=kLoop, calls=%fused_computation.1 | loop fusion | flops 2392064 | bytes 3588096 | tf_op jit(solution)/shard_map/convert_element_type | solution.py:165
  165.2 13.2 %all-to-all-done.4 = bf16[4,1200,128]{2,1,0:T(8,128)(2,1)} async-done(((bf16[4,1200,128]{2,1,0:T(8,128)(2,1)}), bf16[4,1200,128]{2,1,0:T(8,128)(2,1)}, u32[]{:S(2)}, u32[]{:S(2)}) %all-to-all-start.4) | async-done | bytes 1228832 | tf_op jit(solution)/shard_map/all_to_all | solution.py:169
  178.4 5.6 %all-to-all-start.5 = ((bf16[4,1168,128]{2,1,0:T(8,128)(2,1)}), bf16[4,1168,128]{2,1,0:T(8,128)(2,1)S(1)}, u32[]{:S(2)}, u32[]{:S(2)}) async-start(bf16[4,1168,128]{2,1,0:T(8,128)(2,1)} %add_convert_fusion.1), calls=%async_computation.5 | async-start | bytes 2392064 | tf_op jit(solution)/shard_map/all_to_all | solution.py:169
  184.0 1.6 reduce_sum.50
  185.6 5.9 %collective-permute-start.4 = (bf16[1200,128]{1,0:T(8,128)(2,1)S(1)}, bf16[1200,128]{1,0:T(8,128)(2,1)S(1)}, u32[]{:S(2)}, u32[]{:S(2)}) collective-permute-start(bf16[1200,128]{1,0:T(8,128)(2,1)S(1)} %reduce_sum.50), channel_id=1, source_target_pairs={{0,1},{1,0},{2,3},{3,2},{4,5},{5,4},{6,7},{7,6},{8,9},{9,8},{10,11... | collective-permute-start | bytes 921608 | tf_op jit(solution)/shard_map/ppermute | solution.py:171
  191.5 13.4 %collective-permute-done.4 = bf16[1200,128]{1,0:T(8,128)(2,1)S(1)} collective-permute-done((bf16[1200,128]{1,0:T(8,128)(2,1)S(1)}, bf16[1200,128]{1,0:T(8,128)(2,1)S(1)}, u32[]{:S(2)}, u32[]{:S(2)}) %collective-permute-start.4) | collective-permute-done | bytes 307232 | tf_op jit(solution)/shard_map/ppermute | solution.py:171
  205.3 6.7 %collective-permute-start.6 = (bf16[1168,128]{1,0:T(8,128)(2,1)S(1)}, bf16[1168,128]{1,0:T(8,128)(2,1)S(1)}, u32[]{:S(2)}, u32[]{:S(2)}) collective-permute-start(bf16[1168,128]{1,0:T(8,128)(2,1)S(1)} %reduce_sum.51), channel_id=1, source_target_pairs={{0,1},{1,0},{2,3},{3,2},{4,5},{5,4},{6,7},{7,6},{8,9},{9,8},{10,11... | collective-permute-start | bytes 897032 | tf_op jit(solution)/shard_map/ppermute | solution.py:171
  212.1 0.6 slice_bitcast_fusion.2
  212.7 13.4 %all-gather.2 = bf16[3072,128]{1,0:T(8,128)(2,1)S(1)} all-gather(bf16[768,128]{1,0:T(8,128)(2,1)S(1)} %slice.56), channel_id=4, replica_groups={{0,2,4,6},{1,3,5,7},{8,10,12,14},{9,11,13,15},{16,18,20,22},{17,19,21,2..., dimensions={0}, use_global_device_ids=true | all-gather | bytes 983040 | tf_op jit(solution)/shard_map/all_gather | solution.py:251
  226.2 0.5 slice_bitcast_fusion.3
  227.1 14.1 %all-gather.3 = bf16[3072,128]{1,0:T(8,128)(2,1)S(1)} all-gather(bf16[768,128]{1,0:T(8,128)(2,1)S(1)} %pad_maximum_fusion), channel_id=5, replica_groups={{0,2,4,6},{1,3,5,7},{8,10,12,14},{9,11,13,15},{16,18,20,22},{17,19,21,2..., dimensions={0}, use_global_device_ids=true | all-gather | bytes 983040 | tf_op jit(solution)/shard_map/all_gather | solution.py:251
  241.2 13.3 %all-gather.4 = bf16[3072,128]{1,0:T(8,128)(2,1)S(1)} all-gather(bf16[768,128]{1,0:T(8,128)(2,1)S(1)} %slice.59), channel_id=6, replica_groups={{0,2,4,6},{1,3,5,7},{8,10,12,14},{9,11,13,15},{16,18,20,22},{17,19,21,2..., dimensions={0}, use_global_device_ids=true | all-gather | bytes 983040 | tf_op jit(solution)/shard_map/all_gather | solution.py:251
  254.5 1.7 shard_map.105
  (40 shorter events, 1.2 us)
Async XLA Ops:
  2.1 26.2 %all-to-all-start = ((bf16[16,72,128]{2,1,0:T(8,128)(2,1)}), bf16[16,72,128]{2,1,0:T(8,128)(2,1)S(1)}, u32[]{:S(2)}, u32[]{:S(2)}) async-start(bf16[16,72,128]{2,1,0:T(8,128)(2,1)} %bitcast.3), calls=%async_computation | async-start | bytes 589824 | tf_op jit(solution)/shard_map/all_to_all | solution.py:40
  14.6 44.6 %copy-start = (bf16[128,4608]{1,0:T(8,128)(2,1)S(1)}, bf16[128,4608]{1,0:T(8,128)(2,1)}, u32[]{:S(2)}) copy-start(bf16[128,4608]{1,0:T(8,128)(2,1)} %wd_own.3) | copy-start | bytes 3538948
  14.6 43.6 %collective-permute-start = (bf16[4608,128]{1,0:T(8,128)(2,1)}, bf16[4608,128]{1,0:T(8,128)(2,1)}, u32[]{:S(2)}, u32[]{:S(2)}) collective-permute-start(bf16[4608,128]{1,0:T(8,128)(2,1)} %we_own.1), channel_id=1, source_target_pairs={{0,8},{8,0},{16,24},{24,16},{32,40},{40,32},{48,56},{56,48},{64,72... | collective-permute-start | bytes 3538952 | tf_op jit(solution)/shard_map/ppermute | solution.py:192
  17.1 41.2 %collective-permute-start.1 = (bf16[128,4608]{1,0:T(8,128)(2,1)}, bf16[128,4608]{1,0:T(8,128)(2,1)S(1)}, u32[]{:S(2)}, u32[]{:S(2)}) collective-permute-start(bf16[128,4608]{1,0:T(8,128)(2,1)} %wd_own.3), channel_id=1, source_target_pairs={{0,8},{8,0},{16,24},{24,16},{32,40},{40,32},{48,56},{56,48},{64,72... | collective-permute-start | bytes 3538952 | tf_op jit(solution)/shard_map/ppermute | solution.py:193
  20.4 5.1 %collective-permute-start.2 = (f32[2,128]{1,0:T(2,128)S(1)}, f32[2,128]{1,0:T(2,128)S(1)}, u32[]{:S(2)}, u32[]{:S(2)}) collective-permute-start(f32[2,128]{1,0:T(2,128)S(1)} %pad_maximum_fusion.2), channel_id=1, source_target_pairs={{0,8},{8,0},{16,24},{24,16},{32,40},{40,32},{48,56},{56,48},{64,72... | collective-permute-start | bytes 3080 | tf_op jit(solution)/shard_map/ppermute | solution.py:195
  28.3 0.7 copy-start.8
  58.2 1.0 copy-start.1
  59.2 1.3 copy-start.3
  63.9 0.7 copy-start.4
  64.5 0.6 copy-start.6
  82.0 18.3 %all-to-all-start.2 = ((bf16[8,144,128]{2,1,0:T(8,128)(2,1)}), bf16[8,144,128]{2,1,0:T(8,128)(2,1)S(1)}, u32[]{:S(2)}, u32[]{:S(2)}) async-start(bf16[8,144,128]{2,1,0:T(8,128)(2,1)} %reduce_sum.47), calls=%async_computation.2 | async-start | bytes 589824 | tf_op jit(solution)/shard_map/all_to_all | solution.py:40
  101.2 42.8 %copy-start.7 = (bf16[128,256]{1,0:T(8,128)(2,1)S(1)}, bf16[128,256]{1,0:T(8,128)(2,1)}, u32[]{:S(2)}) copy-start(bf16[128,256]{1,0:T(8,128)(2,1)} %copy-done.6) | copy-start | bytes 196612
  145.5 4.8 %collective-permute-start.3 = (bf16[4,1200,128]{2,1,0:T(8,128)(2,1)S(1)}, bf16[4,1200,128]{2,1,0:T(8,128)(2,1)S(1)}, u32[]{:S(2)}, u32[]{:S(2)}) collective-permute-start(bf16[4,1200,128]{2,1,0:T(8,128)(2,1)S(1)} %get-tuple-element.19), channel_id=1, source_target_pairs={{0,8},{8,0},{16,24},{24,16},{32,40},{40,32},{48,56},{56,48},{64,72... | collective-permute-start | bytes 3686408 | tf_op jit(solution)/shard_map/ppermute | solution.py:164
  150.3 1.4 copy-start.2
  150.3 1.4 copy-start.5
  155.7 6.8 %collective-permute-start.5 = (bf16[4,1168,128]{2,1,0:T(8,128)(2,1)}, bf16[4,1168,128]{2,1,0:T(8,128)(2,1)}, u32[]{:S(2)}, u32[]{:S(2)}) collective-permute-start(bf16[4,1168,128]{2,1,0:T(8,128)(2,1)} %get-tuple-element.25), channel_id=1, source_target_pairs={{0,8},{8,0},{16,24},{24,16},{32,40},{40,32},{48,56},{56,48},{64,72... | collective-permute-start | bytes 3588104 | tf_op jit(solution)/shard_map/ppermute | solution.py:164
  157.8 20.6 %all-to-all-start.4 = ((bf16[4,1200,128]{2,1,0:T(8,128)(2,1)}), bf16[4,1200,128]{2,1,0:T(8,128)(2,1)}, u32[]{:S(2)}, u32[]{:S(2)}) async-start(bf16[4,1200,128]{2,1,0:T(8,128)(2,1)} %add_convert_fusion), calls=%async_computation.4 | async-start | bytes 2457600 | tf_op jit(solution)/shard_map/all_to_all | solution.py:169
  178.4 26.6 %all-to-all-start.5 = ((bf16[4,1168,128]{2,1,0:T(8,128)(2,1)}), bf16[4,1168,128]{2,1,0:T(8,128)(2,1)S(1)}, u32[]{:S(2)}, u32[]{:S(2)}) async-start(bf16[4,1168,128]{2,1,0:T(8,128)(2,1)} %add_convert_fusion.1), calls=%async_computation.5 | async-start | bytes 2392064 | tf_op jit(solution)/shard_map/all_to_all | solution.py:169
  185.6 19.3 %collective-permute-start.4 = (bf16[1200,128]{1,0:T(8,128)(2,1)S(1)}, bf16[1200,128]{1,0:T(8,128)(2,1)S(1)}, u32[]{:S(2)}, u32[]{:S(2)}) collective-permute-start(bf16[1200,128]{1,0:T(8,128)(2,1)S(1)} %reduce_sum.50), channel_id=1, source_target_pairs={{0,1},{1,0},{2,3},{3,2},{4,5},{5,4},{6,7},{7,6},{8,9},{9,8},{10,11... | collective-permute-start | bytes 921608 | tf_op jit(solution)/shard_map/ppermute | solution.py:171
  205.0 21.2 %copy-start.9 = (bf16[1200,128]{1,0:T(8,128)(2,1)}, bf16[1200,128]{1,0:T(8,128)(2,1)S(1)}, u32[]{:S(2)}) copy-start(bf16[1200,128]{1,0:T(8,128)(2,1)S(1)} %add_convert_fusion.2) | copy-start | bytes 921604
  205.3 20.8 %collective-permute-start.6 = (bf16[1168,128]{1,0:T(8,128)(2,1)S(1)}, bf16[1168,128]{1,0:T(8,128)(2,1)S(1)}, u32[]{:S(2)}, u32[]{:S(2)}) collective-permute-start(bf16[1168,128]{1,0:T(8,128)(2,1)S(1)} %reduce_sum.51), channel_id=1, source_target_pairs={{0,1},{1,0},{2,3},{3,2},{4,5},{5,4},{6,7},{7,6},{8,9},{9,8},{10,11... | collective-permute-start | bytes 897032 | tf_op jit(solution)/shard_map/ppermute | solution.py:171
  226.2 0.9 slice-start

commit v4 on v3

--- a/solution.py
+++ b/solution.py
@@ -40,12 +40,8 @@
     return lax.all_to_all(parts, "dict", 0, 0, axis_index_groups=groups(axes))
 
 
-def gather_near(blocks):
-    half = blocks.shape[0] // 2
-    return [
-        lax.all_gather(part, "dict", axis=0, axis_index_groups=groups(NEAR))
-        for part in (blocks[:half], blocks[half:])
-    ]
+def spread(block, axes):
+    return exchange(jnp.broadcast_to(block[None], (size_of(axes),) + block.shape), axes)
 
 
 def chip_blocks():
@@ -55,11 +51,10 @@
             yield near, far, y * 8 + z
 
 
-def in_order(first_ref, second_ref, whole_ref):
-    half, cols = first_ref.shape[1:3]
+def in_order(parts_ref, whole_ref):
+    cols = parts_ref.shape[2]
     for near, far, chip in chip_blocks():
-        ref = first_ref if far < half else second_ref
-        whole_ref[chip * cols : (chip + 1) * cols, :] = ref[near, far % half]
+        whole_ref[chip * cols : (chip + 1) * cols, :] = parts_ref[near, far]
 
 
 def dot(a, b, dims):
@@ -67,9 +62,9 @@
 
 
 def forward_kernel(
-    act_0, act_1, we_own, we_other, wd_own, wd_other, row_ref, parts_ref, feat_ref, slope_ref, act
+    act_ref, we_own, we_other, wd_own, wd_other, row_ref, parts_ref, feat_ref, slope_ref, act
 ):
-    in_order(act_0, act_1, act)
+    in_order(act_ref, act)
     for n, we in enumerate((we_own, we_other)):
         lanes = slice(n * TILE, (n + 1) * TILE)
         bias, theta, live = row_ref[0:1, lanes], row_ref[1:2, lanes], row_ref[2:3, lanes]
@@ -90,8 +85,8 @@
             parts_ref[near, far] = turned[i * cols : (i + 1) * cols, :]
 
 
-def decoder_kernel(res_0, res_1, feat_ref, own_ref, other_ref, res, bias):
-    in_order(res_0, res_1, res)
+def decoder_kernel(res_ref, feat_ref, own_ref, other_ref, res, bias):
+    in_order(res_ref, res)
     d = res.shape[0]
     quarter, lat = d // NX, TILE // NX
     feat_t = jnp.concatenate([feat_ref[...].T, jnp.ones((16, TILE), BF16)], axis=0)
@@ -111,10 +106,10 @@
 
 
 def encoder_kernel(
-    res_0, res_1, act_0, act_1, wd_own, wd_other, slope_ref, own_ref, other_ref, act, res
+    res_ref, act_ref, wd_own, wd_other, slope_ref, own_ref, other_ref, act, res
 ):
-    in_order(act_0, act_1, act)
-    in_order(res_0, res_1, res)
+    in_order(act_ref, act)
+    in_order(res_ref, res)
     quarter = act.shape[0] // NX
     res_t = res[...].T
     for n, (wd, out) in enumerate(((wd_own, own_ref), (wd_other, other_ref))):
@@ -129,16 +124,12 @@
             out[x, quarter:, :] = rows
 
 
-def unpack_kernel(first_ref, second_ref, third_ref, enc_ref, dec_ref):
-    quarter, lat = enc_ref.shape[0] // NX, TILE // NX
-    size = first_ref.shape[1]
-    rest = quarter - size
+def unpack_kernel(parts_ref, dec_ref):
+    lat = dec_ref.shape[0] // NX
     for x in range(NX):
-        enc_ref[x * quarter : x * quarter + size - rest, :] = second_ref[x, rest:, :]
-        enc_ref[x * quarter + size - rest : (x + 1) * quarter, :] = third_ref[x]
-        for i in range(enc_ref.shape[0] // TILE):
-            ref, at = (first_ref, i * lat) if i * lat < size else (second_ref, i * lat - size)
-            dec_ref[x * lat : (x + 1) * lat, i * TILE : (i + 1) * TILE] = ref[x, at : at + lat, :]
+        for i in range(dec_ref.shape[1] // TILE):
+            rows, lanes = slice(i * lat, (i + 1) * lat), slice(i * TILE, (i + 1) * TILE)
+            dec_ref[x * lat : (x + 1) * lat, lanes] = parts_ref[x, rows, :]
 
 
 def call(kernel, outs, args, scratch=(), flops=0):
@@ -160,16 +151,20 @@
     return jax.ShapeDtypeStruct(dims, dtype)
 
 
-def sum_cores(own_part, other_part):
-    other_part = lax.ppermute(other_part, "dict", CORE_SWAP)
-    return (own_part.astype(F32) + other_part.astype(F32)).astype(BF16)
-
-
-def sum_dp(total):
-    parts = lax.all_to_all(total, "dp", 0, 0, axis_index_groups=X_GROUPS)
-    piece = lax.optimization_barrier(jnp.sum(parts.astype(F32), axis=0).astype(BF16))
-    swapped = lax.ppermute(piece, "dp", Y_SWAP)
-    return (piece.astype(F32) + swapped.astype(F32)).astype(BF16)
+def exchange_x(parts):
+    return lax.all_to_all(parts, "dp", 0, 0, axis_index_groups=X_GROUPS)
+
+
+def sum_parts(parts):
+    return lax.optimization_barrier(jnp.sum(parts.astype(F32), axis=0).astype(BF16))
+
+
+def add(a, b):
+    return (a.astype(F32) + b.astype(F32)).astype(BF16)
+
+
+def gather_x(piece):
+    return exchange_x(jnp.broadcast_to(piece[None], (NX,) + piece.shape))
 
 
 def local(activations, enc_weight, enc_bias, dec_weight, dec_bias, thresholds, active_blocks):
@@ -187,7 +182,7 @@
     chip = dict_index // 2
     own = lax.dynamic_index_in_dim(act, chip // 16 * 4 + chip % 8 // 2, keepdims=False)
     cols = own.shape[0]
-    act = gather_near(act)
+    act = spread(act, NEAR)
 
     enc_other = lax.ppermute(enc_weight, "dict", CORE_SWAP)
     dec_other = lax.ppermute(dec_weight, "dict", CORE_SWAP)
@@ -202,11 +197,11 @@
     parts, feat, slope = call(
         forward_kernel,
         [
-            shape((size_of(NEAR), far, cols, TILE)),
+            shape(act.shape),
             shape((TILE, 2 * TILE)),
             shape((TILE, 2 * TILE), F32),
         ],
-        (*act, enc_weight, enc_other, dec_weight, dec_other, rows),
+        (act, enc_weight, enc_other, dec_weight, dec_other, rows),
         [pltpu.VMEM((d, TILE), BF16)],
         2 * work,
     )
@@ -215,9 +210,7 @@
     recon = jnp.sum(exchange(near_sum, FAR).astype(F32), axis=0)
     bias = lax.dynamic_slice_in_dim(dec_bias, dict_index // 2 * cols, cols).astype(F32)
     residual = (recon + bias[:, None] - own.astype(F32)) / scale_root
-    residual = residual.astype(BF16)
-    residual = jnp.broadcast_to(residual[None], (far,) + residual.shape)
-    res = gather_near(exchange(residual, FAR))
+    res = spread(spread(residual.astype(BF16), FAR), NEAR)
 
     quarter = d // NX
     packed = shape((NX, quarter + DEC_BIAS_ROWS, TILE))
@@ -225,34 +218,37 @@
     dec_parts = call(
         decoder_kernel,
         [packed, packed],
-        (*res, feat),
+        (res, feat),
         [room, pltpu.VMEM((DEC_BIAS_ROWS, TILE), F32)],
         work,
     )
-    dec_total = sum_cores(*dec_parts)
-    dec_total, res = lax.optimization_barrier((dec_total, res))
+    dec_parts, res = lax.optimization_barrier((dec_parts, res))
     packed = shape((NX, quarter + ENC_BIAS_ROWS, TILE))
     enc_parts = call(
         encoder_kernel,
         [packed, packed],
-        (*res, *act, dec_weight, dec_other, slope),
+        (res, act, dec_weight, dec_other, slope),
         [room, room],
         2 * work,
     )
 
-    dec_piece, enc_piece = sum_dp(dec_total), sum_dp(sum_cores(*enc_parts))
-    size = 2 * quarter // 3
-    pieces = (
-        dec_piece[:size],
-        jnp.concatenate([dec_piece[size:quarter], enc_piece[: 2 * size - quarter]]),
-        enc_piece[2 * size - quarter : quarter],
-    )
-    whole = [
-        lax.all_gather(piece, "dp", axis=0, axis_index_groups=X_GROUPS) for piece in pieces
-    ]
-    enc, dec = call(unpack_kernel, [shape((d, TILE)), shape((TILE, d))], whole)
-    dec_bias_sum = dec_piece[quarter : quarter + d // TILE].reshape(-1)
-    return enc, dec, enc_piece[quarter], dec_bias_sum
+    dec_other = lax.ppermute(dec_parts[1], "dict", CORE_SWAP)
+    enc_other, dec_other = lax.optimization_barrier((enc_parts[1], dec_other))
+    dec_total = add(dec_parts[0], dec_other)
+    enc_total = add(enc_parts[0], lax.ppermute(enc_other, "dict", CORE_SWAP))
+    dec_moved, enc_total = lax.optimization_barrier((exchange_x(dec_total), enc_total))
+    dec_piece = sum_parts(dec_moved)
+    dec_swapped = lax.ppermute(dec_piece, "dp", Y_SWAP)
+    enc_piece = sum_parts(exchange_x(enc_total))
+    enc_swapped = lax.ppermute(enc_piece, "dp", Y_SWAP)
+    dec_swapped, enc_piece = lax.optimization_barrier((dec_swapped, enc_piece))
+    dec_sum = add(dec_piece, dec_swapped)
+    dec_whole = gather_x(dec_sum[:quarter])
+    (dec,) = call(unpack_kernel, [shape((TILE, d))], (dec_whole,))
+    dec_whole, enc_swapped = lax.optimization_barrier((dec_whole, enc_swapped))
+    enc_sum = add(enc_piece, enc_swapped)
+    enc = gather_x(enc_sum[:quarter]).reshape(d, TILE)
+    return enc, dec, enc_sum[quarter], dec_sum[quarter : quarter + d // TILE].reshape(-1)
 
 
 def solution(mesh):

time: 259 us -> 226 us (0.87)
  blocking collectives: 129 us -> 79 us
  waiting for transfers between devices: 43.7 us -> 63.8 us
  starting transfers between devices: 52.3 us -> 49.2 us
    all_gather x7 -> x0, blocking collectives: 97.6 us -> none  [the longest x4 56.7 us: gather_near(): lax.all_gather(part, 'dict', axis=0, axis_index_groups=groups(NEAR))]
    all_to_all x2 -> x4, blocking collectives: 31.1 us -> 79 us  [exchange(): return lax.all_to_all(parts, 'dict', 0, 0, axis_index_groups=groups(axes))]
    all_to_all x2 -> x4, waiting for transfers between devices: 13.2 us -> 31.1 us  [exchange_x(): return lax.all_to_all(parts, 'dp', 0, 0, axis_index_groups=X_GROUPS)]
    all_to_all x2, starting transfers between devices: 18.5 us -> 7.08 us  [exchange(): return lax.all_to_all(parts, 'dict', 0, 0, axis_index_groups=groups(axes))]
    all_to_all x2 -> x4, starting transfers between devices: 10.4 us -> 19.9 us  [exchange_x(): return lax.all_to_all(parts, 'dp', 0, 0, axis_index_groups=X_GROUPS)]
    broadcast_in_dim x1 -> x5, local copies, waits for them, and re-layouts: 0.04 us -> 3.69 us  [the longest x2 2.33 us: gather_x(): return exchange_x(jnp.broadcast_to(piece[None], (NX,) + piece.shape))]
    all_to_all x2, waiting for transfers between devices: 14.1 us -> 16.9 us  [exchange(): return lax.all_to_all(parts, 'dict', 0, 0, axis_index_groups=groups(axes))]
  transfers between devices with their start and end apart: 11 -> 13, of which waited for: 5 -> 7; matrix products, arithmetic and copies ran while one was open for 4% -> 5% of each run, Pallas kernels for 0% -> 2%
where the time goes in v4:
time: 226 us; the launch traced here: 224 us
  blocking collectives  79 us (35%)
  waiting for transfers between devices  63.8 us (28%)
  starting transfers between devices  49.2 us (22%)
  other arithmetic  10.9 us (5%)
  Pallas kernels  10.4 us (5%)
  local copies, waits for them, and re-layouts  9.28 us (4%)
    all_to_all x4, blocking collectives, exchange(): return lax.all_to_all(parts, 'dict', 0, 0, axis_index_groups=groups(axes))  79 us
    all_to_all x4, waiting for transfers between devices, exchange_x(): return lax.all_to_all(parts, 'dp', 0, 0, axis_index_groups=X_GROUPS)  31.1 us
    all_to_all x4, starting transfers between devices, exchange_x(): return lax.all_to_all(parts, 'dp', 0, 0, axis_index_groups=X_GROUPS)  19.9 us
    all_to_all x2, waiting for transfers between devices, exchange(): return lax.all_to_all(parts, 'dict', 0, 0, axis_index_groups=groups(axes))  16.9 us
    pallas_call x4, Pallas kernels, call(): pl.pallas_call(kernel, out_shape=outs, in_specs=[whole] * len(args), out_...  10.4 us
    ppermute x1, waiting for transfers between devices, local(): enc_swapped = lax.ppermute(enc_piece, 'dp', Y_SWAP)  9.55 us
    all_to_all x2, starting transfers between devices, exchange(): return lax.all_to_all(parts, 'dict', 0, 0, axis_index_groups=groups(axes))  7.08 us
    ppermute x1, waiting for transfers between devices, local(): dec_swapped = lax.ppermute(dec_piece, 'dp', Y_SWAP)  6.24 us
  transfers between devices with their start and end apart: 13, of which 7 were waited for; matrix products, arithmetic and copies ran while one was open for 5% of the time, Pallas kernels for 2%

profile of v4, /device:TPU:6, one launch (start us, length us, event | category | flops | bytes accessed | tf_op | source)
XLA Modules:
  0.0 223.6 jit_solution(1570826414279932844)
XLA Ops:
  0.6 0.7 slice_bitcast_fusion.1
  1.4 26.0 %all_to_all.50 = bf16[16,72,128]{2,1,0:T(8,128)(2,1)S(1)} all-to-all(bf16[16,72,128]{2,1,0:T(8,128)(2,1)S(1)} %bitcast.35), channel_id=1, replica_groups={{0,8,32,40,64,72,96,104,256,264,288,296,320,328,352,360},{16,24,48,56,8..., dimensions={0} | all-to-all | bytes 589824 | tf_op jit(solution)/shard_map/all_to_all | solution.py:40
  27.4 0.7 copy-done.7
  28.1 1.2 broadcast_in_dim.22
  29.3 3.7 %all-to-all-start.1 = ((bf16[4,8,144,128]{3,2,1,0:T(8,128)(2,1)}), bf16[4,8,144,128]{3,2,1,0:T(8,128)(2,1)S(1)}, u32[]{:S(2)}, u32[]{:S(2)}) async-start(bf16[4,8,144,128]{3,2,1,0:T(8,128)(2,1)} %broadcast_in_dim.22), calls=%async_computation.1 | async-start | bytes 2359296 | tf_op jit(solution)/shard_map/all_to_all | solution.py:40
  32.9 2.6 %collective-permute-start = (bf16[4608,128]{1,0:T(8,128)(2,1)}, bf16[4608,128]{1,0:T(8,128)(2,1)}, u32[]{:S(2)}, u32[]{:S(2)}) collective-permute-start(bf16[4608,128]{1,0:T(8,128)(2,1)} %we_own.1), channel_id=1, source_target_pairs={{0,8},{8,0},{16,24},{24,16},{32,40},{40,32},{48,56},{56,48},{64,72... | collective-permute-start | bytes 3538952 | tf_op jit(solution)/shard_map/ppermute | solution.py:187
  35.6 1.9 collective-permute-start.1
  37.6 2.4 %collective-permute-start.2 = (f32[2,128]{1,0:T(2,128)S(1)}, f32[2,128]{1,0:T(2,128)S(1)}, u32[]{:S(2)}, u32[]{:S(2)}) collective-permute-start(f32[2,128]{1,0:T(2,128)S(1)} %pad_maximum_fusion.1), channel_id=1, source_target_pairs={{0,8},{8,0},{16,24},{24,16},{32,40},{40,32},{48,56},{56,48},{64,72... | collective-permute-start | bytes 3080 | tf_op jit(solution)/shard_map/ppermute | solution.py:190
  40.0 1.3 compare_reduce_fusion.1
  41.4 1.4 add_convert_fusion.4
  42.9 0.5 copy-done.8
  43.4 0.7 maximum_maximum_fusion.row_ref
  44.1 5.0 %all-to-all-done.1.act_ref = bf16[4,8,144,128]{3,2,1,0:T(8,128)(2,1)S(1)} async-done(((bf16[4,8,144,128]{3,2,1,0:T(8,128)(2,1)}), bf16[4,8,144,128]{3,2,1,0:T(8,128)(2,1)S(1)}, u32[]{:S(2)}, u32[]{:S(2)}) %all-to-all-start.1) | async-done | bytes 1179680 | tf_op jit(solution)/shard_map/all_to_all | solution.py:40
  49.1 3.7 %shard_map.102 = (bf16[4,8,144,128]{3,2,1,0:T(8,128)(2,1)S(1)}, bf16[128,256]{1,0:T(8,128)(2,1)S(1)}, f32[128,256]{1,0:T(8,128)S(1)}) custom-call(bf16[4,8,144,128]{3,2,1,0:T(8,128)(2,1)S(1)} %all-to-all-done.1.act_ref, bf16[4608,128]{1,0:T(8,128)(2,1)} %we_own.1, bf16[4608,128]{1,0:T(8,128)(2,1)} %collective-permute-done.we_other, ...), custom_call_target="tpu_custom_call" | custom-call | flops 603979776 | bytes 7282688 | tf_op jit(solution)/shard_map/pallas_call | solution.py:139
  52.9 0.6 copy-done.3
  53.5 0.6 copy-done.5
  54.1 18.3 %all_to_all.51 = bf16[4,8,144,128]{3,2,1,0:T(8,128)(2,1)S(1)} all-to-all(bf16[4,8,144,128]{3,2,1,0:T(8,128)(2,1)S(1)} %get-tuple-element.21), channel_id=1, replica_groups={{0,16,128,144},{8,24,136,152},{32,48,160,176},{40,56,168,184},{64,80,19..., dimensions={0} | all-to-all | bytes 2359296 | tf_op jit(solution)/shard_map/all_to_all | solution.py:40
  72.4 0.9 reduce_sum.47
  73.3 3.4 %all-to-all-start.3 = ((bf16[8,144,128]{2,1,0:T(8,128)(2,1)}), bf16[8,144,128]{2,1,0:T(8,128)(2,1)S(1)}, u32[]{:S(2)}, u32[]{:S(2)}) async-start(bf16[8,144,128]{2,1,0:T(8,128)(2,1)} %reduce_sum.47), calls=%async_computation.3 | async-start | bytes 589824 | tf_op jit(solution)/shard_map/all_to_all | solution.py:40
  76.9 0.8 dynamic-slice_convert_fusion
  77.6 11.9 %all-to-all-done.3 = bf16[8,144,128]{2,1,0:T(8,128)(2,1)S(1)} async-done(((bf16[8,144,128]{2,1,0:T(8,128)(2,1)}), bf16[8,144,128]{2,1,0:T(8,128)(2,1)S(1)}, u32[]{:S(2)}, u32[]{:S(2)}) %all-to-all-start.3) | async-done | bytes 294944 | tf_op jit(solution)/shard_map/all_to_all | solution.py:40
  89.6 0.9 fusion.3
  90.5 16.6 %all_to_all.52 = bf16[8,144,128]{2,1,0:T(8,128)(2,1)S(1)} all-to-all(bf16[8,144,128]{2,1,0:T(8,128)(2,1)S(1)} %broadcast_in_dim.52), channel_id=1, replica_groups={{0,32,64,96,256,288,320,352},{8,40,72,104,264,296,328,360},{16,48,80,11..., dimensions={0} | all-to-all | bytes 589824 | tf_op jit(solution)/shard_map/all_to_all | solution.py:40
  107.3 18.1 %all_to_all.53.res_ref = bf16[4,8,144,128]{3,2,1,0:T(8,128)(2,1)S(1)} all-to-all(bf16[4,8,144,128]{3,2,1,0:T(8,128)(2,1)S(1)} %broadcast_in_dim.53), channel_id=1, replica_groups={{0,16,128,144},{8,24,136,152},{32,48,160,176},{40,56,168,184},{64,80,19..., dimensions={0} | all-to-all | bytes 2359296 | tf_op jit(solution)/shard_map/all_to_all | solution.py:40
  125.4 1.5 shard_map.103
  126.9 1.9 collective-permute-start.3
  128.9 4.0 %shard_map.104 = (bf16[4,1168,128]{2,1,0:T(8,128)(2,1)S(1)}, bf16[4,1168,128]{2,1,0:T(8,128)(2,1)}) custom-call(bf16[4,8,144,128]{3,2,1,0:T(8,128)(2,1)S(1)} %all_to_all.53.res_ref, bf16[4,8,144,128]{3,2,1,0:T(8,128)(2,1)S(1)} %all-to-all-done.1.act_ref, bf16[128,4608]{1,0:T(8,128)(2,1)S(1)} %copy-done, bf16[128,4608]{1,0:T(8,128)(2,1)S(1)} %copy-done.2, ...), custom_call_target="tpu_custom_call" | custom-call | flops 603979776 | bytes 7241728 | tf_op jit(solution)/shard_map/pallas_call | solution.py:139
  132.9 2.4 %collective-permute-start.4 = (bf16[4,1168,128]{2,1,0:T(8,128)(2,1)}, bf16[4,1168,128]{2,1,0:T(8,128)(2,1)}, u32[]{:S(2)}, u32[]{:S(2)}) collective-permute-start(bf16[4,1168,128]{2,1,0:T(8,128)(2,1)} %get-tuple-element.32), channel_id=1, source_target_pairs={{0,8},{8,0},{16,24},{24,16},{32,40},{40,32},{48,56},{56,48},{64,72... | collective-permute-start | bytes 3588104 | tf_op jit(solution)/shard_map/ppermute | solution.py:238
  135.3 1.4 add_convert_fusion
  136.7 4.8 %all-to-all-start.6 = ((bf16[4,1200,128]{2,1,0:T(8,128)(2,1)}), bf16[4,1200,128]{2,1,0:T(8,128)(2,1)S(1)}, u32[]{:S(2)}, u32[]{:S(2)}) async-start(bf16[4,1200,128]{2,1,0:T(8,128)(2,1)} %add_convert_fusion), calls=%async_computation.6 | async-start | bytes 2457600 | tf_op jit(solution)/shard_map/all_to_all | solution.py:155
  141.5 2.6 %add_convert_fusion.1 = bf16[4,1168,128]{2,1,0:T(8,128)(2,1)} fusion(bf16[4,1168,128]{2,1,0:T(8,128)(2,1)} %collective-permute-done.4, bf16[4,1168,128]{2,1,0:T(8,128)(2,1)S(1)} %get-tuple-element.31), kind=kLoop, calls=%fused_computation.1 | loop fusion | flops 2392064 | bytes 3588096 | tf_op jit(solution)/shard_map/convert_element_type | solution.py:163
  144.1 12.5 %all-to-all-done.6 = bf16[4,1200,128]{2,1,0:T(8,128)(2,1)S(1)} async-done(((bf16[4,1200,128]{2,1,0:T(8,128)(2,1)}), bf16[4,1200,128]{2,1,0:T(8,128)(2,1)S(1)}, u32[]{:S(2)}, u32[]{:S(2)}) %all-to-all-start.6) | async-done | bytes 1228832 | tf_op jit(solution)/shard_map/all_to_all | solution.py:155
  156.6 5.6 %all-to-all-start.7 = ((bf16[4,1168,128]{2,1,0:T(8,128)(2,1)}), bf16[4,1168,128]{2,1,0:T(8,128)(2,1)S(1)}, u32[]{:S(2)}, u32[]{:S(2)}) async-start(bf16[4,1168,128]{2,1,0:T(8,128)(2,1)} %add_convert_fusion.1), calls=%async_computation.7 | async-start | bytes 2392064 | tf_op jit(solution)/shard_map/all_to_all | solution.py:155
  162.2 0.3 reduce_sum.50
  162.5 6.0 %collective-permute-start.5 = (bf16[1200,128]{1,0:T(8,128)(2,1)S(1)}, bf16[1200,128]{1,0:T(8,128)(2,1)S(1)}, u32[]{:S(2)}, u32[]{:S(2)}) collective-permute-start(bf16[1200,128]{1,0:T(8,128)(2,1)S(1)} %reduce_sum.50), channel_id=1, source_target_pairs={{0,1},{1,0},{2,3},{3,2},{4,5},{5,4},{6,7},{7,6},{8,9},{9,8},{10,11... | collective-permute-start | bytes 921608 | tf_op jit(solution)/shard_map/ppermute | solution.py:241
  168.5 7.6 %all-to-all-done.7 = bf16[4,1168,128]{2,1,0:T(8,128)(2,1)S(1)} async-done(((bf16[4,1168,128]{2,1,0:T(8,128)(2,1)}), bf16[4,1168,128]{2,1,0:T(8,128)(2,1)S(1)}, u32[]{:S(2)}, u32[]{:S(2)}) %all-to-all-start.7) | async-done | bytes 1196064 | tf_op jit(solution)/shard_map/all_to_all | solution.py:155
  176.4 6.2 %collective-permute-done.5 = bf16[1200,128]{1,0:T(8,128)(2,1)S(1)} collective-permute-done((bf16[1200,128]{1,0:T(8,128)(2,1)S(1)}, bf16[1200,128]{1,0:T(8,128)(2,1)S(1)}, u32[]{:S(2)}, u32[]{:S(2)}) %collective-permute-start.5) | collective-permute-done | bytes 307232 | tf_op jit(solution)/shard_map/ppermute | solution.py:241
  182.7 1.2 broadcast_in_dim.54
  183.9 4.8 %all-to-all-start.8 = ((bf16[4,1152,128]{2,1,0:T(8,128)(2,1)}), bf16[4,1152,128]{2,1,0:T(8,128)(2,1)S(1)}, u32[]{:S(2)}, u32[]{:S(2)}) async-start(bf16[4,1152,128]{2,1,0:T(8,128)(2,1)} %broadcast_in_dim.54), calls=%async_computation.8 | async-start | bytes 2359296 | tf_op jit(solution)/shard_map/all_to_all | solution.py:155
  188.7 4.9 %collective-permute-start.6 = (bf16[1168,128]{1,0:T(8,128)(2,1)S(1)}, bf16[1168,128]{1,0:T(8,128)(2,1)S(1)}, u32[]{:S(2)}, u32[]{:S(2)}) collective-permute-start(bf16[1168,128]{1,0:T(8,128)(2,1)S(1)} %reduce_sum.51), channel_id=1, source_target_pairs={{0,1},{1,0},{2,3},{3,2},{4,5},{5,4},{6,7},{7,6},{8,9},{9,8},{10,11... | collective-permute-start | bytes 897032 | tf_op jit(solution)/shard_map/ppermute | solution.py:243
  193.6 9.5 %collective-permute-done.6 = bf16[1168,128]{1,0:T(8,128)(2,1)S(1)} collective-permute-done((bf16[1168,128]{1,0:T(8,128)(2,1)S(1)}, bf16[1168,128]{1,0:T(8,128)(2,1)S(1)}, u32[]{:S(2)}, u32[]{:S(2)}) %collective-permute-start.6) | collective-permute-done | bytes 299040 | tf_op jit(solution)/shard_map/ppermute | solution.py:243
  203.3 1.2 broadcast_in_dim.55
  204.4 4.8 %all-to-all-start.9 = ((bf16[4,1152,128]{2,1,0:T(8,128)(2,1)}), bf16[4,1152,128]{2,1,0:T(8,128)(2,1)S(1)}, u32[]{:S(2)}, u32[]{:S(2)}) async-start(bf16[4,1152,128]{2,1,0:T(8,128)(2,1)} %broadcast_in_dim.55), calls=%async_computation.9 | async-start | bytes 2359296 | tf_op jit(solution)/shard_map/all_to_all | solution.py:155
  209.2 0.6 slice_bitcast_fusion.2
  209.8 1.2 shard_map.105
  211.1 0.5 slice_bitcast_fusion.3
  211.6 11.0 %all-to-all-done.9 = bf16[4,1152,128]{2,1,0:T(8,128)(2,1)S(1)} async-done(((bf16[4,1152,128]{2,1,0:T(8,128)(2,1)}), bf16[4,1152,128]{2,1,0:T(8,128)(2,1)S(1)}, u32[]{:S(2)}, u32[]{:S(2)}) %all-to-all-start.9) | async-done | bytes 1179680 | tf_op jit(solution)/shard_map/all_to_all | solution.py:155
  222.6 1.0 copy.12
  (40 shorter events, 1.0 us)
Async XLA Ops:
  27.4 0.7 copy-start.7
  29.3 6.3 %copy-start = (bf16[128,4608]{1,0:T(8,128)(2,1)S(1)}, bf16[128,4608]{1,0:T(8,128)(2,1)}, u32[]{:S(2)}) copy-start(bf16[128,4608]{1,0:T(8,128)(2,1)} %wd_own.3) | copy-start | bytes 3538948
  29.3 8.3 %copy-start.9 = (bf16[128]{0:T(256)(128)(2,1)S(1)}, bf16[128]{0:T(256)(128)(2,1)}, u32[]{:S(2)}) copy-start(bf16[128]{0:T(256)(128)(2,1)} %param.9) | copy-start | bytes 772
  29.3 8.3 %copy-start.10 = (s32[128]{0:T(128)S(1)}, s32[128]{0:T(128)}, u32[]{:S(2)}) copy-start(s32[128]{0:T(128)} %param.12) | copy-start | bytes 1540
  29.3 19.9 %all-to-all-start.1 = ((bf16[4,8,144,128]{3,2,1,0:T(8,128)(2,1)}), bf16[4,8,144,128]{3,2,1,0:T(8,128)(2,1)S(1)}, u32[]{:S(2)}, u32[]{:S(2)}) async-start(bf16[4,8,144,128]{3,2,1,0:T(8,128)(2,1)} %broadcast_in_dim.22), calls=%async_computation.1 | async-start | bytes 2359296 | tf_op jit(solution)/shard_map/all_to_all | solution.py:40
  32.9 11.2 %collective-permute-start = (bf16[4608,128]{1,0:T(8,128)(2,1)}, bf16[4608,128]{1,0:T(8,128)(2,1)}, u32[]{:S(2)}, u32[]{:S(2)}) collective-permute-start(bf16[4608,128]{1,0:T(8,128)(2,1)} %we_own.1), channel_id=1, source_target_pairs={{0,8},{8,0},{16,24},{24,16},{32,40},{40,32},{48,56},{56,48},{64,72... | collective-permute-start | bytes 3538952 | tf_op jit(solution)/shard_map/ppermute | solution.py:187
  35.6 8.5 %collective-permute-start.1 = (bf16[128,4608]{1,0:T(8,128)(2,1)S(1)}, bf16[128,4608]{1,0:T(8,128)(2,1)S(1)}, u32[]{:S(2)}, u32[]{:S(2)}) collective-permute-start(bf16[128,4608]{1,0:T(8,128)(2,1)S(1)} %copy-done), channel_id=1, source_target_pairs={{0,8},{8,0},{16,24},{24,16},{32,40},{40,32},{48,56},{56,48},{64,72... | collective-permute-start | bytes 3538952 | tf_op jit(solution)/shard_map/ppermute | solution.py:188
  37.6 5.2 %collective-permute-start.2 = (f32[2,128]{1,0:T(2,128)S(1)}, f32[2,128]{1,0:T(2,128)S(1)}, u32[]{:S(2)}, u32[]{:S(2)}) collective-permute-start(f32[2,128]{1,0:T(2,128)S(1)} %pad_maximum_fusion.1), channel_id=1, source_target_pairs={{0,8},{8,0},{16,24},{24,16},{32,40},{40,32},{48,56},{56,48},{64,72... | collective-permute-start | bytes 3080 | tf_op jit(solution)/shard_map/ppermute | solution.py:190
  42.8 0.6 copy-start.8
  44.1 5.0 %copy-start.1 = (bf16[128,4608]{1,0:T(8,128)(2,1)}, bf16[128,4608]{1,0:T(8,128)(2,1)S(1)}, u32[]{:S(2)}) copy-start(bf16[128,4608]{1,0:T(8,128)(2,1)S(1)} %collective-permute-done.1.wd_other) | copy-start | bytes 3538948
  52.9 0.7 copy-start.3
  53.5 0.6 copy-start.5
  73.3 16.2 %all-to-all-start.3 = ((bf16[8,144,128]{2,1,0:T(8,128)(2,1)}), bf16[8,144,128]{2,1,0:T(8,128)(2,1)S(1)}, u32[]{:S(2)}, u32[]{:S(2)}) async-start(bf16[8,144,128]{2,1,0:T(8,128)(2,1)} %reduce_sum.47), calls=%async_computation.3 | async-start | bytes 589824 | tf_op jit(solution)/shard_map/all_to_all | solution.py:40
  107.3 18.1 %copy-start.6 = (bf16[128,256]{1,0:T(8,128)(2,1)S(1)}, bf16[128,256]{1,0:T(8,128)(2,1)}, u32[]{:S(2)}) copy-start(bf16[128,256]{1,0:T(8,128)(2,1)} %copy-done.5) | copy-start | bytes 196612
  107.3 21.6 %copy-start.4 = (f32[128,256]{1,0:T(8,128)S(1)}, f32[128,256]{1,0:T(8,128)}, u32[]{:S(2)}) copy-start(f32[128,256]{1,0:T(8,128)} %copy-done.3) | copy-start | bytes 393220
  125.4 3.4 %copy-start.2 = (bf16[128,4608]{1,0:T(8,128)(2,1)S(1)}, bf16[128,4608]{1,0:T(8,128)(2,1)}, u32[]{:S(2)}) copy-start(bf16[128,4608]{1,0:T(8,128)(2,1)} %copy-done.1) | copy-start | bytes 3538948
  126.9 6.0 %collective-permute-start.3 = (bf16[4,1200,128]{2,1,0:T(8,128)(2,1)S(1)}, bf16[4,1200,128]{2,1,0:T(8,128)(2,1)S(1)}, u32[]{:S(2)}, u32[]{:S(2)}) collective-permute-start(bf16[4,1200,128]{2,1,0:T(8,128)(2,1)S(1)} %get-tuple-element.29), channel_id=1, source_target_pairs={{0,8},{8,0},{16,24},{24,16},{32,40},{40,32},{48,56},{56,48},{64,72... | collective-permute-start | bytes 3686408 | tf_op jit(solution)/shard_map/ppermute | solution.py:235
  132.9 8.6 %collective-permute-start.4 = (bf16[4,1168,128]{2,1,0:T(8,128)(2,1)}, bf16[4,1168,128]{2,1,0:T(8,128)(2,1)}, u32[]{:S(2)}, u32[]{:S(2)}) collective-permute-start(bf16[4,1168,128]{2,1,0:T(8,128)(2,1)} %get-tuple-element.32), channel_id=1, source_target_pairs={{0,8},{8,0},{16,24},{24,16},{32,40},{40,32},{48,56},{56,48},{64,72... | collective-permute-start | bytes 3588104 | tf_op jit(solution)/shard_map/ppermute | solution.py:238
  136.7 19.9 %all-to-all-start.6 = ((bf16[4,1200,128]{2,1,0:T(8,128)(2,1)}), bf16[4,1200,128]{2,1,0:T(8,128)(2,1)S(1)}, u32[]{:S(2)}, u32[]{:S(2)}) async-start(bf16[4,1200,128]{2,1,0:T(8,128)(2,1)} %add_convert_fusion), calls=%async_computation.6 | async-start | bytes 2457600 | tf_op jit(solution)/shard_map/all_to_all | solution.py:155
  156.6 19.5 %all-to-all-start.7 = ((bf16[4,1168,128]{2,1,0:T(8,128)(2,1)}), bf16[4,1168,128]{2,1,0:T(8,128)(2,1)S(1)}, u32[]{:S(2)}, u32[]{:S(2)}) async-start(bf16[4,1168,128]{2,1,0:T(8,128)(2,1)} %add_convert_fusion.1), calls=%async_computation.7 | async-start | bytes 2392064 | tf_op jit(solution)/shard_map/all_to_all | solution.py:155
  162.5 20.1 %collective-permute-start.5 = (bf16[1200,128]{1,0:T(8,128)(2,1)S(1)}, bf16[1200,128]{1,0:T(8,128)(2,1)S(1)}, u32[]{:S(2)}, u32[]{:S(2)}) collective-permute-start(bf16[1200,128]{1,0:T(8,128)(2,1)S(1)} %reduce_sum.50), channel_id=1, source_target_pairs={{0,1},{1,0},{2,3},{3,2},{4,5},{5,4},{6,7},{7,6},{8,9},{9,8},{10,11... | collective-permute-start | bytes 921608 | tf_op jit(solution)/shard_map/ppermute | solution.py:241
  183.9 19.3 %all-to-all-start.8 = ((bf16[4,1152,128]{2,1,0:T(8,128)(2,1)}), bf16[4,1152,128]{2,1,0:T(8,128)(2,1)S(1)}, u32[]{:S(2)}, u32[]{:S(2)}) async-start(bf16[4,1152,128]{2,1,0:T(8,128)(2,1)} %broadcast_in_dim.54), calls=%async_computation.8 | async-start | bytes 2359296 | tf_op jit(solution)/shard_map/all_to_all | solution.py:155
  188.7 14.5 %collective-permute-start.6 = (bf16[1168,128]{1,0:T(8,128)(2,1)S(1)}, bf16[1168,128]{1,0:T(8,128)(2,1)S(1)}, u32[]{:S(2)}, u32[]{:S(2)}) collective-permute-start(bf16[1168,128]{1,0:T(8,128)(2,1)S(1)} %reduce_sum.51), channel_id=1, source_target_pairs={{0,1},{1,0},{2,3},{3,2},{4,5},{5,4},{6,7},{7,6},{8,9},{9,8},{10,11... | collective-permute-start | bytes 897032 | tf_op jit(solution)/shard_map/ppermute | solution.py:243
  204.4 18.1 %all-to-all-start.9 = ((bf16[4,1152,128]{2,1,0:T(8,128)(2,1)}), bf16[4,1152,128]{2,1,0:T(8,128)(2,1)S(1)}, u32[]{:S(2)}, u32[]{:S(2)}) async-start(bf16[4,1152,128]{2,1,0:T(8,128)(2,1)} %broadcast_in_dim.55), calls=%async_computation.9 | async-start | bytes 2359296 | tf_op jit(solution)/shard_map/all_to_all | solution.py:155

commit v5 on v4

--- a/solution.py
+++ b/solution.py
@@ -18,7 +18,7 @@
 CHIPS = 32
 NX = 4
 DEC_BIAS_ROWS, ENC_BIAS_ROWS = 48, 16
-VMEM = 48 * 1024 * 1024
+VMEM = 24 * 1024 * 1024
 
 
 def size_of(axes):
@@ -65,13 +65,14 @@
     act_ref, we_own, we_other, wd_own, wd_other, row_ref, parts_ref, feat_ref, slope_ref, act
 ):
     in_order(act_ref, act)
+    act_t = act[...].T
     for n, we in enumerate((we_own, we_other)):
         lanes = slice(n * TILE, (n + 1) * TILE)
         bias, theta, live = row_ref[0:1, lanes], row_ref[1:2, lanes], row_ref[2:3, lanes]
-        pre = dot(act[...], we[...], ((0,), (0,))) + bias
+        pre = dot(act_t, we[...], ((1,), (0,))) + bias
         gate = jax.nn.sigmoid(SHARPNESS * (pre - theta))
         feat_ref[:, lanes] = (live * pre * gate).astype(BF16)
-        slope_ref[:, lanes] = live * (gate + SHARPNESS * pre * gate * (1.0 - gate))
+        slope_ref[lanes, :] = (live * (gate + SHARPNESS * pre * gate * (1.0 - gate))).T
     cols = parts_ref.shape[2]
     step = 8 * cols
     place = {chip: (near, far) for near, far, chip in chip_blocks()}
@@ -111,10 +112,9 @@
     in_order(act_ref, act)
     in_order(res_ref, res)
     quarter = act.shape[0] // NX
-    res_t = res[...].T
     for n, (wd, out) in enumerate(((wd_own, own_ref), (wd_other, other_ref))):
-        dfeat = dot(res_t, wd[...], ((1,), (1,)))
-        dpre = dfeat * slope_ref[:, n * TILE : (n + 1) * TILE]
+        dfeat = dot(wd[...], res[...], ((1,), (0,)))
+        dpre = (dfeat * slope_ref[n * TILE : (n + 1) * TILE, :]).T
         row = jnp.sum(dpre, axis=0, keepdims=True)
         rows = jnp.broadcast_to(row, (ENC_BIAS_ROWS, TILE)).astype(BF16)
         dpre = dpre.astype(BF16)
@@ -199,7 +199,7 @@
         [
             shape(act.shape),
             shape((TILE, 2 * TILE)),
-            shape((TILE, 2 * TILE), F32),
+            shape((2 * TILE, TILE), F32),
         ],
         (act, enc_weight, enc_other, dec_weight, dec_other, rows),
         [pltpu.VMEM((d, TILE), BF16)],
@@ -233,8 +233,8 @@
     )
 
     dec_other = lax.ppermute(dec_parts[1], "dict", CORE_SWAP)
-    enc_other, dec_other = lax.optimization_barrier((enc_parts[1], dec_other))
     dec_total = add(dec_parts[0], dec_other)
+    enc_other, dec_total = lax.optimization_barrier((enc_parts[1], dec_total))
     enc_total = add(enc_parts[0], lax.ppermute(enc_other, "dict", CORE_SWAP))
     dec_moved, enc_total = lax.optimization_barrier((exchange_x(dec_total), enc_total))
     dec_piece = sum_parts(dec_moved)

time: 226 us -> 230 us (1.018)
    unnamed x23 -> x25, local copies, waits for them, and re-layouts: 3.51 us -> 4.77 us
  transfers between devices with their start and end apart: 13 -> 13, of which waited for: 7 -> 8; matrix products, arithmetic and copies ran while one was open for 5% -> 4% of each run, Pallas kernels for 2% -> 2%
where the time goes in v5:
time: 230 us; the launch traced here: 228 us
  blocking collectives  79.8 us (35%)
  waiting for transfers between devices  65.4 us (28%)
  starting transfers between devices  49.2 us (21%)
  other arithmetic  13.2 us (6%)
  local copies, waits for them, and re-layouts  10.5 us (5%)
  Pallas kernels  8.64 us (4%)
    all_to_all x4, blocking collectives, exchange(): return lax.all_to_all(parts, 'dict', 0, 0, axis_index_groups=groups(axes))  79.8 us
    all_to_all x4, waiting for transfers between devices, exchange_x(): return lax.all_to_all(parts, 'dp', 0, 0, axis_index_groups=X_GROUPS)  32.7 us
    all_to_all x4, starting transfers between devices, exchange_x(): return lax.all_to_all(parts, 'dp', 0, 0, axis_index_groups=X_GROUPS)  20.7 us
    all_to_all x2, waiting for transfers between devices, exchange(): return lax.all_to_all(parts, 'dict', 0, 0, axis_index_groups=groups(axes))  17.2 us
    ppermute x1, waiting for transfers between devices, local(): enc_swapped = lax.ppermute(enc_piece, 'dp', Y_SWAP)  9.19 us
    pallas_call x4, Pallas kernels, call(): pl.pallas_call(kernel, out_shape=outs, in_specs=[whole] * len(args), out_...  8.64 us
    all_to_all x2, starting transfers between devices, exchange(): return lax.all_to_all(parts, 'dict', 0, 0, axis_index_groups=groups(axes))  7.74 us
    ppermute x1, waiting for transfers between devices, local(): dec_swapped = lax.ppermute(dec_piece, 'dp', Y_SWAP)  6.24 us
  transfers between devices with their start and end apart: 13, of which 8 were waited for; matrix products, arithmetic and copies ran while one was open for 4% of the time, Pallas kernels for 2%

profile of v5, /device:TPU:6, one launch (start us, length us, event | category | flops | bytes accessed | tf_op | source)
XLA Modules:
  0.0 227.7 jit_solution(11543048699501815087)
XLA Ops:
  0.6 0.7 slice_bitcast_fusion.1
  1.4 26.0 %all_to_all.50 = bf16[16,72,128]{2,1,0:T(8,128)(2,1)S(1)} all-to-all(bf16[16,72,128]{2,1,0:T(8,128)(2,1)S(1)} %bitcast.35), channel_id=1, replica_groups={{0,8,32,40,64,72,96,104,256,264,288,296,320,328,352,360},{16,24,48,56,8..., dimensions={0} | all-to-all | bytes 589824 | tf_op jit(solution)/shard_map/all_to_all | solution.py:40
  27.4 0.7 copy-done.8
  28.1 1.2 broadcast_in_dim.22
  29.3 3.7 %all-to-all-start.1 = ((bf16[4,8,144,128]{3,2,1,0:T(8,128)(2,1)}), bf16[4,8,144,128]{3,2,1,0:T(8,128)(2,1)S(1)}, u32[]{:S(2)}, u32[]{:S(2)}) async-start(bf16[4,8,144,128]{3,2,1,0:T(8,128)(2,1)} %broadcast_in_dim.22), calls=%async_computation.1 | async-start | bytes 2359296 | tf_op jit(solution)/shard_map/all_to_all | solution.py:40
  33.0 2.6 %collective-permute-start.1 = (bf16[128,4608]{1,0:T(8,128)(2,1)S(1)}, bf16[128,4608]{1,0:T(8,128)(2,1)S(1)}, u32[]{:S(2)}, u32[]{:S(2)}) collective-permute-start(bf16[128,4608]{1,0:T(8,128)(2,1)S(1)} %copy-done), channel_id=1, source_target_pairs={{0,8},{8,0},{16,24},{24,16},{32,40},{40,32},{48,56},{56,48},{64,72... | collective-permute-start | bytes 3538952 | tf_op jit(solution)/shard_map/ppermute | solution.py:188
  35.6 1.9 collective-permute-start
  37.6 2.4 %collective-permute-start.2 = (f32[2,128]{1,0:T(2,128)S(1)}, f32[2,128]{1,0:T(2,128)S(1)}, u32[]{:S(2)}, u32[]{:S(2)}) collective-permute-start(f32[2,128]{1,0:T(2,128)S(1)} %pad_maximum_fusion.1), channel_id=1, source_target_pairs={{0,8},{8,0},{16,24},{24,16},{32,40},{40,32},{48,56},{56,48},{64,72... | collective-permute-start | bytes 3080 | tf_op jit(solution)/shard_map/ppermute | solution.py:190
  40.0 1.3 compare_reduce_fusion.1
  41.4 1.4 add_convert_fusion.4
  43.4 0.7 maximum_maximum_fusion.row_ref
  44.1 5.0 %all-to-all-done.1.act_ref = bf16[4,8,144,128]{3,2,1,0:T(8,128)(2,1)S(1)} async-done(((bf16[4,8,144,128]{3,2,1,0:T(8,128)(2,1)}), bf16[4,8,144,128]{3,2,1,0:T(8,128)(2,1)S(1)}, u32[]{:S(2)}, u32[]{:S(2)}) %all-to-all-start.1) | async-done | bytes 1179680 | tf_op jit(solution)/shard_map/all_to_all | solution.py:40
  49.1 1.3 copy-done.3
  50.4 3.0 %shard_map.102 = (bf16[4,8,144,128]{3,2,1,0:T(8,128)(2,1)S(1)}, bf16[128,256]{1,0:T(8,128)(2,1)S(1)}, f32[256,128]{1,0:T(8,128)S(1)}) custom-call(bf16[4,8,144,128]{3,2,1,0:T(8,128)(2,1)S(1)} %all-to-all-done.1.act_ref, bf16[4608,128]{1,0:T(8,128)(2,1)S(1)} %copy-done.3, bf16[4608,128]{1,0:T(8,128)(2,1)} %collective-permute-done.we_other, ...), custom_call_target="tpu_custom_call" | custom-call | flops 603979776 | bytes 7282688 | tf_op jit(solution)/shard_map/pallas_call | solution.py:139
  53.4 0.6 copy-done.4
  54.1 0.6 copy-done.6
  54.7 19.0 %all_to_all.51 = bf16[4,8,144,128]{3,2,1,0:T(8,128)(2,1)} all-to-all(bf16[4,8,144,128]{3,2,1,0:T(8,128)(2,1)S(1)} %get-tuple-element.21), channel_id=1, replica_groups={{0,16,128,144},{8,24,136,152},{32,48,160,176},{40,56,168,184},{64,80,19..., dimensions={0} | all-to-all | bytes 2359296 | tf_op jit(solution)/shard_map/all_to_all | solution.py:40
  73.7 2.2 reduce_sum.47
  75.9 4.1 %all-to-all-start.3 = ((bf16[8,144,128]{2,1,0:T(8,128)(2,1)}), bf16[8,144,128]{2,1,0:T(8,128)(2,1)}, u32[]{:S(2)}, u32[]{:S(2)}) async-start(bf16[8,144,128]{2,1,0:T(8,128)(2,1)} %reduce_sum.47), calls=%async_computation.3 | async-start | bytes 589824 | tf_op jit(solution)/shard_map/all_to_all | solution.py:40
  80.1 0.8 dynamic-slice_convert_fusion
  80.9 12.2 %all-to-all-done.3 = bf16[8,144,128]{2,1,0:T(8,128)(2,1)} async-done(((bf16[8,144,128]{2,1,0:T(8,128)(2,1)}), bf16[8,144,128]{2,1,0:T(8,128)(2,1)}, u32[]{:S(2)}, u32[]{:S(2)}) %all-to-all-start.3) | async-done | bytes 294944 | tf_op jit(solution)/shard_map/all_to_all | solution.py:40
  93.0 1.0 convert_reduce_fusion
  94.1 0.9 fusion.3
  95.0 16.7 %all_to_all.52 = bf16[8,144,128]{2,1,0:T(8,128)(2,1)S(1)} all-to-all(bf16[8,144,128]{2,1,0:T(8,128)(2,1)S(1)} %broadcast_in_dim.52), channel_id=1, replica_groups={{0,32,64,96,256,288,320,352},{8,40,72,104,264,296,328,360},{16,48,80,11..., dimensions={0} | all-to-all | bytes 589824 | tf_op jit(solution)/shard_map/all_to_all | solution.py:40
  111.8 18.2 %all_to_all.53.res_ref = bf16[4,8,144,128]{3,2,1,0:T(8,128)(2,1)S(1)} all-to-all(bf16[4,8,144,128]{3,2,1,0:T(8,128)(2,1)S(1)} %broadcast_in_dim.53), channel_id=1, replica_groups={{0,16,128,144},{8,24,136,152},{32,48,160,176},{40,56,168,184},{64,80,19..., dimensions={0} | all-to-all | bytes 2359296 | tf_op jit(solution)/shard_map/all_to_all | solution.py:40
  130.0 1.5 shard_map.103
  131.5 1.9 collective-permute-start.3
  133.4 2.9 %shard_map.104 = (bf16[4,1168,128]{2,1,0:T(8,128)(2,1)S(1)}, bf16[4,1168,128]{2,1,0:T(8,128)(2,1)}) custom-call(bf16[4,8,144,128]{3,2,1,0:T(8,128)(2,1)S(1)} %all_to_all.53.res_ref, bf16[4,8,144,128]{3,2,1,0:T(8,128)(2,1)S(1)} %all-to-all-done.1.act_ref, bf16[128,4608]{1,0:T(8,128)(2,1)S(1)} %copy-done, ...), custom_call_target="tpu_custom_call" | custom-call | flops 603979776 | bytes 7241728 | tf_op jit(solution)/shard_map/pallas_call | solution.py:139
  136.4 1.4 add_convert_fusion
  137.8 2.5 %collective-permute-start.4 = (bf16[4,1168,128]{2,1,0:T(8,128)(2,1)}, bf16[4,1168,128]{2,1,0:T(8,128)(2,1)}, u32[]{:S(2)}, u32[]{:S(2)}) collective-permute-start(bf16[4,1168,128]{2,1,0:T(8,128)(2,1)} %get-tuple-element.32), channel_id=1, source_target_pairs={{0,8},{8,0},{16,24},{24,16},{32,40},{40,32},{48,56},{56,48},{64,72... | collective-permute-start | bytes 3588104 | tf_op jit(solution)/shard_map/ppermute | solution.py:238
  140.3 4.8 %all-to-all-start.6 = ((bf16[4,1200,128]{2,1,0:T(8,128)(2,1)}), bf16[4,1200,128]{2,1,0:T(8,128)(2,1)S(1)}, u32[]{:S(2)}, u32[]{:S(2)}) async-start(bf16[4,1200,128]{2,1,0:T(8,128)(2,1)} %add_convert_fusion), calls=%async_computation.6 | async-start | bytes 2457600 | tf_op jit(solution)/shard_map/all_to_all | solution.py:155
  145.1 2.6 %add_convert_fusion.1 = bf16[4,1168,128]{2,1,0:T(8,128)(2,1)} fusion(bf16[4,1168,128]{2,1,0:T(8,128)(2,1)} %collective-permute-done.4, bf16[4,1168,128]{2,1,0:T(8,128)(2,1)S(1)} %copy-done.2), kind=kLoop, calls=%fused_computation.1 | loop fusion | flops 2392064 | bytes 3588096 | tf_op jit(solution)/shard_map/convert_element_type | solution.py:163
  147.7 12.5 %all-to-all-done.6 = bf16[4,1200,128]{2,1,0:T(8,128)(2,1)S(1)} async-done(((bf16[4,1200,128]{2,1,0:T(8,128)(2,1)}), bf16[4,1200,128]{2,1,0:T(8,128)(2,1)S(1)}, u32[]{:S(2)}, u32[]{:S(2)}) %all-to-all-start.6) | async-done | bytes 1228832 | tf_op jit(solution)/shard_map/all_to_all | solution.py:155
  160.3 5.6 %all-to-all-start.7 = ((bf16[4,1168,128]{2,1,0:T(8,128)(2,1)}), bf16[4,1168,128]{2,1,0:T(8,128)(2,1)S(1)}, u32[]{:S(2)}, u32[]{:S(2)}) async-start(bf16[4,1168,128]{2,1,0:T(8,128)(2,1)} %add_convert_fusion.1), calls=%async_computation.7 | async-start | bytes 2392064 | tf_op jit(solution)/shard_map/all_to_all | solution.py:155
  166.2 4.6 %collective-permute-start.5 = (bf16[1200,128]{1,0:T(8,128)(2,1)S(1)}, bf16[1200,128]{1,0:T(8,128)(2,1)S(1)}, u32[]{:S(2)}, u32[]{:S(2)}) collective-permute-start(bf16[1200,128]{1,0:T(8,128)(2,1)S(1)} %reduce_sum.50), channel_id=1, source_target_pairs={{0,1},{1,0},{2,3},{3,2},{4,5},{5,4},{6,7},{7,6},{8,9},{9,8},{10,11... | collective-permute-start | bytes 921608 | tf_op jit(solution)/shard_map/ppermute | solution.py:241
  170.8 8.9 %all-to-all-done.7 = bf16[4,1168,128]{2,1,0:T(8,128)(2,1)S(1)} async-done(((bf16[4,1168,128]{2,1,0:T(8,128)(2,1)}), bf16[4,1168,128]{2,1,0:T(8,128)(2,1)S(1)}, u32[]{:S(2)}, u32[]{:S(2)}) %all-to-all-start.7) | async-done | bytes 1196064 | tf_op jit(solution)/shard_map/all_to_all | solution.py:155
  180.0 6.2 %collective-permute-done.5 = bf16[1200,128]{1,0:T(8,128)(2,1)S(1)} collective-permute-done((bf16[1200,128]{1,0:T(8,128)(2,1)S(1)}, bf16[1200,128]{1,0:T(8,128)(2,1)S(1)}, u32[]{:S(2)}, u32[]{:S(2)}) %collective-permute-start.5) | collective-permute-done | bytes 307232 | tf_op jit(solution)/shard_map/ppermute | solution.py:241
  186.4 1.2 broadcast_in_dim.54
  187.6 4.8 %all-to-all-start.8 = ((bf16[4,1152,128]{2,1,0:T(8,128)(2,1)}), bf16[4,1152,128]{2,1,0:T(8,128)(2,1)S(1)}, u32[]{:S(2)}, u32[]{:S(2)}) async-start(bf16[4,1152,128]{2,1,0:T(8,128)(2,1)} %broadcast_in_dim.54), calls=%async_computation.8 | async-start | bytes 2359296 | tf_op jit(solution)/shard_map/all_to_all | solution.py:155
  192.4 4.6 %collective-permute-start.6 = (bf16[1168,128]{1,0:T(8,128)(2,1)S(1)}, bf16[1168,128]{1,0:T(8,128)(2,1)S(1)}, u32[]{:S(2)}, u32[]{:S(2)}) collective-permute-start(bf16[1168,128]{1,0:T(8,128)(2,1)S(1)} %reduce_sum.51), channel_id=1, source_target_pairs={{0,1},{1,0},{2,3},{3,2},{4,5},{5,4},{6,7},{7,6},{8,9},{9,8},{10,11... | collective-permute-start | bytes 897032 | tf_op jit(solution)/shard_map/ppermute | solution.py:243
  197.0 9.2 %collective-permute-done.6 = bf16[1168,128]{1,0:T(8,128)(2,1)S(1)} collective-permute-done((bf16[1168,128]{1,0:T(8,128)(2,1)S(1)}, bf16[1168,128]{1,0:T(8,128)(2,1)S(1)}, u32[]{:S(2)}, u32[]{:S(2)}) %collective-permute-start.6) | collective-permute-done | bytes 299040 | tf_op jit(solution)/shard_map/ppermute | solution.py:243
  206.7 1.2 broadcast_in_dim.55
  207.8 5.6 %all-to-all-start.9 = ((bf16[4,1152,128]{2,1,0:T(8,128)(2,1)}), bf16[4,1152,128]{2,1,0:T(8,128)(2,1)S(1)}, u32[]{:S(2)}, u32[]{:S(2)}) async-start(bf16[4,1152,128]{2,1,0:T(8,128)(2,1)} %broadcast_in_dim.55), calls=%async_computation.9 | async-start | bytes 2359296 | tf_op jit(solution)/shard_map/all_to_all | solution.py:155
  213.4 0.6 slice_bitcast_fusion.2
  214.0 1.2 shard_map.105
  215.2 0.5 slice_bitcast_fusion.3
  215.7 11.0 %all-to-all-done.9 = bf16[4,1152,128]{2,1,0:T(8,128)(2,1)S(1)} async-done(((bf16[4,1152,128]{2,1,0:T(8,128)(2,1)}), bf16[4,1152,128]{2,1,0:T(8,128)(2,1)S(1)}, u32[]{:S(2)}, u32[]{:S(2)}) %all-to-all-start.9) | async-done | bytes 1179680 | tf_op jit(solution)/shard_map/all_to_all | solution.py:155
  226.7 1.0 copy.12
  (42 shorter events, 2.2 us)
Async XLA Ops:
  27.4 0.7 copy-start.8
  29.3 3.7 %copy-start = (bf16[128,4608]{1,0:T(8,128)(2,1)S(1)}, bf16[128,4608]{1,0:T(8,128)(2,1)}, u32[]{:S(2)}) copy-start(bf16[128,4608]{1,0:T(8,128)(2,1)} %wd_own.3) | copy-start | bytes 3538948
  29.3 8.3 %copy-start.10 = (bf16[128]{0:T(256)(128)(2,1)S(1)}, bf16[128]{0:T(256)(128)(2,1)}, u32[]{:S(2)}) copy-start(bf16[128]{0:T(256)(128)(2,1)} %param.9) | copy-start | bytes 772
  29.3 8.3 %copy-start.11 = (s32[128]{0:T(128)S(1)}, s32[128]{0:T(128)}, u32[]{:S(2)}) copy-start(s32[128]{0:T(128)} %param.12) | copy-start | bytes 1540
  29.3 19.9 %all-to-all-start.1 = ((bf16[4,8,144,128]{3,2,1,0:T(8,128)(2,1)}), bf16[4,8,144,128]{3,2,1,0:T(8,128)(2,1)S(1)}, u32[]{:S(2)}, u32[]{:S(2)}) async-start(bf16[4,8,144,128]{3,2,1,0:T(8,128)(2,1)} %broadcast_in_dim.22), calls=%async_computation.1 | async-start | bytes 2359296 | tf_op jit(solution)/shard_map/all_to_all | solution.py:40
  33.0 11.2 %collective-permute-start.1 = (bf16[128,4608]{1,0:T(8,128)(2,1)S(1)}, bf16[128,4608]{1,0:T(8,128)(2,1)S(1)}, u32[]{:S(2)}, u32[]{:S(2)}) collective-permute-start(bf16[128,4608]{1,0:T(8,128)(2,1)S(1)} %copy-done), channel_id=1, source_target_pairs={{0,8},{8,0},{16,24},{24,16},{32,40},{40,32},{48,56},{56,48},{64,72... | collective-permute-start | bytes 3538952 | tf_op jit(solution)/shard_map/ppermute | solution.py:188
  35.6 8.5 %collective-permute-start = (bf16[4608,128]{1,0:T(8,128)(2,1)}, bf16[4608,128]{1,0:T(8,128)(2,1)}, u32[]{:S(2)}, u32[]{:S(2)}) collective-permute-start(bf16[4608,128]{1,0:T(8,128)(2,1)} %we_own.1), channel_id=1, source_target_pairs={{0,8},{8,0},{16,24},{24,16},{32,40},{40,32},{48,56},{56,48},{64,72... | collective-permute-start | bytes 3538952 | tf_op jit(solution)/shard_map/ppermute | solution.py:187
  37.6 5.2 %collective-permute-start.2 = (f32[2,128]{1,0:T(2,128)S(1)}, f32[2,128]{1,0:T(2,128)S(1)}, u32[]{:S(2)}, u32[]{:S(2)}) collective-permute-start(f32[2,128]{1,0:T(2,128)S(1)} %pad_maximum_fusion.1), channel_id=1, source_target_pairs={{0,8},{8,0},{16,24},{24,16},{32,40},{40,32},{48,56},{56,48},{64,72... | collective-permute-start | bytes 3080 | tf_op jit(solution)/shard_map/ppermute | solution.py:190
  42.8 0.6 copy-start.9
  49.1 1.3 copy-start.3
  53.4 0.6 copy-start.4
  54.1 0.6 copy-start.6
  75.9 17.1 %all-to-all-start.3 = ((bf16[8,144,128]{2,1,0:T(8,128)(2,1)}), bf16[8,144,128]{2,1,0:T(8,128)(2,1)}, u32[]{:S(2)}, u32[]{:S(2)}) async-start(bf16[8,144,128]{2,1,0:T(8,128)(2,1)} %reduce_sum.47), calls=%async_computation.3 | async-start | bytes 589824 | tf_op jit(solution)/shard_map/all_to_all | solution.py:40
  111.8 18.2 %copy-start.7 = (bf16[128,256]{1,0:T(8,128)(2,1)S(1)}, bf16[128,256]{1,0:T(8,128)(2,1)}, u32[]{:S(2)}) copy-start(bf16[128,256]{1,0:T(8,128)(2,1)} %copy-done.6) | copy-start | bytes 196612
  130.0 3.4 %copy-start.5 = (f32[256,128]{1,0:T(8,128)S(1)}, f32[256,128]{1,0:T(8,128)}, u32[]{:S(2)}) copy-start(f32[256,128]{1,0:T(8,128)} %copy-done.4) | copy-start | bytes 393220
  131.5 4.9 %collective-permute-start.3 = (bf16[4,1200,128]{2,1,0:T(8,128)(2,1)S(1)}, bf16[4,1200,128]{2,1,0:T(8,128)(2,1)S(1)}, u32[]{:S(2)}, u32[]{:S(2)}) collective-permute-start(bf16[4,1200,128]{2,1,0:T(8,128)(2,1)S(1)} %get-tuple-element.29), channel_id=1, source_target_pairs={{0,8},{8,0},{16,24},{24,16},{32,40},{40,32},{48,56},{56,48},{64,72... | collective-permute-start | bytes 3686408 | tf_op jit(solution)/shard_map/ppermute | solution.py:235
  136.4 1.4 copy-start.1
  137.8 7.3 %copy-start.2 = (bf16[4,1168,128]{2,1,0:T(8,128)(2,1)S(1)}, bf16[4,1168,128]{2,1,0:T(8,128)(2,1)}, u32[]{:S(2)}) copy-start(bf16[4,1168,128]{2,1,0:T(8,128)(2,1)} %copy-done.1) | copy-start | bytes 3588100
  137.8 7.3 %collective-permute-start.4 = (bf16[4,1168,128]{2,1,0:T(8,128)(2,1)}, bf16[4,1168,128]{2,1,0:T(8,128)(2,1)}, u32[]{:S(2)}, u32[]{:S(2)}) collective-permute-start(bf16[4,1168,128]{2,1,0:T(8,128)(2,1)} %get-tuple-element.32), channel_id=1, source_target_pairs={{0,8},{8,0},{16,24},{24,16},{32,40},{40,32},{48,56},{56,48},{64,72... | collective-permute-start | bytes 3588104 | tf_op jit(solution)/shard_map/ppermute | solution.py:238
  140.3 19.9 %all-to-all-start.6 = ((bf16[4,1200,128]{2,1,0:T(8,128)(2,1)}), bf16[4,1200,128]{2,1,0:T(8,128)(2,1)S(1)}, u32[]{:S(2)}, u32[]{:S(2)}) async-start(bf16[4,1200,128]{2,1,0:T(8,128)(2,1)} %add_convert_fusion), calls=%async_computation.6 | async-start | bytes 2457600 | tf_op jit(solution)/shard_map/all_to_all | solution.py:155
  160.3 19.5 %all-to-all-start.7 = ((bf16[4,1168,128]{2,1,0:T(8,128)(2,1)}), bf16[4,1168,128]{2,1,0:T(8,128)(2,1)S(1)}, u32[]{:S(2)}, u32[]{:S(2)}) async-start(bf16[4,1168,128]{2,1,0:T(8,128)(2,1)} %add_convert_fusion.1), calls=%async_computation.7 | async-start | bytes 2392064 | tf_op jit(solution)/shard_map/all_to_all | solution.py:155
  166.2 20.1 %collective-permute-start.5 = (bf16[1200,128]{1,0:T(8,128)(2,1)S(1)}, bf16[1200,128]{1,0:T(8,128)(2,1)S(1)}, u32[]{:S(2)}, u32[]{:S(2)}) collective-permute-start(bf16[1200,128]{1,0:T(8,128)(2,1)S(1)} %reduce_sum.50), channel_id=1, source_target_pairs={{0,1},{1,0},{2,3},{3,2},{4,5},{5,4},{6,7},{7,6},{8,9},{9,8},{10,11... | collective-permute-start | bytes 921608 | tf_op jit(solution)/shard_map/ppermute | solution.py:241
  187.6 19.0 %all-to-all-start.8 = ((bf16[4,1152,128]{2,1,0:T(8,128)(2,1)}), bf16[4,1152,128]{2,1,0:T(8,128)(2,1)S(1)}, u32[]{:S(2)}, u32[]{:S(2)}) async-start(bf16[4,1152,128]{2,1,0:T(8,128)(2,1)} %broadcast_in_dim.54), calls=%async_computation.8 | async-start | bytes 2359296 | tf_op jit(solution)/shard_map/all_to_all | solution.py:155
  192.4 13.8 %collective-permute-start.6 = (bf16[1168,128]{1,0:T(8,128)(2,1)S(1)}, bf16[1168,128]{1,0:T(8,128)(2,1)S(1)}, u32[]{:S(2)}, u32[]{:S(2)}) collective-permute-start(bf16[1168,128]{1,0:T(8,128)(2,1)S(1)} %reduce_sum.51), channel_id=1, source_target_pairs={{0,1},{1,0},{2,3},{3,2},{4,5},{5,4},{6,7},{7,6},{8,9},{9,8},{10,11... | collective-permute-start | bytes 897032 | tf_op jit(solution)/shard_map/ppermute | solution.py:243
  207.8 18.9 %all-to-all-start.9 = ((bf16[4,1152,128]{2,1,0:T(8,128)(2,1)}), bf16[4,1152,128]{2,1,0:T(8,128)(2,1)S(1)}, u32[]{:S(2)}, u32[]{:S(2)}) async-start(bf16[4,1152,128]{2,1,0:T(8,128)(2,1)} %broadcast_in_dim.55), calls=%async_computation.9 | async-start | bytes 2359296 | tf_op jit(solution)/shard_map/all_to_all | solution.py:155

commit v6 on v5

--- a/solution.py
+++ b/solution.py
@@ -18,7 +18,7 @@
 CHIPS = 32
 NX = 4
 DEC_BIAS_ROWS, ENC_BIAS_ROWS = 48, 16
-VMEM = 24 * 1024 * 1024
+VMEM = 48 * 1024 * 1024
 
 
 def size_of(axes):
@@ -31,7 +31,19 @@
     return index.transpose(rest + list(axes)).reshape(-1, size_of(axes)).tolist()
 
 
-X_GROUPS = np.arange(8).reshape(NX, 2).T.tolist()
+ALL = ("dict", "dp")
+
+
+def along_x(sign):
+    pairs = []
+    for d in range(64):
+        step = sign * (1 - 2 * (d % 2))
+        for x in range(NX):
+            pairs += [(d * 8 + x * 2 + h, d * 8 + (x + step) % NX * 2 + h) for h in range(2)]
+    return pairs
+
+
+AHEAD, BACK = along_x(1), along_x(-1)
 CORE_SWAP = [(i, i ^ 1) for i in range(64)]
 Y_SWAP = [(i, i ^ 1) for i in range(8)]
 
@@ -124,22 +136,33 @@
             out[x, quarter:, :] = rows
 
 
-def unpack_kernel(parts_ref, dec_ref):
+def place_dec_kernel(order_ref, *refs):
+    dec_ref = refs[-1]
     lat = dec_ref.shape[0] // NX
-    for x in range(NX):
+    for n, ref in enumerate(refs[:-1]):
+        row = pl.multiple_of(order_ref[n] * lat, lat)
         for i in range(dec_ref.shape[1] // TILE):
-            rows, lanes = slice(i * lat, (i + 1) * lat), slice(i * TILE, (i + 1) * TILE)
-            dec_ref[x * lat : (x + 1) * lat, lanes] = parts_ref[x, rows, :]
+            lanes = slice(i * TILE, (i + 1) * TILE)
+            dec_ref[pl.ds(row, lat), lanes] = ref[i * lat : (i + 1) * lat, :]
+
+
+def place_enc_kernel(order_ref, *refs):
+    enc_ref = refs[-1]
+    quarter = enc_ref.shape[0] // NX
+    for n, ref in enumerate(refs[:-1]):
+        row = pl.multiple_of(order_ref[n] * quarter, quarter)
+        enc_ref[pl.ds(row, quarter), :] = ref[:quarter, :]
 
 
 def call(kernel, outs, args, scratch=(), flops=0):
     whole = pl.BlockSpec(memory_space=pltpu.VMEM)
+    scalars = pl.BlockSpec(memory_space=pltpu.SMEM)
     moved = sum(a.size * a.dtype.itemsize for a in args)
     moved += sum(math.prod(s.shape) * s.dtype.itemsize for s in outs)
     return pl.pallas_call(
         kernel,
         out_shape=outs,
-        in_specs=[whole] * len(args),
+        in_specs=[scalars if a.dtype == jnp.int32 else whole for a in args],
         out_specs=[whole] * len(outs),
         scratch_shapes=list(scratch),
         compiler_params=pltpu.CompilerParams(vmem_limit_bytes=VMEM),
@@ -151,20 +174,24 @@
     return jax.ShapeDtypeStruct(dims, dtype)
 
 
-def exchange_x(parts):
-    return lax.all_to_all(parts, "dp", 0, 0, axis_index_groups=X_GROUPS)
-
-
-def sum_parts(parts):
-    return lax.optimization_barrier(jnp.sum(parts.astype(F32), axis=0).astype(BF16))
-
-
-def add(a, b):
-    return (a.astype(F32) + b.astype(F32)).astype(BF16)
+def add(*terms):
+    return sum(term.astype(F32) for term in terms).astype(BF16)
+
+
+def scatter_x(own, other, ahead, back, x):
+    def quarter(n):
+        return [lax.dynamic_index_in_dim(part, n, keepdims=False) for part in (own, other)]
+
+    relayed = lax.ppermute(add(*quarter((x + 2) % NX)), ALL, AHEAD)
+    direct = lax.ppermute(add(*quarter(back)), ALL, BACK)
+    passed = lax.ppermute(add(*quarter(ahead), relayed), ALL, AHEAD)
+    return lax.optimization_barrier(add(*quarter(x), direct, passed))
 
 
 def gather_x(piece):
-    return exchange_x(jnp.broadcast_to(piece[None], (NX,) + piece.shape))
+    behind = lax.ppermute(piece, ALL, AHEAD)
+    ahead = lax.ppermute(piece, ALL, BACK)
+    return piece, behind, ahead, lax.ppermute(behind, ALL, AHEAD)
 
 
 def local(activations, enc_weight, enc_bias, dec_weight, dec_bias, thresholds, active_blocks):
@@ -232,23 +259,19 @@
         2 * work,
     )
 
+    x = lax.axis_index("dp") // 2
+    ahead, back = (x + 1 + 2 * core) % NX, (x + 3 + 2 * core) % NX
+    order = jnp.stack([x, back, ahead, (x + 2) % NX]).astype(jnp.int32)
     dec_other = lax.ppermute(dec_parts[1], "dict", CORE_SWAP)
-    dec_total = add(dec_parts[0], dec_other)
-    enc_other, dec_total = lax.optimization_barrier((enc_parts[1], dec_total))
-    enc_total = add(enc_parts[0], lax.ppermute(enc_other, "dict", CORE_SWAP))
-    dec_moved, enc_total = lax.optimization_barrier((exchange_x(dec_total), enc_total))
-    dec_piece = sum_parts(dec_moved)
-    dec_swapped = lax.ppermute(dec_piece, "dp", Y_SWAP)
-    enc_piece = sum_parts(exchange_x(enc_total))
-    enc_swapped = lax.ppermute(enc_piece, "dp", Y_SWAP)
-    dec_swapped, enc_piece = lax.optimization_barrier((dec_swapped, enc_piece))
-    dec_sum = add(dec_piece, dec_swapped)
-    dec_whole = gather_x(dec_sum[:quarter])
-    (dec,) = call(unpack_kernel, [shape((TILE, d))], (dec_whole,))
-    dec_whole, enc_swapped = lax.optimization_barrier((dec_whole, enc_swapped))
-    enc_sum = add(enc_piece, enc_swapped)
-    enc = gather_x(enc_sum[:quarter]).reshape(d, TILE)
-    return enc, dec, enc_sum[quarter], dec_sum[quarter : quarter + d // TILE].reshape(-1)
+    enc_other, dec_other = lax.optimization_barrier((enc_parts[1], dec_other))
+    enc_other = lax.ppermute(enc_other, "dict", CORE_SWAP)
+    dec_piece = scatter_x(dec_parts[0], dec_other, ahead, back, x)
+    enc_piece = scatter_x(enc_parts[0], enc_other, ahead, back, x)
+    dec_piece = add(dec_piece, lax.ppermute(dec_piece, "dp", Y_SWAP))
+    enc_piece = add(enc_piece, lax.ppermute(enc_piece, "dp", Y_SWAP))
+    (dec,) = call(place_dec_kernel, [shape((TILE, d))], (order, *gather_x(dec_piece)))
+    (enc,) = call(place_enc_kernel, [shape((d, TILE))], (order, *gather_x(enc_piece)))
+    return enc, dec, enc_piece[quarter], dec_piece[quarter : quarter + d // TILE].reshape(-1)
 
 
 def solution(mesh):

time: 230 us -> 222 us (0.965)
  waiting for transfers between devices: 65.4 us -> 37.7 us
  starting transfers between devices: 49.2 us -> 69.8 us
  Pallas kernels: 8.64 us -> 11.2 us
  local copies, waits for them, and re-layouts: 10.5 us -> 8.2 us
    ppermute x3 -> x15, starting transfers between devices: 11.8 us -> 53.8 us  [the longest x2 10.3 us: gather_x(): return (piece, behind, ahead, lax.ppermute(behind, ALL, AHEAD))]
    all_to_all x4 -> x0, waiting for transfers between devices: 32.7 us -> none  [exchange_x(): return lax.all_to_all(parts, 'dp', 0, 0, axis_index_groups=X_GROUPS)]
    all_to_all x4 -> x0, starting transfers between devices: 20.7 us -> none  [exchange_x(): return lax.all_to_all(parts, 'dp', 0, 0, axis_index_groups=X_GROUPS)]
    ppermute x3 -> x15, waiting for transfers between devices: 15.4 us -> 20.8 us  [the longest x1 14.9 us: local(): dec_piece = add(dec_piece, lax.ppermute(dec_piece, 'dp', Y_SWAP))]
    convert_element_type x4 -> x8, other arithmetic: 4.19 us -> 7.28 us  [add(): return sum((term.astype(F32) for term in terms)).astype(BF16)]
    pallas_call x4 -> x5, Pallas kernels: 8.64 us -> 11.2 us  [call(): pl.pallas_call(kernel, out_shape=outs, in_specs=[scalars if a.dtype == jn...]
    broadcast_in_dim x2 -> x0, local copies, waits for them, and re-layouts: 2.33 us -> none  [gather_x(): return exchange_x(jnp.broadcast_to(piece[None], (NX,) + piece.shape))]
    unnamed x25 -> x30, local copies, waits for them, and re-layouts: 4.77 us -> 4.8 us
  transfers between devices with their start and end apart: 13 -> 21, of which waited for: 8 -> 6; matrix products, arithmetic and copies ran while one was open for 4% -> 6% of each run, Pallas kernels for 2% -> 2%
where the time goes in v6:
time: 222 us; the launch traced here: 221 us
  blocking collectives  79 us (36%)
  starting transfers between devices  69.8 us (31%)
  waiting for transfers between devices  37.7 us (17%)
  other arithmetic  13.4 us (6%)
  Pallas kernels  11.2 us (5%)
  local copies, waits for them, and re-layouts  8.2 us (4%)
    all_to_all x4, blocking collectives, exchange(): return lax.all_to_all(parts, 'dict', 0, 0, axis_index_groups=groups(axes))  79 us
    all_to_all x2, waiting for transfers between devices, exchange(): return lax.all_to_all(parts, 'dict', 0, 0, axis_index_groups=groups(axes))  16.9 us
    ppermute x1, waiting for transfers between devices, local(): dec_piece = add(dec_piece, lax.ppermute(dec_piece, 'dp', Y_SWAP))  14.9 us
    pallas_call x5, Pallas kernels, call(): pl.pallas_call(kernel, out_shape=outs, in_specs=[scalars if a.dtype == jn...  11.2 us
    ppermute x2, starting transfers between devices, gather_x(): return (piece, behind, ahead, lax.ppermute(behind, ALL, AHEAD))  10.3 us
    ppermute x2, starting transfers between devices, gather_x(): behind = lax.ppermute(piece, ALL, AHEAD)  8.74 us
    convert_element_type x8, other arithmetic, add(): return sum((term.astype(F32) for term in terms)).astype(BF16)  7.28 us
    ppermute x2, starting transfers between devices, scatter_x(): direct = lax.ppermute(add(*quarter(back)), ALL, BACK)  7.1 us
  transfers between devices with their start and end apart: 21, of which 6 were waited for; matrix products, arithmetic and copies ran while one was open for 6% of the time, Pallas kernels for 2%

profile of v6, /device:TPU:6, one launch (start us, length us, event | category | flops | bytes accessed | tf_op | source)
XLA Modules:
  0.0 220.5 jit_solution(15997525942640240545)
XLA Ops:
  1.4 26.0 %all_to_all.30 = bf16[16,72,128]{2,1,0:T(8,128)(2,1)S(1)} all-to-all(bf16[16,72,128]{2,1,0:T(8,128)(2,1)S(1)} %bitcast.65), channel_id=1, replica_groups={{0,8,32,40,64,72,96,104,256,264,288,296,320,328,352,360},{16,24,48,56,8..., dimensions={0} | all-to-all | bytes 589824 | tf_op jit(solution)/shard_map/all_to_all | solution.py:52
  28.1 1.2 broadcast_in_dim.36
  29.3 3.7 %all-to-all-start.1 = ((bf16[4,8,144,128]{3,2,1,0:T(8,128)(2,1)}), bf16[4,8,144,128]{3,2,1,0:T(8,128)(2,1)S(1)}, u32[]{:S(2)}, u32[]{:S(2)}) async-start(bf16[4,8,144,128]{3,2,1,0:T(8,128)(2,1)} %broadcast_in_dim.36), calls=%async_computation.1 | async-start | bytes 2359296 | tf_op jit(solution)/shard_map/all_to_all | solution.py:52
  33.0 2.6 %collective-permute-start.1 = (bf16[128,4608]{1,0:T(8,128)(2,1)S(1)}, bf16[128,4608]{1,0:T(8,128)(2,1)S(1)}, u32[]{:S(2)}, u32[]{:S(2)}) collective-permute-start(bf16[128,4608]{1,0:T(8,128)(2,1)S(1)} %copy-done), channel_id=1, source_target_pairs={{0,8},{8,0},{16,24},{24,16},{32,40},{40,32},{48,56},{56,48},{64,72... | collective-permute-start | bytes 3538952 | tf_op jit(solution)/shard_map/ppermute | solution.py:215
  35.6 1.9 collective-permute-start
  37.6 2.4 %collective-permute-start.2 = (f32[2,128]{1,0:T(2,128)S(1)}, f32[2,128]{1,0:T(2,128)S(1)}, u32[]{:S(2)}, u32[]{:S(2)}) collective-permute-start(f32[2,128]{1,0:T(2,128)S(1)} %pad_maximum_fusion.1), channel_id=1, source_target_pairs={{0,8},{8,0},{16,24},{24,16},{32,40},{40,32},{48,56},{56,48},{64,72... | collective-permute-start | bytes 3080 | tf_op jit(solution)/shard_map/ppermute | solution.py:217
  40.0 1.3 compare_reduce_fusion.1
  41.4 1.4 add_convert_fusion.6
  44.1 5.0 %all-to-all-done.1.act_ref = bf16[4,8,144,128]{3,2,1,0:T(8,128)(2,1)S(1)} async-done(((bf16[4,8,144,128]{3,2,1,0:T(8,128)(2,1)}), bf16[4,8,144,128]{3,2,1,0:T(8,128)(2,1)S(1)}, u32[]{:S(2)}, u32[]{:S(2)}) %all-to-all-start.1) | async-done | bytes 1179680 | tf_op jit(solution)/shard_map/all_to_all | solution.py:52
  49.1 1.3 copy-done.5
  50.4 3.4 %shard_map.102 = (bf16[4,8,144,128]{3,2,1,0:T(8,128)(2,1)S(1)}, bf16[128,256]{1,0:T(8,128)(2,1)S(1)}, f32[256,128]{1,0:T(8,128)S(1)}) custom-call(bf16[4,8,144,128]{3,2,1,0:T(8,128)(2,1)S(1)} %all-to-all-done.1.act_ref, bf16[4608,128]{1,0:T(8,128)(2,1)S(1)} %copy-done.5, bf16[4608,128]{1,0:T(8,128)(2,1)} %collective-permute-done.we_other, ...), custom_call_target="tpu_custom_call" | custom-call | flops 603979776 | bytes 7282688 | tf_op jit(solution)/shard_map/pallas_call | solution.py:162
  55.1 18.3 %all_to_all.31 = bf16[4,8,144,128]{3,2,1,0:T(8,128)(2,1)S(1)} all-to-all(bf16[4,8,144,128]{3,2,1,0:T(8,128)(2,1)S(1)} %get-tuple-element.16), channel_id=1, replica_groups={{0,16,128,144},{8,24,136,152},{32,48,160,176},{40,56,168,184},{64,80,19..., dimensions={0} | all-to-all | bytes 2359296 | tf_op jit(solution)/shard_map/all_to_all | solution.py:52
  73.3 0.9 reduce_sum.23
  74.3 3.4 %all-to-all-start.3 = ((bf16[8,144,128]{2,1,0:T(8,128)(2,1)}), bf16[8,144,128]{2,1,0:T(8,128)(2,1)S(1)}, u32[]{:S(2)}, u32[]{:S(2)}) async-start(bf16[8,144,128]{2,1,0:T(8,128)(2,1)} %reduce_sum.23), calls=%async_computation.3 | async-start | bytes 589824 | tf_op jit(solution)/shard_map/all_to_all | solution.py:52
  78.6 11.9 %all-to-all-done.3 = bf16[8,144,128]{2,1,0:T(8,128)(2,1)S(1)} async-done(((bf16[8,144,128]{2,1,0:T(8,128)(2,1)}), bf16[8,144,128]{2,1,0:T(8,128)(2,1)S(1)}, u32[]{:S(2)}, u32[]{:S(2)}) %all-to-all-start.3) | async-done | bytes 294944 | tf_op jit(solution)/shard_map/all_to_all | solution.py:52
  91.4 16.6 %all_to_all.32 = bf16[8,144,128]{2,1,0:T(8,128)(2,1)S(1)} all-to-all(bf16[8,144,128]{2,1,0:T(8,128)(2,1)S(1)} %broadcast_in_dim.40), channel_id=1, replica_groups={{0,32,64,96,256,288,320,352},{8,40,72,104,264,296,328,360},{16,48,80,11..., dimensions={0} | all-to-all | bytes 589824 | tf_op jit(solution)/shard_map/all_to_all | solution.py:52
  108.3 18.1 %all_to_all.33.res_ref = bf16[4,8,144,128]{3,2,1,0:T(8,128)(2,1)S(1)} all-to-all(bf16[4,8,144,128]{3,2,1,0:T(8,128)(2,1)S(1)} %broadcast_in_dim.41), channel_id=1, replica_groups={{0,16,128,144},{8,24,136,152},{32,48,160,176},{40,56,168,184},{64,80,19..., dimensions={0} | all-to-all | bytes 2359296 | tf_op jit(solution)/shard_map/all_to_all | solution.py:52
  126.4 1.5 shard_map.103
  127.9 1.9 collective-permute-start.3
  129.8 2.9 %shard_map.104 = (bf16[4,1168,128]{2,1,0:T(8,128)(2,1)S(1)}, bf16[4,1168,128]{2,1,0:T(8,128)(2,1)}) custom-call(bf16[4,8,144,128]{3,2,1,0:T(8,128)(2,1)S(1)} %all_to_all.33.res_ref, bf16[4,8,144,128]{3,2,1,0:T(8,128)(2,1)S(1)} %all-to-all-done.1.act_ref, bf16[128,4608]{1,0:T(8,128)(2,1)S(1)} %copy-done, bf16[128,4608]{1,0:T(8,128)(2,1)S(1)} %copy-done.2, ...), custom_call_target="tpu_custom_call" | custom-call | flops 603979776 | bytes 7241728 | tf_op jit(solution)/shard_map/pallas_call | solution.py:162
  132.7 1.0 copy-done.11
  133.8 2.4 %collective-permute-start.4 = (bf16[4,1168,128]{2,1,0:T(8,128)(2,1)}, bf16[4,1168,128]{2,1,0:T(8,128)(2,1)}, u32[]{:S(2)}, u32[]{:S(2)}) collective-permute-start(bf16[4,1168,128]{2,1,0:T(8,128)(2,1)} %get-tuple-element.25), channel_id=1, source_target_pairs={{0,8},{8,0},{16,24},{24,16},{32,40},{40,32},{48,56},{56,48},{64,72... | collective-permute-start | bytes 3588104 | tf_op jit(solution)/shard_map/ppermute | solution.py:267
  136.2 1.4 fusion.6
  137.6 2.5 %collective-permute-start.13 = (bf16[1200,128]{1,0:T(8,128)(2,1)S(1)}, bf16[1200,128]{1,0:T(8,128)(2,1)S(1)}, u32[]{:S(2)}, u32[]{:S(2)}) collective-permute-start(bf16[1200,128]{1,0:T(8,128)(2,1)S(1)} %get-tuple-element.31), channel_id=1, source_target_pairs={{0,2},{1,3},{2,4},{3,5},{4,6},{5,7},{6,0},{7,1},{8,14},{9,15},{10,... | collective-permute-start | bytes 921608 | tf_op jit(solution)/shard_map/ppermute | solution.py:185
  140.2 3.4 %collective-permute-start.12 = (bf16[1200,128]{1,0:T(8,128)(2,1)S(1)}, bf16[1200,128]{1,0:T(8,128)(2,1)S(1)}, u32[]{:S(2)}, u32[]{:S(2)}) collective-permute-start(bf16[1200,128]{1,0:T(8,128)(2,1)S(1)} %get-tuple-element.30), channel_id=1, source_target_pairs={{0,6},{1,7},{2,0},{3,1},{4,2},{5,3},{6,4},{7,5},{8,10},{9,11},{10,... | collective-permute-start | bytes 921608 | tf_op jit(solution)/shard_map/ppermute | solution.py:186
  143.7 1.3 fusion.8
  144.9 3.6 %collective-permute-start.6 = (bf16[1168,128]{1,0:T(8,128)(2,1)S(1)}, bf16[1168,128]{1,0:T(8,128)(2,1)S(1)}, u32[]{:S(2)}, u32[]{:S(2)}) collective-permute-start(bf16[1168,128]{1,0:T(8,128)(2,1)S(1)} %get-tuple-element.33), channel_id=1, source_target_pairs={{0,2},{1,3},{2,4},{3,5},{4,6},{5,7},{6,0},{7,1},{8,14},{9,15},{10,... | collective-permute-start | bytes 897032 | tf_op jit(solution)/shard_map/ppermute | solution.py:185
  148.5 1.1 fusion
  149.6 2.2 collective-permute-start.14
  151.8 3.7 %collective-permute-start.5 = (bf16[1168,128]{1,0:T(8,128)(2,1)S(1)}, bf16[1168,128]{1,0:T(8,128)(2,1)S(1)}, u32[]{:S(2)}, u32[]{:S(2)}) collective-permute-start(bf16[1168,128]{1,0:T(8,128)(2,1)S(1)} %get-tuple-element.32), channel_id=1, source_target_pairs={{0,6},{1,7},{2,0},{3,1},{4,2},{5,3},{6,4},{7,5},{8,10},{9,11},{10,... | collective-permute-start | bytes 897032 | tf_op jit(solution)/shard_map/ppermute | solution.py:186
  155.5 1.1 fusion.3
  156.6 3.4 %collective-permute-start.7 = (bf16[1168,128]{1,0:T(8,128)(2,1)S(1)}, bf16[1168,128]{1,0:T(8,128)(2,1)S(1)}, u32[]{:S(2)}, u32[]{:S(2)}) collective-permute-start(bf16[1168,128]{1,0:T(8,128)(2,1)S(1)} %fusion.3), channel_id=1, source_target_pairs={{0,2},{1,3},{2,4},{3,5},{4,6},{5,7},{6,0},{7,1},{8,14},{9,15},{10,... | collective-permute-start | bytes 897032 | tf_op jit(solution)/shard_map/ppermute | solution.py:187
  160.0 1.5 collective-permute-done.14
  161.6 1.1 fusion.2
  162.7 6.0 %collective-permute-start.15 = (bf16[1200,128]{1,0:T(8,128)(2,1)S(1)}, bf16[1200,128]{1,0:T(8,128)(2,1)S(1)}, u32[]{:S(2)}, u32[]{:S(2)}) collective-permute-start(bf16[1200,128]{1,0:T(8,128)(2,1)S(1)} %fusion.2), channel_id=1, source_target_pairs={{0,1},{1,0},{2,3},{3,2},{4,5},{5,4},{6,7},{7,6},{8,9},{9,8},{10,11... | collective-permute-start | bytes 921608 | tf_op jit(solution)/shard_map/ppermute | solution.py:270
  168.7 1.1 fusion.5
  169.8 3.8 %collective-permute-start.8 = (bf16[1168,128]{1,0:T(8,128)(2,1)S(1)}, bf16[1168,128]{1,0:T(8,128)(2,1)S(1)}, u32[]{:S(2)}, u32[]{:S(2)}) collective-permute-start(bf16[1168,128]{1,0:T(8,128)(2,1)S(1)} %fusion.5), channel_id=1, source_target_pairs={{0,1},{1,0},{2,3},{3,2},{4,5},{5,4},{6,7},{7,6},{8,9},{9,8},{10,11... | collective-permute-start | bytes 897032 | tf_op jit(solution)/shard_map/ppermute | solution.py:271
  173.6 14.9 %collective-permute-done.15 = bf16[1200,128]{1,0:T(8,128)(2,1)S(1)} collective-permute-done((bf16[1200,128]{1,0:T(8,128)(2,1)S(1)}, bf16[1200,128]{1,0:T(8,128)(2,1)S(1)}, u32[]{:S(2)}, u32[]{:S(2)}) %collective-permute-start.15) | collective-permute-done | bytes 307232 | tf_op jit(solution)/shard_map/ppermute | solution.py:270
  188.6 4.0 %collective-permute-start.16 = (bf16[1200,128]{1,0:T(8,128)(2,1)S(1)}, bf16[1200,128]{1,0:T(8,128)(2,1)S(1)}, u32[]{:S(2)}, u32[]{:S(2)}) collective-permute-start(bf16[1200,128]{1,0:T(8,128)(2,1)S(1)} %add_convert_fusion.refs_0_), channel_id=1, source_target_pairs={{0,2},{1,3},{2,4},{3,5},{4,6},{5,7},{6,0},{7,1},{8,14},{9,15},{10,... | collective-permute-start | bytes 921608 | tf_op jit(solution)/shard_map/ppermute | solution.py:192
  192.6 1.3 collective-permute-done.8
  193.9 4.8 %collective-permute-start.9 = (bf16[1168,128]{1,0:T(8,128)(2,1)S(1)}, bf16[1168,128]{1,0:T(8,128)(2,1)S(1)}, u32[]{:S(2)}, u32[]{:S(2)}) collective-permute-start(bf16[1168,128]{1,0:T(8,128)(2,1)S(1)} %add_convert_fusion.3.refs_0_), channel_id=1, source_target_pairs={{0,2},{1,3},{2,4},{3,5},{4,6},{5,7},{6,0},{7,1},{8,14},{9,15},{10,... | collective-permute-start | bytes 897032 | tf_op jit(solution)/shard_map/ppermute | solution.py:192
  198.7 1.9 collective-permute-start.17
  200.7 5.1 %collective-permute-start.18 = (bf16[1200,128]{1,0:T(8,128)(2,1)S(1)}, bf16[1200,128]{1,0:T(8,128)(2,1)S(1)}, u32[]{:S(2)}, u32[]{:S(2)}) collective-permute-start(bf16[1200,128]{1,0:T(8,128)(2,1)S(1)} %collective-permute-done.16.refs_1_), channel_id=1, source_target_pairs={{0,2},{1,3},{2,4},{3,5},{4,6},{5,7},{6,0},{7,1},{8,14},{9,15},{10,... | collective-permute-start | bytes 921608 | tf_op jit(solution)/shard_map/ppermute | solution.py:194
  205.9 1.9 collective-permute-start.10
  207.8 5.1 %collective-permute-start.11 = (bf16[1168,128]{1,0:T(8,128)(2,1)S(1)}, bf16[1168,128]{1,0:T(8,128)(2,1)S(1)}, u32[]{:S(2)}, u32[]{:S(2)}) collective-permute-start(bf16[1168,128]{1,0:T(8,128)(2,1)S(1)} %collective-permute-done.9.refs_1_), channel_id=1, source_target_pairs={{0,2},{1,3},{2,4},{3,5},{4,6},{5,7},{6,0},{7,1},{8,14},{9,15},{10,... | collective-permute-start | bytes 897032 | tf_op jit(solution)/shard_map/ppermute | solution.py:194
  213.6 1.8 shard_map.106
  215.8 3.0 %collective-permute-done.10.refs_2_ = bf16[1168,128]{1,0:T(8,128)(2,1)S(1)} collective-permute-done((bf16[1168,128]{1,0:T(8,128)(2,1)S(1)}, bf16[1168,128]{1,0:T(8,128)(2,1)S(1)}, u32[]{:S(2)}, u32[]{:S(2)}) %collective-permute-start.10) | collective-permute-done | bytes 299040 | tf_op jit(solution)/shard_map/ppermute | solution.py:193
  218.9 1.6 shard_map.105
  (63 shorter events, 7.5 us)
Async XLA Ops:
  27.4 0.7 copy-start.10
  29.3 3.7 %copy-start = (bf16[128,4608]{1,0:T(8,128)(2,1)S(1)}, bf16[128,4608]{1,0:T(8,128)(2,1)}, u32[]{:S(2)}) copy-start(bf16[128,4608]{1,0:T(8,128)(2,1)} %wd_own.3) | copy-start | bytes 3538948
  29.3 8.3 %copy-start.13 = (bf16[128]{0:T(256)(128)(2,1)S(1)}, bf16[128]{0:T(256)(128)(2,1)}, u32[]{:S(2)}) copy-start(bf16[128]{0:T(256)(128)(2,1)} %param.9) | copy-start | bytes 772
  29.3 8.3 %copy-start.14 = (s32[128]{0:T(128)S(1)}, s32[128]{0:T(128)}, u32[]{:S(2)}) copy-start(s32[128]{0:T(128)} %param.12) | copy-start | bytes 1540
  29.3 19.9 %all-to-all-start.1 = ((bf16[4,8,144,128]{3,2,1,0:T(8,128)(2,1)}), bf16[4,8,144,128]{3,2,1,0:T(8,128)(2,1)S(1)}, u32[]{:S(2)}, u32[]{:S(2)}) async-start(bf16[4,8,144,128]{3,2,1,0:T(8,128)(2,1)} %broadcast_in_dim.36), calls=%async_computation.1 | async-start | bytes 2359296 | tf_op jit(solution)/shard_map/all_to_all | solution.py:52
  33.0 11.2 %collective-permute-start.1 = (bf16[128,4608]{1,0:T(8,128)(2,1)S(1)}, bf16[128,4608]{1,0:T(8,128)(2,1)S(1)}, u32[]{:S(2)}, u32[]{:S(2)}) collective-permute-start(bf16[128,4608]{1,0:T(8,128)(2,1)S(1)} %copy-done), channel_id=1, source_target_pairs={{0,8},{8,0},{16,24},{24,16},{32,40},{40,32},{48,56},{56,48},{64,72... | collective-permute-start | bytes 3538952 | tf_op jit(solution)/shard_map/ppermute | solution.py:215
  35.6 8.5 %collective-permute-start = (bf16[4608,128]{1,0:T(8,128)(2,1)}, bf16[4608,128]{1,0:T(8,128)(2,1)}, u32[]{:S(2)}, u32[]{:S(2)}) collective-permute-start(bf16[4608,128]{1,0:T(8,128)(2,1)} %we_own.1), channel_id=1, source_target_pairs={{0,8},{8,0},{16,24},{24,16},{32,40},{40,32},{48,56},{56,48},{64,72... | collective-permute-start | bytes 3538952 | tf_op jit(solution)/shard_map/ppermute | solution.py:214
  37.6 5.2 %collective-permute-start.2 = (f32[2,128]{1,0:T(2,128)S(1)}, f32[2,128]{1,0:T(2,128)S(1)}, u32[]{:S(2)}, u32[]{:S(2)}) collective-permute-start(f32[2,128]{1,0:T(2,128)S(1)} %pad_maximum_fusion.1), channel_id=1, source_target_pairs={{0,8},{8,0},{16,24},{24,16},{32,40},{40,32},{48,56},{56,48},{64,72... | collective-permute-start | bytes 3080 | tf_op jit(solution)/shard_map/ppermute | solution.py:217
  42.8 0.6 copy-start.12
  44.1 5.0 %copy-start.1 = (bf16[128,4608]{1,0:T(8,128)(2,1)}, bf16[128,4608]{1,0:T(8,128)(2,1)S(1)}, u32[]{:S(2)}) copy-start(bf16[128,4608]{1,0:T(8,128)(2,1)S(1)} %collective-permute-done.1.wd_other) | copy-start | bytes 3538948
  49.1 1.3 copy-start.5
  53.8 0.7 copy-start.6
  54.4 0.6 copy-start.8
  74.3 16.2 %all-to-all-start.3 = ((bf16[8,144,128]{2,1,0:T(8,128)(2,1)}), bf16[8,144,128]{2,1,0:T(8,128)(2,1)S(1)}, u32[]{:S(2)}, u32[]{:S(2)}) async-start(bf16[8,144,128]{2,1,0:T(8,128)(2,1)} %reduce_sum.23), calls=%async_computation.3 | async-start | bytes 589824 | tf_op jit(solution)/shard_map/all_to_all | solution.py:52
  108.2 18.1 %copy-start.9 = (bf16[128,256]{1,0:T(8,128)(2,1)S(1)}, bf16[128,256]{1,0:T(8,128)(2,1)}, u32[]{:S(2)}) copy-start(bf16[128,256]{1,0:T(8,128)(2,1)} %copy-done.8) | copy-start | bytes 196612
  108.2 21.6 %copy-start.7 = (f32[256,128]{1,0:T(8,128)S(1)}, f32[256,128]{1,0:T(8,128)}, u32[]{:S(2)}) copy-start(f32[256,128]{1,0:T(8,128)} %copy-done.6) | copy-start | bytes 393220
  126.4 3.4 %copy-start.2 = (bf16[128,4608]{1,0:T(8,128)(2,1)S(1)}, bf16[128,4608]{1,0:T(8,128)(2,1)}, u32[]{:S(2)}) copy-start(bf16[128,4608]{1,0:T(8,128)(2,1)} %copy-done.1) | copy-start | bytes 3538948
  127.9 4.9 %copy-start.3 = (bf16[4,1200,128]{2,1,0:T(8,128)(2,1)}, bf16[4,1200,128]{2,1,0:T(8,128)(2,1)S(1)}, u32[]{:S(2)}) copy-start(bf16[4,1200,128]{2,1,0:T(8,128)(2,1)S(1)} %get-tuple-element.26) | copy-start | bytes 3686404
  127.9 4.9 %collective-permute-start.3 = (bf16[4,1200,128]{2,1,0:T(8,128)(2,1)S(1)}, bf16[4,1200,128]{2,1,0:T(8,128)(2,1)S(1)}, u32[]{:S(2)}, u32[]{:S(2)}) collective-permute-start(bf16[4,1200,128]{2,1,0:T(8,128)(2,1)S(1)} %get-tuple-element.24), channel_id=1, source_target_pairs={{0,8},{8,0},{16,24},{24,16},{32,40},{40,32},{48,56},{56,48},{64,72... | collective-permute-start | bytes 3686408 | tf_op jit(solution)/shard_map/ppermute | solution.py:265
  132.7 1.0 copy-start.11
  133.8 9.9 %collective-permute-start.4 = (bf16[4,1168,128]{2,1,0:T(8,128)(2,1)}, bf16[4,1168,128]{2,1,0:T(8,128)(2,1)}, u32[]{:S(2)}, u32[]{:S(2)}) collective-permute-start(bf16[4,1168,128]{2,1,0:T(8,128)(2,1)} %get-tuple-element.25), channel_id=1, source_target_pairs={{0,8},{8,0},{16,24},{24,16},{32,40},{40,32},{48,56},{56,48},{64,72... | collective-permute-start | bytes 3588104 | tf_op jit(solution)/shard_map/ppermute | solution.py:267
  137.6 10.9 %copy-start.4 = (bf16[4,1200,128]{2,1,0:T(8,128)(2,1)S(1)}, bf16[4,1200,128]{2,1,0:T(8,128)(2,1)}, u32[]{:S(2)}) copy-start(bf16[4,1200,128]{2,1,0:T(8,128)(2,1)} %copy-done.3) | copy-start | bytes 3686404
  137.6 10.9 %collective-permute-start.13 = (bf16[1200,128]{1,0:T(8,128)(2,1)S(1)}, bf16[1200,128]{1,0:T(8,128)(2,1)S(1)}, u32[]{:S(2)}, u32[]{:S(2)}) collective-permute-start(bf16[1200,128]{1,0:T(8,128)(2,1)S(1)} %get-tuple-element.31), channel_id=1, source_target_pairs={{0,2},{1,3},{2,4},{3,5},{4,6},{5,7},{6,0},{7,1},{8,14},{9,15},{10,... | collective-permute-start | bytes 921608 | tf_op jit(solution)/shard_map/ppermute | solution.py:185
  140.2 19.8 %collective-permute-start.12 = (bf16[1200,128]{1,0:T(8,128)(2,1)S(1)}, bf16[1200,128]{1,0:T(8,128)(2,1)S(1)}, u32[]{:S(2)}, u32[]{:S(2)}) collective-permute-start(bf16[1200,128]{1,0:T(8,128)(2,1)S(1)} %get-tuple-element.30), channel_id=1, source_target_pairs={{0,6},{1,7},{2,0},{3,1},{4,2},{5,3},{6,4},{7,5},{8,10},{9,11},{10,... | collective-permute-start | bytes 921608 | tf_op jit(solution)/shard_map/ppermute | solution.py:186
  144.9 10.6 %collective-permute-start.6 = (bf16[1168,128]{1,0:T(8,128)(2,1)S(1)}, bf16[1168,128]{1,0:T(8,128)(2,1)S(1)}, u32[]{:S(2)}, u32[]{:S(2)}) collective-permute-start(bf16[1168,128]{1,0:T(8,128)(2,1)S(1)} %get-tuple-element.33), channel_id=1, source_target_pairs={{0,2},{1,3},{2,4},{3,5},{4,6},{5,7},{6,0},{7,1},{8,14},{9,15},{10,... | collective-permute-start | bytes 897032 | tf_op jit(solution)/shard_map/ppermute | solution.py:185
  149.6 11.9 %collective-permute-start.14 = (bf16[1200,128]{1,0:T(8,128)(2,1)S(1)}, bf16[1200,128]{1,0:T(8,128)(2,1)S(1)}, u32[]{:S(2)}, u32[]{:S(2)}) collective-permute-start(bf16[1200,128]{1,0:T(8,128)(2,1)S(1)} %fusion), channel_id=1, source_target_pairs={{0,2},{1,3},{2,4},{3,5},{4,6},{5,7},{6,0},{7,1},{8,14},{9,15},{10,... | collective-permute-start | bytes 921608 | tf_op jit(solution)/shard_map/ppermute | solution.py:187
  151.8 16.9 %collective-permute-start.5 = (bf16[1168,128]{1,0:T(8,128)(2,1)S(1)}, bf16[1168,128]{1,0:T(8,128)(2,1)S(1)}, u32[]{:S(2)}, u32[]{:S(2)}) collective-permute-start(bf16[1168,128]{1,0:T(8,128)(2,1)S(1)} %get-tuple-element.32), channel_id=1, source_target_pairs={{0,6},{1,7},{2,0},{3,1},{4,2},{5,3},{6,4},{7,5},{8,10},{9,11},{10,... | collective-permute-start | bytes 897032 | tf_op jit(solution)/shard_map/ppermute | solution.py:186
  156.6 12.1 %collective-permute-start.7 = (bf16[1168,128]{1,0:T(8,128)(2,1)S(1)}, bf16[1168,128]{1,0:T(8,128)(2,1)S(1)}, u32[]{:S(2)}, u32[]{:S(2)}) collective-permute-start(bf16[1168,128]{1,0:T(8,128)(2,1)S(1)} %fusion.3), channel_id=1, source_target_pairs={{0,2},{1,3},{2,4},{3,5},{4,6},{5,7},{6,0},{7,1},{8,14},{9,15},{10,... | collective-permute-start | bytes 897032 | tf_op jit(solution)/shard_map/ppermute | solution.py:187
  162.7 25.8 %collective-permute-start.15 = (bf16[1200,128]{1,0:T(8,128)(2,1)S(1)}, bf16[1200,128]{1,0:T(8,128)(2,1)S(1)}, u32[]{:S(2)}, u32[]{:S(2)}) collective-permute-start(bf16[1200,128]{1,0:T(8,128)(2,1)S(1)} %fusion.2), channel_id=1, source_target_pairs={{0,1},{1,0},{2,3},{3,2},{4,5},{5,4},{6,7},{7,6},{8,9},{9,8},{10,11... | collective-permute-start | bytes 921608 | tf_op jit(solution)/shard_map/ppermute | solution.py:270
  169.8 24.0 %collective-permute-start.8 = (bf16[1168,128]{1,0:T(8,128)(2,1)S(1)}, bf16[1168,128]{1,0:T(8,128)(2,1)S(1)}, u32[]{:S(2)}, u32[]{:S(2)}) collective-permute-start(bf16[1168,128]{1,0:T(8,128)(2,1)S(1)} %fusion.5), channel_id=1, source_target_pairs={{0,1},{1,0},{2,3},{3,2},{4,5},{5,4},{6,7},{7,6},{8,9},{9,8},{10,11... | collective-permute-start | bytes 897032 | tf_op jit(solution)/shard_map/ppermute | solution.py:271
  188.6 12.0 %collective-permute-start.16 = (bf16[1200,128]{1,0:T(8,128)(2,1)S(1)}, bf16[1200,128]{1,0:T(8,128)(2,1)S(1)}, u32[]{:S(2)}, u32[]{:S(2)}) collective-permute-start(bf16[1200,128]{1,0:T(8,128)(2,1)S(1)} %add_convert_fusion.refs_0_), channel_id=1, source_target_pairs={{0,2},{1,3},{2,4},{3,5},{4,6},{5,7},{6,0},{7,1},{8,14},{9,15},{10,... | collective-permute-start | bytes 921608 | tf_op jit(solution)/shard_map/ppermute | solution.py:192
  193.9 13.9 %collective-permute-start.9 = (bf16[1168,128]{1,0:T(8,128)(2,1)S(1)}, bf16[1168,128]{1,0:T(8,128)(2,1)S(1)}, u32[]{:S(2)}, u32[]{:S(2)}) collective-permute-start(bf16[1168,128]{1,0:T(8,128)(2,1)S(1)} %add_convert_fusion.3.refs_0_), channel_id=1, source_target_pairs={{0,2},{1,3},{2,4},{3,5},{4,6},{5,7},{6,0},{7,1},{8,14},{9,15},{10,... | collective-permute-start | bytes 897032 | tf_op jit(solution)/shard_map/ppermute | solution.py:192
  198.7 14.8 %collective-permute-start.17 = (bf16[1200,128]{1,0:T(8,128)(2,1)S(1)}, bf16[1200,128]{1,0:T(8,128)(2,1)S(1)}, u32[]{:S(2)}, u32[]{:S(2)}) collective-permute-start(bf16[1200,128]{1,0:T(8,128)(2,1)S(1)} %add_convert_fusion.refs_0_), channel_id=1, source_target_pairs={{0,6},{1,7},{2,0},{3,1},{4,2},{5,3},{6,4},{7,5},{8,10},{9,11},{10,... | collective-permute-start | bytes 921608 | tf_op jit(solution)/shard_map/ppermute | solution.py:193
  200.7 12.9 %collective-permute-start.18 = (bf16[1200,128]{1,0:T(8,128)(2,1)S(1)}, bf16[1200,128]{1,0:T(8,128)(2,1)S(1)}, u32[]{:S(2)}, u32[]{:S(2)}) collective-permute-start(bf16[1200,128]{1,0:T(8,128)(2,1)S(1)} %collective-permute-done.16.refs_1_), channel_id=1, source_target_pairs={{0,2},{1,3},{2,4},{3,5},{4,6},{5,7},{6,0},{7,1},{8,14},{9,15},{10,... | collective-permute-start | bytes 921608 | tf_op jit(solution)/shard_map/ppermute | solution.py:194
  205.9 13.0 %collective-permute-start.10 = (bf16[1168,128]{1,0:T(8,128)(2,1)S(1)}, bf16[1168,128]{1,0:T(8,128)(2,1)S(1)}, u32[]{:S(2)}, u32[]{:S(2)}) collective-permute-start(bf16[1168,128]{1,0:T(8,128)(2,1)S(1)} %add_convert_fusion.3.refs_0_), channel_id=1, source_target_pairs={{0,6},{1,7},{2,0},{3,1},{4,2},{5,3},{6,4},{7,5},{8,10},{9,11},{10,... | collective-permute-start | bytes 897032 | tf_op jit(solution)/shard_map/ppermute | solution.py:193
  207.8 11.1 %collective-permute-start.11 = (bf16[1168,128]{1,0:T(8,128)(2,1)S(1)}, bf16[1168,128]{1,0:T(8,128)(2,1)S(1)}, u32[]{:S(2)}, u32[]{:S(2)}) collective-permute-start(bf16[1168,128]{1,0:T(8,128)(2,1)S(1)} %collective-permute-done.9.refs_1_), channel_id=1, source_target_pairs={{0,2},{1,3},{2,4},{3,5},{4,6},{5,7},{6,0},{7,1},{8,14},{9,15},{10,... | collective-permute-start | bytes 897032 | tf_op jit(solution)/shard_map/ppermute | solution.py:194

commit v7 on v6

--- a/solution.py
+++ b/solution.py
@@ -14,11 +14,10 @@
 BF16 = jnp.bfloat16
 
 GRID = (2, 2, 4, 2, 2)
-FAR, NEAR, CORE = (0, 2), (1, 3), (4,)
-CHIPS = 32
+FAR, CORE = (0, 2), (4,)
 NX = 4
 DEC_BIAS_ROWS, ENC_BIAS_ROWS = 48, 16
-VMEM = 48 * 1024 * 1024
+VMEM = 24 * 1024 * 1024
 
 
 def size_of(axes):
@@ -52,21 +51,43 @@
     return lax.all_to_all(parts, "dict", 0, 0, axis_index_groups=groups(axes))
 
 
+NEAR_A = [(d, d ^ (2 if d % 2 else 16)) for d in range(64)]
+NEAR_B = [(d, d ^ (16 if d % 2 else 2)) for d in range(64)]
+
+
+def gather_near(block):
+    first = lax.ppermute(block, "dict", NEAR_A)
+    second = lax.ppermute(block, "dict", NEAR_B)
+    return block, first, second, lax.ppermute(first, "dict", NEAR_B)
+
+
+def scatter_near(own, first, second, opposite):
+    relayed = lax.ppermute(opposite, "dict", NEAR_A)
+    direct = lax.ppermute(first, "dict", NEAR_A)
+    passed = lax.ppermute(add(second, relayed), "dict", NEAR_B)
+    return add(own, direct, passed)
+
+
+def add(*terms):
+    return sum(term.astype(F32) for term in terms).astype(BF16)
+
+
 def spread(block, axes):
     return exchange(jnp.broadcast_to(block[None], (size_of(axes),) + block.shape), axes)
 
 
-def chip_blocks():
-    for near in range(4):
+def chip_rows(near_ref, cols):
+    for n in range(4):
+        near = near_ref[n]
         for far in range(8):
-            y, z = (far // 4) * 2 + near // 2, (far % 4) * 2 + near % 2
-            yield near, far, y * 8 + z
-
-
-def in_order(parts_ref, whole_ref):
-    cols = parts_ref.shape[2]
-    for near, far, chip in chip_blocks():
-        whole_ref[chip * cols : (chip + 1) * cols, :] = parts_ref[near, far]
+            chip = far // 4 * 16 + near // 2 * 8 + far % 4 * 2 + near % 2
+            yield n, far, pl.multiple_of(chip * cols, cols)
+
+
+def in_order(near_ref, refs, whole_ref):
+    cols = refs[0].shape[1]
+    for n, far, row in chip_rows(near_ref, cols):
+        whole_ref[pl.ds(row, cols), :] = refs[n][far]
 
 
 def dot(a, b, dims):
@@ -74,9 +95,10 @@
 
 
 def forward_kernel(
-    act_ref, we_own, we_other, wd_own, wd_other, row_ref, parts_ref, feat_ref, slope_ref, act
+    near_ref, act_0, act_1, act_2, act_3, we_own, we_other, wd_own, wd_other, row_ref,
+    part_0, part_1, part_2, part_3, feat_ref, slope_ref, act, parts,
 ):
-    in_order(act_ref, act)
+    in_order(near_ref, (act_0, act_1, act_2, act_3), act)
     act_t = act[...].T
     for n, we in enumerate((we_own, we_other)):
         lanes = slice(n * TILE, (n + 1) * TILE)
@@ -85,21 +107,21 @@
         gate = jax.nn.sigmoid(SHARPNESS * (pre - theta))
         feat_ref[:, lanes] = (live * pre * gate).astype(BF16)
         slope_ref[lanes, :] = (live * (gate + SHARPNESS * pre * gate * (1.0 - gate))).T
-    cols = parts_ref.shape[2]
-    step = 8 * cols
-    place = {chip: (near, far) for near, far, chip in chip_blocks()}
-    for first in range(0, act.shape[0], step):
-        span = slice(first, first + step)
+    step = 9 * TILE
+    for at in range(0, act.shape[0], step):
+        span = slice(at, at + step)
         total = dot(feat_ref[:, :TILE], wd_own[:, span], ((1,), (0,)))
         total = total + dot(feat_ref[:, TILE:], wd_other[:, span], ((1,), (0,)))
-        turned = total.astype(BF16).T
-        for i in range(8):
-            near, far = place[first // cols + i]
-            parts_ref[near, far] = turned[i * cols : (i + 1) * cols, :]
-
-
-def decoder_kernel(res_ref, feat_ref, own_ref, other_ref, res, bias):
-    in_order(res_ref, res)
+        parts[span, :] = total.astype(BF16).T
+    cols = part_0.shape[1]
+    for n, far, row in chip_rows(near_ref, cols):
+        (part_0, part_1, part_2, part_3)[n][far] = parts[pl.ds(row, cols), :]
+
+
+def decoder_kernel(
+    near_ref, res_0, res_1, res_2, res_3, feat_ref, own_ref, other_ref, res, bias
+):
+    in_order(near_ref, (res_0, res_1, res_2, res_3), res)
     d = res.shape[0]
     quarter, lat = d // NX, TILE // NX
     feat_t = jnp.concatenate([feat_ref[...].T, jnp.ones((16, TILE), BF16)], axis=0)
@@ -119,10 +141,11 @@
 
 
 def encoder_kernel(
-    res_ref, act_ref, wd_own, wd_other, slope_ref, own_ref, other_ref, act, res
+    near_ref, res_0, res_1, res_2, res_3, act_0, act_1, act_2, act_3, wd_own, wd_other, slope_ref,
+    own_ref, other_ref, act, res,
 ):
-    in_order(act_ref, act)
-    in_order(res_ref, res)
+    in_order(near_ref, (act_0, act_1, act_2, act_3), act)
+    in_order(near_ref, (res_0, res_1, res_2, res_3), res)
     quarter = act.shape[0] // NX
     for n, (wd, out) in enumerate(((wd_own, own_ref), (wd_other, other_ref))):
         dfeat = dot(wd[...], res[...], ((1,), (0,)))
@@ -174,24 +197,41 @@
     return jax.ShapeDtypeStruct(dims, dtype)
 
 
-def add(*terms):
-    return sum(term.astype(F32) for term in terms).astype(BF16)
-
-
-def scatter_x(own, other, ahead, back, x):
-    def quarter(n):
-        return [lax.dynamic_index_in_dim(part, n, keepdims=False) for part in (own, other)]
-
-    relayed = lax.ppermute(add(*quarter((x + 2) % NX)), ALL, AHEAD)
-    direct = lax.ppermute(add(*quarter(back)), ALL, BACK)
-    passed = lax.ppermute(add(*quarter(ahead), relayed), ALL, AHEAD)
-    return lax.optimization_barrier(add(*quarter(x), direct, passed))
-
-
-def gather_x(piece):
+def after(value, *others):
+    return lax.optimization_barrier((value, *others))[0]
+
+
+def gather_x(piece, *first):
     behind = lax.ppermute(piece, ALL, AHEAD)
-    ahead = lax.ppermute(piece, ALL, BACK)
+    ahead = lax.ppermute(after(piece, *first), ALL, BACK)
     return piece, behind, ahead, lax.ppermute(behind, ALL, AHEAD)
+
+
+def quarter_of(parts, n):
+    return [lax.dynamic_index_in_dim(part, n, keepdims=False) for part in parts]
+
+
+def reduce_gradients(dec, enc, core, x):
+    ahead, back = (x + 1 + 2 * core) % NX, (x + 3 + 2 * core) % NX
+    dec = dec[0], lax.ppermute(dec[1], "dict", CORE_SWAP)
+    enc = enc[0], lax.ppermute(after(enc[1], dec[1]), "dict", CORE_SWAP)
+
+    relayed = lax.ppermute(add(*quarter_of(dec, (x + 2) % NX)), ALL, AHEAD)
+    direct = lax.ppermute(add(*quarter_of(dec, back)), ALL, BACK)
+    passed = lax.ppermute(add(*quarter_of(dec, ahead), relayed), ALL, AHEAD)
+    dec_piece = lax.optimization_barrier(add(*quarter_of(dec, x), direct, passed))
+    dec_swapped = lax.ppermute(dec_piece, "dp", Y_SWAP)
+
+    relayed = lax.ppermute(after(add(*quarter_of(enc, (x + 2) % NX)), direct), ALL, AHEAD)
+    direct = lax.ppermute(after(add(*quarter_of(enc, back)), dec_piece), ALL, BACK)
+    passed = lax.ppermute(add(*quarter_of(enc, ahead), relayed), ALL, AHEAD)
+    enc_piece = lax.optimization_barrier(add(*quarter_of(enc, x), direct, passed))
+    enc_swapped = lax.ppermute(after(enc_piece, dec_swapped), "dp", Y_SWAP)
+
+    dec_pieces = gather_x(add(dec_piece, dec_swapped))
+    enc_swapped = after(enc_swapped, *dec_pieces[1:3])
+    enc_pieces = gather_x(add(enc_piece, enc_swapped), dec_pieces[3])
+    return dec_pieces, enc_pieces, jnp.stack([x, back, ahead, (x + 2) % NX]).astype(jnp.int32)
 
 
 def local(activations, enc_weight, enc_bias, dec_weight, dec_bias, thresholds, active_blocks):
@@ -209,10 +249,12 @@
     chip = dict_index // 2
     own = lax.dynamic_index_in_dim(act, chip // 16 * 4 + chip % 8 // 2, keepdims=False)
     cols = own.shape[0]
-    act = spread(act, NEAR)
-
-    enc_other = lax.ppermute(enc_weight, "dict", CORE_SWAP)
-    dec_other = lax.ppermute(dec_weight, "dict", CORE_SWAP)
+    near = chip // 8 % 2 * 2 + chip % 2
+    toward = 2 - core
+    nears = jnp.stack([near, near ^ toward, near ^ (3 - toward), near ^ 3]).astype(jnp.int32)
+
+    enc_other = lax.ppermute(after(enc_weight, halves), "dict", CORE_SWAP)
+    dec_other = lax.ppermute(after(dec_weight, halves), "dict", CORE_SWAP)
     rows = jnp.stack([enc_bias.astype(F32), thresholds.astype(F32) / 16.0])
     rows = jnp.concatenate([rows, lax.ppermute(rows, "dict", CORE_SWAP)], axis=1)
     listed = lax.dynamic_slice_in_dim(active_blocks, core, 1)
@@ -220,24 +262,26 @@
     live = jnp.repeat(live.astype(F32), TILE)[None, :]
     rows = jnp.concatenate([rows, live, jnp.zeros((5, 2 * TILE), F32)], axis=0)
 
+    act, rows = lax.optimization_barrier((act, rows))
+    act = gather_near(act)
+
     work = 2 * d * 2 * TILE * TILE
-    parts, feat, slope = call(
+    *parts, feat, slope = call(
         forward_kernel,
         [
-            shape(act.shape),
+            *[shape(act[0].shape)] * 4,
             shape((TILE, 2 * TILE)),
             shape((2 * TILE, TILE), F32),
         ],
-        (act, enc_weight, enc_other, dec_weight, dec_other, rows),
-        [pltpu.VMEM((d, TILE), BF16)],
+        (nears, *act, enc_weight, enc_other, dec_weight, dec_other, rows),
+        [pltpu.VMEM((d, TILE), BF16)] * 2,
         2 * work,
     )
 
-    near_sum = jnp.sum(exchange(parts, NEAR).astype(F32), axis=0).astype(BF16)
-    recon = jnp.sum(exchange(near_sum, FAR).astype(F32), axis=0)
+    recon = jnp.sum(exchange(scatter_near(*parts), FAR).astype(F32), axis=0)
     bias = lax.dynamic_slice_in_dim(dec_bias, dict_index // 2 * cols, cols).astype(F32)
     residual = (recon + bias[:, None] - own.astype(F32)) / scale_root
-    res = spread(spread(residual.astype(BF16), FAR), NEAR)
+    res = gather_near(spread(residual.astype(BF16), FAR))
 
     quarter = d // NX
     packed = shape((NX, quarter + DEC_BIAS_ROWS, TILE))
@@ -245,7 +289,7 @@
     dec_parts = call(
         decoder_kernel,
         [packed, packed],
-        (res, feat),
+        (nears, *res, feat),
         [room, pltpu.VMEM((DEC_BIAS_ROWS, TILE), F32)],
         work,
     )
@@ -254,24 +298,17 @@
     enc_parts = call(
         encoder_kernel,
         [packed, packed],
-        (res, act, dec_weight, dec_other, slope),
+        (nears, *res, *act, dec_weight, dec_other, slope),
         [room, room],
         2 * work,
     )
 
     x = lax.axis_index("dp") // 2
-    ahead, back = (x + 1 + 2 * core) % NX, (x + 3 + 2 * core) % NX
-    order = jnp.stack([x, back, ahead, (x + 2) % NX]).astype(jnp.int32)
-    dec_other = lax.ppermute(dec_parts[1], "dict", CORE_SWAP)
-    enc_other, dec_other = lax.optimization_barrier((enc_parts[1], dec_other))
-    enc_other = lax.ppermute(enc_other, "dict", CORE_SWAP)
-    dec_piece = scatter_x(dec_parts[0], dec_other, ahead, back, x)
-    enc_piece = scatter_x(enc_parts[0], enc_other, ahead, back, x)
-    dec_piece = add(dec_piece, lax.ppermute(dec_piece, "dp", Y_SWAP))
-    enc_piece = add(enc_piece, lax.ppermute(enc_piece, "dp", Y_SWAP))
-    (dec,) = call(place_dec_kernel, [shape((TILE, d))], (order, *gather_x(dec_piece)))
-    (enc,) = call(place_enc_kernel, [shape((d, TILE))], (order, *gather_x(enc_piece)))
-    return enc, dec, enc_piece[quarter], dec_piece[quarter : quarter + d // TILE].reshape(-1)
+    dec_pieces, enc_pieces, order = reduce_gradients(dec_parts, enc_parts, core, x)
+    (dec,) = call(place_dec_kernel, [shape((TILE, d))], (order, *dec_pieces))
+    (enc,) = call(place_enc_kernel, [shape((d, TILE))], (order, *enc_pieces))
+    dec_bias_sum = dec_pieces[0][quarter : quarter + d // TILE].reshape(-1)
+    return enc, dec, enc_pieces[0][quarter], dec_bias_sum
 
 
 def solution(mesh):

time: 222 us -> 226 us (1.018)
  blocking collectives: 79 us -> 17.4 us
  waiting for transfers between devices: 37.7 us -> 72.7 us
  starting transfers between devices: 69.8 us -> 99.4 us
    all_to_all x4 -> x1, blocking collectives: 79 us -> 17.4 us  [exchange(): return lax.all_to_all(parts, 'dict', 0, 0, axis_index_groups=groups(axes))]
    ppermute x14 -> x23, waiting for transfers between devices: 20.8 us -> 51.5 us  [the longest x2 11.3 us: gather_near(): return (block, first, second, lax.ppermute(first, 'dict', NEAR_B))]
    ppermute x14 -> x23, starting transfers between devices: 41.3 us -> 67.9 us  [the longest x2 6.75 us: gather_x(): ahead = lax.ppermute(after(piece, *first), ALL, BACK)]
    all_to_all x2, starting transfers between devices: 7.08 us -> 18.9 us  [exchange(): return lax.all_to_all(parts, 'dict', 0, 0, axis_index_groups=groups(axes))]
    ppermute x2, waiting for transfers between devices: 0.01 us -> 4.97 us  [gather_x(): behind = lax.ppermute(piece, ALL, AHEAD)]
    ppermute x2, starting transfers between devices: 10.3 us -> 5.35 us  [gather_x(): return (piece, behind, ahead, lax.ppermute(behind, ALL, AHEAD))]
    all_to_all x2, waiting for transfers between devices: 16.9 us -> 12.7 us  [exchange(): return lax.all_to_all(parts, 'dict', 0, 0, axis_index_groups=groups(axes))]
    ppermute x2, starting transfers between devices: 8.74 us -> 4.92 us  [gather_x(): behind = lax.ppermute(piece, ALL, AHEAD)]
  transfers between devices with their start and end apart: 21 -> 30, of which waited for: 6 -> 15; matrix products, arithmetic and copies ran while one was open for 6% -> 7% of each run, Pallas kernels for 2% -> 2%
where the time goes in v7:
time: 226 us; the launch traced here: 224 us
  starting transfers between devices  99.4 us (44%)
  waiting for transfers between devices  72.7 us (32%)
  blocking collectives  17.4 us (8%)
  other arithmetic  15.4 us (7%)
  Pallas kernels  12.1 us (5%)
  local copies, waits for them, and re-layouts  6.31 us (3%)
    all_to_all x2, starting transfers between devices, exchange(): return lax.all_to_all(parts, 'dict', 0, 0, axis_index_groups=groups(axes))  18.9 us
    all_to_all x1, blocking collectives, exchange(): return lax.all_to_all(parts, 'dict', 0, 0, axis_index_groups=groups(axes))  17.4 us
    all_to_all x2, waiting for transfers between devices, exchange(): return lax.all_to_all(parts, 'dict', 0, 0, axis_index_groups=groups(axes))  12.7 us
    pallas_call x5, Pallas kernels, call(): pl.pallas_call(kernel, out_shape=outs, in_specs=[scalars if a.dtype == jn...  12.1 us
    ppermute x2, waiting for transfers between devices, gather_near(): return (block, first, second, lax.ppermute(first, 'dict', NEAR_B))  11.3 us
    ppermute x2, waiting for transfers between devices, gather_near(): first = lax.ppermute(block, 'dict', NEAR_A)  10.2 us
    convert_element_type x10, other arithmetic, add(): return sum((term.astype(F32) for term in terms)).astype(BF16)  9.23 us
    ppermute x1, waiting for transfers between devices, reduce_gradients(): enc_swapped = lax.ppermute(after(enc_piece, dec_swapped), 'dp', Y_SWAP)  8.13 us
  transfers between devices with their start and end apart: 30, of which 15 were waited for; matrix products, arithmetic and copies ran while one was open for 7% of the time, Pallas kernels for 2%

profile of v7, /device:TPU:6, one launch (start us, length us, event | category | flops | bytes accessed | tf_op | source)
XLA Modules:
  0.0 224.5 jit_solution(8739229701246278823)
XLA Ops:
  2.2 12.4 %all-to-all-start = ((bf16[16,72,128]{2,1,0:T(8,128)(2,1)}), bf16[16,72,128]{2,1,0:T(8,128)(2,1)S(1)}, u32[]{:S(2)}, u32[]{:S(2)}) async-start(bf16[16,72,128]{2,1,0:T(8,128)(2,1)} %bitcast.11), calls=%async_computation | async-start | bytes 589824 | tf_op jit(solution)/shard_map/all_to_all | solution.py:51
  14.7 2.3 %collective-permute-start.4 = (bf16[4608,128]{1,0:T(8,128)(2,1)}, bf16[4608,128]{1,0:T(8,128)(2,1)}, u32[]{:S(2)}, u32[]{:S(2)}) collective-permute-start(bf16[4608,128]{1,0:T(8,128)(2,1)} %we_own.1), channel_id=1, source_target_pairs={{0,8},{8,0},{16,24},{24,16},{32,40},{40,32},{48,56},{56,48},{64,72... | collective-permute-start | bytes 3538952 | tf_op jit(solution)/shard_map/ppermute | solution.py:256
  17.0 2.0 collective-permute-start.5
  20.4 2.3 %collective-permute-start = (f32[2,128]{1,0:T(2,128)S(1)}, f32[2,128]{1,0:T(2,128)S(1)}, u32[]{:S(2)}, u32[]{:S(2)}) collective-permute-start(f32[2,128]{1,0:T(2,128)S(1)} %pad_maximum_fusion.1), channel_id=1, source_target_pairs={{0,8},{8,0},{16,24},{24,16},{32,40},{40,32},{48,56},{56,48},{64,72... | collective-permute-start | bytes 3080 | tf_op jit(solution)/shard_map/ppermute | solution.py:259
  25.6 2.8 %all-to-all-done = bf16[16,72,128]{2,1,0:T(8,128)(2,1)S(1)} async-done(((bf16[16,72,128]{2,1,0:T(8,128)(2,1)}), bf16[16,72,128]{2,1,0:T(8,128)(2,1)S(1)}, u32[]{:S(2)}, u32[]{:S(2)}) %all-to-all-start) | async-done | bytes 294944 | tf_op jit(solution)/shard_map/all_to_all | solution.py:51
  28.4 1.9 collective-permute-start.1
  30.3 3.2 %collective-permute-start.2 = (bf16[8,144,128]{2,1,0:T(8,128)(2,1)S(1)}, bf16[8,144,128]{2,1,0:T(8,128)(2,1)S(1)}, u32[]{:S(2)}, u32[]{:S(2)}) collective-permute-start(bf16[8,144,128]{2,1,0:T(8,128)(2,1)S(1)} %bitcast.68), channel_id=1, source_target_pairs={{0,16},{8,136},{16,0},{24,152},{32,48},{40,168},{48,32},{56,184},{... | collective-permute-start | bytes 884744 | tf_op jit(solution)/shard_map/ppermute | solution.py:60
  33.6 3.8 %collective-permute-done.1.act_1 = bf16[8,144,128]{2,1,0:T(8,128)(2,1)S(1)} collective-permute-done((bf16[8,144,128]{2,1,0:T(8,128)(2,1)S(1)}, bf16[8,144,128]{2,1,0:T(8,128)(2,1)S(1)}, u32[]{:S(2)}, u32[]{:S(2)}) %collective-permute-start.1) | collective-permute-done | bytes 294944 | tf_op jit(solution)/shard_map/ppermute | solution.py:59
  37.4 3.8 %collective-permute-start.3 = (bf16[8,144,128]{2,1,0:T(8,128)(2,1)S(1)}, bf16[8,144,128]{2,1,0:T(8,128)(2,1)S(1)}, u32[]{:S(2)}, u32[]{:S(2)}) collective-permute-start(bf16[8,144,128]{2,1,0:T(8,128)(2,1)S(1)} %collective-permute-done.1.act_1), channel_id=1, source_target_pairs={{0,16},{8,136},{16,0},{24,152},{32,48},{40,168},{48,32},{56,184},{... | collective-permute-start | bytes 884744 | tf_op jit(solution)/shard_map/ppermute | solution.py:61
  41.4 4.6 %collective-permute-done.3.act_3 = bf16[8,144,128]{2,1,0:T(8,128)(2,1)S(1)} collective-permute-done((bf16[8,144,128]{2,1,0:T(8,128)(2,1)S(1)}, bf16[8,144,128]{2,1,0:T(8,128)(2,1)S(1)}, u32[]{:S(2)}, u32[]{:S(2)}) %collective-permute-start.3) | collective-permute-done | bytes 294944 | tf_op jit(solution)/shard_map/ppermute | solution.py:61
  47.3 3.1 %shard_map.102 = (bf16[8,144,128]{2,1,0:T(8,128)(2,1)S(1)}, bf16[8,144,128]{2,1,0:T(8,128)(2,1)S(1)}, bf16[8,144,128]{2,1,0:T(8,128)(2,1)S(1)}, bf16[8,144,128]{...) custom-call(s32[4]{0:T(128)S(1)} %pad_add_fusion.1.near_ref, ...), custom_call_target="tpu_custom_call" | custom-call | flops 603979776 | bytes 7282704 | tf_op jit(solution)/shard_map/pallas_call | solution.py:185
  50.4 1.9 collective-permute-start.7
  52.4 3.9 %collective-permute-start.6 = (bf16[8,144,128]{2,1,0:T(8,128)(2,1)S(1)}, bf16[8,144,128]{2,1,0:T(8,128)(2,1)S(1)}, u32[]{:S(2)}, u32[]{:S(2)}) collective-permute-start(bf16[8,144,128]{2,1,0:T(8,128)(2,1)S(1)} %get-tuple-element.35), channel_id=1, source_target_pairs={{0,128},{8,24},{16,144},{24,8},{32,160},{40,56},{48,176},{56,40},{... | collective-permute-start | bytes 884744 | tf_op jit(solution)/shard_map/ppermute | solution.py:66
  56.3 2.8 %collective-permute-done.7 = bf16[8,144,128]{2,1,0:T(8,128)(2,1)S(1)} collective-permute-done((bf16[8,144,128]{2,1,0:T(8,128)(2,1)S(1)}, bf16[8,144,128]{2,1,0:T(8,128)(2,1)S(1)}, u32[]{:S(2)}, u32[]{:S(2)}) %collective-permute-start.7) | collective-permute-done | bytes 294944 | tf_op jit(solution)/shard_map/ppermute | solution.py:65
  59.2 3.8 %collective-permute-start.8 = (bf16[8,144,128]{2,1,0:T(8,128)(2,1)S(1)}, bf16[8,144,128]{2,1,0:T(8,128)(2,1)S(1)}, u32[]{:S(2)}, u32[]{:S(2)}) collective-permute-start(bf16[8,144,128]{2,1,0:T(8,128)(2,1)S(1)} %add_convert_fusion.7), channel_id=1, source_target_pairs={{0,16},{8,136},{16,0},{24,152},{32,48},{40,168},{48,32},{56,184},{... | collective-permute-start | bytes 884744 | tf_op jit(solution)/shard_map/ppermute | solution.py:67
  63.0 4.7 %collective-permute-done.8 = bf16[8,144,128]{2,1,0:T(8,128)(2,1)S(1)} collective-permute-done((bf16[8,144,128]{2,1,0:T(8,128)(2,1)S(1)}, bf16[8,144,128]{2,1,0:T(8,128)(2,1)S(1)}, u32[]{:S(2)}, u32[]{:S(2)}) %collective-permute-start.8) | collective-permute-done | bytes 294944 | tf_op jit(solution)/shard_map/ppermute | solution.py:67
  68.6 6.4 %all-to-all-start.1 = ((bf16[8,144,128]{2,1,0:T(8,128)(2,1)}), bf16[8,144,128]{2,1,0:T(8,128)(2,1)}, u32[]{:S(2)}, u32[]{:S(2)}) async-start(bf16[8,144,128]{2,1,0:T(8,128)(2,1)} %add_convert_fusion.6), calls=%async_computation.1 | async-start | bytes 589824 | tf_op jit(solution)/shard_map/all_to_all | solution.py:51
  75.8 9.9 %all-to-all-done.1 = bf16[8,144,128]{2,1,0:T(8,128)(2,1)} async-done(((bf16[8,144,128]{2,1,0:T(8,128)(2,1)}), bf16[8,144,128]{2,1,0:T(8,128)(2,1)}, u32[]{:S(2)}, u32[]{:S(2)}) %all-to-all-start.1) | async-done | bytes 294944 | tf_op jit(solution)/shard_map/all_to_all | solution.py:51
  86.9 17.4 %all_to_all.15.res_0 = bf16[8,144,128]{2,1,0:T(8,128)(2,1)S(1)} all-to-all(bf16[8,144,128]{2,1,0:T(8,128)(2,1)S(1)} %broadcast_in_dim.25), channel_id=1, replica_groups={{0,32,64,96,256,288,320,352},{8,40,72,104,264,296,328,360},{16,48,80,11..., dimensions={0} | all-to-all | bytes 589824 | tf_op jit(solution)/shard_map/all_to_all | solution.py:51
  104.3 1.9 collective-permute-start.9
  106.2 2.8 %collective-permute-start.10 = (bf16[8,144,128]{2,1,0:T(8,128)(2,1)S(1)}, bf16[8,144,128]{2,1,0:T(8,128)(2,1)S(1)}, u32[]{:S(2)}, u32[]{:S(2)}) collective-permute-start(bf16[8,144,128]{2,1,0:T(8,128)(2,1)S(1)} %all_to_all.15.res_0), channel_id=1, source_target_pairs={{0,16},{8,136},{16,0},{24,152},{32,48},{40,168},{48,32},{56,184},{... | collective-permute-start | bytes 884744 | tf_op jit(solution)/shard_map/ppermute | solution.py:60
  109.1 6.3 %collective-permute-done.9.res_1 = bf16[8,144,128]{2,1,0:T(8,128)(2,1)S(1)} collective-permute-done((bf16[8,144,128]{2,1,0:T(8,128)(2,1)S(1)}, bf16[8,144,128]{2,1,0:T(8,128)(2,1)S(1)}, u32[]{:S(2)}, u32[]{:S(2)}) %collective-permute-start.9) | collective-permute-done | bytes 294944 | tf_op jit(solution)/shard_map/ppermute | solution.py:59
  115.4 1.9 collective-permute-start.11
  117.3 6.7 %collective-permute-done.11.res_3 = bf16[8,144,128]{2,1,0:T(8,128)(2,1)S(1)} collective-permute-done((bf16[8,144,128]{2,1,0:T(8,128)(2,1)S(1)}, bf16[8,144,128]{2,1,0:T(8,128)(2,1)S(1)}, u32[]{:S(2)}, u32[]{:S(2)}) %collective-permute-start.11) | collective-permute-done | bytes 294944 | tf_op jit(solution)/shard_map/ppermute | solution.py:61
  124.0 2.1 shard_map.103
  126.1 1.9 collective-permute-start.12
  128.1 3.5 %shard_map.104 = (bf16[4,1168,128]{2,1,0:T(8,128)(2,1)S(1)}, bf16[4,1168,128]{2,1,0:T(8,128)(2,1)}) custom-call(s32[4]{0:T(128)S(1)} %pad_add_fusion.1.near_ref, bf16[8,144,128]{2,1,0:T(8,128)(2,1)S(1)} %all_to_all.15.res_0, bf16[8,144,128]{2,1,0:T(8,128)(2,1)S(1)} %collective-permute-done.9.res_1, bf16[8,144,128]{2,1,0:T(8,128)(2,1)S(1)} %collective-permute-done.10.res_2, ...), custom_call_target="tpu_custom_call" | custom-call | flops 603979776 | bytes 7241744 | tf_op jit(solution)/shard_map/pallas_call | solution.py:185
  133.7 2.5 %collective-permute-start.13 = (bf16[4,1168,128]{2,1,0:T(8,128)(2,1)}, bf16[4,1168,128]{2,1,0:T(8,128)(2,1)}, u32[]{:S(2)}, u32[]{:S(2)}) collective-permute-start(bf16[4,1168,128]{2,1,0:T(8,128)(2,1)} %get-tuple-element.49), channel_id=1, source_target_pairs={{0,8},{8,0},{16,24},{24,16},{32,40},{40,32},{48,56},{56,48},{64,72... | collective-permute-start | bytes 3588104 | tf_op jit(solution)/shard_map/ppermute | solution.py:217
  137.8 2.4 %collective-permute-start.15 = (bf16[1200,128]{1,0:T(8,128)(2,1)S(1)}, bf16[1200,128]{1,0:T(8,128)(2,1)}, u32[]{:S(2)}, u32[]{:S(2)}) collective-permute-start(bf16[1200,128]{1,0:T(8,128)(2,1)S(1)} %get-tuple-element.58), channel_id=1, source_target_pairs={{0,2},{1,3},{2,4},{3,5},{4,6},{5,7},{6,0},{7,1},{8,14},{9,15},{10,... | collective-permute-start | bytes 921608 | tf_op jit(solution)/shard_map/ppermute | solution.py:219
  140.2 3.5 %collective-permute-start.14 = (bf16[1200,128]{1,0:T(8,128)(2,1)S(1)}, bf16[1200,128]{1,0:T(8,128)(2,1)}, u32[]{:S(2)}, u32[]{:S(2)}) collective-permute-start(bf16[1200,128]{1,0:T(8,128)(2,1)S(1)} %get-tuple-element.59), channel_id=1, source_target_pairs={{0,6},{1,7},{2,0},{3,1},{4,2},{5,3},{6,4},{7,5},{8,10},{9,11},{10,... | collective-permute-start | bytes 921608 | tf_op jit(solution)/shard_map/ppermute | solution.py:220
  143.7 5.1 %collective-permute-done.15 = bf16[1200,128]{1,0:T(8,128)(2,1)} collective-permute-done((bf16[1200,128]{1,0:T(8,128)(2,1)S(1)}, bf16[1200,128]{1,0:T(8,128)(2,1)}, u32[]{:S(2)}, u32[]{:S(2)}) %collective-permute-start.15) | collective-permute-done | bytes 307232 | tf_op jit(solution)/shard_map/ppermute | solution.py:219
  150.7 1.9 collective-permute-start.16
  153.9 2.7 %collective-permute-start.18 = (bf16[1168,128]{1,0:T(8,128)(2,1)S(1)}, bf16[1168,128]{1,0:T(8,128)(2,1)S(1)}, u32[]{:S(2)}, u32[]{:S(2)}) collective-permute-start(bf16[1168,128]{1,0:T(8,128)(2,1)S(1)} %get-tuple-element.52), channel_id=1, source_target_pairs={{0,2},{1,3},{2,4},{3,5},{4,6},{5,7},{6,0},{7,1},{8,14},{9,15},{10,... | collective-permute-start | bytes 897032 | tf_op jit(solution)/shard_map/ppermute | solution.py:225
  156.5 3.1 %collective-permute-done.16 = bf16[1200,128]{1,0:T(8,128)(2,1)S(1)} collective-permute-done((bf16[1200,128]{1,0:T(8,128)(2,1)}, bf16[1200,128]{1,0:T(8,128)(2,1)S(1)}, u32[]{:S(2)}, u32[]{:S(2)}) %collective-permute-start.16) | collective-permute-done | bytes 307232 | tf_op jit(solution)/shard_map/ppermute | solution.py:221
  160.8 5.2 %collective-permute-start.20 = (bf16[1200,128]{1,0:T(8,128)(2,1)S(1)}, bf16[1200,128]{1,0:T(8,128)(2,1)S(1)}, u32[]{:S(2)}, u32[]{:S(2)}) collective-permute-start(bf16[1200,128]{1,0:T(8,128)(2,1)S(1)} %fusion.2), channel_id=1, source_target_pairs={{0,1},{1,0},{2,3},{3,2},{4,5},{5,4},{6,7},{7,6},{8,9},{9,8},{10,11... | collective-permute-start | bytes 921608 | tf_op jit(solution)/shard_map/ppermute | solution.py:223
  166.0 3.0 %collective-permute-start.17 = (bf16[1168,128]{1,0:T(8,128)(2,1)S(1)}, bf16[1168,128]{1,0:T(8,128)(2,1)S(1)}, u32[]{:S(2)}, u32[]{:S(2)}) collective-permute-start(bf16[1168,128]{1,0:T(8,128)(2,1)S(1)} %get-tuple-element.51), channel_id=1, source_target_pairs={{0,6},{1,7},{2,0},{3,1},{4,2},{5,3},{6,4},{7,5},{8,10},{9,11},{10,... | collective-permute-start | bytes 897032 | tf_op jit(solution)/shard_map/ppermute | solution.py:226
  170.2 4.0 %collective-permute-start.19 = (bf16[1168,128]{1,0:T(8,128)(2,1)S(1)}, bf16[1168,128]{1,0:T(8,128)(2,1)S(1)}, u32[]{:S(2)}, u32[]{:S(2)}) collective-permute-start(bf16[1168,128]{1,0:T(8,128)(2,1)S(1)} %fusion.3), channel_id=1, source_target_pairs={{0,2},{1,3},{2,4},{3,5},{4,6},{5,7},{6,0},{7,1},{8,14},{9,15},{10,... | collective-permute-start | bytes 897032 | tf_op jit(solution)/shard_map/ppermute | solution.py:227
  174.2 6.3 %collective-permute-done.20 = bf16[1200,128]{1,0:T(8,128)(2,1)S(1)} collective-permute-done((bf16[1200,128]{1,0:T(8,128)(2,1)S(1)}, bf16[1200,128]{1,0:T(8,128)(2,1)S(1)}, u32[]{:S(2)}, u32[]{:S(2)}) %collective-permute-start.20) | collective-permute-done | bytes 307232 | tf_op jit(solution)/shard_map/ppermute | solution.py:223
  180.6 1.9 collective-permute-start.22
  182.5 3.9 %collective-permute-start.23 = (bf16[1200,128]{1,0:T(8,128)(2,1)S(1)}, bf16[1200,128]{1,0:T(8,128)(2,1)S(1)}, u32[]{:S(2)}, u32[]{:S(2)}) collective-permute-start(bf16[1200,128]{1,0:T(8,128)(2,1)S(1)} %add_convert_fusion.refs_0_), channel_id=1, source_target_pairs={{0,6},{1,7},{2,0},{3,1},{4,2},{5,3},{6,4},{7,5},{8,10},{9,11},{10,... | collective-permute-start | bytes 921608 | tf_op jit(solution)/shard_map/ppermute | solution.py:206
  187.6 4.4 %collective-permute-start.21 = (bf16[1168,128]{1,0:T(8,128)(2,1)S(1)}, bf16[1168,128]{1,0:T(8,128)(2,1)S(1)}, u32[]{:S(2)}, u32[]{:S(2)}) collective-permute-start(bf16[1168,128]{1,0:T(8,128)(2,1)S(1)} %fusion.5), channel_id=1, source_target_pairs={{0,1},{1,0},{2,3},{3,2},{4,5},{5,4},{6,7},{7,6},{8,9},{9,8},{10,11... | collective-permute-start | bytes 897032 | tf_op jit(solution)/shard_map/ppermute | solution.py:229
  192.1 3.1 %collective-permute-start.25 = (bf16[1200,128]{1,0:T(8,128)(2,1)S(1)}, bf16[1200,128]{1,0:T(8,128)(2,1)S(1)}, u32[]{:S(2)}, u32[]{:S(2)}) collective-permute-start(bf16[1200,128]{1,0:T(8,128)(2,1)S(1)} %collective-permute-done.22.refs_1_), channel_id=1, source_target_pairs={{0,2},{1,3},{2,4},{3,5},{4,6},{5,7},{6,0},{7,1},{8,14},{9,15},{10,... | collective-permute-start | bytes 921608 | tf_op jit(solution)/shard_map/ppermute | solution.py:207
  195.2 8.1 %collective-permute-done.21 = bf16[1168,128]{1,0:T(8,128)(2,1)S(1)} collective-permute-done((bf16[1168,128]{1,0:T(8,128)(2,1)S(1)}, bf16[1168,128]{1,0:T(8,128)(2,1)S(1)}, u32[]{:S(2)}, u32[]{:S(2)}) %collective-permute-start.21) | collective-permute-done | bytes 299040 | tf_op jit(solution)/shard_map/ppermute | solution.py:229
  203.4 3.0 %collective-permute-start.24 = (bf16[1168,128]{1,0:T(8,128)(2,1)S(1)}, bf16[1168,128]{1,0:T(8,128)(2,1)S(1)}, u32[]{:S(2)}, u32[]{:S(2)}) collective-permute-start(bf16[1168,128]{1,0:T(8,128)(2,1)S(1)} %add_convert_fusion.3.refs_0_), channel_id=1, source_target_pairs={{0,2},{1,3},{2,4},{3,5},{4,6},{5,7},{6,0},{7,1},{8,14},{9,15},{10,... | collective-permute-start | bytes 897032 | tf_op jit(solution)/shard_map/ppermute | solution.py:205
  206.5 2.8 %collective-permute-start.26 = (bf16[1168,128]{1,0:T(8,128)(2,1)S(1)}, bf16[1168,128]{1,0:T(8,128)(2,1)S(1)}, u32[]{:S(2)}, u32[]{:S(2)}) collective-permute-start(bf16[1168,128]{1,0:T(8,128)(2,1)S(1)} %add_convert_fusion.3.refs_0_), channel_id=1, source_target_pairs={{0,6},{1,7},{2,0},{3,1},{4,2},{5,3},{6,4},{7,5},{8,10},{9,11},{10,... | collective-permute-start | bytes 897032 | tf_op jit(solution)/shard_map/ppermute | solution.py:206
  209.3 4.9 %collective-permute-done.24.refs_1_ = bf16[1168,128]{1,0:T(8,128)(2,1)S(1)} collective-permute-done((bf16[1168,128]{1,0:T(8,128)(2,1)S(1)}, bf16[1168,128]{1,0:T(8,128)(2,1)S(1)}, u32[]{:S(2)}, u32[]{:S(2)}) %collective-permute-start.24) | collective-permute-done | bytes 299040 | tf_op jit(solution)/shard_map/ppermute | solution.py:205
  214.2 2.3 %collective-permute-start.27 = (bf16[1168,128]{1,0:T(8,128)(2,1)S(1)}, bf16[1168,128]{1,0:T(8,128)(2,1)S(1)}, u32[]{:S(2)}, u32[]{:S(2)}) collective-permute-start(bf16[1168,128]{1,0:T(8,128)(2,1)S(1)} %collective-permute-done.24.refs_1_), channel_id=1, source_target_pairs={{0,2},{1,3},{2,4},{3,5},{4,6},{5,7},{6,0},{7,1},{8,14},{9,15},{10,... | collective-permute-start | bytes 897032 | tf_op jit(solution)/shard_map/ppermute | solution.py:207
  219.4 3.5 %collective-permute-done.27.refs_3_ = bf16[1168,128]{1,0:T(8,128)(2,1)S(1)} collective-permute-done((bf16[1168,128]{1,0:T(8,128)(2,1)S(1)}, bf16[1168,128]{1,0:T(8,128)(2,1)S(1)}, u32[]{:S(2)}, u32[]{:S(2)}) %collective-permute-start.27) | collective-permute-done | bytes 299040 | tf_op jit(solution)/shard_map/ppermute | solution.py:207
  (70 shorter events, 25.2 us)
Async XLA Ops:
  0.6 45.4 %copy-start = (bf16[128,4608]{1,0:T(8,128)(2,1)S(1)}, bf16[128,4608]{1,0:T(8,128)(2,1)}, u32[]{:S(2)}) copy-start(bf16[128,4608]{1,0:T(8,128)(2,1)} %wd_own.3) | copy-start | bytes 3538948
  2.2 26.2 %all-to-all-start = ((bf16[16,72,128]{2,1,0:T(8,128)(2,1)}), bf16[16,72,128]{2,1,0:T(8,128)(2,1)S(1)}, u32[]{:S(2)}, u32[]{:S(2)}) async-start(bf16[16,72,128]{2,1,0:T(8,128)(2,1)} %bitcast.11), calls=%async_computation | async-start | bytes 589824 | tf_op jit(solution)/shard_map/all_to_all | solution.py:51
  14.7 31.4 %collective-permute-start.4 = (bf16[4608,128]{1,0:T(8,128)(2,1)}, bf16[4608,128]{1,0:T(8,128)(2,1)}, u32[]{:S(2)}, u32[]{:S(2)}) collective-permute-start(bf16[4608,128]{1,0:T(8,128)(2,1)} %we_own.1), channel_id=1, source_target_pairs={{0,8},{8,0},{16,24},{24,16},{32,40},{40,32},{48,56},{56,48},{64,72... | collective-permute-start | bytes 3538952 | tf_op jit(solution)/shard_map/ppermute | solution.py:256
  17.0 29.0 %collective-permute-start.5 = (bf16[128,4608]{1,0:T(8,128)(2,1)}, bf16[128,4608]{1,0:T(8,128)(2,1)S(1)}, u32[]{:S(2)}, u32[]{:S(2)}) collective-permute-start(bf16[128,4608]{1,0:T(8,128)(2,1)} %wd_own.3), channel_id=1, source_target_pairs={{0,8},{8,0},{16,24},{24,16},{32,40},{40,32},{48,56},{56,48},{64,72... | collective-permute-start | bytes 3538952 | tf_op jit(solution)/shard_map/ppermute | solution.py:257
  20.4 5.1 %collective-permute-start = (f32[2,128]{1,0:T(2,128)S(1)}, f32[2,128]{1,0:T(2,128)S(1)}, u32[]{:S(2)}, u32[]{:S(2)}) collective-permute-start(f32[2,128]{1,0:T(2,128)S(1)} %pad_maximum_fusion.1), channel_id=1, source_target_pairs={{0,8},{8,0},{16,24},{24,16},{32,40},{40,32},{48,56},{56,48},{64,72... | collective-permute-start | bytes 3080 | tf_op jit(solution)/shard_map/ppermute | solution.py:259
  28.4 9.0 %collective-permute-start.1 = (bf16[8,144,128]{2,1,0:T(8,128)(2,1)S(1)}, bf16[8,144,128]{2,1,0:T(8,128)(2,1)S(1)}, u32[]{:S(2)}, u32[]{:S(2)}) collective-permute-start(bf16[8,144,128]{2,1,0:T(8,128)(2,1)S(1)} %bitcast.67), channel_id=1, source_target_pairs={{0,128},{8,24},{16,144},{24,8},{32,160},{40,56},{48,176},{56,40},{... | collective-permute-start | bytes 884744 | tf_op jit(solution)/shard_map/ppermute | solution.py:59
  30.3 11.1 %collective-permute-start.2 = (bf16[8,144,128]{2,1,0:T(8,128)(2,1)S(1)}, bf16[8,144,128]{2,1,0:T(8,128)(2,1)S(1)}, u32[]{:S(2)}, u32[]{:S(2)}) collective-permute-start(bf16[8,144,128]{2,1,0:T(8,128)(2,1)S(1)} %bitcast.68), channel_id=1, source_target_pairs={{0,16},{8,136},{16,0},{24,152},{32,48},{40,168},{48,32},{56,184},{... | collective-permute-start | bytes 884744 | tf_op jit(solution)/shard_map/ppermute | solution.py:60
  37.4 8.6 %collective-permute-start.3 = (bf16[8,144,128]{2,1,0:T(8,128)(2,1)S(1)}, bf16[8,144,128]{2,1,0:T(8,128)(2,1)S(1)}, u32[]{:S(2)}, u32[]{:S(2)}) collective-permute-start(bf16[8,144,128]{2,1,0:T(8,128)(2,1)S(1)} %collective-permute-done.1.act_1), channel_id=1, source_target_pairs={{0,16},{8,136},{16,0},{24,152},{32,48},{40,168},{48,32},{56,184},{... | collective-permute-start | bytes 884744 | tf_op jit(solution)/shard_map/ppermute | solution.py:61
  46.0 1.3 copy-start.5
  50.4 8.7 %copy-start.6 = (f32[256,128]{1,0:T(8,128)}, f32[256,128]{1,0:T(8,128)S(1)}, u32[]{:S(2)}) copy-start(f32[256,128]{1,0:T(8,128)S(1)} %get-tuple-element.45.slope_ref) | copy-start | bytes 393220
  50.4 12.6 %copy-start.8 = (bf16[128,256]{1,0:T(8,128)(2,1)}, bf16[128,256]{1,0:T(8,128)(2,1)S(1)}, u32[]{:S(2)}) copy-start(bf16[128,256]{1,0:T(8,128)(2,1)S(1)} %get-tuple-element.38.feat_ref) | copy-start | bytes 196612
  50.4 8.6 %collective-permute-start.7 = (bf16[8,144,128]{2,1,0:T(8,128)(2,1)S(1)}, bf16[8,144,128]{2,1,0:T(8,128)(2,1)S(1)}, u32[]{:S(2)}, u32[]{:S(2)}) collective-permute-start(bf16[8,144,128]{2,1,0:T(8,128)(2,1)S(1)} %get-tuple-element.37), channel_id=1, source_target_pairs={{0,128},{8,24},{16,144},{24,8},{32,160},{40,56},{48,176},{56,40},{... | collective-permute-start | bytes 884744 | tf_op jit(solution)/shard_map/ppermute | solution.py:65
  52.4 10.7 %collective-permute-start.6 = (bf16[8,144,128]{2,1,0:T(8,128)(2,1)S(1)}, bf16[8,144,128]{2,1,0:T(8,128)(2,1)S(1)}, u32[]{:S(2)}, u32[]{:S(2)}) collective-permute-start(bf16[8,144,128]{2,1,0:T(8,128)(2,1)S(1)} %get-tuple-element.35), channel_id=1, source_target_pairs={{0,128},{8,24},{16,144},{24,8},{32,160},{40,56},{48,176},{56,40},{... | collective-permute-start | bytes 884744 | tf_op jit(solution)/shard_map/ppermute | solution.py:66
  59.2 8.6 %collective-permute-start.8 = (bf16[8,144,128]{2,1,0:T(8,128)(2,1)S(1)}, bf16[8,144,128]{2,1,0:T(8,128)(2,1)S(1)}, u32[]{:S(2)}, u32[]{:S(2)}) collective-permute-start(bf16[8,144,128]{2,1,0:T(8,128)(2,1)S(1)} %add_convert_fusion.7), channel_id=1, source_target_pairs={{0,16},{8,136},{16,0},{24,152},{32,48},{40,168},{48,32},{56,184},{... | collective-permute-start | bytes 884744 | tf_op jit(solution)/shard_map/ppermute | solution.py:67
  68.6 17.1 %all-to-all-start.1 = ((bf16[8,144,128]{2,1,0:T(8,128)(2,1)}), bf16[8,144,128]{2,1,0:T(8,128)(2,1)}, u32[]{:S(2)}, u32[]{:S(2)}) async-start(bf16[8,144,128]{2,1,0:T(8,128)(2,1)} %add_convert_fusion.6), calls=%async_computation.1 | async-start | bytes 589824 | tf_op jit(solution)/shard_map/all_to_all | solution.py:51
  85.7 38.3 %copy-start.9 = (bf16[128,256]{1,0:T(8,128)(2,1)S(1)}, bf16[128,256]{1,0:T(8,128)(2,1)}, u32[]{:S(2)}) copy-start(bf16[128,256]{1,0:T(8,128)(2,1)} %copy-done.8) | copy-start | bytes 196612
  86.8 41.3 %copy-start.7 = (f32[256,128]{1,0:T(8,128)S(1)}, f32[256,128]{1,0:T(8,128)}, u32[]{:S(2)}) copy-start(f32[256,128]{1,0:T(8,128)} %copy-done.6) | copy-start | bytes 393220
  104.3 11.1 %collective-permute-start.9 = (bf16[8,144,128]{2,1,0:T(8,128)(2,1)S(1)}, bf16[8,144,128]{2,1,0:T(8,128)(2,1)S(1)}, u32[]{:S(2)}, u32[]{:S(2)}) collective-permute-start(bf16[8,144,128]{2,1,0:T(8,128)(2,1)S(1)} %all_to_all.15.res_0), channel_id=1, source_target_pairs={{0,128},{8,24},{16,144},{24,8},{32,160},{40,56},{48,176},{56,40},{... | collective-permute-start | bytes 884744 | tf_op jit(solution)/shard_map/ppermute | solution.py:59
  106.2 11.1 %collective-permute-start.10 = (bf16[8,144,128]{2,1,0:T(8,128)(2,1)S(1)}, bf16[8,144,128]{2,1,0:T(8,128)(2,1)S(1)}, u32[]{:S(2)}, u32[]{:S(2)}) collective-permute-start(bf16[8,144,128]{2,1,0:T(8,128)(2,1)S(1)} %all_to_all.15.res_0), channel_id=1, source_target_pairs={{0,16},{8,136},{16,0},{24,152},{32,48},{40,168},{48,32},{56,184},{... | collective-permute-start | bytes 884744 | tf_op jit(solution)/shard_map/ppermute | solution.py:60
  115.4 8.6 %collective-permute-start.11 = (bf16[8,144,128]{2,1,0:T(8,128)(2,1)S(1)}, bf16[8,144,128]{2,1,0:T(8,128)(2,1)S(1)}, u32[]{:S(2)}, u32[]{:S(2)}) collective-permute-start(bf16[8,144,128]{2,1,0:T(8,128)(2,1)S(1)} %collective-permute-done.9.res_1), channel_id=1, source_target_pairs={{0,16},{8,136},{16,0},{24,152},{32,48},{40,168},{48,32},{56,184},{... | collective-permute-start | bytes 884744 | tf_op jit(solution)/shard_map/ppermute | solution.py:61
  126.1 5.4 %copy-start.1 = (bf16[4,1200,128]{2,1,0:T(8,128)(2,1)}, bf16[4,1200,128]{2,1,0:T(8,128)(2,1)S(1)}, u32[]{:S(2)}) copy-start(bf16[4,1200,128]{2,1,0:T(8,128)(2,1)S(1)} %get-tuple-element.50) | copy-start | bytes 3686404
  126.1 6.5 %collective-permute-start.12 = (bf16[4,1200,128]{2,1,0:T(8,128)(2,1)S(1)}, bf16[4,1200,128]{2,1,0:T(8,128)(2,1)S(1)}, u32[]{:S(2)}, u32[]{:S(2)}) collective-permute-start(bf16[4,1200,128]{2,1,0:T(8,128)(2,1)S(1)} %get-tuple-element.48), channel_id=1, source_target_pairs={{0,8},{8,0},{16,24},{24,16},{32,40},{40,32},{48,56},{56,48},{64,72... | collective-permute-start | bytes 3686408 | tf_op jit(solution)/shard_map/ppermute | solution.py:216
  131.5 1.1 copy-start.3
  132.6 1.1 copy-start.10
  133.7 15.1 %copy-start.2 = (bf16[4,1200,128]{2,1,0:T(8,128)(2,1)S(1)}, bf16[4,1200,128]{2,1,0:T(8,128)(2,1)}, u32[]{:S(2)}) copy-start(bf16[4,1200,128]{2,1,0:T(8,128)(2,1)} %copy-done.1) | copy-start | bytes 3686404
  133.7 18.9 %collective-permute-start.13 = (bf16[4,1168,128]{2,1,0:T(8,128)(2,1)}, bf16[4,1168,128]{2,1,0:T(8,128)(2,1)}, u32[]{:S(2)}, u32[]{:S(2)}) collective-permute-start(bf16[4,1168,128]{2,1,0:T(8,128)(2,1)} %get-tuple-element.49), channel_id=1, source_target_pairs={{0,8},{8,0},{16,24},{24,16},{32,40},{40,32},{48,56},{56,48},{64,72... | collective-permute-start | bytes 3588104 | tf_op jit(solution)/shard_map/ppermute | solution.py:217
  136.3 16.3 %copy-start.4 = (bf16[4,1168,128]{2,1,0:T(8,128)(2,1)S(1)}, bf16[4,1168,128]{2,1,0:T(8,128)(2,1)}, u32[]{:S(2)}) copy-start(bf16[4,1168,128]{2,1,0:T(8,128)(2,1)} %copy-done.3) | copy-start | bytes 3588100
  137.8 11.0 %collective-permute-start.15 = (bf16[1200,128]{1,0:T(8,128)(2,1)S(1)}, bf16[1200,128]{1,0:T(8,128)(2,1)}, u32[]{:S(2)}, u32[]{:S(2)}) collective-permute-start(bf16[1200,128]{1,0:T(8,128)(2,1)S(1)} %get-tuple-element.58), channel_id=1, source_target_pairs={{0,2},{1,3},{2,4},{3,5},{4,6},{5,7},{6,0},{7,1},{8,14},{9,15},{10,... | collective-permute-start | bytes 921608 | tf_op jit(solution)/shard_map/ppermute | solution.py:219
  140.2 13.6 %collective-permute-start.14 = (bf16[1200,128]{1,0:T(8,128)(2,1)S(1)}, bf16[1200,128]{1,0:T(8,128)(2,1)}, u32[]{:S(2)}, u32[]{:S(2)}) collective-permute-start(bf16[1200,128]{1,0:T(8,128)(2,1)S(1)} %get-tuple-element.59), channel_id=1, source_target_pairs={{0,6},{1,7},{2,0},{3,1},{4,2},{5,3},{6,4},{7,5},{8,10},{9,11},{10,... | collective-permute-start | bytes 921608 | tf_op jit(solution)/shard_map/ppermute | solution.py:220
  150.7 8.9 %collective-permute-start.16 = (bf16[1200,128]{1,0:T(8,128)(2,1)}, bf16[1200,128]{1,0:T(8,128)(2,1)S(1)}, u32[]{:S(2)}, u32[]{:S(2)}) collective-permute-start(bf16[1200,128]{1,0:T(8,128)(2,1)} %fusion), channel_id=1, source_target_pairs={{0,2},{1,3},{2,4},{3,5},{4,6},{5,7},{6,0},{7,1},{8,14},{9,15},{10,... | collective-permute-start | bytes 921608 | tf_op jit(solution)/shard_map/ppermute | solution.py:221
  153.9 15.2 %collective-permute-start.18 = (bf16[1168,128]{1,0:T(8,128)(2,1)S(1)}, bf16[1168,128]{1,0:T(8,128)(2,1)S(1)}, u32[]{:S(2)}, u32[]{:S(2)}) collective-permute-start(bf16[1168,128]{1,0:T(8,128)(2,1)S(1)} %get-tuple-element.52), channel_id=1, source_target_pairs={{0,2},{1,3},{2,4},{3,5},{4,6},{5,7},{6,0},{7,1},{8,14},{9,15},{10,... | collective-permute-start | bytes 897032 | tf_op jit(solution)/shard_map/ppermute | solution.py:225
  160.8 19.6 %collective-permute-start.20 = (bf16[1200,128]{1,0:T(8,128)(2,1)S(1)}, bf16[1200,128]{1,0:T(8,128)(2,1)S(1)}, u32[]{:S(2)}, u32[]{:S(2)}) collective-permute-start(bf16[1200,128]{1,0:T(8,128)(2,1)S(1)} %fusion.2), channel_id=1, source_target_pairs={{0,1},{1,0},{2,3},{3,2},{4,5},{5,4},{6,7},{7,6},{8,9},{9,8},{10,11... | collective-permute-start | bytes 921608 | tf_op jit(solution)/shard_map/ppermute | solution.py:223
  166.0 20.4 %collective-permute-start.17 = (bf16[1168,128]{1,0:T(8,128)(2,1)S(1)}, bf16[1168,128]{1,0:T(8,128)(2,1)S(1)}, u32[]{:S(2)}, u32[]{:S(2)}) collective-permute-start(bf16[1168,128]{1,0:T(8,128)(2,1)S(1)} %get-tuple-element.51), channel_id=1, source_target_pairs={{0,6},{1,7},{2,0},{3,1},{4,2},{5,3},{6,4},{7,5},{8,10},{9,11},{10,... | collective-permute-start | bytes 897032 | tf_op jit(solution)/shard_map/ppermute | solution.py:226
  170.2 16.2 %collective-permute-start.19 = (bf16[1168,128]{1,0:T(8,128)(2,1)S(1)}, bf16[1168,128]{1,0:T(8,128)(2,1)S(1)}, u32[]{:S(2)}, u32[]{:S(2)}) collective-permute-start(bf16[1168,128]{1,0:T(8,128)(2,1)S(1)} %fusion.3), channel_id=1, source_target_pairs={{0,2},{1,3},{2,4},{3,5},{4,6},{5,7},{6,0},{7,1},{8,14},{9,15},{10,... | collective-permute-start | bytes 897032 | tf_op jit(solution)/shard_map/ppermute | solution.py:227
  180.6 11.5 %collective-permute-start.22 = (bf16[1200,128]{1,0:T(8,128)(2,1)S(1)}, bf16[1200,128]{1,0:T(8,128)(2,1)S(1)}, u32[]{:S(2)}, u32[]{:S(2)}) collective-permute-start(bf16[1200,128]{1,0:T(8,128)(2,1)S(1)} %add_convert_fusion.refs_0_), channel_id=1, source_target_pairs={{0,2},{1,3},{2,4},{3,5},{4,6},{5,7},{6,0},{7,1},{8,14},{9,15},{10,... | collective-permute-start | bytes 921608 | tf_op jit(solution)/shard_map/ppermute | solution.py:205
  182.5 12.7 %collective-permute-start.23 = (bf16[1200,128]{1,0:T(8,128)(2,1)S(1)}, bf16[1200,128]{1,0:T(8,128)(2,1)S(1)}, u32[]{:S(2)}, u32[]{:S(2)}) collective-permute-start(bf16[1200,128]{1,0:T(8,128)(2,1)S(1)} %add_convert_fusion.refs_0_), channel_id=1, source_target_pairs={{0,6},{1,7},{2,0},{3,1},{4,2},{5,3},{6,4},{7,5},{8,10},{9,11},{10,... | collective-permute-start | bytes 921608 | tf_op jit(solution)/shard_map/ppermute | solution.py:206
  187.6 15.7 %collective-permute-start.21 = (bf16[1168,128]{1,0:T(8,128)(2,1)S(1)}, bf16[1168,128]{1,0:T(8,128)(2,1)S(1)}, u32[]{:S(2)}, u32[]{:S(2)}) collective-permute-start(bf16[1168,128]{1,0:T(8,128)(2,1)S(1)} %fusion.5), channel_id=1, source_target_pairs={{0,1},{1,0},{2,3},{3,2},{4,5},{5,4},{6,7},{7,6},{8,9},{9,8},{10,11... | collective-permute-start | bytes 897032 | tf_op jit(solution)/shard_map/ppermute | solution.py:229
  192.1 14.4 %collective-permute-start.25 = (bf16[1200,128]{1,0:T(8,128)(2,1)S(1)}, bf16[1200,128]{1,0:T(8,128)(2,1)S(1)}, u32[]{:S(2)}, u32[]{:S(2)}) collective-permute-start(bf16[1200,128]{1,0:T(8,128)(2,1)S(1)} %collective-permute-done.22.refs_1_), channel_id=1, source_target_pairs={{0,2},{1,3},{2,4},{3,5},{4,6},{5,7},{6,0},{7,1},{8,14},{9,15},{10,... | collective-permute-start | bytes 921608 | tf_op jit(solution)/shard_map/ppermute | solution.py:207
  203.4 10.8 %collective-permute-start.24 = (bf16[1168,128]{1,0:T(8,128)(2,1)S(1)}, bf16[1168,128]{1,0:T(8,128)(2,1)S(1)}, u32[]{:S(2)}, u32[]{:S(2)}) collective-permute-start(bf16[1168,128]{1,0:T(8,128)(2,1)S(1)} %add_convert_fusion.3.refs_0_), channel_id=1, source_target_pairs={{0,2},{1,3},{2,4},{3,5},{4,6},{5,7},{6,0},{7,1},{8,14},{9,15},{10,... | collective-permute-start | bytes 897032 | tf_op jit(solution)/shard_map/ppermute | solution.py:205
  206.5 12.9 %collective-permute-start.26 = (bf16[1168,128]{1,0:T(8,128)(2,1)S(1)}, bf16[1168,128]{1,0:T(8,128)(2,1)S(1)}, u32[]{:S(2)}, u32[]{:S(2)}) collective-permute-start(bf16[1168,128]{1,0:T(8,128)(2,1)S(1)} %add_convert_fusion.3.refs_0_), channel_id=1, source_target_pairs={{0,6},{1,7},{2,0},{3,1},{4,2},{5,3},{6,4},{7,5},{8,10},{9,11},{10,... | collective-permute-start | bytes 897032 | tf_op jit(solution)/shard_map/ppermute | solution.py:206
  214.2 8.6 %collective-permute-start.27 = (bf16[1168,128]{1,0:T(8,128)(2,1)S(1)}, bf16[1168,128]{1,0:T(8,128)(2,1)S(1)}, u32[]{:S(2)}, u32[]{:S(2)}) collective-permute-start(bf16[1168,128]{1,0:T(8,128)(2,1)S(1)} %collective-permute-done.24.refs_1_), channel_id=1, source_target_pairs={{0,2},{1,3},{2,4},{3,5},{4,6},{5,7},{6,0},{7,1},{8,14},{9,15},{10,... | collective-permute-start | bytes 897032 | tf_op jit(solution)/shard_map/ppermute | solution.py:207

commit v8 on v7

--- a/solution.py
+++ b/solution.py
@@ -17,7 +17,7 @@
 FAR, CORE = (0, 2), (4,)
 NX = 4
 DEC_BIAS_ROWS, ENC_BIAS_ROWS = 48, 16
-VMEM = 24 * 1024 * 1024
+VMEM = 48 * 1024 * 1024
 
 
 def size_of(axes):
@@ -42,6 +42,7 @@
     return pairs
 
 
+X_GROUPS = np.arange(8).reshape(NX, 2).T.tolist()
 AHEAD, BACK = along_x(1), along_x(-1)
 CORE_SWAP = [(i, i ^ 1) for i in range(64)]
 Y_SWAP = [(i, i ^ 1) for i in range(8)]
@@ -159,14 +160,12 @@
             out[x, quarter:, :] = rows
 
 
-def place_dec_kernel(order_ref, *refs):
-    dec_ref = refs[-1]
+def place_dec_kernel(parts_ref, dec_ref):
     lat = dec_ref.shape[0] // NX
-    for n, ref in enumerate(refs[:-1]):
-        row = pl.multiple_of(order_ref[n] * lat, lat)
+    for x in range(NX):
         for i in range(dec_ref.shape[1] // TILE):
-            lanes = slice(i * TILE, (i + 1) * TILE)
-            dec_ref[pl.ds(row, lat), lanes] = ref[i * lat : (i + 1) * lat, :]
+            rows, lanes = slice(i * lat, (i + 1) * lat), slice(i * TILE, (i + 1) * TILE)
+            dec_ref[x * lat : (x + 1) * lat, lanes] = parts_ref[x, rows, :]
 
 
 def place_enc_kernel(order_ref, *refs):
@@ -189,7 +188,7 @@
         out_specs=[whole] * len(outs),
         scratch_shapes=list(scratch),
         compiler_params=pltpu.CompilerParams(vmem_limit_bytes=VMEM),
-        cost_estimate=pl.CostEstimate(flops=flops, bytes_accessed=moved, transcendentals=0),
+        cost_estimate=pl.CostEstimate(flops=0, bytes_accessed=0, transcendentals=0),
     )(*args)
 
 
@@ -201,9 +200,9 @@
     return lax.optimization_barrier((value, *others))[0]
 
 
-def gather_x(piece, *first):
+def gather_x(piece):
     behind = lax.ppermute(piece, ALL, AHEAD)
-    ahead = lax.ppermute(after(piece, *first), ALL, BACK)
+    ahead = lax.ppermute(piece, ALL, BACK)
     return piece, behind, ahead, lax.ppermute(behind, ALL, AHEAD)
 
 
@@ -211,27 +210,27 @@
     return [lax.dynamic_index_in_dim(part, n, keepdims=False) for part in parts]
 
 
-def reduce_gradients(dec, enc, core, x):
+def reduce_gradients(dec, make_enc, core, x):
     ahead, back = (x + 1 + 2 * core) % NX, (x + 3 + 2 * core) % NX
-    dec = dec[0], lax.ppermute(dec[1], "dict", CORE_SWAP)
-    enc = enc[0], lax.ppermute(after(enc[1], dec[1]), "dict", CORE_SWAP)
-
-    relayed = lax.ppermute(add(*quarter_of(dec, (x + 2) % NX)), ALL, AHEAD)
-    direct = lax.ppermute(add(*quarter_of(dec, back)), ALL, BACK)
-    passed = lax.ppermute(add(*quarter_of(dec, ahead), relayed), ALL, AHEAD)
-    dec_piece = lax.optimization_barrier(add(*quarter_of(dec, x), direct, passed))
-    dec_swapped = lax.ppermute(dec_piece, "dp", Y_SWAP)
-
-    relayed = lax.ppermute(after(add(*quarter_of(enc, (x + 2) % NX)), direct), ALL, AHEAD)
-    direct = lax.ppermute(after(add(*quarter_of(enc, back)), dec_piece), ALL, BACK)
-    passed = lax.ppermute(add(*quarter_of(enc, ahead), relayed), ALL, AHEAD)
+    dec_total = add(dec[0], lax.ppermute(dec[1], "dict", CORE_SWAP))
+    enc = make_enc(dec[0])
+    dec_moved = lax.all_to_all(dec_total, "dp", 0, 0, axis_index_groups=X_GROUPS)
+
+    enc = enc[0], lax.ppermute(after(enc[1], dec_total), "dict", CORE_SWAP)
+    relayed = lax.ppermute(add(*quarter_of(enc, (x + 2) % NX)), ALL, AHEAD)
+    direct = lax.ppermute(add(*quarter_of(enc, back)), ALL, BACK)
+    onward = add(*quarter_of(enc, ahead), relayed)
+    passed = lax.ppermute(onward, ALL, AHEAD)
+    dec_moved = after(dec_moved, onward)
+    dec_piece = lax.optimization_barrier(add(*[dec_moved[n] for n in range(NX)]))
     enc_piece = lax.optimization_barrier(add(*quarter_of(enc, x), direct, passed))
-    enc_swapped = lax.ppermute(after(enc_piece, dec_swapped), "dp", Y_SWAP)
-
-    dec_pieces = gather_x(add(dec_piece, dec_swapped))
-    enc_swapped = after(enc_swapped, *dec_pieces[1:3])
-    enc_pieces = gather_x(add(enc_piece, enc_swapped), dec_pieces[3])
-    return dec_pieces, enc_pieces, jnp.stack([x, back, ahead, (x + 2) % NX]).astype(jnp.int32)
+
+    dec_sum = add(dec_piece, lax.ppermute(dec_piece, "dp", Y_SWAP))
+    enc_sum = add(enc_piece, lax.ppermute(enc_piece, "dp", Y_SWAP))
+    copies = jnp.broadcast_to(dec_sum[None], (NX,) + dec_sum.shape)
+    dec_whole = lax.all_to_all(copies, "dp", 0, 0, axis_index_groups=X_GROUPS)
+    order = jnp.stack([x, back, ahead, (x + 2) % NX]).astype(jnp.int32)
+    return dec_sum, dec_whole, gather_x(enc_sum), order
 
 
 def local(activations, enc_weight, enc_bias, dec_weight, dec_bias, thresholds, active_blocks):
@@ -293,21 +292,22 @@
         [room, pltpu.VMEM((DEC_BIAS_ROWS, TILE), F32)],
         work,
     )
-    dec_parts, res = lax.optimization_barrier((dec_parts, res))
-    packed = shape((NX, quarter + ENC_BIAS_ROWS, TILE))
-    enc_parts = call(
-        encoder_kernel,
-        [packed, packed],
-        (nears, *res, *act, dec_weight, dec_other, slope),
-        [room, room],
-        2 * work,
-    )
+    packed_enc = shape((NX, quarter + ENC_BIAS_ROWS, TILE))
+
+    def make_enc(*first):
+        return call(
+            encoder_kernel,
+            [packed_enc, packed_enc],
+            (nears, *after(res, *first), *act, dec_weight, dec_other, slope),
+            [room, room],
+            2 * work,
+        )
 
     x = lax.axis_index("dp") // 2
-    dec_pieces, enc_pieces, order = reduce_gradients(dec_parts, enc_parts, core, x)
-    (dec,) = call(place_dec_kernel, [shape((TILE, d))], (order, *dec_pieces))
+    dec_sum, dec_whole, enc_pieces, order = reduce_gradients(dec_parts, make_enc, core, x)
+    (dec,) = call(place_dec_kernel, [shape((TILE, d))], (dec_whole,))
     (enc,) = call(place_enc_kernel, [shape((d, TILE))], (order, *enc_pieces))
-    dec_bias_sum = dec_pieces[0][quarter : quarter + d // TILE].reshape(-1)
+    dec_bias_sum = dec_sum[quarter : quarter + d // TILE].reshape(-1)
     return enc, dec, enc_pieces[0][quarter], dec_bias_sum
 
 

time: 226 us -> 235 us (1.040)
  the two profiles are of different devices: /device:TPU:6 before, /device:TPU:8 now
where the time goes in v8:
time: 235 us; the launch traced here: 233 us
  starting transfers between devices  100 us (43%)
  waiting for transfers between devices  86.4 us (37%)
  blocking collectives  15.4 us (7%)
  other arithmetic  12.2 us (5%)
  Pallas kernels  11.9 us (5%)
  local copies, waits for them, and re-layouts  6.42 us (3%)
    all_to_all x2, starting transfers between devices, exchange(): return lax.all_to_all(parts, 'dict', 0, 0, axis_index_groups=groups(axes))  20.6 us
    all_to_all x1, blocking collectives, exchange(): return lax.all_to_all(parts, 'dict', 0, 0, axis_index_groups=groups(axes))  15.4 us
    ppermute x1, waiting for transfers between devices, reduce_gradients(): relayed = lax.ppermute(add(*quarter_of(enc, (x + 2) % NX)), ALL, AHEAD)  15 us
    ppermute x1, waiting for transfers between devices, gather_x(): behind = lax.ppermute(piece, ALL, AHEAD)  13.9 us
    ppermute x1, waiting for transfers between devices, reduce_gradients(): dec_sum = add(dec_piece, lax.ppermute(dec_piece, 'dp', Y_SWAP))  13 us
    pallas_call x5, Pallas kernels, call(): pl.pallas_call(kernel, out_shape=outs, in_specs=[scalars if a.dtype == jn...  11.9 us
    ppermute x2, waiting for transfers between devices, gather_near(): return (block, first, second, lax.ppermute(first, 'dict', NEAR_B))  11.3 us
    all_to_all x2, waiting for transfers between devices, exchange(): return lax.all_to_all(parts, 'dict', 0, 0, axis_index_groups=groups(axes))  9.89 us
  transfers between devices with their start and end apart: 26, of which 14 were waited for; matrix products, arithmetic and copies ran while one was open for 5% of the time, Pallas kernels for 2%

profile of v8, /device:TPU:8, one launch (start us, length us, event | category | flops | bytes accessed | tf_op | source)
XLA Modules:
  0.0 233.5 jit_solution(13757131059547183666)
XLA Ops:
  2.2 12.4 %all-to-all-start = ((bf16[16,72,128]{2,1,0:T(8,128)(2,1)}), bf16[16,72,128]{2,1,0:T(8,128)(2,1)S(1)}, u32[]{:S(2)}, u32[]{:S(2)}) async-start(bf16[16,72,128]{2,1,0:T(8,128)(2,1)} %bitcast.11), calls=%async_computation | async-start | bytes 589824 | tf_op jit(solution)/shard_map/all_to_all | solution.py:52
  14.7 2.3 collective-permute-start.5
  17.0 2.0 collective-permute-start.4
  20.4 2.3 collective-permute-start
  22.7 1.3 compare_reduce_fusion.1
  24.0 1.4 add_convert_fusion.8
  25.6 5.1 %collective-permute-start.1 = (bf16[8,144,128]{2,1,0:T(8,128)(2,1)S(1)}, bf16[8,144,128]{2,1,0:T(8,128)(2,1)S(1)}, u32[]{:S(2)}, u32[]{:S(2)}) collective-permute-start(bf16[8,144,128]{2,1,0:T(8,128)(2,1)S(1)} %bitcast.55), channel_id=1, source_target_pairs={{0,128},{8,24},{16,144},{24,8},{32,160},{40,56},{48,176},{56,40},{... | collective-permute-start | bytes 884744 | tf_op jit(solution)/shard_map/ppermute | solution.py:60
  30.8 3.2 %collective-permute-start.2 = (bf16[8,144,128]{2,1,0:T(8,128)(2,1)S(1)}, bf16[8,144,128]{2,1,0:T(8,128)(2,1)S(1)}, u32[]{:S(2)}, u32[]{:S(2)}) collective-permute-start(bf16[8,144,128]{2,1,0:T(8,128)(2,1)S(1)} %bitcast.56), channel_id=1, source_target_pairs={{0,16},{8,136},{16,0},{24,152},{32,48},{40,168},{48,32},{56,184},{... | collective-permute-start | bytes 884744 | tf_op jit(solution)/shard_map/ppermute | solution.py:61
  34.0 1.6 collective-permute-done.1.act_1
  35.6 3.8 %collective-permute-start.3 = (bf16[8,144,128]{2,1,0:T(8,128)(2,1)S(1)}, bf16[8,144,128]{2,1,0:T(8,128)(2,1)S(1)}, u32[]{:S(2)}, u32[]{:S(2)}) collective-permute-start(bf16[8,144,128]{2,1,0:T(8,128)(2,1)S(1)} %collective-permute-done.1.act_1), channel_id=1, source_target_pairs={{0,16},{8,136},{16,0},{24,152},{32,48},{40,168},{48,32},{56,184},{... | collective-permute-start | bytes 884744 | tf_op jit(solution)/shard_map/ppermute | solution.py:62
  39.6 4.6 %collective-permute-done.3.act_3 = bf16[8,144,128]{2,1,0:T(8,128)(2,1)S(1)} collective-permute-done((bf16[8,144,128]{2,1,0:T(8,128)(2,1)S(1)}, bf16[8,144,128]{2,1,0:T(8,128)(2,1)S(1)}, u32[]{:S(2)}, u32[]{:S(2)}) %collective-permute-start.3) | collective-permute-done | bytes 294944 | tf_op jit(solution)/shard_map/ppermute | solution.py:62
  45.2 1.3 copy-done.5
  46.5 3.4 %shard_map.102 = (bf16[8,144,128]{2,1,0:T(8,128)(2,1)S(1)}, bf16[8,144,128]{2,1,0:T(8,128)(2,1)S(1)}, bf16[8,144,128]{2,1,0:T(8,128)(2,1)S(1)}, bf16[8,144,128]{...) custom-call(s32[4]{0:T(128)S(1)} %pad_add_fusion.1.near_ref, ...), custom_call_target="tpu_custom_call" | custom-call | tf_op jit(solution)/shard_map/pallas_call | solution.py:184
  50.0 4.2 %collective-permute-start.7 = (bf16[8,144,128]{2,1,0:T(8,128)(2,1)S(1)}, bf16[8,144,128]{2,1,0:T(8,128)(2,1)S(1)}, u32[]{:S(2)}, u32[]{:S(2)}) collective-permute-start(bf16[8,144,128]{2,1,0:T(8,128)(2,1)S(1)} %get-tuple-element.31), channel_id=1, source_target_pairs={{0,128},{8,24},{16,144},{24,8},{32,160},{40,56},{48,176},{56,40},{... | collective-permute-start | bytes 884744 | tf_op jit(solution)/shard_map/ppermute | solution.py:66
  54.2 1.9 collective-permute-start.6
  56.1 2.8 %collective-permute-done.7 = bf16[8,144,128]{2,1,0:T(8,128)(2,1)S(1)} collective-permute-done((bf16[8,144,128]{2,1,0:T(8,128)(2,1)S(1)}, bf16[8,144,128]{2,1,0:T(8,128)(2,1)S(1)}, u32[]{:S(2)}, u32[]{:S(2)}) %collective-permute-start.7) | collective-permute-done | bytes 294944 | tf_op jit(solution)/shard_map/ppermute | solution.py:66
  58.9 3.8 %collective-permute-start.8 = (bf16[8,144,128]{2,1,0:T(8,128)(2,1)S(1)}, bf16[8,144,128]{2,1,0:T(8,128)(2,1)S(1)}, u32[]{:S(2)}, u32[]{:S(2)}) collective-permute-start(bf16[8,144,128]{2,1,0:T(8,128)(2,1)S(1)} %add_convert_fusion.7), channel_id=1, source_target_pairs={{0,16},{8,136},{16,0},{24,152},{32,48},{40,168},{48,32},{56,184},{... | collective-permute-start | bytes 884744 | tf_op jit(solution)/shard_map/ppermute | solution.py:68
  63.1 4.5 %collective-permute-done.8 = bf16[8,144,128]{2,1,0:T(8,128)(2,1)S(1)} collective-permute-done((bf16[8,144,128]{2,1,0:T(8,128)(2,1)S(1)}, bf16[8,144,128]{2,1,0:T(8,128)(2,1)S(1)}, u32[]{:S(2)}, u32[]{:S(2)}) %collective-permute-start.8) | collective-permute-done | bytes 294944 | tf_op jit(solution)/shard_map/ppermute | solution.py:68
  68.4 8.1 %all-to-all-start.1 = ((bf16[8,144,128]{2,1,0:T(8,128)(2,1)}), bf16[8,144,128]{2,1,0:T(8,128)(2,1)S(1)}, u32[]{:S(2)}, u32[]{:S(2)}) async-start(bf16[8,144,128]{2,1,0:T(8,128)(2,1)} %add_convert_fusion.6), calls=%async_computation.1 | async-start | bytes 589824 | tf_op jit(solution)/shard_map/all_to_all | solution.py:52
  77.3 9.9 %all-to-all-done.1 = bf16[8,144,128]{2,1,0:T(8,128)(2,1)S(1)} async-done(((bf16[8,144,128]{2,1,0:T(8,128)(2,1)}), bf16[8,144,128]{2,1,0:T(8,128)(2,1)S(1)}, u32[]{:S(2)}, u32[]{:S(2)}) %all-to-all-start.1) | async-done | bytes 294944 | tf_op jit(solution)/shard_map/all_to_all | solution.py:52
  87.4 15.4 %all_to_all.25.res_0 = bf16[8,144,128]{2,1,0:T(8,128)(2,1)S(1)} all-to-all(bf16[8,144,128]{2,1,0:T(8,128)(2,1)S(1)} %broadcast_in_dim.31), channel_id=1, replica_groups={{0,32,64,96,256,288,320,352},{8,40,72,104,264,296,328,360},{16,48,80,11..., dimensions={0} | all-to-all | bytes 589824 | tf_op jit(solution)/shard_map/all_to_all | solution.py:52
  102.7 4.5 %collective-permute-start.9 = (bf16[8,144,128]{2,1,0:T(8,128)(2,1)S(1)}, bf16[8,144,128]{2,1,0:T(8,128)(2,1)S(1)}, u32[]{:S(2)}, u32[]{:S(2)}) collective-permute-start(bf16[8,144,128]{2,1,0:T(8,128)(2,1)S(1)} %all_to_all.25.res_0), channel_id=1, source_target_pairs={{0,128},{8,24},{16,144},{24,8},{32,160},{40,56},{48,176},{56,40},{... | collective-permute-start | bytes 884744 | tf_op jit(solution)/shard_map/ppermute | solution.py:60
  107.2 2.8 %collective-permute-start.10 = (bf16[8,144,128]{2,1,0:T(8,128)(2,1)S(1)}, bf16[8,144,128]{2,1,0:T(8,128)(2,1)S(1)}, u32[]{:S(2)}, u32[]{:S(2)}) collective-permute-start(bf16[8,144,128]{2,1,0:T(8,128)(2,1)S(1)} %all_to_all.25.res_0), channel_id=1, source_target_pairs={{0,16},{8,136},{16,0},{24,152},{32,48},{40,168},{48,32},{56,184},{... | collective-permute-start | bytes 884744 | tf_op jit(solution)/shard_map/ppermute | solution.py:61
  110.0 4.6 %collective-permute-done.9.res_1 = bf16[8,144,128]{2,1,0:T(8,128)(2,1)S(1)} collective-permute-done((bf16[8,144,128]{2,1,0:T(8,128)(2,1)S(1)}, bf16[8,144,128]{2,1,0:T(8,128)(2,1)S(1)}, u32[]{:S(2)}, u32[]{:S(2)}) %collective-permute-start.9) | collective-permute-done | bytes 294944 | tf_op jit(solution)/shard_map/ppermute | solution.py:60
  114.6 1.9 collective-permute-start.11
  116.5 6.7 %collective-permute-done.11.res_3 = bf16[8,144,128]{2,1,0:T(8,128)(2,1)S(1)} collective-permute-done((bf16[8,144,128]{2,1,0:T(8,128)(2,1)S(1)}, bf16[8,144,128]{2,1,0:T(8,128)(2,1)S(1)}, u32[]{:S(2)}, u32[]{:S(2)}) %collective-permute-start.11) | collective-permute-done | bytes 294944 | tf_op jit(solution)/shard_map/ppermute | solution.py:62
  123.2 2.1 shard_map.103
  125.3 1.9 collective-permute-start.12
  127.3 3.5 %shard_map.104 = (bf16[4,1168,128]{2,1,0:T(8,128)(2,1)S(1)}, bf16[4,1168,128]{2,1,0:T(8,128)(2,1)}) custom-call(s32[4]{0:T(128)S(1)} %pad_add_fusion.1.near_ref, bf16[8,144,128]{2,1,0:T(8,128)(2,1)S(1)} %all_to_all.25.res_0, bf16[8,144,128]{2,1,0:T(8,128)(2,1)S(1)} %collective-permute-done.9.res_1, bf16[8,144,128]{2,1,0:T(8,128)(2,1)S(1)} %collective-permute-done.10.res_2, ...), custom_call_target="tpu_custom_call" | custom-call | tf_op jit(solution)/shard_map/pallas_call | solution.py:184
  130.7 1.4 add_convert_fusion
  132.2 2.4 %collective-permute-start.13 = (bf16[4,1168,128]{2,1,0:T(8,128)(2,1)}, bf16[4,1168,128]{2,1,0:T(8,128)(2,1)}, u32[]{:S(2)}, u32[]{:S(2)}) collective-permute-start(bf16[4,1168,128]{2,1,0:T(8,128)(2,1)} %get-tuple-element.42), channel_id=1, source_target_pairs={{0,8},{8,0},{16,24},{24,16},{32,40},{40,32},{48,56},{56,48},{64,72... | collective-permute-start | bytes 3588104 | tf_op jit(solution)/shard_map/ppermute | solution.py:219
  134.6 4.4 %all-to-all-start.3 = ((bf16[4,1200,128]{2,1,0:T(8,128)(2,1)}), bf16[4,1200,128]{2,1,0:T(8,128)(2,1)S(1)}, u32[]{:S(2)}, u32[]{:S(2)}) async-start(bf16[4,1200,128]{2,1,0:T(8,128)(2,1)} %add_convert_fusion), calls=%async_computation.3 | async-start | bytes 2457600 | tf_op jit(solution)/shard_map/all_to_all | solution.py:217
  140.3 3.9 %collective-permute-start.15 = (bf16[1168,128]{1,0:T(8,128)(2,1)S(1)}, bf16[1168,128]{1,0:T(8,128)(2,1)}, u32[]{:S(2)}, u32[]{:S(2)}) collective-permute-start(bf16[1168,128]{1,0:T(8,128)(2,1)S(1)} %get-tuple-element.47), channel_id=1, source_target_pairs={{0,2},{1,3},{2,4},{3,5},{4,6},{5,7},{6,0},{7,1},{8,14},{9,15},{10,... | collective-permute-start | bytes 897032 | tf_op jit(solution)/shard_map/ppermute | solution.py:220
  144.3 3.2 %collective-permute-start.14 = (bf16[1168,128]{1,0:T(8,128)(2,1)S(1)}, bf16[1168,128]{1,0:T(8,128)(2,1)}, u32[]{:S(2)}, u32[]{:S(2)}) collective-permute-start(bf16[1168,128]{1,0:T(8,128)(2,1)S(1)} %get-tuple-element.46), channel_id=1, source_target_pairs={{0,6},{1,7},{2,0},{3,1},{4,2},{5,3},{6,4},{7,5},{8,10},{9,11},{10,... | collective-permute-start | bytes 897032 | tf_op jit(solution)/shard_map/ppermute | solution.py:221
  147.4 15.0 %collective-permute-done.15 = bf16[1168,128]{1,0:T(8,128)(2,1)} collective-permute-done((bf16[1168,128]{1,0:T(8,128)(2,1)S(1)}, bf16[1168,128]{1,0:T(8,128)(2,1)}, u32[]{:S(2)}, u32[]{:S(2)}) %collective-permute-start.15) | collective-permute-done | bytes 299040 | tf_op jit(solution)/shard_map/ppermute | solution.py:220
  162.4 1.9 fusion
  164.3 1.9 collective-permute-start.16
  166.4 5.7 %collective-permute-start.21 = (bf16[1200,128]{1,0:T(8,128)(2,1)S(1)}, bf16[1200,128]{1,0:T(8,128)(2,1)S(1)}, u32[]{:S(2)}, u32[]{:S(2)}) collective-permute-start(bf16[1200,128]{1,0:T(8,128)(2,1)S(1)} %fusion.3), channel_id=1, source_target_pairs={{0,1},{1,0},{2,3},{3,2},{4,5},{5,4},{6,7},{7,6},{8,9},{9,8},{10,11... | collective-permute-start | bytes 921608 | tf_op jit(solution)/shard_map/ppermute | solution.py:228
  172.1 2.3 collective-permute-done.16
  175.6 5.7 %collective-permute-start.17 = (bf16[1168,128]{1,0:T(8,128)(2,1)S(1)}, bf16[1168,128]{1,0:T(8,128)(2,1)S(1)}, u32[]{:S(2)}, u32[]{:S(2)}) collective-permute-start(bf16[1168,128]{1,0:T(8,128)(2,1)S(1)} %fusion.2), channel_id=1, source_target_pairs={{0,1},{1,0},{2,3},{3,2},{4,5},{5,4},{6,7},{7,6},{8,9},{9,8},{10,11... | collective-permute-start | bytes 897032 | tf_op jit(solution)/shard_map/ppermute | solution.py:229
  181.3 13.0 %collective-permute-done.21 = bf16[1200,128]{1,0:T(8,128)(2,1)S(1)} collective-permute-done((bf16[1200,128]{1,0:T(8,128)(2,1)S(1)}, bf16[1200,128]{1,0:T(8,128)(2,1)S(1)}, u32[]{:S(2)}, u32[]{:S(2)}) %collective-permute-start.21) | collective-permute-done | bytes 307232 | tf_op jit(solution)/shard_map/ppermute | solution.py:228
  195.6 3.5 %all-to-all-start.4 = ((bf16[4,1200,128]{2,1,0:T(8,128)(2,1)}), bf16[4,1200,128]{2,1,0:T(8,128)(2,1)S(1)}, u32[]{:S(2)}, u32[]{:S(2)}) async-start(bf16[4,1200,128]{2,1,0:T(8,128)(2,1)} %broadcast_in_dim.32), calls=%async_computation.4 | async-start | bytes 2457600 | tf_op jit(solution)/shard_map/all_to_all | solution.py:231
  199.7 3.4 %collective-permute-start.18 = (bf16[1168,128]{1,0:T(8,128)(2,1)S(1)}, bf16[1168,128]{1,0:T(8,128)(2,1)S(1)}, u32[]{:S(2)}, u32[]{:S(2)}) collective-permute-start(bf16[1168,128]{1,0:T(8,128)(2,1)S(1)} %add_convert_fusion.3.refs_0_), channel_id=1, source_target_pairs={{0,2},{1,3},{2,4},{3,5},{4,6},{5,7},{6,0},{7,1},{8,14},{9,15},{10,... | collective-permute-start | bytes 897032 | tf_op jit(solution)/shard_map/ppermute | solution.py:204
  203.2 3.7 %collective-permute-start.19 = (bf16[1168,128]{1,0:T(8,128)(2,1)S(1)}, bf16[1168,128]{1,0:T(8,128)(2,1)S(1)}, u32[]{:S(2)}, u32[]{:S(2)}) collective-permute-start(bf16[1168,128]{1,0:T(8,128)(2,1)S(1)} %add_convert_fusion.3.refs_0_), channel_id=1, source_target_pairs={{0,6},{1,7},{2,0},{3,1},{4,2},{5,3},{6,4},{7,5},{8,10},{9,11},{10,... | collective-permute-start | bytes 897032 | tf_op jit(solution)/shard_map/ppermute | solution.py:205
  206.9 13.9 %collective-permute-done.18.refs_1_ = bf16[1168,128]{1,0:T(8,128)(2,1)S(1)} collective-permute-done((bf16[1168,128]{1,0:T(8,128)(2,1)S(1)}, bf16[1168,128]{1,0:T(8,128)(2,1)S(1)}, u32[]{:S(2)}, u32[]{:S(2)}) %collective-permute-start.18) | collective-permute-done | bytes 299040 | tf_op jit(solution)/shard_map/ppermute | solution.py:204
  220.7 1.9 collective-permute-start.20
  223.8 6.8 %collective-permute-done.20.refs_3_ = bf16[1168,128]{1,0:T(8,128)(2,1)S(1)} collective-permute-done((bf16[1168,128]{1,0:T(8,128)(2,1)S(1)}, bf16[1168,128]{1,0:T(8,128)(2,1)S(1)}, u32[]{:S(2)}, u32[]{:S(2)}) %collective-permute-start.20) | collective-permute-done | bytes 299040 | tf_op jit(solution)/shard_map/ppermute | solution.py:206
  230.6 1.6 shard_map.105
  (60 shorter events, 13.4 us)
Async XLA Ops:
  0.6 44.6 %copy-start = (bf16[128,4608]{1,0:T(8,128)(2,1)S(1)}, bf16[128,4608]{1,0:T(8,128)(2,1)}, u32[]{:S(2)}) copy-start(bf16[128,4608]{1,0:T(8,128)(2,1)} %wd_own.3) | copy-start | bytes 3538948
  2.2 23.4 %all-to-all-start = ((bf16[16,72,128]{2,1,0:T(8,128)(2,1)}), bf16[16,72,128]{2,1,0:T(8,128)(2,1)S(1)}, u32[]{:S(2)}, u32[]{:S(2)}) async-start(bf16[16,72,128]{2,1,0:T(8,128)(2,1)} %bitcast.11), calls=%async_computation | async-start | bytes 589824 | tf_op jit(solution)/shard_map/all_to_all | solution.py:52
  14.7 29.5 %collective-permute-start.5 = (bf16[128,4608]{1,0:T(8,128)(2,1)}, bf16[128,4608]{1,0:T(8,128)(2,1)S(1)}, u32[]{:S(2)}, u32[]{:S(2)}) collective-permute-start(bf16[128,4608]{1,0:T(8,128)(2,1)} %wd_own.3), channel_id=1, source_target_pairs={{0,8},{8,0},{16,24},{24,16},{32,40},{40,32},{48,56},{56,48},{64,72... | collective-permute-start | bytes 3538952 | tf_op jit(solution)/shard_map/ppermute | solution.py:256
  17.0 27.2 %collective-permute-start.4 = (bf16[4608,128]{1,0:T(8,128)(2,1)}, bf16[4608,128]{1,0:T(8,128)(2,1)}, u32[]{:S(2)}, u32[]{:S(2)}) collective-permute-start(bf16[4608,128]{1,0:T(8,128)(2,1)} %we_own.1), channel_id=1, source_target_pairs={{0,8},{8,0},{16,24},{24,16},{32,40},{40,32},{48,56},{56,48},{64,72... | collective-permute-start | bytes 3538952 | tf_op jit(solution)/shard_map/ppermute | solution.py:255
  20.4 5.1 %collective-permute-start = (f32[2,128]{1,0:T(2,128)S(1)}, f32[2,128]{1,0:T(2,128)S(1)}, u32[]{:S(2)}, u32[]{:S(2)}) collective-permute-start(f32[2,128]{1,0:T(2,128)S(1)} %pad_maximum_fusion.1), channel_id=1, source_target_pairs={{0,8},{8,0},{16,24},{24,16},{32,40},{40,32},{48,56},{56,48},{64,72... | collective-permute-start | bytes 3080 | tf_op jit(solution)/shard_map/ppermute | solution.py:258
  25.6 10.0 %collective-permute-start.1 = (bf16[8,144,128]{2,1,0:T(8,128)(2,1)S(1)}, bf16[8,144,128]{2,1,0:T(8,128)(2,1)S(1)}, u32[]{:S(2)}, u32[]{:S(2)}) collective-permute-start(bf16[8,144,128]{2,1,0:T(8,128)(2,1)S(1)} %bitcast.55), channel_id=1, source_target_pairs={{0,128},{8,24},{16,144},{24,8},{32,160},{40,56},{48,176},{56,40},{... | collective-permute-start | bytes 884744 | tf_op jit(solution)/shard_map/ppermute | solution.py:60
  30.8 8.8 %collective-permute-start.2 = (bf16[8,144,128]{2,1,0:T(8,128)(2,1)S(1)}, bf16[8,144,128]{2,1,0:T(8,128)(2,1)S(1)}, u32[]{:S(2)}, u32[]{:S(2)}) collective-permute-start(bf16[8,144,128]{2,1,0:T(8,128)(2,1)S(1)} %bitcast.56), channel_id=1, source_target_pairs={{0,16},{8,136},{16,0},{24,152},{32,48},{40,168},{48,32},{56,184},{... | collective-permute-start | bytes 884744 | tf_op jit(solution)/shard_map/ppermute | solution.py:61
  35.6 8.6 %collective-permute-start.3 = (bf16[8,144,128]{2,1,0:T(8,128)(2,1)S(1)}, bf16[8,144,128]{2,1,0:T(8,128)(2,1)S(1)}, u32[]{:S(2)}, u32[]{:S(2)}) collective-permute-start(bf16[8,144,128]{2,1,0:T(8,128)(2,1)S(1)} %collective-permute-done.1.act_1), channel_id=1, source_target_pairs={{0,16},{8,136},{16,0},{24,152},{32,48},{40,168},{48,32},{56,184},{... | collective-permute-start | bytes 884744 | tf_op jit(solution)/shard_map/ppermute | solution.py:62
  44.2 1.0 copy-start.1
  45.2 1.3 copy-start.5
  49.9 9.0 %copy-start.6 = (f32[256,128]{1,0:T(8,128)}, f32[256,128]{1,0:T(8,128)S(1)}, u32[]{:S(2)}) copy-start(f32[256,128]{1,0:T(8,128)S(1)} %get-tuple-element.38.slope_ref) | copy-start | bytes 393220
  49.9 12.8 %copy-start.8 = (bf16[128,256]{1,0:T(8,128)(2,1)}, bf16[128,256]{1,0:T(8,128)(2,1)S(1)}, u32[]{:S(2)}) copy-start(bf16[128,256]{1,0:T(8,128)(2,1)S(1)} %get-tuple-element.32.feat_ref) | copy-start | bytes 196612
  50.0 8.9 %collective-permute-start.7 = (bf16[8,144,128]{2,1,0:T(8,128)(2,1)S(1)}, bf16[8,144,128]{2,1,0:T(8,128)(2,1)S(1)}, u32[]{:S(2)}, u32[]{:S(2)}) collective-permute-start(bf16[8,144,128]{2,1,0:T(8,128)(2,1)S(1)} %get-tuple-element.31), channel_id=1, source_target_pairs={{0,128},{8,24},{16,144},{24,8},{32,160},{40,56},{48,176},{56,40},{... | collective-permute-start | bytes 884744 | tf_op jit(solution)/shard_map/ppermute | solution.py:66
  54.2 8.9 %collective-permute-start.6 = (bf16[8,144,128]{2,1,0:T(8,128)(2,1)S(1)}, bf16[8,144,128]{2,1,0:T(8,128)(2,1)S(1)}, u32[]{:S(2)}, u32[]{:S(2)}) collective-permute-start(bf16[8,144,128]{2,1,0:T(8,128)(2,1)S(1)} %get-tuple-element.29), channel_id=1, source_target_pairs={{0,128},{8,24},{16,144},{24,8},{32,160},{40,56},{48,176},{56,40},{... | collective-permute-start | bytes 884744 | tf_op jit(solution)/shard_map/ppermute | solution.py:67
  58.9 8.6 %collective-permute-start.8 = (bf16[8,144,128]{2,1,0:T(8,128)(2,1)S(1)}, bf16[8,144,128]{2,1,0:T(8,128)(2,1)S(1)}, u32[]{:S(2)}, u32[]{:S(2)}) collective-permute-start(bf16[8,144,128]{2,1,0:T(8,128)(2,1)S(1)} %add_convert_fusion.7), channel_id=1, source_target_pairs={{0,16},{8,136},{16,0},{24,152},{32,48},{40,168},{48,32},{56,184},{... | collective-permute-start | bytes 884744 | tf_op jit(solution)/shard_map/ppermute | solution.py:68
  68.4 54.8 %copy-start.9 = (bf16[128,256]{1,0:T(8,128)(2,1)S(1)}, bf16[128,256]{1,0:T(8,128)(2,1)}, u32[]{:S(2)}) copy-start(bf16[128,256]{1,0:T(8,128)(2,1)} %copy-done.8) | copy-start | bytes 196612
  68.4 18.8 %all-to-all-start.1 = ((bf16[8,144,128]{2,1,0:T(8,128)(2,1)}), bf16[8,144,128]{2,1,0:T(8,128)(2,1)S(1)}, u32[]{:S(2)}, u32[]{:S(2)}) async-start(bf16[8,144,128]{2,1,0:T(8,128)(2,1)} %add_convert_fusion.6), calls=%async_computation.1 | async-start | bytes 589824 | tf_op jit(solution)/shard_map/all_to_all | solution.py:52
  87.2 40.1 %copy-start.2 = (bf16[128,4608]{1,0:T(8,128)(2,1)S(1)}, bf16[128,4608]{1,0:T(8,128)(2,1)}, u32[]{:S(2)}) copy-start(bf16[128,4608]{1,0:T(8,128)(2,1)} %copy-done.1) | copy-start | bytes 3538948
  87.2 40.0 %copy-start.7 = (f32[256,128]{1,0:T(8,128)S(1)}, f32[256,128]{1,0:T(8,128)}, u32[]{:S(2)}) copy-start(f32[256,128]{1,0:T(8,128)} %copy-done.6) | copy-start | bytes 393220
  102.7 11.9 %collective-permute-start.9 = (bf16[8,144,128]{2,1,0:T(8,128)(2,1)S(1)}, bf16[8,144,128]{2,1,0:T(8,128)(2,1)S(1)}, u32[]{:S(2)}, u32[]{:S(2)}) collective-permute-start(bf16[8,144,128]{2,1,0:T(8,128)(2,1)S(1)} %all_to_all.25.res_0), channel_id=1, source_target_pairs={{0,128},{8,24},{16,144},{24,8},{32,160},{40,56},{48,176},{56,40},{... | collective-permute-start | bytes 884744 | tf_op jit(solution)/shard_map/ppermute | solution.py:60
  107.2 9.3 %collective-permute-start.10 = (bf16[8,144,128]{2,1,0:T(8,128)(2,1)S(1)}, bf16[8,144,128]{2,1,0:T(8,128)(2,1)S(1)}, u32[]{:S(2)}, u32[]{:S(2)}) collective-permute-start(bf16[8,144,128]{2,1,0:T(8,128)(2,1)S(1)} %all_to_all.25.res_0), channel_id=1, source_target_pairs={{0,16},{8,136},{16,0},{24,152},{32,48},{40,168},{48,32},{56,184},{... | collective-permute-start | bytes 884744 | tf_op jit(solution)/shard_map/ppermute | solution.py:61
  114.6 8.6 %collective-permute-start.11 = (bf16[8,144,128]{2,1,0:T(8,128)(2,1)S(1)}, bf16[8,144,128]{2,1,0:T(8,128)(2,1)S(1)}, u32[]{:S(2)}, u32[]{:S(2)}) collective-permute-start(bf16[8,144,128]{2,1,0:T(8,128)(2,1)S(1)} %collective-permute-done.9.res_1), channel_id=1, source_target_pairs={{0,16},{8,136},{16,0},{24,152},{32,48},{40,168},{48,32},{56,184},{... | collective-permute-start | bytes 884744 | tf_op jit(solution)/shard_map/ppermute | solution.py:62
  125.3 5.4 %collective-permute-start.12 = (bf16[4,1200,128]{2,1,0:T(8,128)(2,1)S(1)}, bf16[4,1200,128]{2,1,0:T(8,128)(2,1)S(1)}, u32[]{:S(2)}, u32[]{:S(2)}) collective-permute-start(bf16[4,1200,128]{2,1,0:T(8,128)(2,1)S(1)} %get-tuple-element.41), channel_id=1, source_target_pairs={{0,8},{8,0},{16,24},{24,16},{32,40},{40,32},{48,56},{56,48},{64,72... | collective-permute-start | bytes 3686408 | tf_op jit(solution)/shard_map/ppermute | solution.py:215
  130.7 1.4 copy-start.3
  132.2 6.9 %collective-permute-start.13 = (bf16[4,1168,128]{2,1,0:T(8,128)(2,1)}, bf16[4,1168,128]{2,1,0:T(8,128)(2,1)}, u32[]{:S(2)}, u32[]{:S(2)}) collective-permute-start(bf16[4,1168,128]{2,1,0:T(8,128)(2,1)} %get-tuple-element.42), channel_id=1, source_target_pairs={{0,8},{8,0},{16,24},{24,16},{32,40},{40,32},{48,56},{56,48},{64,72... | collective-permute-start | bytes 3588104 | tf_op jit(solution)/shard_map/ppermute | solution.py:219
  134.6 4.5 %copy-start.4 = (bf16[4,1168,128]{2,1,0:T(8,128)(2,1)S(1)}, bf16[4,1168,128]{2,1,0:T(8,128)(2,1)}, u32[]{:S(2)}) copy-start(bf16[4,1168,128]{2,1,0:T(8,128)(2,1)} %copy-done.3) | copy-start | bytes 3588100
  134.6 31.6 %all-to-all-start.3 = ((bf16[4,1200,128]{2,1,0:T(8,128)(2,1)}), bf16[4,1200,128]{2,1,0:T(8,128)(2,1)S(1)}, u32[]{:S(2)}, u32[]{:S(2)}) async-start(bf16[4,1200,128]{2,1,0:T(8,128)(2,1)} %add_convert_fusion), calls=%async_computation.3 | async-start | bytes 2457600 | tf_op jit(solution)/shard_map/all_to_all | solution.py:217
  140.3 22.1 %collective-permute-start.15 = (bf16[1168,128]{1,0:T(8,128)(2,1)S(1)}, bf16[1168,128]{1,0:T(8,128)(2,1)}, u32[]{:S(2)}, u32[]{:S(2)}) collective-permute-start(bf16[1168,128]{1,0:T(8,128)(2,1)S(1)} %get-tuple-element.47), channel_id=1, source_target_pairs={{0,2},{1,3},{2,4},{3,5},{4,6},{5,7},{6,0},{7,1},{8,14},{9,15},{10,... | collective-permute-start | bytes 897032 | tf_op jit(solution)/shard_map/ppermute | solution.py:220
  144.3 27.8 %collective-permute-start.14 = (bf16[1168,128]{1,0:T(8,128)(2,1)S(1)}, bf16[1168,128]{1,0:T(8,128)(2,1)}, u32[]{:S(2)}, u32[]{:S(2)}) collective-permute-start(bf16[1168,128]{1,0:T(8,128)(2,1)S(1)} %get-tuple-element.46), channel_id=1, source_target_pairs={{0,6},{1,7},{2,0},{3,1},{4,2},{5,3},{6,4},{7,5},{8,10},{9,11},{10,... | collective-permute-start | bytes 897032 | tf_op jit(solution)/shard_map/ppermute | solution.py:221
  164.3 10.1 %collective-permute-start.16 = (bf16[1168,128]{1,0:T(8,128)(2,1)}, bf16[1168,128]{1,0:T(8,128)(2,1)S(1)}, u32[]{:S(2)}, u32[]{:S(2)}) collective-permute-start(bf16[1168,128]{1,0:T(8,128)(2,1)} %fusion), channel_id=1, source_target_pairs={{0,2},{1,3},{2,4},{3,5},{4,6},{5,7},{6,0},{7,1},{8,14},{9,15},{10,... | collective-permute-start | bytes 897032 | tf_op jit(solution)/shard_map/ppermute | solution.py:223
  166.4 27.8 %collective-permute-start.21 = (bf16[1200,128]{1,0:T(8,128)(2,1)S(1)}, bf16[1200,128]{1,0:T(8,128)(2,1)S(1)}, u32[]{:S(2)}, u32[]{:S(2)}) collective-permute-start(bf16[1200,128]{1,0:T(8,128)(2,1)S(1)} %fusion.3), channel_id=1, source_target_pairs={{0,1},{1,0},{2,3},{3,2},{4,5},{5,4},{6,7},{7,6},{8,9},{9,8},{10,11... | collective-permute-start | bytes 921608 | tf_op jit(solution)/shard_map/ppermute | solution.py:228
  175.6 24.0 %collective-permute-start.17 = (bf16[1168,128]{1,0:T(8,128)(2,1)S(1)}, bf16[1168,128]{1,0:T(8,128)(2,1)S(1)}, u32[]{:S(2)}, u32[]{:S(2)}) collective-permute-start(bf16[1168,128]{1,0:T(8,128)(2,1)S(1)} %fusion.2), channel_id=1, source_target_pairs={{0,1},{1,0},{2,3},{3,2},{4,5},{5,4},{6,7},{7,6},{8,9},{9,8},{10,11... | collective-permute-start | bytes 897032 | tf_op jit(solution)/shard_map/ppermute | solution.py:229
  195.6 36.7 %all-to-all-start.4 = ((bf16[4,1200,128]{2,1,0:T(8,128)(2,1)}), bf16[4,1200,128]{2,1,0:T(8,128)(2,1)S(1)}, u32[]{:S(2)}, u32[]{:S(2)}) async-start(bf16[4,1200,128]{2,1,0:T(8,128)(2,1)} %broadcast_in_dim.32), calls=%async_computation.4 | async-start | bytes 2457600 | tf_op jit(solution)/shard_map/all_to_all | solution.py:231
  199.7 21.0 %collective-permute-start.18 = (bf16[1168,128]{1,0:T(8,128)(2,1)S(1)}, bf16[1168,128]{1,0:T(8,128)(2,1)S(1)}, u32[]{:S(2)}, u32[]{:S(2)}) collective-permute-start(bf16[1168,128]{1,0:T(8,128)(2,1)S(1)} %add_convert_fusion.3.refs_0_), channel_id=1, source_target_pairs={{0,2},{1,3},{2,4},{3,5},{4,6},{5,7},{6,0},{7,1},{8,14},{9,15},{10,... | collective-permute-start | bytes 897032 | tf_op jit(solution)/shard_map/ppermute | solution.py:204
  203.2 20.6 %collective-permute-start.19 = (bf16[1168,128]{1,0:T(8,128)(2,1)S(1)}, bf16[1168,128]{1,0:T(8,128)(2,1)S(1)}, u32[]{:S(2)}, u32[]{:S(2)}) collective-permute-start(bf16[1168,128]{1,0:T(8,128)(2,1)S(1)} %add_convert_fusion.3.refs_0_), channel_id=1, source_target_pairs={{0,6},{1,7},{2,0},{3,1},{4,2},{5,3},{6,4},{7,5},{8,10},{9,11},{10,... | collective-permute-start | bytes 897032 | tf_op jit(solution)/shard_map/ppermute | solution.py:205
  220.7 9.9 %collective-permute-start.20 = (bf16[1168,128]{1,0:T(8,128)(2,1)S(1)}, bf16[1168,128]{1,0:T(8,128)(2,1)S(1)}, u32[]{:S(2)}, u32[]{:S(2)}) collective-permute-start(bf16[1168,128]{1,0:T(8,128)(2,1)S(1)} %collective-permute-done.18.refs_1_), channel_id=1, source_target_pairs={{0,2},{1,3},{2,4},{3,5},{4,6},{5,7},{6,0},{7,1},{8,14},{9,15},{10,... | collective-permute-start | bytes 897032 | tf_op jit(solution)/shard_map/ppermute | solution.py:206

commit v9 on v6

--- a/solution.py
+++ b/solution.py
@@ -73,12 +73,24 @@
     return lax.dot_general(a, b, (dims, ((), ())), preferred_element_type=F32)
 
 
+def load(refs, rooms, sems):
+    copies = [
+        pltpu.make_async_copy(ref, room, sems.at[n]) for n, (ref, room) in enumerate(zip(refs, rooms))
+    ]
+    for copy in copies:
+        copy.start()
+    return copies
+
+
 def forward_kernel(
-    act_ref, we_own, we_other, wd_own, wd_other, row_ref, parts_ref, feat_ref, slope_ref, act
+    act_ref, we_own, we_other, wd_own, wd_other, row_ref, parts_ref, feat_ref, slope_ref, act,
+    we_0, we_1, wd_0, wd_1, sems,
 ):
+    loads = load((we_own, we_other, wd_own, wd_other), (we_0, we_1, wd_0, wd_1), sems)
     in_order(act_ref, act)
     act_t = act[...].T
-    for n, we in enumerate((we_own, we_other)):
+    for n, we in enumerate((we_0, we_1)):
+        loads[n].wait()
         lanes = slice(n * TILE, (n + 1) * TILE)
         bias, theta, live = row_ref[0:1, lanes], row_ref[1:2, lanes], row_ref[2:3, lanes]
         pre = dot(act_t, we[...], ((1,), (0,))) + bias
@@ -88,10 +100,12 @@
     cols = parts_ref.shape[2]
     step = 8 * cols
     place = {chip: (near, far) for near, far, chip in chip_blocks()}
+    loads[2].wait()
+    loads[3].wait()
     for first in range(0, act.shape[0], step):
         span = slice(first, first + step)
-        total = dot(feat_ref[:, :TILE], wd_own[:, span], ((1,), (0,)))
-        total = total + dot(feat_ref[:, TILE:], wd_other[:, span], ((1,), (0,)))
+        total = dot(feat_ref[:, :TILE], wd_0[:, span], ((1,), (0,)))
+        total = total + dot(feat_ref[:, TILE:], wd_1[:, span], ((1,), (0,)))
         turned = total.astype(BF16).T
         for i in range(8):
             near, far = place[first // cols + i]
@@ -119,12 +133,14 @@
 
 
 def encoder_kernel(
-    res_ref, act_ref, wd_own, wd_other, slope_ref, own_ref, other_ref, act, res
+    res_ref, act_ref, wd_own, wd_other, slope_ref, own_ref, other_ref, act, res, wd_0, wd_1, sems
 ):
+    loads = load((wd_own, wd_other), (wd_0, wd_1), sems)
     in_order(act_ref, act)
     in_order(res_ref, res)
     quarter = act.shape[0] // NX
-    for n, (wd, out) in enumerate(((wd_own, own_ref), (wd_other, other_ref))):
+    for n, (wd, out) in enumerate(((wd_0, own_ref), (wd_1, other_ref))):
+        loads[n].wait()
         dfeat = dot(wd[...], res[...], ((1,), (0,)))
         dpre = (dfeat * slope_ref[n * TILE : (n + 1) * TILE, :]).T
         row = jnp.sum(dpre, axis=0, keepdims=True)
@@ -154,15 +170,19 @@
         enc_ref[pl.ds(row, quarter), :] = ref[:quarter, :]
 
 
-def call(kernel, outs, args, scratch=(), flops=0):
+def call(kernel, outs, args, scratch=(), flops=0, unloaded=()):
     whole = pl.BlockSpec(memory_space=pltpu.VMEM)
     scalars = pl.BlockSpec(memory_space=pltpu.SMEM)
+    left = pl.BlockSpec(memory_space=pl.ANY)
     moved = sum(a.size * a.dtype.itemsize for a in args)
     moved += sum(math.prod(s.shape) * s.dtype.itemsize for s in outs)
     return pl.pallas_call(
         kernel,
         out_shape=outs,
-        in_specs=[scalars if a.dtype == jnp.int32 else whole for a in args],
+        in_specs=[
+            scalars if a.dtype == jnp.int32 else left if n in unloaded else whole
+            for n, a in enumerate(args)
+        ],
         out_specs=[whole] * len(outs),
         scratch_shapes=list(scratch),
         compiler_params=pltpu.CompilerParams(vmem_limit_bytes=VMEM),
@@ -229,8 +249,14 @@
             shape((2 * TILE, TILE), F32),
         ],
         (act, enc_weight, enc_other, dec_weight, dec_other, rows),
-        [pltpu.VMEM((d, TILE), BF16)],
+        [
+            pltpu.VMEM((d, TILE), BF16),
+            *[pltpu.VMEM((d, TILE), BF16)] * 2,
+            *[pltpu.VMEM((TILE, d), BF16)] * 2,
+            pltpu.SemaphoreType.DMA((4,)),
+        ],
         2 * work,
+        (1, 2, 3, 4),
     )
 
     near_sum = jnp.sum(exchange(parts, NEAR).astype(F32), axis=0).astype(BF16)
@@ -255,8 +281,9 @@
         encoder_kernel,
         [packed, packed],
         (res, act, dec_weight, dec_other, slope),
-        [room, room],
+        [room, room, *[pltpu.VMEM((TILE, d), BF16)] * 2, pltpu.SemaphoreType.DMA((2,))],
         2 * work,
+        (2, 3),
     )
 
     x = lax.axis_index("dp") // 2

time: 222 us -> 223 us (level)
  no operation moved by 1% of the time
where the time goes in v9:
time: 223 us; the launch traced here: 221 us
  blocking collectives  79 us (35%)
  starting transfers between devices  69.7 us (31%)
  waiting for transfers between devices  37.8 us (17%)
  other arithmetic  13.4 us (6%)
  Pallas kernels  11.4 us (5%)
  local copies, waits for them, and re-layouts  8.19 us (4%)
    all_to_all x4, blocking collectives, exchange(): return lax.all_to_all(parts, 'dict', 0, 0, axis_index_groups=groups(axes))  79 us
    all_to_all x2, waiting for transfers between devices, exchange(): return lax.all_to_all(parts, 'dict', 0, 0, axis_index_groups=groups(axes))  16.9 us
    ppermute x1, waiting for transfers between devices, local(): dec_piece = add(dec_piece, lax.ppermute(dec_piece, 'dp', Y_SWAP))  14.9 us
    pallas_call x5, Pallas kernels, call(): pl.pallas_call(kernel, out_shape=outs, in_specs=[scalars if a.dtype == jn...  11.4 us
    ppermute x2, starting transfers between devices, gather_x(): return (piece, behind, ahead, lax.ppermute(behind, ALL, AHEAD))  10.3 us
    ppermute x2, starting transfers between devices, gather_x(): behind = lax.ppermute(piece, ALL, AHEAD)  8.67 us
    convert_element_type x8, other arithmetic, add(): return sum((term.astype(F32) for term in terms)).astype(BF16)  7.28 us
    ppermute x2, starting transfers between devices, scatter_x(): direct = lax.ppermute(add(*quarter(back)), ALL, BACK)  7.11 us
  transfers between devices with their start and end apart: 21, of which 6 were waited for; matrix products, arithmetic and copies ran while one was open for 6% of the time, Pallas kernels for 2%

profile of v9, /device:TPU:6, one launch (start us, length us, event | category | flops | bytes accessed | tf_op | source)
XLA Modules:
  0.0 220.9 jit_solution(5317739753988019010)
XLA Ops:
  1.4 26.0 %all_to_all.30 = bf16[16,72,128]{2,1,0:T(8,128)(2,1)S(1)} all-to-all(bf16[16,72,128]{2,1,0:T(8,128)(2,1)S(1)} %bitcast.65), channel_id=1, replica_groups={{0,8,32,40,64,72,96,104,256,264,288,296,320,328,352,360},{16,24,48,56,8..., dimensions={0} | all-to-all | bytes 589824 | tf_op jit(solution)/shard_map/all_to_all | solution.py:52
  28.1 1.2 broadcast_in_dim.36
  29.3 3.7 %all-to-all-start.1 = ((bf16[4,8,144,128]{3,2,1,0:T(8,128)(2,1)}), bf16[4,8,144,128]{3,2,1,0:T(8,128)(2,1)S(1)}, u32[]{:S(2)}, u32[]{:S(2)}) async-start(bf16[4,8,144,128]{3,2,1,0:T(8,128)(2,1)} %broadcast_in_dim.36), calls=%async_computation.1 | async-start | bytes 2359296 | tf_op jit(solution)/shard_map/all_to_all | solution.py:52
  33.0 2.6 %collective-permute-start.1 = (bf16[128,4608]{1,0:T(8,128)(2,1)S(1)}, bf16[128,4608]{1,0:T(8,128)(2,1)S(1)}, u32[]{:S(2)}, u32[]{:S(2)}) collective-permute-start(bf16[128,4608]{1,0:T(8,128)(2,1)S(1)} %copy-done), channel_id=1, source_target_pairs={{0,8},{8,0},{16,24},{24,16},{32,40},{40,32},{48,56},{56,48},{64,72... | collective-permute-start | bytes 3538952 | tf_op jit(solution)/shard_map/ppermute | solution.py:235
  35.6 1.9 collective-permute-start
  37.6 2.4 %collective-permute-start.2 = (f32[2,128]{1,0:T(2,128)S(1)}, f32[2,128]{1,0:T(2,128)S(1)}, u32[]{:S(2)}, u32[]{:S(2)}) collective-permute-start(f32[2,128]{1,0:T(2,128)S(1)} %pad_maximum_fusion.1), channel_id=1, source_target_pairs={{0,8},{8,0},{16,24},{24,16},{32,40},{40,32},{48,56},{56,48},{64,72... | collective-permute-start | bytes 3080 | tf_op jit(solution)/shard_map/ppermute | solution.py:237
  40.0 1.3 compare_reduce_fusion.1
  41.4 1.4 add_convert_fusion.6
  44.1 5.0 %all-to-all-done.1.act_ref = bf16[4,8,144,128]{3,2,1,0:T(8,128)(2,1)S(1)} async-done(((bf16[4,8,144,128]{3,2,1,0:T(8,128)(2,1)}), bf16[4,8,144,128]{3,2,1,0:T(8,128)(2,1)S(1)}, u32[]{:S(2)}, u32[]{:S(2)}) %all-to-all-start.1) | async-done | bytes 1179680 | tf_op jit(solution)/shard_map/all_to_all | solution.py:52
  49.1 1.3 copy-done.5
  50.4 2.9 %shard_map.102 = (bf16[4,8,144,128]{3,2,1,0:T(8,128)(2,1)S(1)}, bf16[128,256]{1,0:T(8,128)(2,1)S(1)}, f32[256,128]{1,0:T(8,128)S(1)}) custom-call(bf16[4,8,144,128]{3,2,1,0:T(8,128)(2,1)S(1)} %all-to-all-done.1.act_ref, bf16[4608,128]{1,0:T(8,128)(2,1)S(1)} %copy-done.5, bf16[4608,128]{1,0:T(8,128)(2,1)} %collective-permute-done.we_other, ...), custom_call_target="tpu_custom_call" | custom-call | flops 603979776 | bytes 7282688 | tf_op jit(solution)/shard_map/pallas_call | solution.py:179
  54.6 18.3 %all_to_all.31 = bf16[4,8,144,128]{3,2,1,0:T(8,128)(2,1)S(1)} all-to-all(bf16[4,8,144,128]{3,2,1,0:T(8,128)(2,1)S(1)} %get-tuple-element.16), channel_id=1, replica_groups={{0,16,128,144},{8,24,136,152},{32,48,160,176},{40,56,168,184},{64,80,19..., dimensions={0} | all-to-all | bytes 2359296 | tf_op jit(solution)/shard_map/all_to_all | solution.py:52
  72.9 0.9 reduce_sum.23
  73.9 3.4 %all-to-all-start.3 = ((bf16[8,144,128]{2,1,0:T(8,128)(2,1)}), bf16[8,144,128]{2,1,0:T(8,128)(2,1)S(1)}, u32[]{:S(2)}, u32[]{:S(2)}) async-start(bf16[8,144,128]{2,1,0:T(8,128)(2,1)} %reduce_sum.23), calls=%async_computation.3 | async-start | bytes 589824 | tf_op jit(solution)/shard_map/all_to_all | solution.py:52
  78.1 11.9 %all-to-all-done.3 = bf16[8,144,128]{2,1,0:T(8,128)(2,1)S(1)} async-done(((bf16[8,144,128]{2,1,0:T(8,128)(2,1)}), bf16[8,144,128]{2,1,0:T(8,128)(2,1)S(1)}, u32[]{:S(2)}, u32[]{:S(2)}) %all-to-all-start.3) | async-done | bytes 294944 | tf_op jit(solution)/shard_map/all_to_all | solution.py:52
  91.0 16.6 %all_to_all.32 = bf16[8,144,128]{2,1,0:T(8,128)(2,1)S(1)} all-to-all(bf16[8,144,128]{2,1,0:T(8,128)(2,1)S(1)} %broadcast_in_dim.40), channel_id=1, replica_groups={{0,32,64,96,256,288,320,352},{8,40,72,104,264,296,328,360},{16,48,80,11..., dimensions={0} | all-to-all | bytes 589824 | tf_op jit(solution)/shard_map/all_to_all | solution.py:52
  107.8 18.1 %all_to_all.33.res_ref = bf16[4,8,144,128]{3,2,1,0:T(8,128)(2,1)S(1)} all-to-all(bf16[4,8,144,128]{3,2,1,0:T(8,128)(2,1)S(1)} %broadcast_in_dim.41), channel_id=1, replica_groups={{0,16,128,144},{8,24,136,152},{32,48,160,176},{40,56,168,184},{64,80,19..., dimensions={0} | all-to-all | bytes 2359296 | tf_op jit(solution)/shard_map/all_to_all | solution.py:52
  126.0 1.5 shard_map.103
  127.5 1.9 collective-permute-start.3
  129.4 3.6 %shard_map.104 = (bf16[4,1168,128]{2,1,0:T(8,128)(2,1)S(1)}, bf16[4,1168,128]{2,1,0:T(8,128)(2,1)}) custom-call(bf16[4,8,144,128]{3,2,1,0:T(8,128)(2,1)S(1)} %all_to_all.33.res_ref, bf16[4,8,144,128]{3,2,1,0:T(8,128)(2,1)S(1)} %all-to-all-done.1.act_ref, bf16[128,4608]{1,0:T(8,128)(2,1)S(1)} %copy-done, bf16[128,4608]{1,0:T(8,128)(2,1)S(1)} %copy-done.2, ...), custom_call_target="tpu_custom_call" | custom-call | flops 603979776 | bytes 7241728 | tf_op jit(solution)/shard_map/pallas_call | solution.py:179
  133.1 1.0 copy-done.11
  134.1 2.4 %collective-permute-start.4 = (bf16[4,1168,128]{2,1,0:T(8,128)(2,1)}, bf16[4,1168,128]{2,1,0:T(8,128)(2,1)}, u32[]{:S(2)}, u32[]{:S(2)}) collective-permute-start(bf16[4,1168,128]{2,1,0:T(8,128)(2,1)} %get-tuple-element.25), channel_id=1, source_target_pairs={{0,8},{8,0},{16,24},{24,16},{32,40},{40,32},{48,56},{56,48},{64,72... | collective-permute-start | bytes 3588104 | tf_op jit(solution)/shard_map/ppermute | solution.py:294
  136.5 1.4 fusion.6
  138.0 2.5 %collective-permute-start.13 = (bf16[1200,128]{1,0:T(8,128)(2,1)S(1)}, bf16[1200,128]{1,0:T(8,128)(2,1)S(1)}, u32[]{:S(2)}, u32[]{:S(2)}) collective-permute-start(bf16[1200,128]{1,0:T(8,128)(2,1)S(1)} %get-tuple-element.31), channel_id=1, source_target_pairs={{0,2},{1,3},{2,4},{3,5},{4,6},{5,7},{6,0},{7,1},{8,14},{9,15},{10,... | collective-permute-start | bytes 921608 | tf_op jit(solution)/shard_map/ppermute | solution.py:205
  140.5 3.5 %collective-permute-start.12 = (bf16[1200,128]{1,0:T(8,128)(2,1)S(1)}, bf16[1200,128]{1,0:T(8,128)(2,1)S(1)}, u32[]{:S(2)}, u32[]{:S(2)}) collective-permute-start(bf16[1200,128]{1,0:T(8,128)(2,1)S(1)} %get-tuple-element.30), channel_id=1, source_target_pairs={{0,6},{1,7},{2,0},{3,1},{4,2},{5,3},{6,4},{7,5},{8,10},{9,11},{10,... | collective-permute-start | bytes 921608 | tf_op jit(solution)/shard_map/ppermute | solution.py:206
  144.0 1.3 fusion.8
  145.2 3.6 %collective-permute-start.6 = (bf16[1168,128]{1,0:T(8,128)(2,1)S(1)}, bf16[1168,128]{1,0:T(8,128)(2,1)S(1)}, u32[]{:S(2)}, u32[]{:S(2)}) collective-permute-start(bf16[1168,128]{1,0:T(8,128)(2,1)S(1)} %get-tuple-element.33), channel_id=1, source_target_pairs={{0,2},{1,3},{2,4},{3,5},{4,6},{5,7},{6,0},{7,1},{8,14},{9,15},{10,... | collective-permute-start | bytes 897032 | tf_op jit(solution)/shard_map/ppermute | solution.py:205
  148.8 1.1 fusion
  149.9 2.2 collective-permute-start.14
  152.1 3.6 %collective-permute-start.5 = (bf16[1168,128]{1,0:T(8,128)(2,1)S(1)}, bf16[1168,128]{1,0:T(8,128)(2,1)S(1)}, u32[]{:S(2)}, u32[]{:S(2)}) collective-permute-start(bf16[1168,128]{1,0:T(8,128)(2,1)S(1)} %get-tuple-element.32), channel_id=1, source_target_pairs={{0,6},{1,7},{2,0},{3,1},{4,2},{5,3},{6,4},{7,5},{8,10},{9,11},{10,... | collective-permute-start | bytes 897032 | tf_op jit(solution)/shard_map/ppermute | solution.py:206
  155.8 1.1 fusion.3
  156.9 3.4 %collective-permute-start.7 = (bf16[1168,128]{1,0:T(8,128)(2,1)S(1)}, bf16[1168,128]{1,0:T(8,128)(2,1)S(1)}, u32[]{:S(2)}, u32[]{:S(2)}) collective-permute-start(bf16[1168,128]{1,0:T(8,128)(2,1)S(1)} %fusion.3), channel_id=1, source_target_pairs={{0,2},{1,3},{2,4},{3,5},{4,6},{5,7},{6,0},{7,1},{8,14},{9,15},{10,... | collective-permute-start | bytes 897032 | tf_op jit(solution)/shard_map/ppermute | solution.py:207
  160.3 1.6 collective-permute-done.14
  161.9 1.1 fusion.2
  163.0 6.0 %collective-permute-start.15 = (bf16[1200,128]{1,0:T(8,128)(2,1)S(1)}, bf16[1200,128]{1,0:T(8,128)(2,1)S(1)}, u32[]{:S(2)}, u32[]{:S(2)}) collective-permute-start(bf16[1200,128]{1,0:T(8,128)(2,1)S(1)} %fusion.2), channel_id=1, source_target_pairs={{0,1},{1,0},{2,3},{3,2},{4,5},{5,4},{6,7},{7,6},{8,9},{9,8},{10,11... | collective-permute-start | bytes 921608 | tf_op jit(solution)/shard_map/ppermute | solution.py:297
  169.0 1.1 fusion.5
  170.1 3.8 %collective-permute-start.8 = (bf16[1168,128]{1,0:T(8,128)(2,1)S(1)}, bf16[1168,128]{1,0:T(8,128)(2,1)S(1)}, u32[]{:S(2)}, u32[]{:S(2)}) collective-permute-start(bf16[1168,128]{1,0:T(8,128)(2,1)S(1)} %fusion.5), channel_id=1, source_target_pairs={{0,1},{1,0},{2,3},{3,2},{4,5},{5,4},{6,7},{7,6},{8,9},{9,8},{10,11... | collective-permute-start | bytes 897032 | tf_op jit(solution)/shard_map/ppermute | solution.py:298
  173.9 14.9 %collective-permute-done.15 = bf16[1200,128]{1,0:T(8,128)(2,1)S(1)} collective-permute-done((bf16[1200,128]{1,0:T(8,128)(2,1)S(1)}, bf16[1200,128]{1,0:T(8,128)(2,1)S(1)}, u32[]{:S(2)}, u32[]{:S(2)}) %collective-permute-start.15) | collective-permute-done | bytes 307232 | tf_op jit(solution)/shard_map/ppermute | solution.py:297
  188.9 3.9 %collective-permute-start.16 = (bf16[1200,128]{1,0:T(8,128)(2,1)S(1)}, bf16[1200,128]{1,0:T(8,128)(2,1)S(1)}, u32[]{:S(2)}, u32[]{:S(2)}) collective-permute-start(bf16[1200,128]{1,0:T(8,128)(2,1)S(1)} %add_convert_fusion.refs_0_), channel_id=1, source_target_pairs={{0,2},{1,3},{2,4},{3,5},{4,6},{5,7},{6,0},{7,1},{8,14},{9,15},{10,... | collective-permute-start | bytes 921608 | tf_op jit(solution)/shard_map/ppermute | solution.py:212
  192.8 1.3 collective-permute-done.8
  194.3 4.8 %collective-permute-start.9 = (bf16[1168,128]{1,0:T(8,128)(2,1)S(1)}, bf16[1168,128]{1,0:T(8,128)(2,1)S(1)}, u32[]{:S(2)}, u32[]{:S(2)}) collective-permute-start(bf16[1168,128]{1,0:T(8,128)(2,1)S(1)} %add_convert_fusion.3.refs_0_), channel_id=1, source_target_pairs={{0,2},{1,3},{2,4},{3,5},{4,6},{5,7},{6,0},{7,1},{8,14},{9,15},{10,... | collective-permute-start | bytes 897032 | tf_op jit(solution)/shard_map/ppermute | solution.py:212
  199.0 1.9 collective-permute-start.17
  201.0 5.1 %collective-permute-start.18 = (bf16[1200,128]{1,0:T(8,128)(2,1)S(1)}, bf16[1200,128]{1,0:T(8,128)(2,1)S(1)}, u32[]{:S(2)}, u32[]{:S(2)}) collective-permute-start(bf16[1200,128]{1,0:T(8,128)(2,1)S(1)} %collective-permute-done.16.refs_1_), channel_id=1, source_target_pairs={{0,2},{1,3},{2,4},{3,5},{4,6},{5,7},{6,0},{7,1},{8,14},{9,15},{10,... | collective-permute-start | bytes 921608 | tf_op jit(solution)/shard_map/ppermute | solution.py:214
  206.2 1.9 collective-permute-start.10
  208.1 5.1 %collective-permute-start.11 = (bf16[1168,128]{1,0:T(8,128)(2,1)S(1)}, bf16[1168,128]{1,0:T(8,128)(2,1)S(1)}, u32[]{:S(2)}, u32[]{:S(2)}) collective-permute-start(bf16[1168,128]{1,0:T(8,128)(2,1)S(1)} %collective-permute-done.9.refs_1_), channel_id=1, source_target_pairs={{0,2},{1,3},{2,4},{3,5},{4,6},{5,7},{6,0},{7,1},{8,14},{9,15},{10,... | collective-permute-start | bytes 897032 | tf_op jit(solution)/shard_map/ppermute | solution.py:214
  213.9 1.8 shard_map.106
  216.1 3.1 %collective-permute-done.10.refs_2_ = bf16[1168,128]{1,0:T(8,128)(2,1)S(1)} collective-permute-done((bf16[1168,128]{1,0:T(8,128)(2,1)S(1)}, bf16[1168,128]{1,0:T(8,128)(2,1)S(1)}, u32[]{:S(2)}, u32[]{:S(2)}) %collective-permute-start.10) | collective-permute-done | bytes 299040 | tf_op jit(solution)/shard_map/ppermute | solution.py:213
  219.2 1.6 shard_map.105
  (63 shorter events, 7.5 us)
Async XLA Ops:
  27.4 0.7 copy-start.10
  29.3 3.7 %copy-start = (bf16[128,4608]{1,0:T(8,128)(2,1)S(1)}, bf16[128,4608]{1,0:T(8,128)(2,1)}, u32[]{:S(2)}) copy-start(bf16[128,4608]{1,0:T(8,128)(2,1)} %wd_own.3) | copy-start | bytes 3538948
  29.3 8.3 %copy-start.13 = (bf16[128]{0:T(256)(128)(2,1)S(1)}, bf16[128]{0:T(256)(128)(2,1)}, u32[]{:S(2)}) copy-start(bf16[128]{0:T(256)(128)(2,1)} %param.9) | copy-start | bytes 772
  29.3 8.3 %copy-start.14 = (s32[128]{0:T(128)S(1)}, s32[128]{0:T(128)}, u32[]{:S(2)}) copy-start(s32[128]{0:T(128)} %param.12) | copy-start | bytes 1540
  29.3 19.9 %all-to-all-start.1 = ((bf16[4,8,144,128]{3,2,1,0:T(8,128)(2,1)}), bf16[4,8,144,128]{3,2,1,0:T(8,128)(2,1)S(1)}, u32[]{:S(2)}, u32[]{:S(2)}) async-start(bf16[4,8,144,128]{3,2,1,0:T(8,128)(2,1)} %broadcast_in_dim.36), calls=%async_computation.1 | async-start | bytes 2359296 | tf_op jit(solution)/shard_map/all_to_all | solution.py:52
  33.0 11.2 %collective-permute-start.1 = (bf16[128,4608]{1,0:T(8,128)(2,1)S(1)}, bf16[128,4608]{1,0:T(8,128)(2,1)S(1)}, u32[]{:S(2)}, u32[]{:S(2)}) collective-permute-start(bf16[128,4608]{1,0:T(8,128)(2,1)S(1)} %copy-done), channel_id=1, source_target_pairs={{0,8},{8,0},{16,24},{24,16},{32,40},{40,32},{48,56},{56,48},{64,72... | collective-permute-start | bytes 3538952 | tf_op jit(solution)/shard_map/ppermute | solution.py:235
  35.6 8.5 %collective-permute-start = (bf16[4608,128]{1,0:T(8,128)(2,1)}, bf16[4608,128]{1,0:T(8,128)(2,1)}, u32[]{:S(2)}, u32[]{:S(2)}) collective-permute-start(bf16[4608,128]{1,0:T(8,128)(2,1)} %we_own.1), channel_id=1, source_target_pairs={{0,8},{8,0},{16,24},{24,16},{32,40},{40,32},{48,56},{56,48},{64,72... | collective-permute-start | bytes 3538952 | tf_op jit(solution)/shard_map/ppermute | solution.py:234
  37.6 5.2 %collective-permute-start.2 = (f32[2,128]{1,0:T(2,128)S(1)}, f32[2,128]{1,0:T(2,128)S(1)}, u32[]{:S(2)}, u32[]{:S(2)}) collective-permute-start(f32[2,128]{1,0:T(2,128)S(1)} %pad_maximum_fusion.1), channel_id=1, source_target_pairs={{0,8},{8,0},{16,24},{24,16},{32,40},{40,32},{48,56},{56,48},{64,72... | collective-permute-start | bytes 3080 | tf_op jit(solution)/shard_map/ppermute | solution.py:237
  42.8 0.6 copy-start.12
  44.1 5.0 %copy-start.1 = (bf16[128,4608]{1,0:T(8,128)(2,1)}, bf16[128,4608]{1,0:T(8,128)(2,1)S(1)}, u32[]{:S(2)}) copy-start(bf16[128,4608]{1,0:T(8,128)(2,1)S(1)} %collective-permute-done.1.wd_other) | copy-start | bytes 3538948
  49.1 1.3 copy-start.5
  53.4 0.7 copy-start.6
  54.0 0.6 copy-start.8
  73.9 16.2 %all-to-all-start.3 = ((bf16[8,144,128]{2,1,0:T(8,128)(2,1)}), bf16[8,144,128]{2,1,0:T(8,128)(2,1)S(1)}, u32[]{:S(2)}, u32[]{:S(2)}) async-start(bf16[8,144,128]{2,1,0:T(8,128)(2,1)} %reduce_sum.23), calls=%async_computation.3 | async-start | bytes 589824 | tf_op jit(solution)/shard_map/all_to_all | solution.py:52
  107.8 18.2 %copy-start.9 = (bf16[128,256]{1,0:T(8,128)(2,1)S(1)}, bf16[128,256]{1,0:T(8,128)(2,1)}, u32[]{:S(2)}) copy-start(bf16[128,256]{1,0:T(8,128)(2,1)} %copy-done.8) | copy-start | bytes 196612
  107.8 21.6 %copy-start.7 = (f32[256,128]{1,0:T(8,128)S(1)}, f32[256,128]{1,0:T(8,128)}, u32[]{:S(2)}) copy-start(f32[256,128]{1,0:T(8,128)} %copy-done.6) | copy-start | bytes 393220
  126.0 3.5 %copy-start.2 = (bf16[128,4608]{1,0:T(8,128)(2,1)S(1)}, bf16[128,4608]{1,0:T(8,128)(2,1)}, u32[]{:S(2)}) copy-start(bf16[128,4608]{1,0:T(8,128)(2,1)} %copy-done.1) | copy-start | bytes 3538948
  127.5 5.6 %copy-start.3 = (bf16[4,1200,128]{2,1,0:T(8,128)(2,1)}, bf16[4,1200,128]{2,1,0:T(8,128)(2,1)S(1)}, u32[]{:S(2)}) copy-start(bf16[4,1200,128]{2,1,0:T(8,128)(2,1)S(1)} %get-tuple-element.26) | copy-start | bytes 3686404
  127.5 5.6 %collective-permute-start.3 = (bf16[4,1200,128]{2,1,0:T(8,128)(2,1)S(1)}, bf16[4,1200,128]{2,1,0:T(8,128)(2,1)S(1)}, u32[]{:S(2)}, u32[]{:S(2)}) collective-permute-start(bf16[4,1200,128]{2,1,0:T(8,128)(2,1)S(1)} %get-tuple-element.24), channel_id=1, source_target_pairs={{0,8},{8,0},{16,24},{24,16},{32,40},{40,32},{48,56},{56,48},{64,72... | collective-permute-start | bytes 3686408 | tf_op jit(solution)/shard_map/ppermute | solution.py:292
  133.0 1.0 copy-start.11
  134.1 9.9 %collective-permute-start.4 = (bf16[4,1168,128]{2,1,0:T(8,128)(2,1)}, bf16[4,1168,128]{2,1,0:T(8,128)(2,1)}, u32[]{:S(2)}, u32[]{:S(2)}) collective-permute-start(bf16[4,1168,128]{2,1,0:T(8,128)(2,1)} %get-tuple-element.25), channel_id=1, source_target_pairs={{0,8},{8,0},{16,24},{24,16},{32,40},{40,32},{48,56},{56,48},{64,72... | collective-permute-start | bytes 3588104 | tf_op jit(solution)/shard_map/ppermute | solution.py:294
  137.9 10.9 %copy-start.4 = (bf16[4,1200,128]{2,1,0:T(8,128)(2,1)S(1)}, bf16[4,1200,128]{2,1,0:T(8,128)(2,1)}, u32[]{:S(2)}) copy-start(bf16[4,1200,128]{2,1,0:T(8,128)(2,1)} %copy-done.3) | copy-start | bytes 3686404
  138.0 10.9 %collective-permute-start.13 = (bf16[1200,128]{1,0:T(8,128)(2,1)S(1)}, bf16[1200,128]{1,0:T(8,128)(2,1)S(1)}, u32[]{:S(2)}, u32[]{:S(2)}) collective-permute-start(bf16[1200,128]{1,0:T(8,128)(2,1)S(1)} %get-tuple-element.31), channel_id=1, source_target_pairs={{0,2},{1,3},{2,4},{3,5},{4,6},{5,7},{6,0},{7,1},{8,14},{9,15},{10,... | collective-permute-start | bytes 921608 | tf_op jit(solution)/shard_map/ppermute | solution.py:205
  140.5 19.8 %collective-permute-start.12 = (bf16[1200,128]{1,0:T(8,128)(2,1)S(1)}, bf16[1200,128]{1,0:T(8,128)(2,1)S(1)}, u32[]{:S(2)}, u32[]{:S(2)}) collective-permute-start(bf16[1200,128]{1,0:T(8,128)(2,1)S(1)} %get-tuple-element.30), channel_id=1, source_target_pairs={{0,6},{1,7},{2,0},{3,1},{4,2},{5,3},{6,4},{7,5},{8,10},{9,11},{10,... | collective-permute-start | bytes 921608 | tf_op jit(solution)/shard_map/ppermute | solution.py:206
  145.2 10.5 %collective-permute-start.6 = (bf16[1168,128]{1,0:T(8,128)(2,1)S(1)}, bf16[1168,128]{1,0:T(8,128)(2,1)S(1)}, u32[]{:S(2)}, u32[]{:S(2)}) collective-permute-start(bf16[1168,128]{1,0:T(8,128)(2,1)S(1)} %get-tuple-element.33), channel_id=1, source_target_pairs={{0,2},{1,3},{2,4},{3,5},{4,6},{5,7},{6,0},{7,1},{8,14},{9,15},{10,... | collective-permute-start | bytes 897032 | tf_op jit(solution)/shard_map/ppermute | solution.py:205
  149.9 11.9 %collective-permute-start.14 = (bf16[1200,128]{1,0:T(8,128)(2,1)S(1)}, bf16[1200,128]{1,0:T(8,128)(2,1)S(1)}, u32[]{:S(2)}, u32[]{:S(2)}) collective-permute-start(bf16[1200,128]{1,0:T(8,128)(2,1)S(1)} %fusion), channel_id=1, source_target_pairs={{0,2},{1,3},{2,4},{3,5},{4,6},{5,7},{6,0},{7,1},{8,14},{9,15},{10,... | collective-permute-start | bytes 921608 | tf_op jit(solution)/shard_map/ppermute | solution.py:207
  152.1 16.8 %collective-permute-start.5 = (bf16[1168,128]{1,0:T(8,128)(2,1)S(1)}, bf16[1168,128]{1,0:T(8,128)(2,1)S(1)}, u32[]{:S(2)}, u32[]{:S(2)}) collective-permute-start(bf16[1168,128]{1,0:T(8,128)(2,1)S(1)} %get-tuple-element.32), channel_id=1, source_target_pairs={{0,6},{1,7},{2,0},{3,1},{4,2},{5,3},{6,4},{7,5},{8,10},{9,11},{10,... | collective-permute-start | bytes 897032 | tf_op jit(solution)/shard_map/ppermute | solution.py:206
  156.9 12.1 %collective-permute-start.7 = (bf16[1168,128]{1,0:T(8,128)(2,1)S(1)}, bf16[1168,128]{1,0:T(8,128)(2,1)S(1)}, u32[]{:S(2)}, u32[]{:S(2)}) collective-permute-start(bf16[1168,128]{1,0:T(8,128)(2,1)S(1)} %fusion.3), channel_id=1, source_target_pairs={{0,2},{1,3},{2,4},{3,5},{4,6},{5,7},{6,0},{7,1},{8,14},{9,15},{10,... | collective-permute-start | bytes 897032 | tf_op jit(solution)/shard_map/ppermute | solution.py:207
  163.0 25.8 %collective-permute-start.15 = (bf16[1200,128]{1,0:T(8,128)(2,1)S(1)}, bf16[1200,128]{1,0:T(8,128)(2,1)S(1)}, u32[]{:S(2)}, u32[]{:S(2)}) collective-permute-start(bf16[1200,128]{1,0:T(8,128)(2,1)S(1)} %fusion.2), channel_id=1, source_target_pairs={{0,1},{1,0},{2,3},{3,2},{4,5},{5,4},{6,7},{7,6},{8,9},{9,8},{10,11... | collective-permute-start | bytes 921608 | tf_op jit(solution)/shard_map/ppermute | solution.py:297
  170.1 24.0 %collective-permute-start.8 = (bf16[1168,128]{1,0:T(8,128)(2,1)S(1)}, bf16[1168,128]{1,0:T(8,128)(2,1)S(1)}, u32[]{:S(2)}, u32[]{:S(2)}) collective-permute-start(bf16[1168,128]{1,0:T(8,128)(2,1)S(1)} %fusion.5), channel_id=1, source_target_pairs={{0,1},{1,0},{2,3},{3,2},{4,5},{5,4},{6,7},{7,6},{8,9},{9,8},{10,11... | collective-permute-start | bytes 897032 | tf_op jit(solution)/shard_map/ppermute | solution.py:298
  188.9 12.0 %collective-permute-start.16 = (bf16[1200,128]{1,0:T(8,128)(2,1)S(1)}, bf16[1200,128]{1,0:T(8,128)(2,1)S(1)}, u32[]{:S(2)}, u32[]{:S(2)}) collective-permute-start(bf16[1200,128]{1,0:T(8,128)(2,1)S(1)} %add_convert_fusion.refs_0_), channel_id=1, source_target_pairs={{0,2},{1,3},{2,4},{3,5},{4,6},{5,7},{6,0},{7,1},{8,14},{9,15},{10,... | collective-permute-start | bytes 921608 | tf_op jit(solution)/shard_map/ppermute | solution.py:212
  194.3 13.8 %collective-permute-start.9 = (bf16[1168,128]{1,0:T(8,128)(2,1)S(1)}, bf16[1168,128]{1,0:T(8,128)(2,1)S(1)}, u32[]{:S(2)}, u32[]{:S(2)}) collective-permute-start(bf16[1168,128]{1,0:T(8,128)(2,1)S(1)} %add_convert_fusion.3.refs_0_), channel_id=1, source_target_pairs={{0,2},{1,3},{2,4},{3,5},{4,6},{5,7},{6,0},{7,1},{8,14},{9,15},{10,... | collective-permute-start | bytes 897032 | tf_op jit(solution)/shard_map/ppermute | solution.py:212
  199.0 14.8 %collective-permute-start.17 = (bf16[1200,128]{1,0:T(8,128)(2,1)S(1)}, bf16[1200,128]{1,0:T(8,128)(2,1)S(1)}, u32[]{:S(2)}, u32[]{:S(2)}) collective-permute-start(bf16[1200,128]{1,0:T(8,128)(2,1)S(1)} %add_convert_fusion.refs_0_), channel_id=1, source_target_pairs={{0,6},{1,7},{2,0},{3,1},{4,2},{5,3},{6,4},{7,5},{8,10},{9,11},{10,... | collective-permute-start | bytes 921608 | tf_op jit(solution)/shard_map/ppermute | solution.py:213
  201.0 12.9 %collective-permute-start.18 = (bf16[1200,128]{1,0:T(8,128)(2,1)S(1)}, bf16[1200,128]{1,0:T(8,128)(2,1)S(1)}, u32[]{:S(2)}, u32[]{:S(2)}) collective-permute-start(bf16[1200,128]{1,0:T(8,128)(2,1)S(1)} %collective-permute-done.16.refs_1_), channel_id=1, source_target_pairs={{0,2},{1,3},{2,4},{3,5},{4,6},{5,7},{6,0},{7,1},{8,14},{9,15},{10,... | collective-permute-start | bytes 921608 | tf_op jit(solution)/shard_map/ppermute | solution.py:214
  206.2 13.0 %collective-permute-start.10 = (bf16[1168,128]{1,0:T(8,128)(2,1)S(1)}, bf16[1168,128]{1,0:T(8,128)(2,1)S(1)}, u32[]{:S(2)}, u32[]{:S(2)}) collective-permute-start(bf16[1168,128]{1,0:T(8,128)(2,1)S(1)} %add_convert_fusion.3.refs_0_), channel_id=1, source_target_pairs={{0,6},{1,7},{2,0},{3,1},{4,2},{5,3},{6,4},{7,5},{8,10},{9,11},{10,... | collective-permute-start | bytes 897032 | tf_op jit(solution)/shard_map/ppermute | solution.py:213
  208.1 11.1 %collective-permute-start.11 = (bf16[1168,128]{1,0:T(8,128)(2,1)S(1)}, bf16[1168,128]{1,0:T(8,128)(2,1)S(1)}, u32[]{:S(2)}, u32[]{:S(2)}) collective-permute-start(bf16[1168,128]{1,0:T(8,128)(2,1)S(1)} %collective-permute-done.9.refs_1_), channel_id=1, source_target_pairs={{0,2},{1,3},{2,4},{3,5},{4,6},{5,7},{6,0},{7,1},{8,14},{9,15},{10,... | collective-permute-start | bytes 897032 | tf_op jit(solution)/shard_map/ppermute | solution.py:214

commit v10 on v9

--- a/solution.py
+++ b/solution.py
@@ -163,14 +163,19 @@
 
 
 def place_enc_kernel(order_ref, *refs):
-    enc_ref = refs[-1]
+    *pieces, enc_ref, sems = refs
     quarter = enc_ref.shape[0] // NX
-    for n, ref in enumerate(refs[:-1]):
+    copies = []
+    for n, ref in enumerate(pieces):
         row = pl.multiple_of(order_ref[n] * quarter, quarter)
-        enc_ref[pl.ds(row, quarter), :] = ref[:quarter, :]
-
-
-def call(kernel, outs, args, scratch=(), flops=0, unloaded=()):
+        rows = enc_ref.at[pl.ds(row, quarter), :]
+        copies.append(pltpu.make_async_copy(ref.at[pl.ds(0, quarter), :], rows, sems.at[n]))
+        copies[-1].start()
+    for copy in copies:
+        copy.wait()
+
+
+def call(kernel, outs, args, scratch=(), flops=0, unloaded=(), in_place=False):
     whole = pl.BlockSpec(memory_space=pltpu.VMEM)
     scalars = pl.BlockSpec(memory_space=pltpu.SMEM)
     left = pl.BlockSpec(memory_space=pl.ANY)
@@ -183,7 +188,7 @@
             scalars if a.dtype == jnp.int32 else left if n in unloaded else whole
             for n, a in enumerate(args)
         ],
-        out_specs=[whole] * len(outs),
+        out_specs=[left if in_place else whole] * len(outs),
         scratch_shapes=list(scratch),
         compiler_params=pltpu.CompilerParams(vmem_limit_bytes=VMEM),
         cost_estimate=pl.CostEstimate(flops=flops, bytes_accessed=moved, transcendentals=0),
@@ -297,7 +302,14 @@
     dec_piece = add(dec_piece, lax.ppermute(dec_piece, "dp", Y_SWAP))
     enc_piece = add(enc_piece, lax.ppermute(enc_piece, "dp", Y_SWAP))
     (dec,) = call(place_dec_kernel, [shape((TILE, d))], (order, *gather_x(dec_piece)))
-    (enc,) = call(place_enc_kernel, [shape((d, TILE))], (order, *gather_x(enc_piece)))
+    (enc,) = call(
+        place_enc_kernel,
+        [shape((d, TILE))],
+        (order, *gather_x(enc_piece)),
+        [pltpu.SemaphoreType.DMA((NX,))],
+        unloaded=(1, 2, 3, 4),
+        in_place=True,
+    )
     return enc, dec, enc_piece[quarter], dec_piece[quarter : quarter + d // TILE].reshape(-1)
 
 

time: 223 us -> 222 us (level)
  no operation moved by 1% of the time
where the time goes in v10:
time: 222 us; the launch traced here: 221 us
  blocking collectives  79 us (36%)
  starting transfers between devices  69.7 us (31%)
  waiting for transfers between devices  37.8 us (17%)
  other arithmetic  13.4 us (6%)
  Pallas kernels  11.4 us (5%)
  local copies, waits for them, and re-layouts  8.19 us (4%)
    all_to_all x4, blocking collectives, exchange(): return lax.all_to_all(parts, 'dict', 0, 0, axis_index_groups=groups(axes))  79 us
    all_to_all x2, waiting for transfers between devices, exchange(): return lax.all_to_all(parts, 'dict', 0, 0, axis_index_groups=groups(axes))  16.9 us
    ppermute x1, waiting for transfers between devices, local(): dec_piece = add(dec_piece, lax.ppermute(dec_piece, 'dp', Y_SWAP))  14.9 us
    pallas_call x5, Pallas kernels, call(): pl.pallas_call(kernel, out_shape=outs, in_specs=[scalars if a.dtype == jn...  11.4 us
    ppermute x2, starting transfers between devices, gather_x(): return (piece, behind, ahead, lax.ppermute(behind, ALL, AHEAD))  10.3 us
    ppermute x2, starting transfers between devices, gather_x(): behind = lax.ppermute(piece, ALL, AHEAD)  8.67 us
    convert_element_type x8, other arithmetic, add(): return sum((term.astype(F32) for term in terms)).astype(BF16)  7.28 us
    ppermute x2, starting transfers between devices, scatter_x(): direct = lax.ppermute(add(*quarter(back)), ALL, BACK)  7.11 us
  transfers between devices with their start and end apart: 21, of which 6 were waited for; matrix products, arithmetic and copies ran while one was open for 6% of the time, Pallas kernels for 2%

profile of v10, /device:TPU:6, one launch (start us, length us, event | category | flops | bytes accessed | tf_op | source)
XLA Modules:
  0.0 220.8 jit_solution(11519294920063513428)
XLA Ops:
  1.4 26.0 %all_to_all.30 = bf16[16,72,128]{2,1,0:T(8,128)(2,1)S(1)} all-to-all(bf16[16,72,128]{2,1,0:T(8,128)(2,1)S(1)} %bitcast.65), channel_id=1, replica_groups={{0,8,32,40,64,72,96,104,256,264,288,296,320,328,352,360},{16,24,48,56,8..., dimensions={0} | all-to-all | bytes 589824 | tf_op jit(solution)/shard_map/all_to_all | solution.py:52
  28.1 1.2 broadcast_in_dim.36
  29.3 3.7 %all-to-all-start.1 = ((bf16[4,8,144,128]{3,2,1,0:T(8,128)(2,1)}), bf16[4,8,144,128]{3,2,1,0:T(8,128)(2,1)S(1)}, u32[]{:S(2)}, u32[]{:S(2)}) async-start(bf16[4,8,144,128]{3,2,1,0:T(8,128)(2,1)} %broadcast_in_dim.36), calls=%async_computation.1 | async-start | bytes 2359296 | tf_op jit(solution)/shard_map/all_to_all | solution.py:52
  33.0 2.6 %collective-permute-start.1 = (bf16[128,4608]{1,0:T(8,128)(2,1)S(1)}, bf16[128,4608]{1,0:T(8,128)(2,1)S(1)}, u32[]{:S(2)}, u32[]{:S(2)}) collective-permute-start(bf16[128,4608]{1,0:T(8,128)(2,1)S(1)} %copy-done), channel_id=1, source_target_pairs={{0,8},{8,0},{16,24},{24,16},{32,40},{40,32},{48,56},{56,48},{64,72... | collective-permute-start | bytes 3538952 | tf_op jit(solution)/shard_map/ppermute | solution.py:240
  35.6 1.9 collective-permute-start
  37.6 2.4 %collective-permute-start.2 = (f32[2,128]{1,0:T(2,128)S(1)}, f32[2,128]{1,0:T(2,128)S(1)}, u32[]{:S(2)}, u32[]{:S(2)}) collective-permute-start(f32[2,128]{1,0:T(2,128)S(1)} %pad_maximum_fusion.1), channel_id=1, source_target_pairs={{0,8},{8,0},{16,24},{24,16},{32,40},{40,32},{48,56},{56,48},{64,72... | collective-permute-start | bytes 3080 | tf_op jit(solution)/shard_map/ppermute | solution.py:242
  40.0 1.3 compare_reduce_fusion.1
  41.4 1.4 add_convert_fusion.6
  44.1 5.0 %all-to-all-done.1.act_ref = bf16[4,8,144,128]{3,2,1,0:T(8,128)(2,1)S(1)} async-done(((bf16[4,8,144,128]{3,2,1,0:T(8,128)(2,1)}), bf16[4,8,144,128]{3,2,1,0:T(8,128)(2,1)S(1)}, u32[]{:S(2)}, u32[]{:S(2)}) %all-to-all-start.1) | async-done | bytes 1179680 | tf_op jit(solution)/shard_map/all_to_all | solution.py:52
  49.1 1.3 copy-done.5
  50.4 2.9 %shard_map.102 = (bf16[4,8,144,128]{3,2,1,0:T(8,128)(2,1)S(1)}, bf16[128,256]{1,0:T(8,128)(2,1)S(1)}, f32[256,128]{1,0:T(8,128)S(1)}) custom-call(bf16[4,8,144,128]{3,2,1,0:T(8,128)(2,1)S(1)} %all-to-all-done.1.act_ref, bf16[4608,128]{1,0:T(8,128)(2,1)S(1)} %copy-done.5, bf16[4608,128]{1,0:T(8,128)(2,1)} %collective-permute-done.we_other, ...), custom_call_target="tpu_custom_call" | custom-call | flops 603979776 | bytes 7282688 | tf_op jit(solution)/shard_map/pallas_call | solution.py:184
  54.6 18.3 %all_to_all.31 = bf16[4,8,144,128]{3,2,1,0:T(8,128)(2,1)S(1)} all-to-all(bf16[4,8,144,128]{3,2,1,0:T(8,128)(2,1)S(1)} %get-tuple-element.16), channel_id=1, replica_groups={{0,16,128,144},{8,24,136,152},{32,48,160,176},{40,56,168,184},{64,80,19..., dimensions={0} | all-to-all | bytes 2359296 | tf_op jit(solution)/shard_map/all_to_all | solution.py:52
  72.9 0.9 reduce_sum.23
  73.9 3.4 %all-to-all-start.3 = ((bf16[8,144,128]{2,1,0:T(8,128)(2,1)}), bf16[8,144,128]{2,1,0:T(8,128)(2,1)S(1)}, u32[]{:S(2)}, u32[]{:S(2)}) async-start(bf16[8,144,128]{2,1,0:T(8,128)(2,1)} %reduce_sum.23), calls=%async_computation.3 | async-start | bytes 589824 | tf_op jit(solution)/shard_map/all_to_all | solution.py:52
  78.1 11.9 %all-to-all-done.3 = bf16[8,144,128]{2,1,0:T(8,128)(2,1)S(1)} async-done(((bf16[8,144,128]{2,1,0:T(8,128)(2,1)}), bf16[8,144,128]{2,1,0:T(8,128)(2,1)S(1)}, u32[]{:S(2)}, u32[]{:S(2)}) %all-to-all-start.3) | async-done | bytes 294944 | tf_op jit(solution)/shard_map/all_to_all | solution.py:52
  91.0 16.6 %all_to_all.32 = bf16[8,144,128]{2,1,0:T(8,128)(2,1)S(1)} all-to-all(bf16[8,144,128]{2,1,0:T(8,128)(2,1)S(1)} %broadcast_in_dim.40), channel_id=1, replica_groups={{0,32,64,96,256,288,320,352},{8,40,72,104,264,296,328,360},{16,48,80,11..., dimensions={0} | all-to-all | bytes 589824 | tf_op jit(solution)/shard_map/all_to_all | solution.py:52
  107.8 18.1 %all_to_all.33.res_ref = bf16[4,8,144,128]{3,2,1,0:T(8,128)(2,1)S(1)} all-to-all(bf16[4,8,144,128]{3,2,1,0:T(8,128)(2,1)S(1)} %broadcast_in_dim.41), channel_id=1, replica_groups={{0,16,128,144},{8,24,136,152},{32,48,160,176},{40,56,168,184},{64,80,19..., dimensions={0} | all-to-all | bytes 2359296 | tf_op jit(solution)/shard_map/all_to_all | solution.py:52
  126.0 1.5 shard_map.103
  127.5 1.9 collective-permute-start.3
  129.4 3.6 %shard_map.104 = (bf16[4,1168,128]{2,1,0:T(8,128)(2,1)S(1)}, bf16[4,1168,128]{2,1,0:T(8,128)(2,1)}) custom-call(bf16[4,8,144,128]{3,2,1,0:T(8,128)(2,1)S(1)} %all_to_all.33.res_ref, bf16[4,8,144,128]{3,2,1,0:T(8,128)(2,1)S(1)} %all-to-all-done.1.act_ref, bf16[128,4608]{1,0:T(8,128)(2,1)S(1)} %copy-done, bf16[128,4608]{1,0:T(8,128)(2,1)S(1)} %copy-done.2, ...), custom_call_target="tpu_custom_call" | custom-call | flops 603979776 | bytes 7241728 | tf_op jit(solution)/shard_map/pallas_call | solution.py:184
  133.1 1.0 copy-done.11
  134.1 2.4 %collective-permute-start.4 = (bf16[4,1168,128]{2,1,0:T(8,128)(2,1)}, bf16[4,1168,128]{2,1,0:T(8,128)(2,1)}, u32[]{:S(2)}, u32[]{:S(2)}) collective-permute-start(bf16[4,1168,128]{2,1,0:T(8,128)(2,1)} %get-tuple-element.25), channel_id=1, source_target_pairs={{0,8},{8,0},{16,24},{24,16},{32,40},{40,32},{48,56},{56,48},{64,72... | collective-permute-start | bytes 3588104 | tf_op jit(solution)/shard_map/ppermute | solution.py:299
  136.5 1.4 fusion.6
  138.0 2.5 %collective-permute-start.13 = (bf16[1200,128]{1,0:T(8,128)(2,1)S(1)}, bf16[1200,128]{1,0:T(8,128)(2,1)S(1)}, u32[]{:S(2)}, u32[]{:S(2)}) collective-permute-start(bf16[1200,128]{1,0:T(8,128)(2,1)S(1)} %get-tuple-element.31), channel_id=1, source_target_pairs={{0,2},{1,3},{2,4},{3,5},{4,6},{5,7},{6,0},{7,1},{8,14},{9,15},{10,... | collective-permute-start | bytes 921608 | tf_op jit(solution)/shard_map/ppermute | solution.py:210
  140.5 3.5 %collective-permute-start.12 = (bf16[1200,128]{1,0:T(8,128)(2,1)S(1)}, bf16[1200,128]{1,0:T(8,128)(2,1)S(1)}, u32[]{:S(2)}, u32[]{:S(2)}) collective-permute-start(bf16[1200,128]{1,0:T(8,128)(2,1)S(1)} %get-tuple-element.30), channel_id=1, source_target_pairs={{0,6},{1,7},{2,0},{3,1},{4,2},{5,3},{6,4},{7,5},{8,10},{9,11},{10,... | collective-permute-start | bytes 921608 | tf_op jit(solution)/shard_map/ppermute | solution.py:211
  144.0 1.3 fusion.8
  145.2 3.6 %collective-permute-start.6 = (bf16[1168,128]{1,0:T(8,128)(2,1)S(1)}, bf16[1168,128]{1,0:T(8,128)(2,1)S(1)}, u32[]{:S(2)}, u32[]{:S(2)}) collective-permute-start(bf16[1168,128]{1,0:T(8,128)(2,1)S(1)} %get-tuple-element.33), channel_id=1, source_target_pairs={{0,2},{1,3},{2,4},{3,5},{4,6},{5,7},{6,0},{7,1},{8,14},{9,15},{10,... | collective-permute-start | bytes 897032 | tf_op jit(solution)/shard_map/ppermute | solution.py:210
  148.8 1.1 fusion
  149.9 2.2 collective-permute-start.14
  152.1 3.6 %collective-permute-start.5 = (bf16[1168,128]{1,0:T(8,128)(2,1)S(1)}, bf16[1168,128]{1,0:T(8,128)(2,1)S(1)}, u32[]{:S(2)}, u32[]{:S(2)}) collective-permute-start(bf16[1168,128]{1,0:T(8,128)(2,1)S(1)} %get-tuple-element.32), channel_id=1, source_target_pairs={{0,6},{1,7},{2,0},{3,1},{4,2},{5,3},{6,4},{7,5},{8,10},{9,11},{10,... | collective-permute-start | bytes 897032 | tf_op jit(solution)/shard_map/ppermute | solution.py:211
  155.8 1.1 fusion.3
  156.9 3.4 %collective-permute-start.7 = (bf16[1168,128]{1,0:T(8,128)(2,1)S(1)}, bf16[1168,128]{1,0:T(8,128)(2,1)S(1)}, u32[]{:S(2)}, u32[]{:S(2)}) collective-permute-start(bf16[1168,128]{1,0:T(8,128)(2,1)S(1)} %fusion.3), channel_id=1, source_target_pairs={{0,2},{1,3},{2,4},{3,5},{4,6},{5,7},{6,0},{7,1},{8,14},{9,15},{10,... | collective-permute-start | bytes 897032 | tf_op jit(solution)/shard_map/ppermute | solution.py:212
  160.3 1.6 collective-permute-done.14
  161.9 1.1 fusion.2
  163.0 6.0 %collective-permute-start.15 = (bf16[1200,128]{1,0:T(8,128)(2,1)S(1)}, bf16[1200,128]{1,0:T(8,128)(2,1)S(1)}, u32[]{:S(2)}, u32[]{:S(2)}) collective-permute-start(bf16[1200,128]{1,0:T(8,128)(2,1)S(1)} %fusion.2), channel_id=1, source_target_pairs={{0,1},{1,0},{2,3},{3,2},{4,5},{5,4},{6,7},{7,6},{8,9},{9,8},{10,11... | collective-permute-start | bytes 921608 | tf_op jit(solution)/shard_map/ppermute | solution.py:302
  169.0 1.1 fusion.5
  170.1 3.8 %collective-permute-start.8 = (bf16[1168,128]{1,0:T(8,128)(2,1)S(1)}, bf16[1168,128]{1,0:T(8,128)(2,1)S(1)}, u32[]{:S(2)}, u32[]{:S(2)}) collective-permute-start(bf16[1168,128]{1,0:T(8,128)(2,1)S(1)} %fusion.5), channel_id=1, source_target_pairs={{0,1},{1,0},{2,3},{3,2},{4,5},{5,4},{6,7},{7,6},{8,9},{9,8},{10,11... | collective-permute-start | bytes 897032 | tf_op jit(solution)/shard_map/ppermute | solution.py:303
  173.9 14.9 %collective-permute-done.15 = bf16[1200,128]{1,0:T(8,128)(2,1)S(1)} collective-permute-done((bf16[1200,128]{1,0:T(8,128)(2,1)S(1)}, bf16[1200,128]{1,0:T(8,128)(2,1)S(1)}, u32[]{:S(2)}, u32[]{:S(2)}) %collective-permute-start.15) | collective-permute-done | bytes 307232 | tf_op jit(solution)/shard_map/ppermute | solution.py:302
  188.9 3.9 %collective-permute-start.16 = (bf16[1200,128]{1,0:T(8,128)(2,1)S(1)}, bf16[1200,128]{1,0:T(8,128)(2,1)S(1)}, u32[]{:S(2)}, u32[]{:S(2)}) collective-permute-start(bf16[1200,128]{1,0:T(8,128)(2,1)S(1)} %add_convert_fusion.refs_0_), channel_id=1, source_target_pairs={{0,2},{1,3},{2,4},{3,5},{4,6},{5,7},{6,0},{7,1},{8,14},{9,15},{10,... | collective-permute-start | bytes 921608 | tf_op jit(solution)/shard_map/ppermute | solution.py:217
  192.8 1.3 collective-permute-done.8
  194.3 4.8 %collective-permute-start.9 = (bf16[1168,128]{1,0:T(8,128)(2,1)S(1)}, bf16[1168,128]{1,0:T(8,128)(2,1)S(1)}, u32[]{:S(2)}, u32[]{:S(2)}) collective-permute-start(bf16[1168,128]{1,0:T(8,128)(2,1)S(1)} %add_convert_fusion.3.refs_0_), channel_id=1, source_target_pairs={{0,2},{1,3},{2,4},{3,5},{4,6},{5,7},{6,0},{7,1},{8,14},{9,15},{10,... | collective-permute-start | bytes 897032 | tf_op jit(solution)/shard_map/ppermute | solution.py:217
  199.0 1.9 collective-permute-start.17
  201.0 5.1 %collective-permute-start.18 = (bf16[1200,128]{1,0:T(8,128)(2,1)S(1)}, bf16[1200,128]{1,0:T(8,128)(2,1)S(1)}, u32[]{:S(2)}, u32[]{:S(2)}) collective-permute-start(bf16[1200,128]{1,0:T(8,128)(2,1)S(1)} %collective-permute-done.16.refs_1_), channel_id=1, source_target_pairs={{0,2},{1,3},{2,4},{3,5},{4,6},{5,7},{6,0},{7,1},{8,14},{9,15},{10,... | collective-permute-start | bytes 921608 | tf_op jit(solution)/shard_map/ppermute | solution.py:219
  206.2 1.9 collective-permute-start.10
  208.1 5.1 %collective-permute-start.11 = (bf16[1168,128]{1,0:T(8,128)(2,1)S(1)}, bf16[1168,128]{1,0:T(8,128)(2,1)S(1)}, u32[]{:S(2)}, u32[]{:S(2)}) collective-permute-start(bf16[1168,128]{1,0:T(8,128)(2,1)S(1)} %collective-permute-done.9.refs_1_), channel_id=1, source_target_pairs={{0,2},{1,3},{2,4},{3,5},{4,6},{5,7},{6,0},{7,1},{8,14},{9,15},{10,... | collective-permute-start | bytes 897032 | tf_op jit(solution)/shard_map/ppermute | solution.py:219
  213.9 1.8 shard_map.106
  216.1 3.1 %collective-permute-done.10.refs_2_ = bf16[1168,128]{1,0:T(8,128)(2,1)S(1)} collective-permute-done((bf16[1168,128]{1,0:T(8,128)(2,1)S(1)}, bf16[1168,128]{1,0:T(8,128)(2,1)S(1)}, u32[]{:S(2)}, u32[]{:S(2)}) %collective-permute-start.10) | collective-permute-done | bytes 299040 | tf_op jit(solution)/shard_map/ppermute | solution.py:218
  219.2 1.6 shard_map.105
  (63 shorter events, 7.5 us)
Async XLA Ops:
  27.4 0.7 copy-start.10
  29.3 3.7 %copy-start = (bf16[128,4608]{1,0:T(8,128)(2,1)S(1)}, bf16[128,4608]{1,0:T(8,128)(2,1)}, u32[]{:S(2)}) copy-start(bf16[128,4608]{1,0:T(8,128)(2,1)} %wd_own.3) | copy-start | bytes 3538948
  29.3 8.3 %copy-start.13 = (bf16[128]{0:T(256)(128)(2,1)S(1)}, bf16[128]{0:T(256)(128)(2,1)}, u32[]{:S(2)}) copy-start(bf16[128]{0:T(256)(128)(2,1)} %param.9) | copy-start | bytes 772
  29.3 8.3 %copy-start.14 = (s32[128]{0:T(128)S(1)}, s32[128]{0:T(128)}, u32[]{:S(2)}) copy-start(s32[128]{0:T(128)} %param.12) | copy-start | bytes 1540
  29.3 19.9 %all-to-all-start.1 = ((bf16[4,8,144,128]{3,2,1,0:T(8,128)(2,1)}), bf16[4,8,144,128]{3,2,1,0:T(8,128)(2,1)S(1)}, u32[]{:S(2)}, u32[]{:S(2)}) async-start(bf16[4,8,144,128]{3,2,1,0:T(8,128)(2,1)} %broadcast_in_dim.36), calls=%async_computation.1 | async-start | bytes 2359296 | tf_op jit(solution)/shard_map/all_to_all | solution.py:52
  33.0 11.2 %collective-permute-start.1 = (bf16[128,4608]{1,0:T(8,128)(2,1)S(1)}, bf16[128,4608]{1,0:T(8,128)(2,1)S(1)}, u32[]{:S(2)}, u32[]{:S(2)}) collective-permute-start(bf16[128,4608]{1,0:T(8,128)(2,1)S(1)} %copy-done), channel_id=1, source_target_pairs={{0,8},{8,0},{16,24},{24,16},{32,40},{40,32},{48,56},{56,48},{64,72... | collective-permute-start | bytes 3538952 | tf_op jit(solution)/shard_map/ppermute | solution.py:240
  35.6 8.5 %collective-permute-start = (bf16[4608,128]{1,0:T(8,128)(2,1)}, bf16[4608,128]{1,0:T(8,128)(2,1)}, u32[]{:S(2)}, u32[]{:S(2)}) collective-permute-start(bf16[4608,128]{1,0:T(8,128)(2,1)} %we_own.1), channel_id=1, source_target_pairs={{0,8},{8,0},{16,24},{24,16},{32,40},{40,32},{48,56},{56,48},{64,72... | collective-permute-start | bytes 3538952 | tf_op jit(solution)/shard_map/ppermute | solution.py:239
  37.6 5.2 %collective-permute-start.2 = (f32[2,128]{1,0:T(2,128)S(1)}, f32[2,128]{1,0:T(2,128)S(1)}, u32[]{:S(2)}, u32[]{:S(2)}) collective-permute-start(f32[2,128]{1,0:T(2,128)S(1)} %pad_maximum_fusion.1), channel_id=1, source_target_pairs={{0,8},{8,0},{16,24},{24,16},{32,40},{40,32},{48,56},{56,48},{64,72... | collective-permute-start | bytes 3080 | tf_op jit(solution)/shard_map/ppermute | solution.py:242
  42.8 0.6 copy-start.12
  44.1 5.0 %copy-start.1 = (bf16[128,4608]{1,0:T(8,128)(2,1)}, bf16[128,4608]{1,0:T(8,128)(2,1)S(1)}, u32[]{:S(2)}) copy-start(bf16[128,4608]{1,0:T(8,128)(2,1)S(1)} %collective-permute-done.1.wd_other) | copy-start | bytes 3538948
  49.1 1.3 copy-start.5
  53.4 0.7 copy-start.6
  54.0 0.6 copy-start.8
  73.9 16.2 %all-to-all-start.3 = ((bf16[8,144,128]{2,1,0:T(8,128)(2,1)}), bf16[8,144,128]{2,1,0:T(8,128)(2,1)S(1)}, u32[]{:S(2)}, u32[]{:S(2)}) async-start(bf16[8,144,128]{2,1,0:T(8,128)(2,1)} %reduce_sum.23), calls=%async_computation.3 | async-start | bytes 589824 | tf_op jit(solution)/shard_map/all_to_all | solution.py:52
  107.8 18.2 %copy-start.9 = (bf16[128,256]{1,0:T(8,128)(2,1)S(1)}, bf16[128,256]{1,0:T(8,128)(2,1)}, u32[]{:S(2)}) copy-start(bf16[128,256]{1,0:T(8,128)(2,1)} %copy-done.8) | copy-start | bytes 196612
  107.8 21.6 %copy-start.7 = (f32[256,128]{1,0:T(8,128)S(1)}, f32[256,128]{1,0:T(8,128)}, u32[]{:S(2)}) copy-start(f32[256,128]{1,0:T(8,128)} %copy-done.6) | copy-start | bytes 393220
  126.0 3.5 %copy-start.2 = (bf16[128,4608]{1,0:T(8,128)(2,1)S(1)}, bf16[128,4608]{1,0:T(8,128)(2,1)}, u32[]{:S(2)}) copy-start(bf16[128,4608]{1,0:T(8,128)(2,1)} %copy-done.1) | copy-start | bytes 3538948
  127.5 5.6 %copy-start.3 = (bf16[4,1200,128]{2,1,0:T(8,128)(2,1)}, bf16[4,1200,128]{2,1,0:T(8,128)(2,1)S(1)}, u32[]{:S(2)}) copy-start(bf16[4,1200,128]{2,1,0:T(8,128)(2,1)S(1)} %get-tuple-element.26) | copy-start | bytes 3686404
  127.5 5.6 %collective-permute-start.3 = (bf16[4,1200,128]{2,1,0:T(8,128)(2,1)S(1)}, bf16[4,1200,128]{2,1,0:T(8,128)(2,1)S(1)}, u32[]{:S(2)}, u32[]{:S(2)}) collective-permute-start(bf16[4,1200,128]{2,1,0:T(8,128)(2,1)S(1)} %get-tuple-element.24), channel_id=1, source_target_pairs={{0,8},{8,0},{16,24},{24,16},{32,40},{40,32},{48,56},{56,48},{64,72... | collective-permute-start | bytes 3686408 | tf_op jit(solution)/shard_map/ppermute | solution.py:297
  133.0 1.0 copy-start.11
  134.1 9.9 %collective-permute-start.4 = (bf16[4,1168,128]{2,1,0:T(8,128)(2,1)}, bf16[4,1168,128]{2,1,0:T(8,128)(2,1)}, u32[]{:S(2)}, u32[]{:S(2)}) collective-permute-start(bf16[4,1168,128]{2,1,0:T(8,128)(2,1)} %get-tuple-element.25), channel_id=1, source_target_pairs={{0,8},{8,0},{16,24},{24,16},{32,40},{40,32},{48,56},{56,48},{64,72... | collective-permute-start | bytes 3588104 | tf_op jit(solution)/shard_map/ppermute | solution.py:299
  137.9 10.9 %copy-start.4 = (bf16[4,1200,128]{2,1,0:T(8,128)(2,1)S(1)}, bf16[4,1200,128]{2,1,0:T(8,128)(2,1)}, u32[]{:S(2)}) copy-start(bf16[4,1200,128]{2,1,0:T(8,128)(2,1)} %copy-done.3) | copy-start | bytes 3686404
  138.0 10.9 %collective-permute-start.13 = (bf16[1200,128]{1,0:T(8,128)(2,1)S(1)}, bf16[1200,128]{1,0:T(8,128)(2,1)S(1)}, u32[]{:S(2)}, u32[]{:S(2)}) collective-permute-start(bf16[1200,128]{1,0:T(8,128)(2,1)S(1)} %get-tuple-element.31), channel_id=1, source_target_pairs={{0,2},{1,3},{2,4},{3,5},{4,6},{5,7},{6,0},{7,1},{8,14},{9,15},{10,... | collective-permute-start | bytes 921608 | tf_op jit(solution)/shard_map/ppermute | solution.py:210
  140.5 19.8 %collective-permute-start.12 = (bf16[1200,128]{1,0:T(8,128)(2,1)S(1)}, bf16[1200,128]{1,0:T(8,128)(2,1)S(1)}, u32[]{:S(2)}, u32[]{:S(2)}) collective-permute-start(bf16[1200,128]{1,0:T(8,128)(2,1)S(1)} %get-tuple-element.30), channel_id=1, source_target_pairs={{0,6},{1,7},{2,0},{3,1},{4,2},{5,3},{6,4},{7,5},{8,10},{9,11},{10,... | collective-permute-start | bytes 921608 | tf_op jit(solution)/shard_map/ppermute | solution.py:211
  145.2 10.5 %collective-permute-start.6 = (bf16[1168,128]{1,0:T(8,128)(2,1)S(1)}, bf16[1168,128]{1,0:T(8,128)(2,1)S(1)}, u32[]{:S(2)}, u32[]{:S(2)}) collective-permute-start(bf16[1168,128]{1,0:T(8,128)(2,1)S(1)} %get-tuple-element.33), channel_id=1, source_target_pairs={{0,2},{1,3},{2,4},{3,5},{4,6},{5,7},{6,0},{7,1},{8,14},{9,15},{10,... | collective-permute-start | bytes 897032 | tf_op jit(solution)/shard_map/ppermute | solution.py:210
  149.9 11.9 %collective-permute-start.14 = (bf16[1200,128]{1,0:T(8,128)(2,1)S(1)}, bf16[1200,128]{1,0:T(8,128)(2,1)S(1)}, u32[]{:S(2)}, u32[]{:S(2)}) collective-permute-start(bf16[1200,128]{1,0:T(8,128)(2,1)S(1)} %fusion), channel_id=1, source_target_pairs={{0,2},{1,3},{2,4},{3,5},{4,6},{5,7},{6,0},{7,1},{8,14},{9,15},{10,... | collective-permute-start | bytes 921608 | tf_op jit(solution)/shard_map/ppermute | solution.py:212
  152.1 16.8 %collective-permute-start.5 = (bf16[1168,128]{1,0:T(8,128)(2,1)S(1)}, bf16[1168,128]{1,0:T(8,128)(2,1)S(1)}, u32[]{:S(2)}, u32[]{:S(2)}) collective-permute-start(bf16[1168,128]{1,0:T(8,128)(2,1)S(1)} %get-tuple-element.32), channel_id=1, source_target_pairs={{0,6},{1,7},{2,0},{3,1},{4,2},{5,3},{6,4},{7,5},{8,10},{9,11},{10,... | collective-permute-start | bytes 897032 | tf_op jit(solution)/shard_map/ppermute | solution.py:211
  156.9 12.1 %collective-permute-start.7 = (bf16[1168,128]{1,0:T(8,128)(2,1)S(1)}, bf16[1168,128]{1,0:T(8,128)(2,1)S(1)}, u32[]{:S(2)}, u32[]{:S(2)}) collective-permute-start(bf16[1168,128]{1,0:T(8,128)(2,1)S(1)} %fusion.3), channel_id=1, source_target_pairs={{0,2},{1,3},{2,4},{3,5},{4,6},{5,7},{6,0},{7,1},{8,14},{9,15},{10,... | collective-permute-start | bytes 897032 | tf_op jit(solution)/shard_map/ppermute | solution.py:212
  163.0 25.8 %collective-permute-start.15 = (bf16[1200,128]{1,0:T(8,128)(2,1)S(1)}, bf16[1200,128]{1,0:T(8,128)(2,1)S(1)}, u32[]{:S(2)}, u32[]{:S(2)}) collective-permute-start(bf16[1200,128]{1,0:T(8,128)(2,1)S(1)} %fusion.2), channel_id=1, source_target_pairs={{0,1},{1,0},{2,3},{3,2},{4,5},{5,4},{6,7},{7,6},{8,9},{9,8},{10,11... | collective-permute-start | bytes 921608 | tf_op jit(solution)/shard_map/ppermute | solution.py:302
  170.1 24.0 %collective-permute-start.8 = (bf16[1168,128]{1,0:T(8,128)(2,1)S(1)}, bf16[1168,128]{1,0:T(8,128)(2,1)S(1)}, u32[]{:S(2)}, u32[]{:S(2)}) collective-permute-start(bf16[1168,128]{1,0:T(8,128)(2,1)S(1)} %fusion.5), channel_id=1, source_target_pairs={{0,1},{1,0},{2,3},{3,2},{4,5},{5,4},{6,7},{7,6},{8,9},{9,8},{10,11... | collective-permute-start | bytes 897032 | tf_op jit(solution)/shard_map/ppermute | solution.py:303
  188.9 12.0 %collective-permute-start.16 = (bf16[1200,128]{1,0:T(8,128)(2,1)S(1)}, bf16[1200,128]{1,0:T(8,128)(2,1)S(1)}, u32[]{:S(2)}, u32[]{:S(2)}) collective-permute-start(bf16[1200,128]{1,0:T(8,128)(2,1)S(1)} %add_convert_fusion.refs_0_), channel_id=1, source_target_pairs={{0,2},{1,3},{2,4},{3,5},{4,6},{5,7},{6,0},{7,1},{8,14},{9,15},{10,... | collective-permute-start | bytes 921608 | tf_op jit(solution)/shard_map/ppermute | solution.py:217
  194.3 13.8 %collective-permute-start.9 = (bf16[1168,128]{1,0:T(8,128)(2,1)S(1)}, bf16[1168,128]{1,0:T(8,128)(2,1)S(1)}, u32[]{:S(2)}, u32[]{:S(2)}) collective-permute-start(bf16[1168,128]{1,0:T(8,128)(2,1)S(1)} %add_convert_fusion.3.refs_0_), channel_id=1, source_target_pairs={{0,2},{1,3},{2,4},{3,5},{4,6},{5,7},{6,0},{7,1},{8,14},{9,15},{10,... | collective-permute-start | bytes 897032 | tf_op jit(solution)/shard_map/ppermute | solution.py:217
  199.0 14.8 %collective-permute-start.17 = (bf16[1200,128]{1,0:T(8,128)(2,1)S(1)}, bf16[1200,128]{1,0:T(8,128)(2,1)S(1)}, u32[]{:S(2)}, u32[]{:S(2)}) collective-permute-start(bf16[1200,128]{1,0:T(8,128)(2,1)S(1)} %add_convert_fusion.refs_0_), channel_id=1, source_target_pairs={{0,6},{1,7},{2,0},{3,1},{4,2},{5,3},{6,4},{7,5},{8,10},{9,11},{10,... | collective-permute-start | bytes 921608 | tf_op jit(solution)/shard_map/ppermute | solution.py:218
  201.0 12.9 %collective-permute-start.18 = (bf16[1200,128]{1,0:T(8,128)(2,1)S(1)}, bf16[1200,128]{1,0:T(8,128)(2,1)S(1)}, u32[]{:S(2)}, u32[]{:S(2)}) collective-permute-start(bf16[1200,128]{1,0:T(8,128)(2,1)S(1)} %collective-permute-done.16.refs_1_), channel_id=1, source_target_pairs={{0,2},{1,3},{2,4},{3,5},{4,6},{5,7},{6,0},{7,1},{8,14},{9,15},{10,... | collective-permute-start | bytes 921608 | tf_op jit(solution)/shard_map/ppermute | solution.py:219
  206.2 13.0 %collective-permute-start.10 = (bf16[1168,128]{1,0:T(8,128)(2,1)S(1)}, bf16[1168,128]{1,0:T(8,128)(2,1)S(1)}, u32[]{:S(2)}, u32[]{:S(2)}) collective-permute-start(bf16[1168,128]{1,0:T(8,128)(2,1)S(1)} %add_convert_fusion.3.refs_0_), channel_id=1, source_target_pairs={{0,6},{1,7},{2,0},{3,1},{4,2},{5,3},{6,4},{7,5},{8,10},{9,11},{10,... | collective-permute-start | bytes 897032 | tf_op jit(solution)/shard_map/ppermute | solution.py:218
  208.1 11.1 %collective-permute-start.11 = (bf16[1168,128]{1,0:T(8,128)(2,1)S(1)}, bf16[1168,128]{1,0:T(8,128)(2,1)S(1)}, u32[]{:S(2)}, u32[]{:S(2)}) collective-permute-start(bf16[1168,128]{1,0:T(8,128)(2,1)S(1)} %collective-permute-done.9.refs_1_), channel_id=1, source_target_pairs={{0,2},{1,3},{2,4},{3,5},{4,6},{5,7},{6,0},{7,1},{8,14},{9,15},{10,... | collective-permute-start | bytes 897032 | tf_op jit(solution)/shard_map/ppermute | solution.py:219
